TPU v7x, 256 devices: a whole 4x4x8 slice. The times are simulated.
256 devices in a mesh: ctx: 32 (over x, z), tp: 8 (over y, core).
Axes of the slice: x: 4, y: 4, z: 8, core: 2. Of those that a mesh axis runs over, the one named last changes fastest.
Arguments:
- tokens: bfloat16 [16384, 4096], P(('ctx', 'tp')), may hold values from -6 to 6
- in_x: bfloat16 [4096, 4096], P(None, 'tp'), may hold values from -0.09375 to 0.09375
- in_bc: bfloat16 [4096, 256], replicated, may hold values from -0.09375 to 0.09375
- in_dt: bfloat16 [4096, 64], P(None, 'tp'), may hold values from -0.09375 to 0.09375
- conv_x: float32 [4, 4096], P(None, 'tp'), may hold values from -3 to 3
- conv_bc: float32 [4, 256], replicated, may hold values from -3 to 3
- dt_bias: float32 [64], P('tp'), may hold values from -7.5 to -3.5
- a_log: float32 [64], P('tp'), may hold values from -4.61 to 0.41
- skip_d: float32 [64], P('tp'), may hold values from 0.5 to 1.5
- norm_gain: float32 [4096], P('tp'), may hold values from 0.1 to 1.9
- out_w: bfloat16 [4096, 4096], P('tp'), may hold values from -0.09375 to 0.09375
Outputs:
- mixed: bfloat16 [16384, 4096], P(('ctx', 'tp'))
All inputs are finite; a program needn't handle non-finite values.
Results may differ from a plain program's by a relative error of at most 0.019.
Values may be sent and summed in bfloat16 or wider, within the bound.
No kernel may reach another device: no remote copies, remote signals or barrier semaphores. Data moves between devices by JAX's collectives and lax.ppermute only.
A program may use at most 64 MiB of HBM per device.

v0:
```python
import jax
import jax.numpy as jnp
from jax import lax
from jax.sharding import PartitionSpec as P

BLOCK = 256


def passed_along(shard, axis, by):
    devices = lax.axis_size(axis)
    pairs = [(i, i + by) for i in range(devices) if 0 <= i + by < devices]
    return lax.ppermute(shard, axis, pairs)


def causal_conv(prev, cur, kernel):
    ext = jnp.concatenate([prev, cur], 0).astype(jnp.float32)
    rows = cur.shape[0]
    taps = kernel.shape[0]
    total = kernel[0][None, :] * ext[0:rows]
    for k in range(1, taps):
        total = total + kernel[k][None, :] * ext[k : k + rows]
    return jax.nn.silu(total)


def ssd_block(state, xb, bb, cb, lab, dtb):
    hi = lax.Precision.HIGHEST
    length = lab.shape[0]
    cs = jnp.cumsum(lab, axis=0)
    cs_heads = cs.T
    scores = jnp.dot(cb, bb.T, precision=hi)
    diff = cs_heads[:, :, None] - cs_heads[:, None, :]
    later = lax.broadcasted_iota(jnp.int32, (length, length), 0)
    earlier = lax.broadcasted_iota(jnp.int32, (length, length), 1)
    tri = (later >= earlier)[None, :, :]
    decay = jnp.exp(jnp.where(tri, diff, -jnp.inf))
    xdt = xb * dtb[:, :, None]
    weighted = scores[None, :, :] * decay
    y_in = jnp.einsum("hts,shp->thp", weighted, xdt, precision=hi)
    y_st = jnp.exp(cs)[:, :, None] * jnp.einsum("tn,hpn->thp", cb, state, precision=hi)
    tail = jnp.exp(cs[-1][None, :] - cs)
    fresh = jnp.einsum("shp,sn->hpn", xdt * tail[:, :, None], bb, precision=hi)
    new_state = jnp.exp(cs[-1])[:, None, None] * state + fresh
    return (new_state, y_in + y_st, cs)


def per_device(
    tokens, in_x, in_bc, in_dt, conv_x, conv_bc, dt_bias, a_log, skip_d, norm_gain, out_w
):
    hi = lax.Precision.HIGHEST
    gathered = lax.all_gather(tokens, "tp", axis=0, tiled=True)
    bc_raw = jnp.dot(gathered, in_bc, preferred_element_type=jnp.float32).astype(jnp.bfloat16)
    x_raw = jnp.dot(gathered, in_x, preferred_element_type=jnp.float32).astype(jnp.bfloat16)
    dt_raw = jnp.dot(gathered, in_dt, preferred_element_type=jnp.float32)
    span_rows = gathered.shape[0]
    margin = conv_x.shape[0] - 1
    prev_x, prev_bc = passed_along(
        (x_raw[span_rows - margin :], bc_raw[span_rows - margin :]), "ctx", 1
    )
    x_conv = causal_conv(prev_x, x_raw, conv_x)
    bc_conv = causal_conv(prev_bc, bc_raw, conv_bc)
    states = in_bc.shape[1] // 2
    b_all = bc_conv[:, :states]
    c_all = bc_conv[:, states:]
    heads_here = a_log.shape[0]
    head_width = x_conv.shape[1] // heads_here
    step_dt = jax.nn.softplus(dt_raw + dt_bias[None, :])
    log_decay = -jnp.exp(a_log)[None, :] * step_dt
    blocks = span_rows // BLOCK

    def scan_step(carry, inputs):
        state, offset = carry
        xb, bb, cb, lab, dtb = inputs
        new_state, y_blk, cs = ssd_block(state, xb, bb, cb, lab, dtb)
        return ((new_state, offset + cs[-1]), (y_blk, cs + offset[None, :]))

    start = (
        jnp.zeros((heads_here, head_width, states), jnp.float32),
        jnp.zeros((heads_here,), jnp.float32),
    )
    (end_state, total_log), (y_blocks, cum_blocks) = lax.scan(
        scan_step,
        start,
        (
            x_conv.reshape(blocks, BLOCK, heads_here, head_width),
            b_all.reshape(blocks, BLOCK, states),
            c_all.reshape(blocks, BLOCK, states),
            log_decay.reshape(blocks, BLOCK, heads_here),
            step_dt.reshape(blocks, BLOCK, heads_here),
        ),
    )
    span_decay = jnp.exp(total_log)

    def relay(turn, incoming):
        outgoing = span_decay[:, None, None] * incoming + end_state
        return passed_along(outgoing, "ctx", 1)

    entering = lax.fori_loop(0, lax.axis_size("ctx") - 1, relay, jnp.zeros_like(end_state))
    cum_all = cum_blocks.reshape(span_rows, heads_here)
    x_flat = x_conv.reshape(span_rows, heads_here, head_width)
    carried = jnp.exp(cum_all)[:, :, None] * jnp.einsum(
        "tn,hpn->thp", c_all, entering, precision=hi
    )
    y_all = (
        y_blocks.reshape(span_rows, heads_here, head_width)
        + carried
        + skip_d[None, :, None] * x_flat
    )
    mean_sq = jnp.mean(y_all * y_all, axis=-1, keepdims=True)
    normed = (
        (y_all * lax.rsqrt(mean_sq + 1e-05) * norm_gain.reshape(heads_here, head_width)[None])
        .reshape(span_rows, heads_here * head_width)
        .astype(jnp.bfloat16)
    )
    return lax.psum_scatter(
        jnp.dot(normed, out_w, preferred_element_type=jnp.float32).astype(jnp.bfloat16),
        "tp",
        scatter_dimension=0,
        tiled=True,
    )


def solution(mesh):
    return jax.shard_map(
        per_device,
        mesh=mesh,
        in_specs=(
            P(("ctx", "tp"), None),
            P(None, "tp"),
            P(),
            P(None, "tp"),
            P(None, "tp"),
            P(),
            P("tp"),
            P("tp"),
            P("tp"),
            P("tp"),
            P("tp", None),
        ),
        out_specs=P(("ctx", "tp"), None),
        check_vma=False,
    )
```

profile of v0, /device:TPU:32, one launch (start us, length us, event | category | flops | bytes accessed | tf_op | source)
XLA Modules:
  0.0 516.1 jit_solution(15587162299473158658)
XLA Ops:
  10.5 36.1 %all-gather.2.cloned.1.call-done = bf16[512,4096]{1,0:T(8,128)(2,1)} async-done(((bf16[64,4096]{1,0:T(8,128)(2,1)}), bf16[512,4096]{1,0:T(8,128)(2,1)}) %all-gather.2.cloned.1.call-update) | async-done | bytes 4194320 | tf_op jit(solution)/shard_map/all_gather | solution.py:50
  71.3 42.9 %while.28 = (s32[]{:T(128)}, f32[8,64,128]{2,1,0:T(8,128)S(1)}, f32[8]{0:T(128)S(1)}, f32[2,256,8,64]{1,0,3,2:T(2,128)}, f32[2,256,8]{1,2,0:T(8,128)S(1)}, /*ind...) while((s32[]{:T(128)}, f32[8,64,128]{2,1,0:T(8,128)S(1)}, ...), condition=%wide.region_3.4_spmd.clone, body=%wide.region_0.3_spmd.clone.sunk | while | flops 908793920 | bytes 7902669 | solution.py:80
  81.3 11.5 %dynamic_update_slice.14 = f32[2,256,8,64]{1,0,3,2:T(2,128)} dynamic-update-slice(f32[2,256,8,64]{1,0,3,2:T(2,128)} %get-tuple-element.312, f32[1,256,8,64]{1,0,3,2:T(1,128)S(1)} %copy.34, s32[]{:T(128)S(6)} %copy.42, s32[]{:T(128)} %constant.32.clone.1..sunk, s32[]{:T(128)} %constant.32.clone.1..sunk, s32[]{:T(128)} %constant.32.clone.1..sunk) | dynamic-update-slice | bytes 1048580 | tf_op jit(solution)/shard_map/while/body/jit(dynamic_update_index_in_dim)/dynamic_update_slice | solution.py:80
  102.7 11.5 %dynamic_update_slice.14 = f32[2,256,8,64]{1,0,3,2:T(2,128)} dynamic-update-slice(f32[2,256,8,64]{1,0,3,2:T(2,128)} %get-tuple-element.312, f32[1,256,8,64]{1,0,3,2:T(1,128)S(1)} %copy.34, s32[]{:T(128)S(6)} %copy.42, s32[]{:T(128)} %constant.32.clone.1..sunk, s32[]{:T(128)} %constant.32.clone.1..sunk, s32[]{:T(128)} %constant.32.clone.1..sunk) | dynamic-update-slice | bytes 1048580 | tf_op jit(solution)/shard_map/while/body/jit(dynamic_update_index_in_dim)/dynamic_update_slice | solution.py:80
  117.4 326.4 %while.27 = (s32[]{:T(128)}, f32[8,64,128]{2,1,0:T(8,128)S(1)}, f32[8]{0:T(128)S(1)}, f32[8,64,128]{2,1,0:T(8,128)S(1)}, s32[]{:T(128)}) while((s32[]{:T(128)}, f32[8,64,128]{2,1,0:T(8,128)S(1)}, f32[8]{0:T(128)S(1)}, f32[8,64,128]{2,1,0:T(8,128)S(1)}, s32[]{:T(128)}) %tuple.59), condition=%wide.region_5.6_spmd, body=%wide.region_4.5_spmd.sunk | while | flops 131074 | bytes 1835141 | solution.py:97
  178.2 6.4 %collective-permute-done = f32[8,64,128]{2,1,0:T(8,128)S(1)} collective-permute-done((f32[8,64,128]{2,1,0:T(8,128)S(1)}, f32[8,64,128]{2,1,0:T(8,128)S(1)}, u32[]{:S(2)}, u32[]{:S(2)}) %collective-permute-start) | collective-permute-done | bytes 262176 | tf_op jit(solution)/shard_map/while/body/eval_jaxpr/ppermute | solution.py:12
  184.7 6.2 %collective-permute-start = (f32[8,64,128]{2,1,0:T(8,128)S(1)}, f32[8,64,128]{2,1,0:T(8,128)S(1)}, u32[]{:S(2)}, u32[]{:S(2)}) collective-permute-start(f32[8,64,128]{2,1,0:T(8,128)S(1)} %multiply_add_fusion.2), channel_id=1, source_target_pairs={{0,8},{8,16},{16,24},{24,32},{32,40},{40,48},{48,56},{56,64},{64,7... | collective-permute-start | bytes 786440 | tf_op jit(solution)/shard_map/while/body/eval_jaxpr/ppermute | solution.py:12
  245.0 6.0 %collective-permute-start = (f32[8,64,128]{2,1,0:T(8,128)S(1)}, f32[8,64,128]{2,1,0:T(8,128)S(1)}, u32[]{:S(2)}, u32[]{:S(2)}) collective-permute-start(f32[8,64,128]{2,1,0:T(8,128)S(1)} %multiply_add_fusion.2), channel_id=1, source_target_pairs={{0,8},{8,16},{16,24},{24,32},{32,40},{40,48},{48,56},{56,64},{64,7... | collective-permute-start | bytes 786440 | tf_op jit(solution)/shard_map/while/body/eval_jaxpr/ppermute | solution.py:12
  256.1 6.2 %collective-permute-start = (f32[8,64,128]{2,1,0:T(8,128)S(1)}, f32[8,64,128]{2,1,0:T(8,128)S(1)}, u32[]{:S(2)}, u32[]{:S(2)}) collective-permute-start(f32[8,64,128]{2,1,0:T(8,128)S(1)} %multiply_add_fusion.2), channel_id=1, source_target_pairs={{0,8},{8,16},{16,24},{24,32},{32,40},{40,48},{48,56},{56,64},{64,7... | collective-permute-start | bytes 786440 | tf_op jit(solution)/shard_map/while/body/eval_jaxpr/ppermute | solution.py:12
  262.3 6.3 %collective-permute-done = f32[8,64,128]{2,1,0:T(8,128)S(1)} collective-permute-done((f32[8,64,128]{2,1,0:T(8,128)S(1)}, f32[8,64,128]{2,1,0:T(8,128)S(1)}, u32[]{:S(2)}, u32[]{:S(2)}) %collective-permute-start) | collective-permute-done | bytes 262176 | tf_op jit(solution)/shard_map/while/body/eval_jaxpr/ppermute | solution.py:12
  268.7 6.2 %collective-permute-start = (f32[8,64,128]{2,1,0:T(8,128)S(1)}, f32[8,64,128]{2,1,0:T(8,128)S(1)}, u32[]{:S(2)}, u32[]{:S(2)}) collective-permute-start(f32[8,64,128]{2,1,0:T(8,128)S(1)} %multiply_add_fusion.2), channel_id=1, source_target_pairs={{0,8},{8,16},{16,24},{24,32},{32,40},{40,48},{48,56},{56,64},{64,7... | collective-permute-start | bytes 786440 | tf_op jit(solution)/shard_map/while/body/eval_jaxpr/ppermute | solution.py:12
  274.9 6.0 %collective-permute-done = f32[8,64,128]{2,1,0:T(8,128)S(1)} collective-permute-done((f32[8,64,128]{2,1,0:T(8,128)S(1)}, f32[8,64,128]{2,1,0:T(8,128)S(1)}, u32[]{:S(2)}, u32[]{:S(2)}) %collective-permute-start) | collective-permute-done | bytes 262176 | tf_op jit(solution)/shard_map/while/body/eval_jaxpr/ppermute | solution.py:12
  310.3 6.4 %collective-permute-start = (f32[8,64,128]{2,1,0:T(8,128)S(1)}, f32[8,64,128]{2,1,0:T(8,128)S(1)}, u32[]{:S(2)}, u32[]{:S(2)}) collective-permute-start(f32[8,64,128]{2,1,0:T(8,128)S(1)} %multiply_add_fusion.2), channel_id=1, source_target_pairs={{0,8},{8,16},{16,24},{24,32},{32,40},{40,48},{48,56},{56,64},{64,7... | collective-permute-start | bytes 786440 | tf_op jit(solution)/shard_map/while/body/eval_jaxpr/ppermute | solution.py:12
  320.7 7.8 %collective-permute-start = (f32[8,64,128]{2,1,0:T(8,128)S(1)}, f32[8,64,128]{2,1,0:T(8,128)S(1)}, u32[]{:S(2)}, u32[]{:S(2)}) collective-permute-start(f32[8,64,128]{2,1,0:T(8,128)S(1)} %multiply_add_fusion.2), channel_id=1, source_target_pairs={{0,8},{8,16},{16,24},{24,32},{32,40},{40,48},{48,56},{56,64},{64,7... | collective-permute-start | bytes 786440 | tf_op jit(solution)/shard_map/while/body/eval_jaxpr/ppermute | solution.py:12
  351.8 6.4 %collective-permute-start = (f32[8,64,128]{2,1,0:T(8,128)S(1)}, f32[8,64,128]{2,1,0:T(8,128)S(1)}, u32[]{:S(2)}, u32[]{:S(2)}) collective-permute-start(f32[8,64,128]{2,1,0:T(8,128)S(1)} %multiply_add_fusion.2), channel_id=1, source_target_pairs={{0,8},{8,16},{16,24},{24,32},{32,40},{40,48},{48,56},{56,64},{64,7... | collective-permute-start | bytes 786440 | tf_op jit(solution)/shard_map/while/body/eval_jaxpr/ppermute | solution.py:12
  362.4 6.3 %collective-permute-start = (f32[8,64,128]{2,1,0:T(8,128)S(1)}, f32[8,64,128]{2,1,0:T(8,128)S(1)}, u32[]{:S(2)}, u32[]{:S(2)}) collective-permute-start(f32[8,64,128]{2,1,0:T(8,128)S(1)} %multiply_add_fusion.2), channel_id=1, source_target_pairs={{0,8},{8,16},{16,24},{24,32},{32,40},{40,48},{48,56},{56,64},{64,7... | collective-permute-start | bytes 786440 | tf_op jit(solution)/shard_map/while/body/eval_jaxpr/ppermute | solution.py:12
  373.5 7.1 %collective-permute-start = (f32[8,64,128]{2,1,0:T(8,128)S(1)}, f32[8,64,128]{2,1,0:T(8,128)S(1)}, u32[]{:S(2)}, u32[]{:S(2)}) collective-permute-start(f32[8,64,128]{2,1,0:T(8,128)S(1)} %multiply_add_fusion.2), channel_id=1, source_target_pairs={{0,8},{8,16},{16,24},{24,32},{32,40},{40,48},{48,56},{56,64},{64,7... | collective-permute-start | bytes 786440 | tf_op jit(solution)/shard_map/while/body/eval_jaxpr/ppermute | solution.py:12
  386.5 7.5 %collective-permute-start = (f32[8,64,128]{2,1,0:T(8,128)S(1)}, f32[8,64,128]{2,1,0:T(8,128)S(1)}, u32[]{:S(2)}, u32[]{:S(2)}) collective-permute-start(f32[8,64,128]{2,1,0:T(8,128)S(1)} %multiply_add_fusion.2), channel_id=1, source_target_pairs={{0,8},{8,16},{16,24},{24,32},{32,40},{40,48},{48,56},{56,64},{64,7... | collective-permute-start | bytes 786440 | tf_op jit(solution)/shard_map/while/body/eval_jaxpr/ppermute | solution.py:12
  393.9 6.3 %collective-permute-done = f32[8,64,128]{2,1,0:T(8,128)S(1)} collective-permute-done((f32[8,64,128]{2,1,0:T(8,128)S(1)}, f32[8,64,128]{2,1,0:T(8,128)S(1)}, u32[]{:S(2)}, u32[]{:S(2)}) %collective-permute-start) | collective-permute-done | bytes 262176 | tf_op jit(solution)/shard_map/while/body/eval_jaxpr/ppermute | solution.py:12
  400.4 6.9 %collective-permute-start = (f32[8,64,128]{2,1,0:T(8,128)S(1)}, f32[8,64,128]{2,1,0:T(8,128)S(1)}, u32[]{:S(2)}, u32[]{:S(2)}) collective-permute-start(f32[8,64,128]{2,1,0:T(8,128)S(1)} %multiply_add_fusion.2), channel_id=1, source_target_pairs={{0,8},{8,16},{16,24},{24,32},{32,40},{40,48},{48,56},{56,64},{64,7... | collective-permute-start | bytes 786440 | tf_op jit(solution)/shard_map/while/body/eval_jaxpr/ppermute | solution.py:12
  412.8 7.0 %collective-permute-start = (f32[8,64,128]{2,1,0:T(8,128)S(1)}, f32[8,64,128]{2,1,0:T(8,128)S(1)}, u32[]{:S(2)}, u32[]{:S(2)}) collective-permute-start(f32[8,64,128]{2,1,0:T(8,128)S(1)} %multiply_add_fusion.2), channel_id=1, source_target_pairs={{0,8},{8,16},{16,24},{24,32},{32,40},{40,48},{48,56},{56,64},{64,7... | collective-permute-start | bytes 786440 | tf_op jit(solution)/shard_map/while/body/eval_jaxpr/ppermute | solution.py:12
  423.8 6.3 %collective-permute-start = (f32[8,64,128]{2,1,0:T(8,128)S(1)}, f32[8,64,128]{2,1,0:T(8,128)S(1)}, u32[]{:S(2)}, u32[]{:S(2)}) collective-permute-start(f32[8,64,128]{2,1,0:T(8,128)S(1)} %multiply_add_fusion.2), channel_id=1, source_target_pairs={{0,8},{8,16},{16,24},{24,32},{32,40},{40,48},{48,56},{56,64},{64,7... | collective-permute-start | bytes 786440 | tf_op jit(solution)/shard_map/while/body/eval_jaxpr/ppermute | solution.py:12
  434.0 5.9 %collective-permute-start = (f32[8,64,128]{2,1,0:T(8,128)S(1)}, f32[8,64,128]{2,1,0:T(8,128)S(1)}, u32[]{:S(2)}, u32[]{:S(2)}) collective-permute-start(f32[8,64,128]{2,1,0:T(8,128)S(1)} %multiply_add_fusion.2), channel_id=1, source_target_pairs={{0,8},{8,16},{16,24},{24,32},{32,40},{40,48},{48,56},{56,64},{64,7... | collective-permute-start | bytes 786440 | tf_op jit(solution)/shard_map/while/body/eval_jaxpr/ppermute | solution.py:12
  451.2 58.0 %reduce-scatter.2.cloned.1.call-done = bf16[64,4096]{1,0:T(8,128)(2,1)} async-done(((bf16[512,4096]{1,0:T(8,128)(2,1)}), bf16[64,4096]{1,0:T(8,128)(2,1)}) %reduce-scatter.2.cloned.1.call-update) | async-done | bytes 524304 | tf_op jit(solution)/shard_map/reduce_scatter | solution.py:114
  (168 shorter events, 267.4 us)
Async XLA Ops:
  6.5 40.0 %all-gather.2.cloned.1.call-start = ((), (), s32[]{:S(2)}) async-start(), calls=%async_computation.1 | async-start | bytes 4718592 | tf_op jit(solution)/shard_map/all_gather | solution.py:50
  7.3 502.0 %reduce-scatter.2.cloned.1.call-start = ((), (), s32[]{:S(2)}) async-start(), calls=%async_computation.2 | async-start | bytes 4718592 | tf_op jit(solution)/shard_map/reduce_scatter | solution.py:114
  117.5 10.1 %collective-permute-start = (f32[8,64,128]{2,1,0:T(8,128)S(1)}, f32[8,64,128]{2,1,0:T(8,128)S(1)}, u32[]{:S(2)}, u32[]{:S(2)}) collective-permute-start(f32[8,64,128]{2,1,0:T(8,128)S(1)} %multiply_add_fusion.2), channel_id=1, source_target_pairs={{0,8},{8,16},{16,24},{24,32},{32,40},{40,48},{48,56},{56,64},{64,7... | collective-permute-start | bytes 786440 | tf_op jit(solution)/shard_map/while/body/eval_jaxpr/ppermute | solution.py:12
  162.7 10.0 %collective-permute-start = (f32[8,64,128]{2,1,0:T(8,128)S(1)}, f32[8,64,128]{2,1,0:T(8,128)S(1)}, u32[]{:S(2)}, u32[]{:S(2)}) collective-permute-start(f32[8,64,128]{2,1,0:T(8,128)S(1)} %multiply_add_fusion.2), channel_id=1, source_target_pairs={{0,8},{8,16},{16,24},{24,32},{32,40},{40,48},{48,56},{56,64},{64,7... | collective-permute-start | bytes 786440 | tf_op jit(solution)/shard_map/while/body/eval_jaxpr/ppermute | solution.py:12
  172.8 11.8 %collective-permute-start = (f32[8,64,128]{2,1,0:T(8,128)S(1)}, f32[8,64,128]{2,1,0:T(8,128)S(1)}, u32[]{:S(2)}, u32[]{:S(2)}) collective-permute-start(f32[8,64,128]{2,1,0:T(8,128)S(1)} %multiply_add_fusion.2), channel_id=1, source_target_pairs={{0,8},{8,16},{16,24},{24,32},{32,40},{40,48},{48,56},{56,64},{64,7... | collective-permute-start | bytes 786440 | tf_op jit(solution)/shard_map/while/body/eval_jaxpr/ppermute | solution.py:12
  184.7 12.0 %collective-permute-start = (f32[8,64,128]{2,1,0:T(8,128)S(1)}, f32[8,64,128]{2,1,0:T(8,128)S(1)}, u32[]{:S(2)}, u32[]{:S(2)}) collective-permute-start(f32[8,64,128]{2,1,0:T(8,128)S(1)} %multiply_add_fusion.2), channel_id=1, source_target_pairs={{0,8},{8,16},{16,24},{24,32},{32,40},{40,48},{48,56},{56,64},{64,7... | collective-permute-start | bytes 786440 | tf_op jit(solution)/shard_map/while/body/eval_jaxpr/ppermute | solution.py:12
  196.8 9.8 %collective-permute-start = (f32[8,64,128]{2,1,0:T(8,128)S(1)}, f32[8,64,128]{2,1,0:T(8,128)S(1)}, u32[]{:S(2)}, u32[]{:S(2)}) collective-permute-start(f32[8,64,128]{2,1,0:T(8,128)S(1)} %multiply_add_fusion.2), channel_id=1, source_target_pairs={{0,8},{8,16},{16,24},{24,32},{32,40},{40,48},{48,56},{56,64},{64,7... | collective-permute-start | bytes 786440 | tf_op jit(solution)/shard_map/while/body/eval_jaxpr/ppermute | solution.py:12
  225.8 9.5 %collective-permute-start = (f32[8,64,128]{2,1,0:T(8,128)S(1)}, f32[8,64,128]{2,1,0:T(8,128)S(1)}, u32[]{:S(2)}, u32[]{:S(2)}) collective-permute-start(f32[8,64,128]{2,1,0:T(8,128)S(1)} %multiply_add_fusion.2), channel_id=1, source_target_pairs={{0,8},{8,16},{16,24},{24,32},{32,40},{40,48},{48,56},{56,64},{64,7... | collective-permute-start | bytes 786440 | tf_op jit(solution)/shard_map/while/body/eval_jaxpr/ppermute | solution.py:12
  245.0 11.0 %collective-permute-start = (f32[8,64,128]{2,1,0:T(8,128)S(1)}, f32[8,64,128]{2,1,0:T(8,128)S(1)}, u32[]{:S(2)}, u32[]{:S(2)}) collective-permute-start(f32[8,64,128]{2,1,0:T(8,128)S(1)} %multiply_add_fusion.2), channel_id=1, source_target_pairs={{0,8},{8,16},{16,24},{24,32},{32,40},{40,48},{48,56},{56,64},{64,7... | collective-permute-start | bytes 786440 | tf_op jit(solution)/shard_map/while/body/eval_jaxpr/ppermute | solution.py:12
  256.1 12.5 %collective-permute-start = (f32[8,64,128]{2,1,0:T(8,128)S(1)}, f32[8,64,128]{2,1,0:T(8,128)S(1)}, u32[]{:S(2)}, u32[]{:S(2)}) collective-permute-start(f32[8,64,128]{2,1,0:T(8,128)S(1)} %multiply_add_fusion.2), channel_id=1, source_target_pairs={{0,8},{8,16},{16,24},{24,32},{32,40},{40,48},{48,56},{56,64},{64,7... | collective-permute-start | bytes 786440 | tf_op jit(solution)/shard_map/while/body/eval_jaxpr/ppermute | solution.py:12
  268.7 12.2 %collective-permute-start = (f32[8,64,128]{2,1,0:T(8,128)S(1)}, f32[8,64,128]{2,1,0:T(8,128)S(1)}, u32[]{:S(2)}, u32[]{:S(2)}) collective-permute-start(f32[8,64,128]{2,1,0:T(8,128)S(1)} %multiply_add_fusion.2), channel_id=1, source_target_pairs={{0,8},{8,16},{16,24},{24,32},{32,40},{40,48},{48,56},{56,64},{64,7... | collective-permute-start | bytes 786440 | tf_op jit(solution)/shard_map/while/body/eval_jaxpr/ppermute | solution.py:12
  281.0 10.0 %collective-permute-start = (f32[8,64,128]{2,1,0:T(8,128)S(1)}, f32[8,64,128]{2,1,0:T(8,128)S(1)}, u32[]{:S(2)}, u32[]{:S(2)}) collective-permute-start(f32[8,64,128]{2,1,0:T(8,128)S(1)} %multiply_add_fusion.2), channel_id=1, source_target_pairs={{0,8},{8,16},{16,24},{24,32},{32,40},{40,48},{48,56},{56,64},{64,7... | collective-permute-start | bytes 786440 | tf_op jit(solution)/shard_map/while/body/eval_jaxpr/ppermute | solution.py:12
  291.1 9.5 %collective-permute-start = (f32[8,64,128]{2,1,0:T(8,128)S(1)}, f32[8,64,128]{2,1,0:T(8,128)S(1)}, u32[]{:S(2)}, u32[]{:S(2)}) collective-permute-start(f32[8,64,128]{2,1,0:T(8,128)S(1)} %multiply_add_fusion.2), channel_id=1, source_target_pairs={{0,8},{8,16},{16,24},{24,32},{32,40},{40,48},{48,56},{56,64},{64,7... | collective-permute-start | bytes 786440 | tf_op jit(solution)/shard_map/while/body/eval_jaxpr/ppermute | solution.py:12
  310.3 10.3 %collective-permute-start = (f32[8,64,128]{2,1,0:T(8,128)S(1)}, f32[8,64,128]{2,1,0:T(8,128)S(1)}, u32[]{:S(2)}, u32[]{:S(2)}) collective-permute-start(f32[8,64,128]{2,1,0:T(8,128)S(1)} %multiply_add_fusion.2), channel_id=1, source_target_pairs={{0,8},{8,16},{16,24},{24,32},{32,40},{40,48},{48,56},{56,64},{64,7... | collective-permute-start | bytes 786440 | tf_op jit(solution)/shard_map/while/body/eval_jaxpr/ppermute | solution.py:12
  320.7 11.6 %collective-permute-start = (f32[8,64,128]{2,1,0:T(8,128)S(1)}, f32[8,64,128]{2,1,0:T(8,128)S(1)}, u32[]{:S(2)}, u32[]{:S(2)}) collective-permute-start(f32[8,64,128]{2,1,0:T(8,128)S(1)} %multiply_add_fusion.2), channel_id=1, source_target_pairs={{0,8},{8,16},{16,24},{24,32},{32,40},{40,48},{48,56},{56,64},{64,7... | collective-permute-start | bytes 786440 | tf_op jit(solution)/shard_map/while/body/eval_jaxpr/ppermute | solution.py:12
  332.4 9.8 %collective-permute-start = (f32[8,64,128]{2,1,0:T(8,128)S(1)}, f32[8,64,128]{2,1,0:T(8,128)S(1)}, u32[]{:S(2)}, u32[]{:S(2)}) collective-permute-start(f32[8,64,128]{2,1,0:T(8,128)S(1)} %multiply_add_fusion.2), channel_id=1, source_target_pairs={{0,8},{8,16},{16,24},{24,32},{32,40},{40,48},{48,56},{56,64},{64,7... | collective-permute-start | bytes 786440 | tf_op jit(solution)/shard_map/while/body/eval_jaxpr/ppermute | solution.py:12
  351.8 10.5 %collective-permute-start = (f32[8,64,128]{2,1,0:T(8,128)S(1)}, f32[8,64,128]{2,1,0:T(8,128)S(1)}, u32[]{:S(2)}, u32[]{:S(2)}) collective-permute-start(f32[8,64,128]{2,1,0:T(8,128)S(1)} %multiply_add_fusion.2), channel_id=1, source_target_pairs={{0,8},{8,16},{16,24},{24,32},{32,40},{40,48},{48,56},{56,64},{64,7... | collective-permute-start | bytes 786440 | tf_op jit(solution)/shard_map/while/body/eval_jaxpr/ppermute | solution.py:12
  362.4 11.0 %collective-permute-start = (f32[8,64,128]{2,1,0:T(8,128)S(1)}, f32[8,64,128]{2,1,0:T(8,128)S(1)}, u32[]{:S(2)}, u32[]{:S(2)}) collective-permute-start(f32[8,64,128]{2,1,0:T(8,128)S(1)} %multiply_add_fusion.2), channel_id=1, source_target_pairs={{0,8},{8,16},{16,24},{24,32},{32,40},{40,48},{48,56},{56,64},{64,7... | collective-permute-start | bytes 786440 | tf_op jit(solution)/shard_map/while/body/eval_jaxpr/ppermute | solution.py:12
  373.5 12.9 %collective-permute-start = (f32[8,64,128]{2,1,0:T(8,128)S(1)}, f32[8,64,128]{2,1,0:T(8,128)S(1)}, u32[]{:S(2)}, u32[]{:S(2)}) collective-permute-start(f32[8,64,128]{2,1,0:T(8,128)S(1)} %multiply_add_fusion.2), channel_id=1, source_target_pairs={{0,8},{8,16},{16,24},{24,32},{32,40},{40,48},{48,56},{56,64},{64,7... | collective-permute-start | bytes 786440 | tf_op jit(solution)/shard_map/while/body/eval_jaxpr/ppermute | solution.py:12
  386.5 13.8 %collective-permute-start = (f32[8,64,128]{2,1,0:T(8,128)S(1)}, f32[8,64,128]{2,1,0:T(8,128)S(1)}, u32[]{:S(2)}, u32[]{:S(2)}) collective-permute-start(f32[8,64,128]{2,1,0:T(8,128)S(1)} %multiply_add_fusion.2), channel_id=1, source_target_pairs={{0,8},{8,16},{16,24},{24,32},{32,40},{40,48},{48,56},{56,64},{64,7... | collective-permute-start | bytes 786440 | tf_op jit(solution)/shard_map/while/body/eval_jaxpr/ppermute | solution.py:12
  400.4 12.3 %collective-permute-start = (f32[8,64,128]{2,1,0:T(8,128)S(1)}, f32[8,64,128]{2,1,0:T(8,128)S(1)}, u32[]{:S(2)}, u32[]{:S(2)}) collective-permute-start(f32[8,64,128]{2,1,0:T(8,128)S(1)} %multiply_add_fusion.2), channel_id=1, source_target_pairs={{0,8},{8,16},{16,24},{24,32},{32,40},{40,48},{48,56},{56,64},{64,7... | collective-permute-start | bytes 786440 | tf_op jit(solution)/shard_map/while/body/eval_jaxpr/ppermute | solution.py:12
  412.8 10.9 %collective-permute-start = (f32[8,64,128]{2,1,0:T(8,128)S(1)}, f32[8,64,128]{2,1,0:T(8,128)S(1)}, u32[]{:S(2)}, u32[]{:S(2)}) collective-permute-start(f32[8,64,128]{2,1,0:T(8,128)S(1)} %multiply_add_fusion.2), channel_id=1, source_target_pairs={{0,8},{8,16},{16,24},{24,32},{32,40},{40,48},{48,56},{56,64},{64,7... | collective-permute-start | bytes 786440 | tf_op jit(solution)/shard_map/while/body/eval_jaxpr/ppermute | solution.py:12
  423.8 10.1 %collective-permute-start = (f32[8,64,128]{2,1,0:T(8,128)S(1)}, f32[8,64,128]{2,1,0:T(8,128)S(1)}, u32[]{:S(2)}, u32[]{:S(2)}) collective-permute-start(f32[8,64,128]{2,1,0:T(8,128)S(1)} %multiply_add_fusion.2), channel_id=1, source_target_pairs={{0,8},{8,16},{16,24},{24,32},{32,40},{40,48},{48,56},{56,64},{64,7... | collective-permute-start | bytes 786440 | tf_op jit(solution)/shard_map/while/body/eval_jaxpr/ppermute | solution.py:12
  434.0 9.8 %collective-permute-start = (f32[8,64,128]{2,1,0:T(8,128)S(1)}, f32[8,64,128]{2,1,0:T(8,128)S(1)}, u32[]{:S(2)}, u32[]{:S(2)}) collective-permute-start(f32[8,64,128]{2,1,0:T(8,128)S(1)} %multiply_add_fusion.2), channel_id=1, source_target_pairs={{0,8},{8,16},{16,24},{24,32},{32,40},{40,48},{48,56},{56,64},{64,7... | collective-permute-start | bytes 786440 | tf_op jit(solution)/shard_map/while/body/eval_jaxpr/ppermute | solution.py:12
  (21 other events, 842.6 us)
Sparse Core Ops, SparseCore 0:
  9.2 37.2 all-gather.1
  451.3 57.8 reduce-scatter.1
where the time goes:
time: 519 us; the launch traced here: 516 us
  waiting for transfers between devices  238 us (46%)
  starting transfers between devices  187 us (36%)
  local copies, waits for them, and re-layouts  37.7 us (7%)
  matrix products  32.6 us (6%)
  between operations  13.6 us (3%)
  other arithmetic  6.59 us (1%)
    ppermute x33, starting transfers between devices, passed_along(): return lax.ppermute(shard, axis, pairs)  187 us
    ppermute x33, waiting for transfers between devices, passed_along(): return lax.ppermute(shard, axis, pairs)  143 us
    reduce_scatter x1, waiting for transfers between devices, per_device(): lax.psum_scatter(jnp.dot(normed, out_w, preferred_element_type=jnp.float3...  58 us
    all_gather x1, waiting for transfers between devices, per_device(): gathered = lax.all_gather(tokens, 'tp', axis=0, tiled=True)  36.1 us
    dynamic_update_slice x4, local copies, waits for them, and re-layouts, per_device(): lax.scan(scan_step, start, (x_conv.reshape(blocks, BLOCK, heads_here, hea...  24.2 us
  transfers between devices with their start and end apart: 35, of which 33 were waited for; matrix products, arithmetic and copies ran while one was open for 1% of the time, Pallas kernels for 0%

commit v1 on v0

v1 whole, which is shorter than its diff:
```python
import functools

import jax
import jax.numpy as jnp
from jax import lax
from jax.experimental import pallas as pl
from jax.experimental.pallas import tpu as pltpu
from jax.sharding import PartitionSpec as P

BF = jnp.bfloat16
F32 = jnp.float32
VMEM = pl.BlockSpec(memory_space=pltpu.VMEM)
SMEM = pl.BlockSpec(memory_space=pltpu.SMEM)
LIMIT = 56 * 1024 * 1024

Q = 128
NQ = 4
HH = 8
HD = 64
NS = 128
CH = 512
BCW = 256


def params():
    return pltpu.CompilerParams(vmem_limit_bytes=LIMIT)


def dot_tn(a, b):
    return lax.dot_general(a, b, (((0,), (0,)), ((), ())), preferred_element_type=F32)


def dot_nt(a, b):
    return lax.dot_general(a, b, (((1,), (1,)), ((), ())), preferred_element_type=F32)


def two_parts(v):
    hi = v.astype(BF)
    return hi, (v - hi.astype(F32)).astype(BF)


def head_spread():
    row = lax.broadcasted_iota(jnp.int32, (2 * HH, CH), 0)
    lane = lax.broadcasted_iota(jnp.int32, (2 * HH, CH), 1)
    return jnp.where(lane // HD == row % HH, 1.0, 0.0).astype(BF)


def spread(v, ones):
    hi, lo = two_parts(v)
    both = jnp.concatenate([hi.astype(F32), lo.astype(F32)], 0).astype(BF)
    return dot_tn(both, ones)


def project_kernel(n_own, idx, *refs):
    own, other = refs[:n_own], refs[n_own : 2 * n_own]
    wx, wbc, wdt, xo, bco, dto, tok = refs[2 * n_own :]
    core = idx[1]
    for group, half in ((own, core), (other, 1 - core)):
        at = half * 64
        step = 64 // n_own
        for j, r in enumerate(group):
            tok[pl.ds(pl.multiple_of(at + j * step, step), step), :] = r[...]
    rows = tok[...]
    xo[...] = jnp.dot(rows, wx[...], preferred_element_type=F32).astype(BF)
    bco[...] = jnp.dot(rows, wbc[...], preferred_element_type=F32).astype(BF)
    dt = jnp.dot(rows, wdt[...], preferred_element_type=F32)
    dto[...] = dt.T


def project(idx, own, other, in_x, in_bc, in_dt, name):
    n_own = len(own)
    return pl.pallas_call(
        functools.partial(project_kernel, n_own),
        out_shape=(
            jax.ShapeDtypeStruct((Q, CH), BF),
            jax.ShapeDtypeStruct((Q, BCW), BF),
            jax.ShapeDtypeStruct((HH, Q), F32),
        ),
        in_specs=[SMEM] + [VMEM] * (2 * n_own + 3),
        out_specs=(VMEM, VMEM, VMEM),
        scratch_shapes=[pltpu.VMEM((Q, 4096), BF)],
        compiler_params=params(),
        name=name,
    )(idx, *own, *other, in_x, in_bc, in_dt)


def silu(v):
    return v / (1.0 + jnp.exp(-v))


def softplus(v):
    return jnp.maximum(v, 0.0) + jnp.log1p(jnp.exp(-jnp.abs(v)))


OFFS = (0, 3, 1, 2)


def local_kernel(idx, *refs):
    xs, bcs, dts = refs[0:4], refs[4:8], refs[8:12]
    (hx, hbc, kx, kbc, bias, alog) = refs[12:18]
    (xo, bo, co, cso, dto, eo, do, send) = refs[18:26]
    ext, extb, dtr = refs[26:29]
    y = idx[0]
    keep = idx[2].astype(F32)
    ext[0:8, :] = hx[...].astype(F32) * keep
    extb[0:8, :] = hbc[...].astype(F32) * keep
    for k in range(4):
        a = lax.rem(y + OFFS[k], NQ)
        at = pl.multiple_of(a * Q + 8, 8)
        ext[pl.ds(at, Q), :] = xs[k][...].astype(F32)
        extb[pl.ds(at, Q), :] = bcs[k][...].astype(F32)
        dtr[a] = dts[k][...]
    ones = head_spread()
    lane = lax.broadcasted_iota(jnp.int32, (HH, Q), 1)
    decay = -jnp.exp(alog[...])
    total = jnp.zeros((HH, Q), F32)
    state = jnp.zeros((NS, CH), F32)
    for a in range(NQ):
        dt = softplus(dtr[a] + bias[...])
        cs = decay * dt
        for s in (1, 2, 4, 8, 16, 32, 64):
            cs = cs + jnp.where(lane >= s, pltpu.roll(cs, s, 1), 0.0)
        end = jnp.broadcast_to(cs[:, Q - 1 : Q], (HH, Q))
        dto[a] = dt
        cso[a] = cs
        total = total + end
        v = kbc[0:1, :] * extb[a * Q + 5 : a * Q + 5 + Q, :]
        for j in range(1, 4):
            v = v + kbc[j : j + 1, :] * extb[a * Q + 5 + j : a * Q + 5 + j + Q, :]
        bc = silu(v).astype(BF)
        b = bc[:, :NS]
        bo[a] = b
        co[a] = bc[:, NS:]
        v = kx[0:1, :] * ext[a * Q + 5 : a * Q + 5 + Q, :]
        for j in range(1, 4):
            v = v + kx[j : j + 1, :] * ext[a * Q + 5 + j : a * Q + 5 + j + Q, :]
        x = silu(v)
        xo[a] = x.astype(BF)
        w = spread(dt * jnp.exp(end - cs), ones)
        e = dot_tn(b, (x * w).astype(BF))
        eo[a] = e
        d = spread(jnp.exp(end), ones)[0:8, :]
        do[a] = d
        state = state * d[0:1, :] + e
    st = state.T
    dec = jnp.exp(total)
    hi = dec.astype(BF).astype(F32)
    mid = (dec - hi).astype(BF).astype(F32)
    low = dec - hi - mid
    row = lax.broadcasted_iota(jnp.int32, (HH, Q), 0)
    for h in range(HH):
        p = lambda t: jnp.broadcast_to(t[h : h + 1, :], (8, Q))
        tail = jnp.where(row == 0, p(hi), jnp.where(row == 1, p(mid), jnp.where(row == 2, p(low), 0.0)))
        for q in range(4):
            d = h * 4 + q
            send[d] = jnp.concatenate([st[16 * d : 16 * d + 16, :], tail], 0).astype(BF)


def local_part(idx, xs, bcs, dts, hx, hbc, kx, kbc, bias, alog):
    s = jax.ShapeDtypeStruct
    return pl.pallas_call(
        local_kernel,
        out_shape=(
            s((NQ, Q, CH), BF),
            s((NQ, Q, NS), BF),
            s((NQ, Q, NS), BF),
            s((NQ, HH, Q), F32),
            s((NQ, HH, Q), F32),
            s((NQ, NS, CH), F32),
            s((NQ, 8, CH), F32),
            s((32, 24, 128), BF),
        ),
        in_specs=[SMEM] + [VMEM] * 18,
        out_specs=(VMEM,) * 8,
        scratch_shapes=[
            pltpu.VMEM((8 + NQ * Q, CH), F32),
            pltpu.VMEM((8 + NQ * Q, BCW), F32),
            pltpu.VMEM((NQ, HH, Q), F32),
        ],
        compiler_params=params(),
        name="local_part",
    )(idx, *xs, *bcs, *dts, hx, hbc, kx, kbc, bias, alog)


def prefix_kernel(r, o):
    s = jnp.zeros((16, 128), F32)
    for j in range(32):
        o[j] = s.astype(BF)
        v = r[j].astype(F32)
        s = s * (v[16:17] + v[17:18] + v[18:19]) + v[0:16]


def prefix(r):
    return pl.pallas_call(
        prefix_kernel,
        out_shape=jax.ShapeDtypeStruct((32, 16, 128), BF),
        in_specs=[VMEM],
        out_specs=VMEM,
        compiler_params=params(),
        name="prefix",
    )(r)


def diag_kernel(x, b, c, cs, dt, skip, y):
    t = lax.broadcasted_iota(jnp.int32, (Q, Q), 0)
    u = lax.broadcasted_iota(jnp.int32, (Q, Q), 1)
    tri = t >= u
    left = u < HD
    for a in range(NQ):
        scores = dot_nt(c[a], b[a])
        csr = cs[a]
        csc = csr.T
        dtr = dt[a]
        for p in range(HH // 2):
            xp = x[a, :, 128 * p : 128 * p + 128]
            ms = []
            for h in (2 * p, 2 * p + 1):
                diff = csc[:, h : h + 1] - csr[h : h + 1, :]
                m = scores * jnp.exp(jnp.where(tri, diff, -jnp.inf)) * dtr[h : h + 1, :]
                ms.append(m.astype(BF))
            xf = xp.astype(F32)
            xx = jnp.concatenate([jnp.where(left, xf, 0.0), jnp.where(left, 0.0, xf)], 0).astype(BF)
            yy = jnp.dot(jnp.concatenate(ms, 1), xx, preferred_element_type=F32)
            y[a, :, 128 * p : 128 * p + 128] = yy + skip[0:1, 128 * p : 128 * p + 128] * xf


def diag_part(x, b, c, cs, dt, skip):
    return pl.pallas_call(
        diag_kernel,
        out_shape=jax.ShapeDtypeStruct((NQ, Q, CH), F32),
        in_specs=[VMEM] * 6,
        out_specs=VMEM,
        compiler_params=params(),
        name="diag_part",
    )(x, b, c, cs, dt, skip)


def norm_kernel(idx, s_in, e, d, c, cs, ydiag, gain, n2, n1, nm, n0, nb):
    y = idx[0]
    core = idx[1]
    ones = head_spread()
    r = lax.broadcasted_iota(jnp.int32, (Q, Q), 0) // HD
    l = lax.broadcasted_iota(jnp.int32, (Q, Q), 1) // HD
    mean = jnp.where(r == l, 1.0 / HD, 0.0).astype(BF)
    state = s_in[...].astype(F32).T
    for a in range(NQ):
        yst = jnp.dot(c[a], state.astype(BF), preferred_element_type=F32)
        g = spread(jnp.exp(cs[a]), ones)
        v = ydiag[a] + g * yst
        if a < NQ - 1:
            state = state * d[a][0:1, :] + e[a]
        hi, lo = two_parts(v * v)
        for p in range(HH // 2):
            at = slice(128 * p, 128 * p + 128)
            ms = jnp.dot(hi[:, at], mean, preferred_element_type=F32)
            ms = ms + jnp.dot(lo[:, at], mean, preferred_element_type=F32)
            nb[a, :, at] = (v[:, at] * lax.rsqrt(ms + 1e-05) * gain[0:1, at]).astype(BF)
    for k, o in ((2, n2), (1, n1), (3, nm), (0, n0)):
        a = lax.rem(y + k, NQ)
        o[0:64, :] = nb[a, pl.ds(pl.multiple_of((1 - core) * 64, 64), 64), :]
        o[64:128, :] = nb[a, pl.ds(pl.multiple_of(core * 64, 64), 64), :]


def norm_part(idx, s_in, e, d, c, cs, ydiag, gain):
    s = jax.ShapeDtypeStruct
    return pl.pallas_call(
        norm_kernel,
        out_shape=(s((Q, CH), BF),) * 4,
        in_specs=[SMEM] + [VMEM] * 7,
        out_specs=(VMEM,) * 4,
        scratch_shapes=[pltpu.VMEM((NQ, Q, CH), BF)],
        compiler_params=params(),
        name="norm_part",
    )(idx, s_in, e, d, c, cs, ydiag, gain)


def out_kernel(n, w, other, own):
    v = jnp.dot(n[...], w[...], preferred_element_type=F32).astype(BF)
    other[...] = v[0:64]
    own[...] = v[64:128]


def out_part(n, w, name):
    s = jax.ShapeDtypeStruct
    return pl.pallas_call(
        out_kernel,
        out_shape=(s((64, 4096), BF),) * 2,
        in_specs=[VMEM] * 2,
        out_specs=(VMEM,) * 2,
        compiler_params=params(),
        name=name,
    )(n, w)


UP = [(y * 2 + c, ((y + 1) % 4) * 2 + c) for y in range(4) for c in range(2)]
DOWN = [(y * 2 + c, ((y - 1) % 4) * 2 + c) for y in range(4) for c in range(2)]
SWAP = [(y * 2 + c, y * 2 + 1 - c) for y in range(4) for c in range(2)]


def up(v):
    return lax.ppermute(v, "tp", UP)


def down(v):
    return lax.ppermute(v, "tp", DOWN)


def swap(v):
    return lax.ppermute(v, "tp", SWAP)


def per_device(tokens, in_x, in_bc, in_dt, conv_x, conv_bc, dt_bias, a_log, skip_d, norm_gain, out_w):
    tp = lax.axis_index("tp")
    ctx = lax.axis_index("ctx")
    idx = jnp.stack([tp // 2, tp % 2, jnp.where(ctx > 0, 1, 0)]).astype(jnp.int32)
    lanes = lambda v: jnp.broadcast_to(v[:, None], (HH, Q))
    weights = (in_x, in_bc, in_dt)

    lo, hi = tokens[:32], tokens[32:]
    partner = swap(tokens)
    ua, db = up(lo), down(hi)
    ub, da = up(hi), down(lo)
    uua, ddb = up(ua), down(db)
    piece0 = project(idx, [tokens], [partner], *weights, "project_0")
    piece1 = project(idx, [ua, ub], [swap(ua), swap(ub)], *weights, "project_1")
    piece2 = project(idx, [da, db], [swap(da), swap(db)], *weights, "project_2")
    piece3 = project(idx, [uua, ddb], [swap(uua), swap(ddb)], *weights, "project_3")
    xs, bcs, dts = zip(piece0, piece1, piece2, piece3)

    y = tp // 2
    last = lambda vs: jnp.where(
        y == 3, vs[0][Q - 8 :], jnp.where(y == 2, vs[2][Q - 8 :], jnp.where(y == 0, vs[1][Q - 8 :], vs[3][Q - 8 :]))
    )
    halo = jnp.concatenate([last(xs), last(bcs)], 1)
    halo = lax.ppermute(halo, "ctx", [(i, i + 1) for i in range(lax.axis_size("ctx") - 1)])
    hx, hbc = halo[:, :CH], halo[:, CH:]

    xc, b, c, cs, dt, e, d, send = local_part(
        idx, xs, bcs, dts, hx, hbc, conv_x, conv_bc, lanes(dt_bias), lanes(a_log)
    )
    got = lax.all_to_all(send, "ctx", 0, 0, tiled=True)
    skip = jnp.repeat(skip_d, HD)[None, :]
    ydiag = diag_part(xc, b, c, cs, dt, skip)
    back = lax.all_to_all(prefix(got), "ctx", 0, 0, tiled=True)
    s_in = back.reshape(CH, NS)
    n2, n1, nm, n0 = norm_part(idx, s_in, e, d, c, cs, ydiag, norm_gain[None, :])

    def summed(n, name):
        other, own = out_part(n, out_w, name)
        return own.astype(F32) + swap(other).astype(F32)

    q2 = summed(n2, "out_2").astype(BF)
    u2, d2 = up(q2[:32]), down(q2[32:])
    q1 = summed(n1, "out_1")
    u1b = up(q1[32:].astype(BF))
    qm = summed(nm, "out_m")
    dma = down(qm[:32].astype(BF))
    u1a = up((q1[:32] + u2.astype(F32)).astype(BF))
    dmb = down((qm[32:] + d2.astype(F32)).astype(BF))
    q0 = summed(n0, "out_0")
    top = q0[:32] + u1a.astype(F32) + dma.astype(F32)
    bottom = q0[32:] + u1b.astype(F32) + dmb.astype(F32)
    return jnp.concatenate([top.astype(BF), bottom.astype(BF)], 0)


def solution(mesh):
    return jax.shard_map(
        per_device,
        mesh=mesh,
        in_specs=(
            P(("ctx", "tp"), None),
            P(None, "tp"),
            P(),
            P(None, "tp"),
            P(None, "tp"),
            P(),
            P("tp"),
            P("tp"),
            P("tp"),
            P("tp"),
            P("tp", None),
        ),
        out_specs=P(("ctx", "tp"), None),
        check_vma=False,
    )
```

time: 519 us -> 151 us (0.29)
  waiting for transfers between devices: 238 us -> 30.4 us
  starting transfers between devices: 187 us -> 30.6 us
  Pallas kernels: 0 us -> 51.9 us
  matrix products: 32.6 us -> 0 us
  local copies, waits for them, and re-layouts: 37.7 us -> 10.1 us
  blocking collectives: 0 us -> 22.8 us
  between operations: 13.6 us -> 0.28 us
    ppermute x33 -> x24, starting transfers between devices: 187 us -> 26.1 us  [the longest x6 15.7 us: down(): return lax.ppermute(v, 'tp', DOWN)]
    ppermute x33 -> x24, waiting for transfers between devices: 143 us -> 24.8 us  [the longest x6 16.4 us: up(): return lax.ppermute(v, 'tp', UP)]
    reduce_scatter x1 -> x0, waiting for transfers between devices: 58 us -> none  [per_device(): lax.psum_scatter(jnp.dot(normed, out_w, preferred_element_type=jnp.float3...]
    pallas_call x0 -> x12, Pallas kernels: none -> 51.9 us  [the longest x4 21.3 us: project(): pl.pallas_call(functools.partial(project_kernel, n_own), out_shape=(jax.S...]
    all_gather x1 -> x0, waiting for transfers between devices: 36.1 us -> none  [per_device(): gathered = lax.all_gather(tokens, 'tp', axis=0, tiled=True)]
    dot_general x13 -> x0, matrix products: 32.6 us -> none  [the longest x2 6.97 us: ssd_block(): y_in = jnp.einsum('hts,shp->thp', weighted, xdt, precision=hi)]
    dynamic_update_slice x4 -> x0, local copies, waits for them, and re-layouts: 24.2 us -> none  [per_device(): lax.scan(scan_step, start, (x_conv.reshape(blocks, BLOCK, heads_here, hea...]
    all_to_all x0 -> x1, blocking collectives: none -> 22.8 us  [per_device(): got = lax.all_to_all(send, 'ctx', 0, 0, tiled=True)]
  transfers between devices with their start and end apart: 35 -> 25, of which waited for: 33 -> 9; matrix products, arithmetic and copies ran while one was open for 1% -> 3% of each run, Pallas kernels for 0% -> 21%
where the time goes in v1:
time: 151 us; the launch traced here: 150 us
  Pallas kernels  51.9 us (34%)
  starting transfers between devices  30.6 us (20%)
  waiting for transfers between devices  30.4 us (20%)
  blocking collectives  22.8 us (15%)
  local copies, waits for them, and re-layouts  10.1 us (7%)
  other arithmetic  3.57 us (2%)
    all_to_all x1, blocking collectives, per_device(): got = lax.all_to_all(send, 'ctx', 0, 0, tiled=True)  22.8 us
    pallas_call x4, Pallas kernels, project(): pl.pallas_call(functools.partial(project_kernel, n_own), out_shape=(jax.S...  21.3 us
    ppermute x6, waiting for transfers between devices, up(): return lax.ppermute(v, 'tp', UP)  16.4 us
    pallas_call x4, Pallas kernels, out_part(): pl.pallas_call(out_kernel, out_shape=(s((64, 4096), BF),) * 2, in_specs=[...  16 us
    ppermute x6, starting transfers between devices, down(): return lax.ppermute(v, 'tp', DOWN)  15.7 us
    ppermute x6, waiting for transfers between devices, down(): return lax.ppermute(v, 'tp', DOWN)  6.72 us
    pallas_call x1, Pallas kernels, local_part(): pl.pallas_call(local_kernel, out_shape=(s((NQ, Q, CH), BF), s((NQ, Q, NS)...  5.77 us
    unnamed x41, local copies, waits for them, and re-layouts  5.7 us
  transfers between devices with their start and end apart: 25, of which 9 were waited for; matrix products, arithmetic and copies ran while one was open for 3% of the time, Pallas kernels for 21%

profile of v1, /device:TPU:32, one launch (start us, length us, event | category | flops | bytes accessed | tf_op | source)
XLA Modules:
  0.0 149.5 jit_solution(13464020953579275783)
XLA Ops:
  6.4 4.1 %collective-permute-done.1.refs_0_ = bf16[32,4096]{1,0:T(8,128)(2,1)S(1)} collective-permute-done((bf16[32,4096]{1,0:T(8,128)(2,1)S(1)}, bf16[32,4096]{1,0:T(8,128)(2,1)S(1)}, u32[]{:S(2)}, u32[]{:S(2)}) %collective-permute-start.1) | collective-permute-done | bytes 262176 | tf_op jit(solution)/shard_map/ppermute | solution.py:301
  12.0 2.9 %collective-permute-start.10 = (bf16[32,4096]{1,0:T(8,128)(2,1)S(1)}, bf16[32,4096]{1,0:T(8,128)(2,1)S(1)}, u32[]{:S(2)}, u32[]{:S(2)}) collective-permute-start(bf16[32,4096]{1,0:T(8,128)(2,1)S(1)} %collective-permute-done.6.refs_1_), channel_id=1, source_target_pairs={{0,6},{1,7},{2,0},{3,1},{4,2},{5,3},{6,4},{7,5},{8,14},{9,15},{10,... | collective-permute-start | bytes 786440 | tf_op jit(solution)/shard_map/ppermute | solution.py:305
  18.1 3.6 %collective-permute-done.9.refs_0_ = bf16[32,4096]{1,0:T(8,128)(2,1)S(1)} collective-permute-done((bf16[32,4096]{1,0:T(8,128)(2,1)S(1)}, bf16[32,4096]{1,0:T(8,128)(2,1)S(1)}, u32[]{:S(2)}, u32[]{:S(2)}) %collective-permute-start.9) | collective-permute-done | bytes 262176 | tf_op jit(solution)/shard_map/ppermute | solution.py:301
  25.6 5.3 %project_0.1 = (bf16[128,512]{1,0:T(8,128)(2,1)}, bf16[128,256]{1,0:T(8,128)(2,1)}, f32[8,128]{1,0:T(8,128)}) custom-call(s32[3]{0:T(128)} %pad_add_fusion.idx, bf16[64,4096]{1,0:T(8,128)(2,1)} %refs_0_.1, bf16[64,4096]{1,0:T(8,128)(2,1)} %copy-done, bf16[4096,512]{1,0:T(8,128)(2,1)} %refs_4_.6, bf16[4096,256]{1,0:T(8,128)(2,1)} %refs_5_.5, ...), custom_call_target="tpu_custom_call" | custom-call | tf_op jit(solution)/shard_map/project_0/pallas_call | solution.py:72
  31.0 5.3 %project_2.1 = (bf16[128,512]{1,0:T(8,128)(2,1)}, bf16[128,256]{1,0:T(8,128)(2,1)}, f32[8,128]{1,0:T(8,128)}) custom-call(s32[3]{0:T(128)} %pad_add_fusion.idx, bf16[32,4096]{1,0:T(8,128)(2,1)} %copy-done.11, bf16[32,4096]{1,0:T(8,128)(2,1)} %copy-done.10, bf16[32,4096]{1,0:T(8,128)(2,1)} %collective-permute-done.7.refs_2_, bf16[32,4096]{1,0:T(8,128)(2,1)} %copy-done.13, ...), custom_call_target="tpu_custom_call" | custom-call | tf_op jit(solution)/shard_map/project_2/pallas_call | solution.py:72
  37.7 5.4 %project_1.1 = (bf16[128,512]{1,0:T(8,128)(2,1)}, bf16[128,256]{1,0:T(8,128)(2,1)}, f32[8,128]{1,0:T(8,128)}) custom-call(s32[3]{0:T(128)} %pad_add_fusion.idx, bf16[32,4096]{1,0:T(8,128)(2,1)} %copy-done.6, bf16[32,4096]{1,0:T(8,128)(2,1)} %copy-done.8, bf16[32,4096]{1,0:T(8,128)(2,1)} %copy-done.12, bf16[32,4096]{1,0:T(8,128)(2,1)} %copy-done.15, ...), custom_call_target="tpu_custom_call" | custom-call | tf_op jit(solution)/shard_map/project_1/pallas_call | solution.py:72
  44.5 5.3 %project_3.1 = (bf16[128,512]{1,0:T(8,128)(2,1)}, bf16[128,256]{1,0:T(8,128)(2,1)}, f32[8,128]{1,0:T(8,128)}) custom-call(s32[3]{0:T(128)} %pad_add_fusion.idx, bf16[32,4096]{1,0:T(8,128)(2,1)} %copy-done.7, bf16[32,4096]{1,0:T(8,128)(2,1)} %copy-done.9, bf16[32,4096]{1,0:T(8,128)(2,1)} %copy-done.14, bf16[32,4096]{1,0:T(8,128)(2,1)} %copy-done.16, ...), custom_call_target="tpu_custom_call" | custom-call | tf_op jit(solution)/shard_map/project_3/pallas_call | solution.py:72
  51.3 3.8 %collective-permute-start.13 = (bf16[8,768]{1,0:T(8,128)(2,1)S(1)}, bf16[8,768]{1,0:T(8,128)(2,1)S(1)}, u32[]{:S(2)}, u32[]{:S(2)}) collective-permute-start(bf16[8,768]{1,0:T(8,128)(2,1)S(1)} %pad_maximum_fusion.1), channel_id=1, source_target_pairs={{0,8},{8,16},{16,24},{24,32},{32,40},{40,48},{48,56},{56,64},{64,7... | collective-permute-start | bytes 36872 | tf_op jit(solution)/shard_map/ppermute | solution.py:335
  59.4 5.8 %local_part.1 = (bf16[4,128,512]{2,1,0:T(8,128)(2,1)}, bf16[4,128,128]{2,1,0:T(8,128)(2,1)}, bf16[4,128,128]{2,1,0:T(8,128)(2,1)}, f32[4,8,128]{2,1,0:T(8,128)},...) custom-call(s32[3]{0:T(128)} %pad_add_fusion.idx, ...), custom_call_target="tpu_custom_call" | custom-call | tf_op jit(solution)/shard_map/local_part/pallas_call | solution.py:161
  65.2 22.8 %all_to_all.10.r = bf16[32,24,128]{2,1,0:T(8,128)(2,1)} all-to-all(bf16[32,24,128]{2,1,0:T(8,128)(2,1)} %get-tuple-element.49), channel_id=1, replica_groups=mesh['ctx'=32,'tp'=8] {'ctx'}, dimensions={0} | all-to-all | bytes 393216 | tf_op jit(solution)/shard_map/all_to_all | solution.py:341
  89.6 4.5 %all-to-all-start.1 = ((bf16[32,16,128]{2,1,0:T(8,128)(2,1)}), bf16[32,16,128]{2,1,0:T(8,128)(2,1)S(1)}, u32[]{:S(2)}, u32[]{:S(2)}) async-start(bf16[32,16,128]{2,1,0:T(8,128)(2,1)} %prefix.1), calls=%async_computation.1 | async-start | bytes 262144 | tf_op jit(solution)/shard_map/all_to_all | solution.py:344
  94.9 3.4 %diag_part.1.ydiag = f32[4,128,512]{2,1,0:T(8,128)} custom-call(bf16[4,128,512]{2,1,0:T(8,128)(2,1)} %get-tuple-element.54.x, bf16[4,128,128]{2,1,0:T(8,128)(2,1)} %get-tuple-element.55.b, bf16[4,128,128]{2,1,0:T(8,128)(2,1)} %get-tuple-element.52.c, f32[4,8,128]{2,1,0:T(8,128)} %get-tuple-element.53.cs, f32[4,8,128]{2,1,0:T(8,128)} %get-tuple-element.56.dt, ...), custom_call_target="tpu_custom_call" | custom-call | tf_op jit(solution)/shard_map/diag_part/pallas_call | solution.py:228
  98.3 5.5 %all-to-all-done.1 = bf16[32,16,128]{2,1,0:T(8,128)(2,1)S(1)} async-done(((bf16[32,16,128]{2,1,0:T(8,128)(2,1)}), bf16[32,16,128]{2,1,0:T(8,128)(2,1)S(1)}, u32[]{:S(2)}, u32[]{:S(2)}) %all-to-all-start.1) | async-done | bytes 131104 | tf_op jit(solution)/shard_map/all_to_all | solution.py:344
  104.4 3.7 %norm_part.1 = (bf16[128,512]{1,0:T(8,128)(2,1)}, bf16[128,512]{1,0:T(8,128)(2,1)}, bf16[128,512]{1,0:T(8,128)(2,1)}, bf16[128,512]{1,0:T(8,128)(2,1)}) custom-call(s32[3]{0:T(128)} %pad_add_fusion.idx, bf16[512,128]{1,0:T(8,128)(2,1)} %bitcast.5, f32[4,128,512]{2,1,0:T(8,128)} %get-tuple-element.50.e, f32[4,8,512]{2,1,0:T(8,128)} %get-tuple-element.51.d, ...), custom_call_target="tpu_custom_call" | custom-call | tf_op jit(solution)/shard_map/norm_part/pallas_call | solution.py:266
  108.1 4.0 %out_2.1 = (bf16[64,4096]{1,0:T(8,128)(2,1)}, bf16[64,4096]{1,0:T(8,128)(2,1)}) custom-call(bf16[128,512]{1,0:T(8,128)(2,1)} %get-tuple-element.63.n, bf16[512,4096]{1,0:T(8,128)(2,1)} %w.7), custom_call_target="tpu_custom_call" | custom-call | tf_op jit(solution)/shard_map/out_2/pallas_call | solution.py:285
  112.1 4.0 %out_m.1 = (bf16[64,4096]{1,0:T(8,128)(2,1)}, bf16[64,4096]{1,0:T(8,128)(2,1)}) custom-call(bf16[128,512]{1,0:T(8,128)(2,1)} %get-tuple-element.66.n, bf16[512,4096]{1,0:T(8,128)(2,1)} %w.7), custom_call_target="tpu_custom_call" | custom-call | tf_op jit(solution)/shard_map/out_m/pallas_call | solution.py:285
  116.6 4.0 %out_1.1 = (bf16[64,4096]{1,0:T(8,128)(2,1)}, bf16[64,4096]{1,0:T(8,128)(2,1)}) custom-call(bf16[128,512]{1,0:T(8,128)(2,1)} %get-tuple-element.60.n, bf16[512,4096]{1,0:T(8,128)(2,1)} %w.7), custom_call_target="tpu_custom_call" | custom-call | tf_op jit(solution)/shard_map/out_1/pallas_call | solution.py:285
  120.6 4.0 %out_0.1 = (bf16[64,4096]{1,0:T(8,128)(2,1)}, bf16[64,4096]{1,0:T(8,128)(2,1)}) custom-call(bf16[128,512]{1,0:T(8,128)(2,1)} %get-tuple-element.57.n, bf16[512,4096]{1,0:T(8,128)(2,1)} %w.7), custom_call_target="tpu_custom_call" | custom-call | tf_op jit(solution)/shard_map/out_0/pallas_call | solution.py:285
  125.3 2.8 %collective-permute-start.22 = (bf16[32,4096]{1,0:T(8,128)(2,1)S(1)}, bf16[32,4096]{1,0:T(8,128)(2,1)S(1)}, u32[]{:S(2)}, u32[]{:S(2)}) collective-permute-start(bf16[32,4096]{1,0:T(8,128)(2,1)S(1)} %get-tuple-element.72), channel_id=1, source_target_pairs={{0,6},{1,7},{2,0},{3,1},{4,2},{5,3},{6,4},{7,5},{8,14},{9,15},{10,... | collective-permute-start | bytes 786440 | tf_op jit(solution)/shard_map/ppermute | solution.py:305
  129.1 2.8 %collective-permute-start.20 = (bf16[32,4096]{1,0:T(8,128)(2,1)S(1)}, bf16[32,4096]{1,0:T(8,128)(2,1)S(1)}, u32[]{:S(2)}, u32[]{:S(2)}) collective-permute-start(bf16[32,4096]{1,0:T(8,128)(2,1)S(1)} %slice.119), channel_id=1, source_target_pairs={{0,6},{1,7},{2,0},{3,1},{4,2},{5,3},{6,4},{7,5},{8,14},{9,15},{10,... | collective-permute-start | bytes 786440 | tf_op jit(solution)/shard_map/ppermute | solution.py:305
  131.9 3.0 %collective-permute-done.22 = bf16[32,4096]{1,0:T(8,128)(2,1)S(1)} collective-permute-done((bf16[32,4096]{1,0:T(8,128)(2,1)S(1)}, bf16[32,4096]{1,0:T(8,128)(2,1)S(1)}, u32[]{:S(2)}, u32[]{:S(2)}) %collective-permute-start.22) | collective-permute-done | bytes 262176 | tf_op jit(solution)/shard_map/ppermute | solution.py:305
  134.9 3.8 %collective-permute-start.23 = (bf16[32,4096]{1,0:T(8,128)(2,1)S(1)}, bf16[32,4096]{1,0:T(8,128)(2,1)S(1)}, u32[]{:S(2)}, u32[]{:S(2)}) collective-permute-start(bf16[32,4096]{1,0:T(8,128)(2,1)S(1)} %fusion), channel_id=1, source_target_pairs={{0,6},{1,7},{2,0},{3,1},{4,2},{5,3},{6,4},{7,5},{8,14},{9,15},{10,... | collective-permute-start | bytes 786440 | tf_op jit(solution)/shard_map/ppermute | solution.py:305
  138.9 5.2 %collective-permute-done.21 = bf16[32,4096]{1,0:T(8,128)(2,1)S(1)} collective-permute-done((bf16[32,4096]{1,0:T(8,128)(2,1)S(1)}, bf16[32,4096]{1,0:T(8,128)(2,1)S(1)}, u32[]{:S(2)}, u32[]{:S(2)}) %collective-permute-start.21) | collective-permute-done | bytes 262176 | tf_op jit(solution)/shard_map/ppermute | solution.py:301
  145.1 3.4 %collective-permute-done.18 = bf16[32,4096]{1,0:T(8,128)(2,1)S(1)} collective-permute-done((bf16[32,4096]{1,0:T(8,128)(2,1)S(1)}, bf16[32,4096]{1,0:T(8,128)(2,1)S(1)}, u32[]{:S(2)}, u32[]{:S(2)}) %collective-permute-start.18) | collective-permute-done | bytes 262176 | tf_op jit(solution)/shard_map/ppermute | solution.py:301
  (102 shorter events, 30.9 us)
Async XLA Ops:
  1.1 9.4 %collective-permute-start.1 = (bf16[32,4096]{1,0:T(8,128)(2,1)S(1)}, bf16[32,4096]{1,0:T(8,128)(2,1)S(1)}, u32[]{:S(2)}, u32[]{:S(2)}) collective-permute-start(bf16[32,4096]{1,0:T(8,128)(2,1)S(1)} %get-tuple-element.74), channel_id=1, source_target_pairs={{0,2},{1,3},{2,4},{3,5},{4,6},{5,7},{6,0},{7,1},{8,10},{9,11},{10,... | collective-permute-start | bytes 786440 | tf_op jit(solution)/shard_map/ppermute | solution.py:301
  2.7 9.2 %collective-permute-start.6 = (bf16[32,4096]{1,0:T(8,128)(2,1)S(1)}, bf16[32,4096]{1,0:T(8,128)(2,1)S(1)}, u32[]{:S(2)}, u32[]{:S(2)}) collective-permute-start(bf16[32,4096]{1,0:T(8,128)(2,1)S(1)} %get-tuple-element.73), channel_id=1, source_target_pairs={{0,6},{1,7},{2,0},{3,1},{4,2},{5,3},{6,4},{7,5},{8,14},{9,15},{10,... | collective-permute-start | bytes 786440 | tf_op jit(solution)/shard_map/ppermute | solution.py:305
  4.4 13.2 %collective-permute-start.5 = (bf16[32,4096]{1,0:T(8,128)(2,1)S(1)}, bf16[32,4096]{1,0:T(8,128)(2,1)S(1)}, u32[]{:S(2)}, u32[]{:S(2)}) collective-permute-start(bf16[32,4096]{1,0:T(8,128)(2,1)S(1)} %get-tuple-element.74), channel_id=1, source_target_pairs={{0,6},{1,7},{2,0},{3,1},{4,2},{5,3},{6,4},{7,5},{8,14},{9,15},{10,... | collective-permute-start | bytes 786440 | tf_op jit(solution)/shard_map/ppermute | solution.py:305
  6.2 16.2 %collective-permute-start = (bf16[64,4096]{1,0:T(8,128)(2,1)}, bf16[64,4096]{1,0:T(8,128)(2,1)S(1)}, u32[]{:S(2)}, u32[]{:S(2)}) collective-permute-start(bf16[64,4096]{1,0:T(8,128)(2,1)} %refs_0_.1), channel_id=1, source_target_pairs={{0,1},{1,0},{2,3},{3,2},{4,5},{5,4},{6,7},{7,6},{8,9},{9,8},{10,11... | collective-permute-start | bytes 1572872 | tf_op jit(solution)/shard_map/ppermute | solution.py:309
  6.2 11.4 %collective-permute-start.2 = (bf16[32,4096]{1,0:T(8,128)(2,1)S(1)}, bf16[32,4096]{1,0:T(8,128)(2,1)S(1)}, u32[]{:S(2)}, u32[]{:S(2)}) collective-permute-start(bf16[32,4096]{1,0:T(8,128)(2,1)S(1)} %get-tuple-element.73), channel_id=1, source_target_pairs={{0,2},{1,3},{2,4},{3,5},{4,6},{5,7},{6,0},{7,1},{8,10},{9,11},{10,... | collective-permute-start | bytes 786440 | tf_op jit(solution)/shard_map/ppermute | solution.py:301
  10.5 11.3 %collective-permute-start.9 = (bf16[32,4096]{1,0:T(8,128)(2,1)S(1)}, bf16[32,4096]{1,0:T(8,128)(2,1)S(1)}, u32[]{:S(2)}, u32[]{:S(2)}) collective-permute-start(bf16[32,4096]{1,0:T(8,128)(2,1)S(1)} %collective-permute-done.1.refs_0_), channel_id=1, source_target_pairs={{0,2},{1,3},{2,4},{3,5},{4,6},{5,7},{6,0},{7,1},{8,10},{9,11},{10,... | collective-permute-start | bytes 786440 | tf_op jit(solution)/shard_map/ppermute | solution.py:301
  12.0 9.8 %collective-permute-start.10 = (bf16[32,4096]{1,0:T(8,128)(2,1)S(1)}, bf16[32,4096]{1,0:T(8,128)(2,1)S(1)}, u32[]{:S(2)}, u32[]{:S(2)}) collective-permute-start(bf16[32,4096]{1,0:T(8,128)(2,1)S(1)} %collective-permute-done.6.refs_1_), channel_id=1, source_target_pairs={{0,6},{1,7},{2,0},{3,1},{4,2},{5,3},{6,4},{7,5},{8,14},{9,15},{10,... | collective-permute-start | bytes 786440 | tf_op jit(solution)/shard_map/ppermute | solution.py:305
  17.6 18.7 %collective-permute-start.3 = (bf16[32,4096]{1,0:T(8,128)(2,1)S(1)}, bf16[32,4096]{1,0:T(8,128)(2,1)S(1)}, u32[]{:S(2)}, u32[]{:S(2)}) collective-permute-start(bf16[32,4096]{1,0:T(8,128)(2,1)S(1)} %collective-permute-done.1.refs_0_), channel_id=1, source_target_pairs={{0,1},{1,0},{2,3},{3,2},{4,5},{5,4},{6,7},{7,6},{8,9},{9,8},{10,11... | collective-permute-start | bytes 786440 | tf_op jit(solution)/shard_map/ppermute | solution.py:309
  21.7 9.2 %collective-permute-start.7 = (bf16[32,4096]{1,0:T(8,128)(2,1)S(1)}, bf16[32,4096]{1,0:T(8,128)(2,1)}, u32[]{:S(2)}, u32[]{:S(2)}) collective-permute-start(bf16[32,4096]{1,0:T(8,128)(2,1)S(1)} %collective-permute-done.5.refs_0_), channel_id=1, source_target_pairs={{0,1},{1,0},{2,3},{3,2},{4,5},{5,4},{6,7},{7,6},{8,9},{9,8},{10,11... | collective-permute-start | bytes 786440 | tf_op jit(solution)/shard_map/ppermute | solution.py:309
  21.8 14.5 %collective-permute-start.4 = (bf16[32,4096]{1,0:T(8,128)(2,1)S(1)}, bf16[32,4096]{1,0:T(8,128)(2,1)S(1)}, u32[]{:S(2)}, u32[]{:S(2)}) collective-permute-start(bf16[32,4096]{1,0:T(8,128)(2,1)S(1)} %collective-permute-done.2.refs_1_), channel_id=1, source_target_pairs={{0,1},{1,0},{2,3},{3,2},{4,5},{5,4},{6,7},{7,6},{8,9},{9,8},{10,11... | collective-permute-start | bytes 786440 | tf_op jit(solution)/shard_map/ppermute | solution.py:309
  22.3 20.8 %collective-permute-start.11 = (bf16[32,4096]{1,0:T(8,128)(2,1)S(1)}, bf16[32,4096]{1,0:T(8,128)(2,1)S(1)}, u32[]{:S(2)}, u32[]{:S(2)}) collective-permute-start(bf16[32,4096]{1,0:T(8,128)(2,1)S(1)} %collective-permute-done.9.refs_0_), channel_id=1, source_target_pairs={{0,1},{1,0},{2,3},{3,2},{4,5},{5,4},{6,7},{7,6},{8,9},{9,8},{10,11... | collective-permute-start | bytes 786440 | tf_op jit(solution)/shard_map/ppermute | solution.py:309
  22.4 20.7 %collective-permute-start.12 = (bf16[32,4096]{1,0:T(8,128)(2,1)S(1)}, bf16[32,4096]{1,0:T(8,128)(2,1)S(1)}, u32[]{:S(2)}, u32[]{:S(2)}) collective-permute-start(bf16[32,4096]{1,0:T(8,128)(2,1)S(1)} %collective-permute-done.10.refs_1_), channel_id=1, source_target_pairs={{0,1},{1,0},{2,3},{3,2},{4,5},{5,4},{6,7},{7,6},{8,9},{9,8},{10,11... | collective-permute-start | bytes 786440 | tf_op jit(solution)/shard_map/ppermute | solution.py:309
  51.3 5.6 %collective-permute-start.13 = (bf16[8,768]{1,0:T(8,128)(2,1)S(1)}, bf16[8,768]{1,0:T(8,128)(2,1)S(1)}, u32[]{:S(2)}, u32[]{:S(2)}) collective-permute-start(bf16[8,768]{1,0:T(8,128)(2,1)S(1)} %pad_maximum_fusion.1), channel_id=1, source_target_pairs={{0,8},{8,16},{16,24},{24,32},{32,40},{40,48},{48,56},{56,64},{64,7... | collective-permute-start | bytes 36872 | tf_op jit(solution)/shard_map/ppermute | solution.py:335
  89.6 14.1 %all-to-all-start.1 = ((bf16[32,16,128]{2,1,0:T(8,128)(2,1)}), bf16[32,16,128]{2,1,0:T(8,128)(2,1)S(1)}, u32[]{:S(2)}, u32[]{:S(2)}) async-start(bf16[32,16,128]{2,1,0:T(8,128)(2,1)} %prefix.1), calls=%async_computation.1 | async-start | bytes 262144 | tf_op jit(solution)/shard_map/all_to_all | solution.py:344
  112.1 13.0 %collective-permute-start.16 = (bf16[64,4096]{1,0:T(8,128)(2,1)}, bf16[64,4096]{1,0:T(8,128)(2,1)S(1)}, u32[]{:S(2)}, u32[]{:S(2)}) collective-permute-start(bf16[64,4096]{1,0:T(8,128)(2,1)} %get-tuple-element.65), channel_id=1, source_target_pairs={{0,1},{1,0},{2,3},{3,2},{4,5},{5,4},{6,7},{7,6},{8,9},{9,8},{10,11... | collective-permute-start | bytes 1572872 | tf_op jit(solution)/shard_map/ppermute | solution.py:309
  116.1 12.8 %collective-permute-start.19 = (bf16[64,4096]{1,0:T(8,128)(2,1)}, bf16[64,4096]{1,0:T(8,128)(2,1)S(1)}, u32[]{:S(2)}, u32[]{:S(2)}) collective-permute-start(bf16[64,4096]{1,0:T(8,128)(2,1)} %get-tuple-element.68), channel_id=1, source_target_pairs={{0,1},{1,0},{2,3},{3,2},{4,5},{5,4},{6,7},{7,6},{8,9},{9,8},{10,11... | collective-permute-start | bytes 1572872 | tf_op jit(solution)/shard_map/ppermute | solution.py:309
  120.6 7.5 %collective-permute-start.15 = (bf16[64,4096]{1,0:T(8,128)(2,1)}, bf16[64,4096]{1,0:T(8,128)(2,1)S(1)}, u32[]{:S(2)}, u32[]{:S(2)}) collective-permute-start(bf16[64,4096]{1,0:T(8,128)(2,1)} %get-tuple-element.62), channel_id=1, source_target_pairs={{0,1},{1,0},{2,3},{3,2},{4,5},{5,4},{6,7},{7,6},{8,9},{9,8},{10,11... | collective-permute-start | bytes 1572872 | tf_op jit(solution)/shard_map/ppermute | solution.py:309
  124.6 14.2 %collective-permute-start.14 = (bf16[64,4096]{1,0:T(8,128)(2,1)}, bf16[64,4096]{1,0:T(8,128)(2,1)S(1)}, u32[]{:S(2)}, u32[]{:S(2)}) collective-permute-start(bf16[64,4096]{1,0:T(8,128)(2,1)} %get-tuple-element.59), channel_id=1, source_target_pairs={{0,1},{1,0},{2,3},{3,2},{4,5},{5,4},{6,7},{7,6},{8,9},{9,8},{10,11... | collective-permute-start | bytes 1572872 | tf_op jit(solution)/shard_map/ppermute | solution.py:309
  125.3 9.5 %collective-permute-start.22 = (bf16[32,4096]{1,0:T(8,128)(2,1)S(1)}, bf16[32,4096]{1,0:T(8,128)(2,1)S(1)}, u32[]{:S(2)}, u32[]{:S(2)}) collective-permute-start(bf16[32,4096]{1,0:T(8,128)(2,1)S(1)} %get-tuple-element.72), channel_id=1, source_target_pairs={{0,6},{1,7},{2,0},{3,1},{4,2},{5,3},{6,4},{7,5},{8,14},{9,15},{10,... | collective-permute-start | bytes 786440 | tf_op jit(solution)/shard_map/ppermute | solution.py:305
  128.1 10.5 %collective-permute-start.17 = (bf16[32,4096]{1,0:T(8,128)(2,1)S(1)}, bf16[32,4096]{1,0:T(8,128)(2,1)S(1)}, u32[]{:S(2)}, u32[]{:S(2)}) collective-permute-start(bf16[32,4096]{1,0:T(8,128)(2,1)S(1)} %get-tuple-element.71), channel_id=1, source_target_pairs={{0,2},{1,3},{2,4},{3,5},{4,6},{5,7},{6,0},{7,1},{8,10},{9,11},{10,... | collective-permute-start | bytes 786440 | tf_op jit(solution)/shard_map/ppermute | solution.py:301
  128.3 15.9 %collective-permute-start.21 = (bf16[32,4096]{1,0:T(8,128)(2,1)S(1)}, bf16[32,4096]{1,0:T(8,128)(2,1)S(1)}, u32[]{:S(2)}, u32[]{:S(2)}) collective-permute-start(bf16[32,4096]{1,0:T(8,128)(2,1)S(1)} %slice.118), channel_id=1, source_target_pairs={{0,2},{1,3},{2,4},{3,5},{4,6},{5,7},{6,0},{7,1},{8,10},{9,11},{10,... | collective-permute-start | bytes 786440 | tf_op jit(solution)/shard_map/ppermute | solution.py:301
  129.1 15.1 %collective-permute-start.20 = (bf16[32,4096]{1,0:T(8,128)(2,1)S(1)}, bf16[32,4096]{1,0:T(8,128)(2,1)S(1)}, u32[]{:S(2)}, u32[]{:S(2)}) collective-permute-start(bf16[32,4096]{1,0:T(8,128)(2,1)S(1)} %slice.119), channel_id=1, source_target_pairs={{0,6},{1,7},{2,0},{3,1},{4,2},{5,3},{6,4},{7,5},{8,14},{9,15},{10,... | collective-permute-start | bytes 786440 | tf_op jit(solution)/shard_map/ppermute | solution.py:305
  134.9 10.3 %collective-permute-start.23 = (bf16[32,4096]{1,0:T(8,128)(2,1)S(1)}, bf16[32,4096]{1,0:T(8,128)(2,1)S(1)}, u32[]{:S(2)}, u32[]{:S(2)}) collective-permute-start(bf16[32,4096]{1,0:T(8,128)(2,1)S(1)} %fusion), channel_id=1, source_target_pairs={{0,6},{1,7},{2,0},{3,1},{4,2},{5,3},{6,4},{7,5},{8,14},{9,15},{10,... | collective-permute-start | bytes 786440 | tf_op jit(solution)/shard_map/ppermute | solution.py:305
  138.7 9.9 %collective-permute-start.18 = (bf16[32,4096]{1,0:T(8,128)(2,1)S(1)}, bf16[32,4096]{1,0:T(8,128)(2,1)S(1)}, u32[]{:S(2)}, u32[]{:S(2)}) collective-permute-start(bf16[32,4096]{1,0:T(8,128)(2,1)S(1)} %fusion.3), channel_id=1, source_target_pairs={{0,2},{1,3},{2,4},{3,5},{4,6},{5,7},{6,0},{7,1},{8,10},{9,11},{10,... | collective-permute-start | bytes 786440 | tf_op jit(solution)/shard_map/ppermute | solution.py:301
  (21 other events, 241.7 us)

commit v2 on v1

v2 whole, which is shorter than its diff:
```python
import functools

import jax
import jax.numpy as jnp
from jax import lax
from jax.experimental import pallas as pl
from jax.experimental.pallas import tpu as pltpu
from jax.sharding import PartitionSpec as P

BF = jnp.bfloat16
F32 = jnp.float32
VMEM = pl.BlockSpec(memory_space=pltpu.VMEM)
SMEM = pl.BlockSpec(memory_space=pltpu.SMEM)
LIMIT = 12 * 1024 * 1024

Q = 128
NQ = 4
HH = 8
HD = 64
NS = 128
CH = 512
BCW = 256


def params():
    return pltpu.CompilerParams(vmem_limit_bytes=LIMIT)


def dot_tn(a, b):
    return lax.dot_general(a, b, (((0,), (0,)), ((), ())), preferred_element_type=F32)


def dot_nt(a, b):
    return lax.dot_general(a, b, (((1,), (1,)), ((), ())), preferred_element_type=F32)


def two_parts(v):
    hi = v.astype(BF)
    return hi, (v - hi.astype(F32)).astype(BF)


def head_spread():
    row = lax.broadcasted_iota(jnp.int32, (2 * HH, CH), 0)
    lane = lax.broadcasted_iota(jnp.int32, (2 * HH, CH), 1)
    return jnp.where(lane // HD == row % HH, 1.0, 0.0).astype(BF)


def spread(v, ones):
    hi, lo = two_parts(v)
    both = jnp.concatenate([hi.astype(F32), lo.astype(F32)], 0).astype(BF)
    return dot_tn(both, ones)


def chip():
    return lax.axis_index("tp") // 2


def core():
    return lax.rem(lax.axis_index("tp"), 2)


def in_vmem(v):
    return pltpu.with_memory_space_constraint(v, pltpu.VMEM)


def fill(tok, own, other):
    c = core()
    for group, half in ((own, c), (other, 1 - c)):
        step = 64 // len(group)
        for j, r in enumerate(group):
            at = pl.multiple_of(half * 64 + j * step, step)
            tok[pl.ds(at, step), :] = r[0:step, :]


def project_kernel(n, *refs):
    own, other = refs[:n], refs[n : 2 * n]
    wx, wbc, wdt, xo, bco, dto, tok = refs[2 * n :]
    fill(tok, own, other)
    rows = tok[...]
    xo[...] = jnp.dot(rows, wx[...], preferred_element_type=F32).astype(BF)
    bco[...] = jnp.dot(rows, wbc[...], preferred_element_type=F32).astype(BF)
    dto[...] = dot_nt(rows, wdt[...]).T


def project(own, other, weights, name):
    n = len(own)
    return pl.pallas_call(
        functools.partial(project_kernel, n),
        out_shape=(
            pltpu.VMEM((Q, CH), BF),
            pltpu.VMEM((Q, BCW), BF),
            pltpu.VMEM((HH, Q), F32),
        ),
        in_specs=[VMEM] * (2 * n + 3),
        out_specs=(VMEM, VMEM, VMEM),
        scratch_shapes=[pltpu.VMEM((Q, 4096), BF)],
        compiler_params=params(),
        name=name,
    )(*[in_vmem(v) for v in (*own, *other, *weights)])


def silu(v):
    return v / (1.0 + jnp.exp(-v))


def softplus(v):
    return jnp.maximum(v, 0.0) + jnp.log1p(jnp.exp(-jnp.abs(v)))


def column(ref):
    row = lax.broadcasted_iota(jnp.int32, (HH, Q), 0)
    v = jnp.full((HH, Q), ref[0], F32)
    for h in range(1, HH):
        v = jnp.where(row == h, ref[h], v)
    return v


OFFS = (0, 3, 1, 2)


def local_kernel(bias, alog, *refs):
    xs, bcs, dts = refs[0:3], refs[3:6], refs[6:9]
    far, halo, haloswap = refs[9:13], refs[13], refs[14]
    wx, wbc, wdt, kx, kbc = refs[15:20]
    (xo, bo, co, cso, dto, eo, do, send) = refs[20:28]
    ext, extb, dtr, tok = refs[28:32]
    y = chip()
    fill(tok, far[0:2], far[2:4])
    mine = core() == 1
    edge = jnp.where(mine, halo[...].astype(F32), haloswap[...].astype(F32))
    tok[Q : Q + 16, :] = jnp.concatenate([edge, edge], 0).astype(BF)
    rows = tok[...]
    x3 = jnp.dot(rows, wx[...], preferred_element_type=F32).astype(BF).astype(F32)
    bc3 = jnp.dot(rows, wbc[...], preferred_element_type=F32).astype(BF).astype(F32)
    dt3 = dot_nt(rows[0:Q], wdt[...]).T
    ext[0:8, :] = x3[Q : Q + 8]
    extb[0:8, :] = bc3[Q : Q + 8]
    for k in range(4):
        a = lax.rem(y + OFFS[k], NQ)
        at = pl.multiple_of(a * Q + 8, 8)
        ext[pl.ds(at, Q), :] = x3[0:Q] if k == 3 else xs[k][...].astype(F32)
        extb[pl.ds(at, Q), :] = bc3[0:Q] if k == 3 else bcs[k][...].astype(F32)
        dtr[a] = dt3 if k == 3 else dts[k][...]
    ones = head_spread()
    lane = lax.broadcasted_iota(jnp.int32, (HH, Q), 1)
    decay = -jnp.exp(column(alog))
    bias_col = column(bias)
    total = jnp.zeros((HH, Q), F32)
    state = jnp.zeros((NS, CH), F32)
    for a in range(NQ):
        dt = softplus(dtr[a] + bias_col)
        cs = decay * dt
        for s in (1, 2, 4, 8, 16, 32, 64):
            cs = cs + jnp.where(lane >= s, pltpu.roll(cs, s, 1), 0.0)
        end = jnp.broadcast_to(cs[:, Q - 1 : Q], (HH, Q))
        dto[a] = dt
        cso[a] = cs
        total = total + end
        v = kbc[0:1, :] * extb[a * Q + 5 : a * Q + 5 + Q, :]
        for j in range(1, 4):
            v = v + kbc[j : j + 1, :] * extb[a * Q + 5 + j : a * Q + 5 + j + Q, :]
        bc = silu(v).astype(BF)
        b = bc[:, :NS]
        bo[a] = b
        co[a] = bc[:, NS:]
        v = kx[0:1, :] * ext[a * Q + 5 : a * Q + 5 + Q, :]
        for j in range(1, 4):
            v = v + kx[j : j + 1, :] * ext[a * Q + 5 + j : a * Q + 5 + j + Q, :]
        x = silu(v)
        xo[a] = x.astype(BF)
        w = spread(dt * jnp.exp(end - cs), ones)
        e = dot_tn(b, (x * w).astype(BF))
        eo[a] = e
        d = spread(jnp.exp(end), ones)[0:8, :]
        do[a] = d
        state = state * d[0:1, :] + e
    st = state.T
    dec = jnp.exp(total)
    hi = dec.astype(BF).astype(F32)
    mid = (dec - hi).astype(BF).astype(F32)
    low = dec - hi - mid
    row = lax.broadcasted_iota(jnp.int32, (HH, Q), 0)
    for h in range(HH):
        p = lambda t: jnp.broadcast_to(t[h : h + 1, :], (8, Q))
        tail = jnp.where(row == 0, p(hi), jnp.where(row == 1, p(mid), jnp.where(row == 2, p(low), 0.0)))
        for q in range(4):
            d = h * 4 + q
            send[d] = jnp.concatenate([st[16 * d : 16 * d + 16, :], tail], 0).astype(BF)


def local_part(bias, alog, xs, bcs, dts, far, halo, haloswap, weights, kx, kbc):
    s = pltpu.VMEM
    return pl.pallas_call(
        local_kernel,
        out_shape=(
            s((NQ, Q, CH), BF),
            s((NQ, Q, NS), BF),
            s((NQ, Q, NS), BF),
            s((NQ, HH, Q), F32),
            s((NQ, HH, Q), F32),
            s((NQ, NS, CH), F32),
            s((NQ, 8, CH), F32),
            s((32, 24, 128), BF),
        ),
        in_specs=[SMEM] * 2 + [VMEM] * 20,
        out_specs=(VMEM,) * 8,
        scratch_shapes=[
            pltpu.VMEM((8 + NQ * Q, CH), F32),
            pltpu.VMEM((8 + NQ * Q, BCW), F32),
            pltpu.VMEM((NQ, HH, Q), F32),
            pltpu.VMEM((Q + 16, 4096), BF),
        ],
        compiler_params=params(),
        name="local_part",
    )(bias, alog, *[in_vmem(v) for v in (*xs, *bcs, *dts, *far, halo, haloswap, *weights, kx, kbc)])


def prefix_kernel(r, o):
    s = jnp.zeros((16, 128), F32)
    for j in range(32):
        o[j] = s.astype(BF)
        v = r[j].astype(F32)
        s = s * (v[16:17] + v[17:18] + v[18:19]) + v[0:16]


def prefix(r):
    return pl.pallas_call(
        prefix_kernel,
        out_shape=pltpu.VMEM((32, 16, 128), BF),
        in_specs=[VMEM],
        out_specs=VMEM,
        compiler_params=params(),
        name="prefix",
    )(in_vmem(r))


def diag_kernel(skip, x, b, c, cs, dt, y):
    t = lax.broadcasted_iota(jnp.int32, (Q, Q), 0)
    u = lax.broadcasted_iota(jnp.int32, (Q, Q), 1)
    tri = t >= u
    left = u < HD
    for a in range(NQ):
        scores = dot_nt(c[a], b[a])
        csr = cs[a]
        csc = csr.T
        dtr = dt[a]
        for p in range(HH // 2):
            xp = x[a, :, 128 * p : 128 * p + 128]
            ms = []
            for h in (2 * p, 2 * p + 1):
                diff = csc[:, h : h + 1] - csr[h : h + 1, :]
                m = scores * jnp.exp(jnp.where(tri, diff, -jnp.inf)) * dtr[h : h + 1, :]
                ms.append(m.astype(BF))
            xf = xp.astype(F32)
            xx = jnp.concatenate([jnp.where(left, xf, 0.0), jnp.where(left, 0.0, xf)], 0).astype(BF)
            yy = jnp.dot(jnp.concatenate(ms, 1), xx, preferred_element_type=F32)
            y[a, :, 128 * p : 128 * p + 128] = yy + jnp.where(left, skip[2 * p], skip[2 * p + 1]) * xf


def diag_part(skip, *args):
    return pl.pallas_call(
        diag_kernel,
        out_shape=pltpu.VMEM((NQ, Q, CH), F32),
        in_specs=[SMEM] + [VMEM] * 5,
        out_specs=VMEM,
        compiler_params=params(),
        name="diag_part",
    )(skip, *[in_vmem(v) for v in args])


def norm_kernel(s_in, e, d, c, cs, ydiag, gain, w, other, own, rest, nb):
    y = chip()
    mine = core()
    ones = head_spread()
    r = lax.broadcasted_iota(jnp.int32, (Q, Q), 0) // HD
    l = lax.broadcasted_iota(jnp.int32, (Q, Q), 1) // HD
    mean = jnp.where(r == l, 1.0 / HD, 0.0).astype(BF)
    state = s_in[...].astype(F32).T
    for a in range(NQ):
        yst = jnp.dot(c[a], state.astype(BF), preferred_element_type=F32)
        g = spread(jnp.exp(cs[a]), ones)
        v = ydiag[a] + g * yst
        if a < NQ - 1:
            state = state * d[a][0:1, :] + e[a]
        hi, lo = two_parts(v * v)
        for p in range(HH // 2):
            at = slice(128 * p, 128 * p + 128)
            ms = jnp.dot(hi[:, at], mean, preferred_element_type=F32)
            ms = ms + jnp.dot(lo[:, at], mean, preferred_element_type=F32)
            nb[a, :, at] = (v[:, at] * lax.rsqrt(ms + 1e-05) * gain[0:1, at]).astype(BF)

    def half(a, h):
        return nb[a, pl.ds(pl.multiple_of(h * 64, 64), 64), :]

    a = lax.rem(y + 2, NQ)
    v = jnp.concatenate([half(a, 1 - mine), half(a, mine)], 0)
    v = jnp.dot(v, w[...], preferred_element_type=F32).astype(BF)
    other[...] = v[0:64]
    own[...] = v[64:128]
    for j, k in enumerate((1, 3, 0)):
        a = lax.rem(y + k, NQ)
        rest[64 * j : 64 * j + 64, :] = half(a, 1 - mine)
        rest[192 + 64 * j : 256 + 64 * j, :] = half(a, mine)


def norm_part(*args):
    s = pltpu.VMEM
    return pl.pallas_call(
        norm_kernel,
        out_shape=(s((64, 4096), BF), s((64, 4096), BF), s((384, CH), BF)),
        in_specs=[VMEM] * 8,
        out_specs=(VMEM,) * 3,
        scratch_shapes=[pltpu.VMEM((NQ, Q, CH), BF)],
        compiler_params=params(),
        name="norm_part",
    )(*[in_vmem(v) for v in args])


def out_kernel(n, w, other, own):
    other[...] = jnp.dot(n[0:192], w[...], preferred_element_type=F32).astype(BF)
    own[...] = jnp.dot(n[192:384], w[...], preferred_element_type=F32).astype(BF)


def out_part(n, w):
    s = pltpu.VMEM
    return pl.pallas_call(
        out_kernel,
        out_shape=(s((192, 4096), BF),) * 2,
        in_specs=[VMEM] * 2,
        out_specs=(VMEM,) * 2,
        compiler_params=params(),
        name="out_part",
    )(in_vmem(n), in_vmem(w))


UP = [(y * 2 + c, ((y + 1) % 4) * 2 + c) for y in range(4) for c in range(2)]
DOWN = [(y * 2 + c, ((y - 1) % 4) * 2 + c) for y in range(4) for c in range(2)]
SWAP = [(y * 2 + c, y * 2 + 1 - c) for y in range(4) for c in range(2)]


def up(v):
    return lax.ppermute(v, "tp", UP)


def down(v):
    return lax.ppermute(v, "tp", DOWN)


def swap(v):
    return lax.ppermute(v, "tp", SWAP)


def per_device(tokens, in_x, in_bc, in_dt, conv_x, conv_bc, dt_bias, a_log, skip_d, norm_gain, out_w):
    y = lax.axis_index("tp") // 2
    after = lax.optimization_barrier
    weights = (in_x, in_bc, in_dt.T)

    lo, hi = tokens[:32], tokens[32:]
    h = lax.ppermute(tokens[56:], "ctx", [(i, i + 1) for i in range(lax.axis_size("ctx") - 1)])
    partner = swap(tokens)
    ua, db = up(lo), down(hi)
    piece0 = project([tokens], [partner], weights, "project_0")
    up_b, down_a = jnp.concatenate([hi, h], 0), jnp.concatenate([lo, h], 0)
    ua, db, piece0, up_b, down_a = after((ua, db, piece0, up_b, down_a))
    ub, da = up(up_b), down(down_a)
    uua, ddb = up(ua), down(db)
    huu = up(ub[32:])
    edge = jnp.where(y == 3, h, jnp.where(y == 0, ub[32:], jnp.where(y == 2, da[32:], huu)))
    piece1 = project([ua, ub], [swap(ua), swap(ub)], weights, "project_1")
    piece2 = project([da, db], [swap(da), swap(db)], weights, "project_2")
    uua, ddb, piece1, piece2 = after((uua, ddb, piece1, piece2))
    xs, bcs, dts = zip(piece0, piece1, piece2)
    far = [uua, ddb, swap(uua), swap(ddb)]

    xc, b, c, cs, dt, e, d, send = local_part(
        dt_bias, a_log, xs, bcs, dts, far, edge, swap(edge), weights, conv_x, conv_bc
    )
    got = lax.all_to_all(send, "ctx", 0, 0, tiled=True)
    ydiag = diag_part(skip_d, xc, b, c, cs, dt)
    back = lax.all_to_all(prefix(got), "ctx", 0, 0, tiled=True)
    other, own, rest = norm_part(back.reshape(CH, NS), e, d, c, cs, ydiag, norm_gain[None, :], out_w)

    q2 = (own.astype(F32) + swap(other).astype(F32)).astype(BF)
    q2, rest = after((q2, rest))
    u2, d2 = up(q2[:32]), down(q2[32:])
    other, own = out_part(rest, out_w)
    q = own.astype(F32) + swap(other).astype(F32)
    u1b, dma = up(q[32:64].astype(BF)), down(q[64:96].astype(BF))
    u1a = up((q[:32] + u2.astype(F32)).astype(BF))
    dmb = down((q[96:128] + d2.astype(F32)).astype(BF))
    top = q[128:160] + u1a.astype(F32) + dma.astype(F32)
    bottom = q[160:192] + u1b.astype(F32) + dmb.astype(F32)
    return jnp.concatenate([top.astype(BF), bottom.astype(BF)], 0)


def solution(mesh):
    return jax.shard_map(
        per_device,
        mesh=mesh,
        in_specs=(
            P(("ctx", "tp"), None),
            P(None, "tp"),
            P(),
            P(None, "tp"),
            P(None, "tp"),
            P(),
            P("tp"),
            P("tp"),
            P("tp"),
            P("tp"),
            P("tp", None),
        ),
        out_specs=P(("ctx", "tp"), None),
        check_vma=False,
    )
```

time: 151 us -> 123 us (0.81)
  Pallas kernels: 51.9 us -> 17.6 us
  local copies, waits for them, and re-layouts: 10.1 us -> 15.9 us
  waiting for transfers between devices: 30.4 us -> 34.3 us
  starting transfers between devices: 30.6 us -> 28.8 us
    pallas_call x11 -> x7, Pallas kernels: 46.1 us -> 12.4 us  [the longest x3 6.03 us: project(): pl.pallas_call(functools.partial(project_kernel, n), out_shape=(pltpu.VME...]
    unnamed x41 -> x54, local copies, waits for them, and re-layouts: 5.7 us -> 13.2 us
    ppermute x6 -> x7, waiting for transfers between devices: 16.4 us -> 21.6 us  [up(): return lax.ppermute(v, 'tp', UP)]
    ppermute x11 -> x10, waiting for transfers between devices: 0.03 us -> 2.89 us  [swap(): return lax.ppermute(v, 'tp', SWAP)]
    ppermute x6, waiting for transfers between devices: 6.72 us -> 4.27 us  [down(): return lax.ppermute(v, 'tp', DOWN)]
    ppermute x1, waiting for transfers between devices: 1.73 us -> 0.01 us  [per_device(): lax.ppermute(tokens[56:], 'ctx', [(i, i + 1) for i in range(lax.axis_size...]
    ppermute x6 -> x7, starting transfers between devices: 4.05 us -> 2.52 us  [up(): return lax.ppermute(v, 'tp', UP)]
  transfers between devices with their start and end apart: 25 -> 25, of which waited for: 9 -> 10; matrix products, arithmetic and copies ran while one was open for 3% -> 4% of each run, Pallas kernels for 21% -> 6%
where the time goes in v2:
time: 123 us; the launch traced here: 121 us
  waiting for transfers between devices  34.3 us (28%)
  starting transfers between devices  28.8 us (23%)
  blocking collectives  21.6 us (18%)
  Pallas kernels  17.6 us (14%)
  local copies, waits for them, and re-layouts  15.9 us (13%)
  other arithmetic  2.76 us (2%)
    all_to_all x1, blocking collectives, per_device(): got = lax.all_to_all(send, 'ctx', 0, 0, tiled=True)  21.6 us
    ppermute x7, waiting for transfers between devices, up(): return lax.ppermute(v, 'tp', UP)  21.6 us
    ppermute x6, starting transfers between devices, down(): return lax.ppermute(v, 'tp', DOWN)  16.1 us
    unnamed x54, local copies, waits for them, and re-layouts  13.2 us
    pallas_call x3, Pallas kernels, project(): pl.pallas_call(functools.partial(project_kernel, n), out_shape=(pltpu.VME...  6.03 us
    all_to_all x1, waiting for transfers between devices, per_device(): back = lax.all_to_all(prefix(got), 'ctx', 0, 0, tiled=True)  5.52 us
    pallas_call x1, Pallas kernels, local_part(): pl.pallas_call(local_kernel, out_shape=(s((NQ, Q, CH), BF), s((NQ, Q, NS)...  5.15 us
    all_to_all x1, starting transfers between devices, per_device(): back = lax.all_to_all(prefix(got), 'ctx', 0, 0, tiled=True)  4.58 us
  transfers between devices with their start and end apart: 25, of which 10 were waited for; matrix products, arithmetic and copies ran while one was open for 4% of the time, Pallas kernels for 6%

profile of v2, /device:TPU:32, one launch (start us, length us, event | category | flops | bytes accessed | tf_op | source)
XLA Modules:
  0.0 121.3 jit_solution(8741852695350515905)
XLA Ops:
  1.0 3.8 %collective-permute-start.3 = (bf16[8,4096]{1,0:T(8,128)(2,1)S(1)}, bf16[8,4096]{1,0:T(8,128)(2,1)S(1)}, u32[]{:S(2)}, u32[]{:S(2)}) collective-permute-start(bf16[8,4096]{1,0:T(8,128)(2,1)S(1)} %slice.44), channel_id=1, source_target_pairs={{0,8},{8,16},{16,24},{24,32},{32,40},{40,48},{48,56},{56,64},{64,7... | collective-permute-start | bytes 196616 | tf_op jit(solution)/shard_map/ppermute | solution.py:359
  5.9 3.1 %collective-permute-start.1 = (bf16[32,4096]{1,0:T(8,128)(2,1)S(1)}, bf16[32,4096]{1,0:T(8,128)(2,1)}, u32[]{:S(2)}, u32[]{:S(2)}) collective-permute-start(bf16[32,4096]{1,0:T(8,128)(2,1)S(1)} %get-tuple-element.93), channel_id=1, source_target_pairs={{0,6},{1,7},{2,0},{3,1},{4,2},{5,3},{6,4},{7,5},{8,14},{9,15},{10,... | collective-permute-start | bytes 786440 | tf_op jit(solution)/shard_map/ppermute | solution.py:346
  9.1 2.2 %copy-done = bf16[4096,512]{1,0:T(8,128)(2,1)S(1)} copy-done((bf16[4096,512]{1,0:T(8,128)(2,1)S(1)}, bf16[4096,512]{1,0:T(8,128)(2,1)}, u32[]{:S(2)}) %copy-start) | copy-done | bytes 4194328
  14.8 3.5 %collective-permute-done.refs_0_ = bf16[32,4096]{1,0:T(8,128)(2,1)} collective-permute-done((bf16[32,4096]{1,0:T(8,128)(2,1)S(1)}, bf16[32,4096]{1,0:T(8,128)(2,1)}, u32[]{:S(2)}, u32[]{:S(2)}) %collective-permute-start) | collective-permute-done | bytes 262176 | tf_op jit(solution)/shard_map/ppermute | solution.py:342
  18.3 3.2 %collective-permute-start.9 = (bf16[40,4096]{1,0:T(8,128)(2,1)S(1)}, bf16[40,4096]{1,0:T(8,128)(2,1)S(1)}, u32[]{:S(2)}, u32[]{:S(2)}) collective-permute-start(bf16[40,4096]{1,0:T(8,128)(2,1)S(1)} %get-tuple-element.54), channel_id=1, source_target_pairs={{0,6},{1,7},{2,0},{3,1},{4,2},{5,3},{6,4},{7,5},{8,14},{9,15},{10,... | collective-permute-start | bytes 983048 | tf_op jit(solution)/shard_map/ppermute | solution.py:346
  21.6 6.5 %collective-permute-done.6.refs_1_ = bf16[40,4096]{1,0:T(8,128)(2,1)S(1)} collective-permute-done((bf16[40,4096]{1,0:T(8,128)(2,1)S(1)}, bf16[40,4096]{1,0:T(8,128)(2,1)S(1)}, u32[]{:S(2)}, u32[]{:S(2)}) %collective-permute-start.6) | collective-permute-done | bytes 327712 | tf_op jit(solution)/shard_map/ppermute | solution.py:342
  29.3 3.2 %collective-permute-start.5 = (bf16[32,4096]{1,0:T(8,128)(2,1)}, bf16[32,4096]{1,0:T(8,128)(2,1)}, u32[]{:S(2)}, u32[]{:S(2)}) collective-permute-start(bf16[32,4096]{1,0:T(8,128)(2,1)} %collective-permute-done.1.refs_1_), channel_id=1, source_target_pairs={{0,6},{1,7},{2,0},{3,1},{4,2},{5,3},{6,4},{7,5},{8,14},{9,15},{10,... | collective-permute-start | bytes 786440 | tf_op jit(solution)/shard_map/ppermute | solution.py:346
  33.2 2.2 %copy-done.1 = bf16[4096,512]{1,0:T(8,128)(2,1)S(1)} copy-done((bf16[4096,512]{1,0:T(8,128)(2,1)S(1)}, bf16[4096,512]{1,0:T(8,128)(2,1)}, u32[]{:S(2)}) %copy-start.1) | copy-done | bytes 4194328
  36.3 2.2 %project_1.1 = (bf16[128,512]{1,0:T(8,128)(2,1)S(1)}, bf16[128,256]{1,0:T(8,128)(2,1)S(1)}, f32[8,128]{1,0:T(8,128)S(1)}) custom-call(bf16[32,4096]{1,0:T(8,128)(2,1)} %collective-permute-done.refs_0_, bf16[40,4096]{1,0:T(8,128)(2,1)S(1)} %collective-permute-done.6.refs_1_, bf16[32,4096]{1,0:T(8,128)(2,1)S(1)} %copy-done.10, ...), custom_call_target="tpu_custom_call" | custom-call | tf_op jit(solution)/shard_map/project_1/pallas_call | solution.py:87
  38.6 2.4 %project_2.1 = (bf16[128,512]{1,0:T(8,128)(2,1)S(1)}, bf16[128,256]{1,0:T(8,128)(2,1)S(1)}, f32[8,128]{1,0:T(8,128)S(1)}) custom-call(bf16[40,4096]{1,0:T(8,128)(2,1)S(1)} %collective-permute-done.9.refs_0_, bf16[32,4096]{1,0:T(8,128)(2,1)} %collective-permute-done.1.refs_1_, bf16[40,4096]{1,0:T(8,128)(2,1)S(1)} %collective-permute-done.10.refs_2_, ...), custom_call_target="tpu_custom_call" | custom-call | tf_op jit(solution)/shard_map/project_2/pallas_call | solution.py:87
  43.9 5.2 %local_part.1 = (bf16[4,128,512]{2,1,0:T(8,128)(2,1)S(1)}, bf16[4,128,128]{2,1,0:T(8,128)(2,1)S(1)}, bf16[4,128,128]{2,1,0:T(8,128)(2,1)S(1)}, f32[4,8,128]{2,1,...) custom-call(f32[8]{0:T(128)S(1)} %copy-done.22, ...), custom_call_target="tpu_custom_call" | custom-call | tf_op jit(solution)/shard_map/local_part/pallas_call | solution.py:193
  49.9 21.6 %all_to_all.10.r = bf16[32,24,128]{2,1,0:T(8,128)(2,1)S(1)} all-to-all(bf16[32,24,128]{2,1,0:T(8,128)(2,1)S(1)} %get-tuple-element.68), channel_id=1, replica_groups=mesh['ctx'=32,'tp'=8] {'ctx'}, dimensions={0} | all-to-all | bytes 393216 | tf_op jit(solution)/shard_map/all_to_all | solution.py:378
  72.3 4.6 %all-to-all-start.1 = ((bf16[32,16,128]{2,1,0:T(8,128)(2,1)}), bf16[32,16,128]{2,1,0:T(8,128)(2,1)S(1)}, u32[]{:S(2)}, u32[]{:S(2)}) async-start(bf16[32,16,128]{2,1,0:T(8,128)(2,1)} %prefix.1), calls=%async_computation.1 | async-start | bytes 262144 | tf_op jit(solution)/shard_map/all_to_all | solution.py:380
  79.3 1.8 %diag_part.1.ydiag = f32[4,128,512]{2,1,0:T(8,128)S(1)} custom-call(f32[8]{0:T(128)S(1)} %copy-done.24, bf16[4,128,512]{2,1,0:T(8,128)(2,1)S(1)} %copy-done.8, bf16[4,128,128]{2,1,0:T(8,128)(2,1)S(1)} %get-tuple-element.74.b, bf16[4,128,128]{2,1,0:T(8,128)(2,1)S(1)} %get-tuple-element.71.c, f32[4,8,128]{2,1,0:T(8,128)S(1)} %get-tuple-element.72.cs, ...), custom_call_target="tpu_custom_call" | custom-call | tf_op jit(solution)/shard_map/diag_part/pallas_call | solution.py:261
  81.1 5.5 %all-to-all-done.1 = bf16[32,16,128]{2,1,0:T(8,128)(2,1)S(1)} async-done(((bf16[32,16,128]{2,1,0:T(8,128)(2,1)}), bf16[32,16,128]{2,1,0:T(8,128)(2,1)S(1)}, u32[]{:S(2)}, u32[]{:S(2)}) %all-to-all-start.1) | async-done | bytes 131104 | tf_op jit(solution)/shard_map/all_to_all | solution.py:380
  86.6 2.2 %copy-done.3 = bf16[512,4096]{1,0:T(8,128)(2,1)S(1)} copy-done((bf16[512,4096]{1,0:T(8,128)(2,1)S(1)}, bf16[512,4096]{1,0:T(8,128)(2,1)}, u32[]{:S(2)}) %copy-start.3) | copy-done | bytes 4194328
  88.8 2.1 %norm_part.1 = (bf16[64,4096]{1,0:T(8,128)(2,1)S(1)}, bf16[64,4096]{1,0:T(8,128)(2,1)S(1)}, bf16[384,512]{1,0:T(8,128)(2,1)S(1)}) custom-call(bf16[512,128]{1,0:T(8,128)(2,1)S(1)} %bitcast.7, f32[4,128,512]{2,1,0:T(8,128)S(1)} %get-tuple-element.69.e, f32[4,8,512]{2,1,0:T(8,128)S(1)} %copy-done.14, bf16[4,128,128]{2,1,0:T(8,128)(2,1)S(1)} %get-tuple-element.71.c, ...), custom_call_target="tpu_custom_call" | custom-call | tf_op jit(solution)/shard_map/norm_part/pallas_call | solution.py:308
  91.0 1.9 %collective-permute-done.16 = bf16[64,4096]{1,0:T(8,128)(2,1)S(1)} collective-permute-done((bf16[64,4096]{1,0:T(8,128)(2,1)S(1)}, bf16[64,4096]{1,0:T(8,128)(2,1)S(1)}, u32[]{:S(2)}, u32[]{:S(2)}) %collective-permute-start.16) | collective-permute-done | bytes 524320 | tf_op jit(solution)/shard_map/ppermute | solution.py:350
  96.3 2.4 %collective-permute-start.22 = (bf16[32,4096]{1,0:T(8,128)(2,1)S(1)}, bf16[32,4096]{1,0:T(8,128)(2,1)S(1)}, u32[]{:S(2)}, u32[]{:S(2)}) collective-permute-start(bf16[32,4096]{1,0:T(8,128)(2,1)S(1)} %get-tuple-element.92), channel_id=1, source_target_pairs={{0,6},{1,7},{2,0},{3,1},{4,2},{5,3},{6,4},{7,5},{8,14},{9,15},{10,... | collective-permute-start | bytes 786440 | tf_op jit(solution)/shard_map/ppermute | solution.py:346
  99.4 5.9 %collective-permute-done.18 = bf16[32,4096]{1,0:T(8,128)(2,1)S(1)} collective-permute-done((bf16[32,4096]{1,0:T(8,128)(2,1)S(1)}, bf16[32,4096]{1,0:T(8,128)(2,1)S(1)}, u32[]{:S(2)}, u32[]{:S(2)}) %collective-permute-start.18) | collective-permute-done | bytes 262176 | tf_op jit(solution)/shard_map/ppermute | solution.py:342
  106.5 2.2 %collective-permute-start.23 = (bf16[32,4096]{1,0:T(8,128)(2,1)S(1)}, bf16[32,4096]{1,0:T(8,128)(2,1)S(1)}, u32[]{:S(2)}, u32[]{:S(2)}) collective-permute-start(bf16[32,4096]{1,0:T(8,128)(2,1)S(1)} %get-tuple-element.86), channel_id=1, source_target_pairs={{0,6},{1,7},{2,0},{3,1},{4,2},{5,3},{6,4},{7,5},{8,14},{9,15},{10,... | collective-permute-start | bytes 786440 | tf_op jit(solution)/shard_map/ppermute | solution.py:346
  108.8 1.9 %collective-permute-start.20 = (bf16[32,4096]{1,0:T(8,128)(2,1)S(1)}, bf16[32,4096]{1,0:T(8,128)(2,1)S(1)}, u32[]{:S(2)}, u32[]{:S(2)}) collective-permute-start(bf16[32,4096]{1,0:T(8,128)(2,1)S(1)} %get-tuple-element.89), channel_id=1, source_target_pairs={{0,6},{1,7},{2,0},{3,1},{4,2},{5,3},{6,4},{7,5},{8,14},{9,15},{10,... | collective-permute-start | bytes 786440 | tf_op jit(solution)/shard_map/ppermute | solution.py:346
  110.8 5.1 %collective-permute-done.19 = bf16[32,4096]{1,0:T(8,128)(2,1)S(1)} collective-permute-done((bf16[32,4096]{1,0:T(8,128)(2,1)S(1)}, bf16[32,4096]{1,0:T(8,128)(2,1)S(1)}, u32[]{:S(2)}, u32[]{:S(2)}) %collective-permute-start.19) | collective-permute-done | bytes 262176 | tf_op jit(solution)/shard_map/ppermute | solution.py:342
  115.8 3.8 %collective-permute-done.20 = bf16[32,4096]{1,0:T(8,128)(2,1)S(1)} collective-permute-done((bf16[32,4096]{1,0:T(8,128)(2,1)S(1)}, bf16[32,4096]{1,0:T(8,128)(2,1)S(1)}, u32[]{:S(2)}, u32[]{:S(2)}) %collective-permute-start.20) | collective-permute-done | bytes 262176 | tf_op jit(solution)/shard_map/ppermute | solution.py:346
  (101 shorter events, 22.4 us)
Async XLA Ops:
  0.0 9.1 %collective-permute-start.2 = (bf16[64,4096]{1,0:T(8,128)(2,1)}, bf16[64,4096]{1,0:T(8,128)(2,1)S(1)}, u32[]{:S(2)}, u32[]{:S(2)}) collective-permute-start(bf16[64,4096]{1,0:T(8,128)(2,1)} %refs_0_.1), channel_id=1, source_target_pairs={{0,1},{1,0},{2,3},{3,2},{4,5},{5,4},{6,7},{7,6},{8,9},{9,8},{10,11... | collective-permute-start | bytes 1572872 | tf_op jit(solution)/shard_map/ppermute | solution.py:350
  1.0 8.0 %collective-permute-start.3 = (bf16[8,4096]{1,0:T(8,128)(2,1)S(1)}, bf16[8,4096]{1,0:T(8,128)(2,1)S(1)}, u32[]{:S(2)}, u32[]{:S(2)}) collective-permute-start(bf16[8,4096]{1,0:T(8,128)(2,1)S(1)} %slice.44), channel_id=1, source_target_pairs={{0,8},{8,16},{16,24},{24,32},{32,40},{40,48},{48,56},{56,64},{64,7... | collective-permute-start | bytes 196616 | tf_op jit(solution)/shard_map/ppermute | solution.py:359
  5.9 8.9 %collective-permute-start.1 = (bf16[32,4096]{1,0:T(8,128)(2,1)S(1)}, bf16[32,4096]{1,0:T(8,128)(2,1)}, u32[]{:S(2)}, u32[]{:S(2)}) collective-permute-start(bf16[32,4096]{1,0:T(8,128)(2,1)S(1)} %get-tuple-element.93), channel_id=1, source_target_pairs={{0,6},{1,7},{2,0},{3,1},{4,2},{5,3},{6,4},{7,5},{8,14},{9,15},{10,... | collective-permute-start | bytes 786440 | tf_op jit(solution)/shard_map/ppermute | solution.py:346
  9.0 9.3 %collective-permute-start = (bf16[32,4096]{1,0:T(8,128)(2,1)S(1)}, bf16[32,4096]{1,0:T(8,128)(2,1)}, u32[]{:S(2)}, u32[]{:S(2)}) collective-permute-start(bf16[32,4096]{1,0:T(8,128)(2,1)S(1)} %get-tuple-element.94), channel_id=1, source_target_pairs={{0,2},{1,3},{2,4},{3,5},{4,6},{5,7},{6,0},{7,1},{8,10},{9,11},{10,... | collective-permute-start | bytes 786440 | tf_op jit(solution)/shard_map/ppermute | solution.py:342
  18.3 9.7 %collective-permute-start.6 = (bf16[40,4096]{1,0:T(8,128)(2,1)S(1)}, bf16[40,4096]{1,0:T(8,128)(2,1)S(1)}, u32[]{:S(2)}, u32[]{:S(2)}) collective-permute-start(bf16[40,4096]{1,0:T(8,128)(2,1)S(1)} %get-tuple-element.50), channel_id=1, source_target_pairs={{0,2},{1,3},{2,4},{3,5},{4,6},{5,7},{6,0},{7,1},{8,10},{9,11},{10,... | collective-permute-start | bytes 983048 | tf_op jit(solution)/shard_map/ppermute | solution.py:342
  18.3 9.7 %collective-permute-start.9 = (bf16[40,4096]{1,0:T(8,128)(2,1)S(1)}, bf16[40,4096]{1,0:T(8,128)(2,1)S(1)}, u32[]{:S(2)}, u32[]{:S(2)}) collective-permute-start(bf16[40,4096]{1,0:T(8,128)(2,1)S(1)} %get-tuple-element.54), channel_id=1, source_target_pairs={{0,6},{1,7},{2,0},{3,1},{4,2},{5,3},{6,4},{7,5},{8,14},{9,15},{10,... | collective-permute-start | bytes 983048 | tf_op jit(solution)/shard_map/ppermute | solution.py:346
  21.5 7.0 %collective-permute-start.7 = (bf16[32,4096]{1,0:T(8,128)(2,1)}, bf16[32,4096]{1,0:T(8,128)(2,1)S(1)}, u32[]{:S(2)}, u32[]{:S(2)}) collective-permute-start(bf16[32,4096]{1,0:T(8,128)(2,1)} %collective-permute-done.refs_0_), channel_id=1, source_target_pairs={{0,1},{1,0},{2,3},{3,2},{4,5},{5,4},{6,7},{7,6},{8,9},{9,8},{10,11... | collective-permute-start | bytes 786440 | tf_op jit(solution)/shard_map/ppermute | solution.py:350
  28.0 5.1 %collective-permute-start.8 = (bf16[40,4096]{1,0:T(8,128)(2,1)S(1)}, bf16[40,4096]{1,0:T(8,128)(2,1)S(1)}, u32[]{:S(2)}, u32[]{:S(2)}) collective-permute-start(bf16[40,4096]{1,0:T(8,128)(2,1)S(1)} %collective-permute-done.6.refs_1_), channel_id=1, source_target_pairs={{0,1},{1,0},{2,3},{3,2},{4,5},{5,4},{6,7},{7,6},{8,9},{9,8},{10,11... | collective-permute-start | bytes 983048 | tf_op jit(solution)/shard_map/ppermute | solution.py:350
  28.1 10.6 %collective-permute-start.10 = (bf16[40,4096]{1,0:T(8,128)(2,1)S(1)}, bf16[40,4096]{1,0:T(8,128)(2,1)S(1)}, u32[]{:S(2)}, u32[]{:S(2)}) collective-permute-start(bf16[40,4096]{1,0:T(8,128)(2,1)S(1)} %collective-permute-done.9.refs_0_), channel_id=1, source_target_pairs={{0,1},{1,0},{2,3},{3,2},{4,5},{5,4},{6,7},{7,6},{8,9},{9,8},{10,11... | collective-permute-start | bytes 983048 | tf_op jit(solution)/shard_map/ppermute | solution.py:350
  28.6 10.0 %collective-permute-start.11 = (bf16[32,4096]{1,0:T(8,128)(2,1)}, bf16[32,4096]{1,0:T(8,128)(2,1)}, u32[]{:S(2)}, u32[]{:S(2)}) collective-permute-start(bf16[32,4096]{1,0:T(8,128)(2,1)} %collective-permute-done.1.refs_1_), channel_id=1, source_target_pairs={{0,1},{1,0},{2,3},{3,2},{4,5},{5,4},{6,7},{7,6},{8,9},{9,8},{10,11... | collective-permute-start | bytes 786440 | tf_op jit(solution)/shard_map/ppermute | solution.py:350
  28.6 12.5 %collective-permute-start.4 = (bf16[32,4096]{1,0:T(8,128)(2,1)}, bf16[32,4096]{1,0:T(8,128)(2,1)}, u32[]{:S(2)}, u32[]{:S(2)}) collective-permute-start(bf16[32,4096]{1,0:T(8,128)(2,1)} %collective-permute-done.refs_0_), channel_id=1, source_target_pairs={{0,2},{1,3},{2,4},{3,5},{4,6},{5,7},{6,0},{7,1},{8,10},{9,11},{10,... | collective-permute-start | bytes 786440 | tf_op jit(solution)/shard_map/ppermute | solution.py:342
  29.3 11.8 %collective-permute-start.5 = (bf16[32,4096]{1,0:T(8,128)(2,1)}, bf16[32,4096]{1,0:T(8,128)(2,1)}, u32[]{:S(2)}, u32[]{:S(2)}) collective-permute-start(bf16[32,4096]{1,0:T(8,128)(2,1)} %collective-permute-done.1.refs_1_), channel_id=1, source_target_pairs={{0,6},{1,7},{2,0},{3,1},{4,2},{5,3},{6,4},{7,5},{8,14},{9,15},{10,... | collective-permute-start | bytes 786440 | tf_op jit(solution)/shard_map/ppermute | solution.py:346
  33.1 8.5 %collective-permute-start.14 = (bf16[8,4096]{1,0:T(8,128)(2,1)}, bf16[8,4096]{1,0:T(8,128)(2,1)}, u32[]{:S(2)}, u32[]{:S(2)}) collective-permute-start(bf16[8,4096]{1,0:T(8,128)(2,1)} %slice.55), channel_id=1, source_target_pairs={{0,2},{1,3},{2,4},{3,5},{4,6},{5,7},{6,0},{7,1},{8,10},{9,11},{10,... | collective-permute-start | bytes 196616 | tf_op jit(solution)/shard_map/ppermute | solution.py:342
  41.1 2.8 %collective-permute-start.12 = (bf16[32,4096]{1,0:T(8,128)(2,1)}, bf16[32,4096]{1,0:T(8,128)(2,1)S(1)}, u32[]{:S(2)}, u32[]{:S(2)}) collective-permute-start(bf16[32,4096]{1,0:T(8,128)(2,1)} %collective-permute-done.4.refs_9_), channel_id=1, source_target_pairs={{0,1},{1,0},{2,3},{3,2},{4,5},{5,4},{6,7},{7,6},{8,9},{9,8},{10,11... | collective-permute-start | bytes 786440 | tf_op jit(solution)/shard_map/ppermute | solution.py:350
  41.1 2.7 %collective-permute-start.13 = (bf16[32,4096]{1,0:T(8,128)(2,1)}, bf16[32,4096]{1,0:T(8,128)(2,1)S(1)}, u32[]{:S(2)}, u32[]{:S(2)}) collective-permute-start(bf16[32,4096]{1,0:T(8,128)(2,1)} %collective-permute-done.5.refs_10_), channel_id=1, source_target_pairs={{0,1},{1,0},{2,3},{3,2},{4,5},{5,4},{6,7},{7,6},{8,9},{9,8},{10,11... | collective-permute-start | bytes 786440 | tf_op jit(solution)/shard_map/ppermute | solution.py:350
  72.3 14.3 %all-to-all-start.1 = ((bf16[32,16,128]{2,1,0:T(8,128)(2,1)}), bf16[32,16,128]{2,1,0:T(8,128)(2,1)S(1)}, u32[]{:S(2)}, u32[]{:S(2)}) async-start(bf16[32,16,128]{2,1,0:T(8,128)(2,1)} %prefix.1), calls=%async_computation.1 | async-start | bytes 262144 | tf_op jit(solution)/shard_map/all_to_all | solution.py:380
  90.9 2.0 %collective-permute-start.16 = (bf16[64,4096]{1,0:T(8,128)(2,1)S(1)}, bf16[64,4096]{1,0:T(8,128)(2,1)S(1)}, u32[]{:S(2)}, u32[]{:S(2)}) collective-permute-start(bf16[64,4096]{1,0:T(8,128)(2,1)S(1)} %get-tuple-element.77), channel_id=1, source_target_pairs={{0,1},{1,0},{2,3},{3,2},{4,5},{5,4},{6,7},{7,6},{8,9},{9,8},{10,11... | collective-permute-start | bytes 1572872 | tf_op jit(solution)/shard_map/ppermute | solution.py:350
  94.8 3.9 %collective-permute-start.17 = (bf16[192,4096]{1,0:T(8,128)(2,1)S(1)}, bf16[192,4096]{1,0:T(8,128)(2,1)S(1)}, u32[]{:S(2)}, u32[]{:S(2)}) collective-permute-start(bf16[192,4096]{1,0:T(8,128)(2,1)S(1)} %get-tuple-element.81), channel_id=1, source_target_pairs={{0,1},{1,0},{2,3},{3,2},{4,5},{5,4},{6,7},{7,6},{8,9},{9,8},{10,11... | collective-permute-start | bytes 4718600 | tf_op jit(solution)/shard_map/ppermute | solution.py:350
  95.1 10.1 %collective-permute-start.18 = (bf16[32,4096]{1,0:T(8,128)(2,1)S(1)}, bf16[32,4096]{1,0:T(8,128)(2,1)S(1)}, u32[]{:S(2)}, u32[]{:S(2)}) collective-permute-start(bf16[32,4096]{1,0:T(8,128)(2,1)S(1)} %get-tuple-element.91), channel_id=1, source_target_pairs={{0,2},{1,3},{2,4},{3,5},{4,6},{5,7},{6,0},{7,1},{8,10},{9,11},{10,... | collective-permute-start | bytes 786440 | tf_op jit(solution)/shard_map/ppermute | solution.py:342
  96.3 8.9 %collective-permute-start.22 = (bf16[32,4096]{1,0:T(8,128)(2,1)S(1)}, bf16[32,4096]{1,0:T(8,128)(2,1)S(1)}, u32[]{:S(2)}, u32[]{:S(2)}) collective-permute-start(bf16[32,4096]{1,0:T(8,128)(2,1)S(1)} %get-tuple-element.92), channel_id=1, source_target_pairs={{0,6},{1,7},{2,0},{3,1},{4,2},{5,3},{6,4},{7,5},{8,14},{9,15},{10,... | collective-permute-start | bytes 786440 | tf_op jit(solution)/shard_map/ppermute | solution.py:346
  105.3 10.5 %collective-permute-start.19 = (bf16[32,4096]{1,0:T(8,128)(2,1)S(1)}, bf16[32,4096]{1,0:T(8,128)(2,1)S(1)}, u32[]{:S(2)}, u32[]{:S(2)}) collective-permute-start(bf16[32,4096]{1,0:T(8,128)(2,1)S(1)} %get-tuple-element.85), channel_id=1, source_target_pairs={{0,2},{1,3},{2,4},{3,5},{4,6},{5,7},{6,0},{7,1},{8,10},{9,11},{10,... | collective-permute-start | bytes 786440 | tf_op jit(solution)/shard_map/ppermute | solution.py:342
  106.5 9.3 %collective-permute-start.23 = (bf16[32,4096]{1,0:T(8,128)(2,1)S(1)}, bf16[32,4096]{1,0:T(8,128)(2,1)S(1)}, u32[]{:S(2)}, u32[]{:S(2)}) collective-permute-start(bf16[32,4096]{1,0:T(8,128)(2,1)S(1)} %get-tuple-element.86), channel_id=1, source_target_pairs={{0,6},{1,7},{2,0},{3,1},{4,2},{5,3},{6,4},{7,5},{8,14},{9,15},{10,... | collective-permute-start | bytes 786440 | tf_op jit(solution)/shard_map/ppermute | solution.py:346
  108.8 10.9 %collective-permute-start.20 = (bf16[32,4096]{1,0:T(8,128)(2,1)S(1)}, bf16[32,4096]{1,0:T(8,128)(2,1)S(1)}, u32[]{:S(2)}, u32[]{:S(2)}) collective-permute-start(bf16[32,4096]{1,0:T(8,128)(2,1)S(1)} %get-tuple-element.89), channel_id=1, source_target_pairs={{0,6},{1,7},{2,0},{3,1},{4,2},{5,3},{6,4},{7,5},{8,14},{9,15},{10,... | collective-permute-start | bytes 786440 | tf_op jit(solution)/shard_map/ppermute | solution.py:346
  110.7 9.6 %collective-permute-start.21 = (bf16[32,4096]{1,0:T(8,128)(2,1)S(1)}, bf16[32,4096]{1,0:T(8,128)(2,1)S(1)}, u32[]{:S(2)}, u32[]{:S(2)}) collective-permute-start(bf16[32,4096]{1,0:T(8,128)(2,1)S(1)} %get-tuple-element.90), channel_id=1, source_target_pairs={{0,2},{1,3},{2,4},{3,5},{4,6},{5,7},{6,0},{7,1},{8,10},{9,11},{10,... | collective-permute-start | bytes 786440 | tf_op jit(solution)/shard_map/ppermute | solution.py:342
  (28 other events, 189.7 us)

commit v3 on v2

--- a/solution.py
+++ b/solution.py
@@ -11,7 +11,7 @@
 F32 = jnp.float32
 VMEM = pl.BlockSpec(memory_space=pltpu.VMEM)
 SMEM = pl.BlockSpec(memory_space=pltpu.SMEM)
-LIMIT = 12 * 1024 * 1024
+LIMIT = 14 * 1024 * 1024
 
 Q = 128
 NQ = 4
@@ -63,23 +63,26 @@
     return pltpu.with_memory_space_constraint(v, pltpu.VMEM)
 
 
-def fill(tok, own, other):
+def fill(tok, own, other, base=0):
     c = core()
     for group, half in ((own, c), (other, 1 - c)):
         step = 64 // len(group)
         for j, r in enumerate(group):
-            at = pl.multiple_of(half * 64 + j * step, step)
-            tok[pl.ds(at, step), :] = r[0:step, :]
+            at = pl.multiple_of(base + half * 64 + j * step, step)
+            tok[pl.ds(at, step), :] = r[...]
 
 
 def project_kernel(n, *refs):
     own, other = refs[:n], refs[n : 2 * n]
     wx, wbc, wdt, xo, bco, dto, tok = refs[2 * n :]
-    fill(tok, own, other)
+    for j in range(n):
+        fill(tok, [own[j]], [other[j]], j * Q)
     rows = tok[...]
     xo[...] = jnp.dot(rows, wx[...], preferred_element_type=F32).astype(BF)
     bco[...] = jnp.dot(rows, wbc[...], preferred_element_type=F32).astype(BF)
-    dto[...] = dot_nt(rows, wdt[...]).T
+    dt = dot_nt(rows, wdt[...])
+    for j in range(n):
+        dto[j] = dt[j * Q : (j + 1) * Q].T
 
 
 def project(own, other, weights, name):
@@ -87,13 +90,13 @@
     return pl.pallas_call(
         functools.partial(project_kernel, n),
         out_shape=(
-            pltpu.VMEM((Q, CH), BF),
-            pltpu.VMEM((Q, BCW), BF),
-            pltpu.VMEM((HH, Q), F32),
+            pltpu.VMEM((n * Q, CH), BF),
+            pltpu.VMEM((n * Q, BCW), BF),
+            pltpu.VMEM((n, HH, Q), F32),
         ),
         in_specs=[VMEM] * (2 * n + 3),
         out_specs=(VMEM, VMEM, VMEM),
-        scratch_shapes=[pltpu.VMEM((Q, 4096), BF)],
+        scratch_shapes=[pltpu.VMEM((n * Q, 4096), BF)],
         compiler_params=params(),
         name=name,
     )(*[in_vmem(v) for v in (*own, *other, *weights)])
@@ -119,15 +122,14 @@
 
 
 def local_kernel(bias, alog, *refs):
-    xs, bcs, dts = refs[0:3], refs[3:6], refs[6:9]
-    far, halo, haloswap = refs[9:13], refs[13], refs[14]
-    wx, wbc, wdt, kx, kbc = refs[15:20]
-    (xo, bo, co, cso, dto, eo, do, send) = refs[20:28]
-    ext, extb, dtr, tok = refs[28:32]
+    x0, bc0, dt0, x12, bc12, dt12 = refs[0:6]
+    far, halo, haloswap = refs[6:10], refs[10], refs[11]
+    wx, wbc, wdt, kx, kbc = refs[12:17]
+    (xo, bo, co, cso, dto, eo, do, send) = refs[17:25]
+    ext, extb, dtr, tok = refs[25:29]
     y = chip()
     fill(tok, far[0:2], far[2:4])
-    mine = core() == 1
-    edge = jnp.where(mine, halo[...].astype(F32), haloswap[...].astype(F32))
+    edge = halo[...].astype(F32) + haloswap[...].astype(F32)
     tok[Q : Q + 16, :] = jnp.concatenate([edge, edge], 0).astype(BF)
     rows = tok[...]
     x3 = jnp.dot(rows, wx[...], preferred_element_type=F32).astype(BF).astype(F32)
@@ -135,12 +137,18 @@
     dt3 = dot_nt(rows[0:Q], wdt[...]).T
     ext[0:8, :] = x3[Q : Q + 8]
     extb[0:8, :] = bc3[Q : Q + 8]
-    for k in range(4):
+    pieces = (
+        (x0[...], bc0[...], dt0[0]),
+        (x12[0:Q], bc12[0:Q], dt12[0]),
+        (x12[Q : 2 * Q], bc12[Q : 2 * Q], dt12[1]),
+        (x3[0:Q], bc3[0:Q], dt3),
+    )
+    for k, (px, pbc, pdt) in enumerate(pieces):
         a = lax.rem(y + OFFS[k], NQ)
         at = pl.multiple_of(a * Q + 8, 8)
-        ext[pl.ds(at, Q), :] = x3[0:Q] if k == 3 else xs[k][...].astype(F32)
-        extb[pl.ds(at, Q), :] = bc3[0:Q] if k == 3 else bcs[k][...].astype(F32)
-        dtr[a] = dt3 if k == 3 else dts[k][...]
+        ext[pl.ds(at, Q), :] = px.astype(F32)
+        extb[pl.ds(at, Q), :] = pbc.astype(F32)
+        dtr[a] = pdt
     ones = head_spread()
     lane = lax.broadcasted_iota(jnp.int32, (HH, Q), 1)
     decay = -jnp.exp(column(alog))
@@ -188,7 +196,7 @@
             send[d] = jnp.concatenate([st[16 * d : 16 * d + 16, :], tail], 0).astype(BF)
 
 
-def local_part(bias, alog, xs, bcs, dts, far, halo, haloswap, weights, kx, kbc):
+def local_part(bias, alog, *args):
     s = pltpu.VMEM
     return pl.pallas_call(
         local_kernel,
@@ -202,7 +210,7 @@
             s((NQ, 8, CH), F32),
             s((32, 24, 128), BF),
         ),
-        in_specs=[SMEM] * 2 + [VMEM] * 20,
+        in_specs=[SMEM] * 2 + [VMEM] * 17,
         out_specs=(VMEM,) * 8,
         scratch_shapes=[
             pltpu.VMEM((8 + NQ * Q, CH), F32),
@@ -212,7 +220,7 @@
         ],
         compiler_params=params(),
         name="local_part",
-    )(bias, alog, *[in_vmem(v) for v in (*xs, *bcs, *dts, *far, halo, haloswap, *weights, kx, kbc)])
+    )(bias, alog, *[in_vmem(v) for v in args])
 
 
 def prefix_kernel(r, o):
@@ -351,29 +359,31 @@
 
 
 def per_device(tokens, in_x, in_bc, in_dt, conv_x, conv_bc, dt_bias, a_log, skip_d, norm_gain, out_w):
-    y = lax.axis_index("tp") // 2
     after = lax.optimization_barrier
     weights = (in_x, in_bc, in_dt.T)
 
-    lo, hi = tokens[:32], tokens[32:]
-    h = lax.ppermute(tokens[56:], "ctx", [(i, i + 1) for i in range(lax.axis_size("ctx") - 1)])
+    u, d = up(tokens), down(tokens)
     partner = swap(tokens)
-    ua, db = up(lo), down(hi)
-    piece0 = project([tokens], [partner], weights, "project_0")
-    up_b, down_a = jnp.concatenate([hi, h], 0), jnp.concatenate([lo, h], 0)
-    ua, db, piece0, up_b, down_a = after((ua, db, piece0, up_b, down_a))
-    ub, da = up(up_b), down(down_a)
-    uua, ddb = up(ua), down(db)
-    huu = up(ub[32:])
-    edge = jnp.where(y == 3, h, jnp.where(y == 0, ub[32:], jnp.where(y == 2, da[32:], huu)))
-    piece1 = project([ua, ub], [swap(ua), swap(ub)], weights, "project_1")
-    piece2 = project([da, db], [swap(da), swap(db)], weights, "project_2")
-    uua, ddb, piece1, piece2 = after((uua, ddb, piece1, piece2))
-    xs, bcs, dts = zip(piece0, piece1, piece2)
-    far = [uua, ddb, swap(uua), swap(ddb)]
+    piece0 = project([tokens], [partner], weights, "project_near")
+    u, d, piece0, partner = after((u, d, piece0, partner))
+    tp = lax.axis_index("tp")
+    tail = jnp.where(
+        tp == 7, tokens[56:], jnp.where(tp == 6, partner[56:], jnp.where(tp == 1, u[56:], d[56:]))
+    )
+    uu, dd = up(u[:32]), down(d[32:])
+    spans = lax.axis_size("ctx")
+    route = ((1, 1), (5, 5), (7, 7), (6, 3))
+    edge = lax.ppermute(
+        tail, ("ctx", "tp"), [(i * 8 + f, i * 8 + 8 + t) for i in range(spans - 1) for f, t in route]
+    )
+    su, sd, edge = after((swap(u), swap(d), edge))
+    edges = swap(edge)
+    piece12 = project([u, d], [su, sd], weights, "project_next")
+    uu, dd, piece12 = after((uu, dd, piece12))
+    far = [uu, dd, swap(uu), swap(dd)]
 
     xc, b, c, cs, dt, e, d, send = local_part(
-        dt_bias, a_log, xs, bcs, dts, far, edge, swap(edge), weights, conv_x, conv_bc
+        dt_bias, a_log, *piece0, *piece12, *far, edge, edges, *weights, conv_x, conv_bc
     )
     got = lax.all_to_all(send, "ctx", 0, 0, tiled=True)
     ydiag = diag_part(skip_d, xc, b, c, cs, dt)
@@ -381,7 +391,6 @@
     other, own, rest = norm_part(back.reshape(CH, NS), e, d, c, cs, ydiag, norm_gain[None, :], out_w)
 
     q2 = (own.astype(F32) + swap(other).astype(F32)).astype(BF)
-    q2, rest = after((q2, rest))
     u2, d2 = up(q2[:32]), down(q2[32:])
     other, own = out_part(rest, out_w)
     q = own.astype(F32) + swap(other).astype(F32)

time: 123 us -> 108 us (0.88)
  local copies, waits for them, and re-layouts: 15.9 us -> 8.02 us
  starting transfers between devices: 28.8 us -> 21 us
  waiting for transfers between devices: 34.3 us -> 37.8 us
  Pallas kernels: 17.6 us -> 14.7 us
  blocking collectives: 21.6 us -> 23.3 us
    ppermute x6 -> x5, starting transfers between devices: 16.1 us -> 6.73 us  [down(): return lax.ppermute(v, 'tp', DOWN)]
    ppermute x6 -> x5, waiting for transfers between devices: 4.27 us -> 12.3 us  [down(): return lax.ppermute(v, 'tp', DOWN)]
    ppermute x7 -> x5, waiting for transfers between devices: 21.6 us -> 16.1 us  [up(): return lax.ppermute(v, 'tp', UP)]
    unnamed x54 -> x30, local copies, waits for them, and re-layouts: 13.2 us -> 7.91 us
    ppermute x7 -> x5, starting transfers between devices: 2.52 us -> 7.18 us  [up(): return lax.ppermute(v, 'tp', UP)]
    ppermute x1, starting transfers between devices: 3.81 us -> 0.8 us  [per_device(): lax.ppermute(tail, ('ctx', 'tp'), [(i * 8 + f, i * 8 + 8 + t) for i in ra...]
    slice x3 -> x2, local copies, waits for them, and re-layouts: 2.68 us -> 0.04 us  [per_device(): uu, dd = (up(u[:32]), down(d[32:]))]
    pallas_call x3 -> x2, Pallas kernels: 6.03 us -> 3.71 us  [project(): pl.pallas_call(functools.partial(project_kernel, n), out_shape=(pltpu.VME...]
  transfers between devices with their start and end apart: 25 -> 20, of which waited for: 10 -> 11; matrix products, arithmetic and copies ran while one was open for 4% -> 1% of each run, Pallas kernels for 6% -> 7%
where the time goes in v3:
time: 108 us; the launch traced here: 107 us
  waiting for transfers between devices  37.8 us (35%)
  blocking collectives  23.3 us (22%)
  starting transfers between devices  21 us (19%)
  Pallas kernels  14.7 us (14%)
  local copies, waits for them, and re-layouts  8.02 us (7%)
  other arithmetic  1.86 us (2%)
    all_to_all x1, blocking collectives, per_device(): got = lax.all_to_all(send, 'ctx', 0, 0, tiled=True)  23.3 us
    ppermute x5, waiting for transfers between devices, up(): return lax.ppermute(v, 'tp', UP)  16.1 us
    ppermute x5, waiting for transfers between devices, down(): return lax.ppermute(v, 'tp', DOWN)  12.3 us
    unnamed x30, local copies, waits for them, and re-layouts  7.91 us
    all_to_all x1, waiting for transfers between devices, per_device(): back = lax.all_to_all(prefix(got), 'ctx', 0, 0, tiled=True)  7.83 us
    ppermute x5, starting transfers between devices, up(): return lax.ppermute(v, 'tp', UP)  7.18 us
    ppermute x5, starting transfers between devices, down(): return lax.ppermute(v, 'tp', DOWN)  6.73 us
    pallas_call x1, Pallas kernels, local_part(): pl.pallas_call(local_kernel, out_shape=(s((NQ, Q, CH), BF), s((NQ, Q, NS)...  4.63 us
  transfers between devices with their start and end apart: 20, of which 11 were waited for; matrix products, arithmetic and copies ran while one was open for 1% of the time, Pallas kernels for 7%

profile of v3, /device:TPU:32, one launch (start us, length us, event | category | flops | bytes accessed | tf_op | source)
XLA Modules:
  0.0 107.0 jit_solution(636568356414972118)
XLA Ops:
  0.0 3.0 %collective-permute-start.1 = (bf16[64,4096]{1,0:T(8,128)(2,1)}, bf16[64,4096]{1,0:T(8,128)(2,1)S(1)}, u32[]{:S(2)}, u32[]{:S(2)}) collective-permute-start(bf16[64,4096]{1,0:T(8,128)(2,1)} %refs_0_.1), channel_id=1, source_target_pairs={{0,6},{1,7},{2,0},{3,1},{4,2},{5,3},{6,4},{7,5},{8,14},{9,15},{10,... | collective-permute-start | bytes 1572872 | tf_op jit(solution)/shard_map/ppermute | solution.py:354
  3.0 2.2 %copy-done = bf16[4096,512]{1,0:T(8,128)(2,1)S(1)} copy-done((bf16[4096,512]{1,0:T(8,128)(2,1)S(1)}, bf16[4096,512]{1,0:T(8,128)(2,1)}, u32[]{:S(2)}) %copy-start) | copy-done | bytes 4194328
  5.2 1.6 %copy-done.2 = bf16[4096,256]{1,0:T(8,128)(2,1)S(1)} copy-done((bf16[4096,256]{1,0:T(8,128)(2,1)S(1)}, bf16[4096,256]{1,0:T(8,128)(2,1)}, u32[]{:S(2)}) %copy-start.2) | copy-done | bytes 2097176
  10.0 5.2 %collective-permute-done.1.refs_1_ = bf16[64,4096]{1,0:T(8,128)(2,1)S(1)} collective-permute-done((bf16[64,4096]{1,0:T(8,128)(2,1)}, bf16[64,4096]{1,0:T(8,128)(2,1)S(1)}, u32[]{:S(2)}, u32[]{:S(2)}) %collective-permute-start.1) | collective-permute-done | bytes 524320 | tf_op jit(solution)/shard_map/ppermute | solution.py:354
  15.2 3.3 %collective-permute-done.refs_0_ = bf16[64,4096]{1,0:T(8,128)(2,1)S(1)} collective-permute-done((bf16[64,4096]{1,0:T(8,128)(2,1)}, bf16[64,4096]{1,0:T(8,128)(2,1)S(1)}, u32[]{:S(2)}, u32[]{:S(2)}) %collective-permute-start) | collective-permute-done | bytes 524320 | tf_op jit(solution)/shard_map/ppermute | solution.py:350
  19.5 1.7 %collective-permute-start.3 = (bf16[32,4096]{1,0:T(8,128)(2,1)S(1)}, bf16[32,4096]{1,0:T(8,128)(2,1)S(1)}, u32[]{:S(2)}, u32[]{:S(2)}) collective-permute-start(bf16[32,4096]{1,0:T(8,128)(2,1)S(1)} %slice.44), channel_id=1, source_target_pairs={{0,2},{1,3},{2,4},{3,5},{4,6},{5,7},{6,0},{7,1},{8,10},{9,11},{10,... | collective-permute-start | bytes 786440 | tf_op jit(solution)/shard_map/ppermute | solution.py:350
  22.2 2.4 %project_next.1 = (bf16[256,512]{1,0:T(8,128)(2,1)S(1)}, bf16[256,256]{1,0:T(8,128)(2,1)S(1)}, f32[2,8,128]{2,1,0:T(8,128)S(1)}) custom-call(bf16[64,4096]{1,0:T(8,128)(2,1)S(1)} %collective-permute-done.refs_0_, bf16[64,4096]{1,0:T(8,128)(2,1)S(1)} %collective-permute-done.1.refs_1_, bf16[64,4096]{1,0:T(8,128)(2,1)S(1)} %collective-permute-done.5.refs_2_, ...), custom_call_target="tpu_custom_call" | custom-call | tf_op jit(solution)/shard_map/project_next/pallas_call | solution.py:90
  24.6 3.0 %collective-permute-done.4.refs_7_ = bf16[32,4096]{1,0:T(8,128)(2,1)S(1)} collective-permute-done((bf16[32,4096]{1,0:T(8,128)(2,1)S(1)}, bf16[32,4096]{1,0:T(8,128)(2,1)S(1)}, u32[]{:S(2)}, u32[]{:S(2)}) %collective-permute-start.4) | collective-permute-done | bytes 262176 | tf_op jit(solution)/shard_map/ppermute | solution.py:354
  29.3 1.5 %collective-permute-done.10.refs_11_ = bf16[8,4096]{1,0:T(8,128)(2,1)S(1)} collective-permute-done((bf16[8,4096]{1,0:T(8,128)(2,1)S(1)}, bf16[8,4096]{1,0:T(8,128)(2,1)S(1)}, u32[]{:S(2)}, u32[]{:S(2)}) %collective-permute-start.10) | collective-permute-done | bytes 65568 | tf_op jit(solution)/shard_map/ppermute | solution.py:358
  30.9 4.6 %local_part.1 = (bf16[4,128,512]{2,1,0:T(8,128)(2,1)S(1)}, bf16[4,128,128]{2,1,0:T(8,128)(2,1)S(1)}, bf16[4,128,128]{2,1,0:T(8,128)(2,1)S(1)}, f32[4,8,128]{2,1,...) custom-call(f32[8]{0:T(128)S(1)} %copy-done.12, ...), custom_call_target="tpu_custom_call" | custom-call | tf_op jit(solution)/shard_map/local_part/pallas_call | solution.py:201
  35.5 23.3 %all_to_all.10.r = bf16[32,24,128]{2,1,0:T(8,128)(2,1)S(1)} all-to-all(bf16[32,24,128]{2,1,0:T(8,128)(2,1)S(1)} %get-tuple-element.58), channel_id=1, replica_groups=mesh['ctx'=32,'tp'=8] {'ctx'}, dimensions={0} | all-to-all | bytes 393216 | tf_op jit(solution)/shard_map/all_to_all | solution.py:388
  59.6 4.5 %all-to-all-start.1 = ((bf16[32,16,128]{2,1,0:T(8,128)(2,1)}), bf16[32,16,128]{2,1,0:T(8,128)(2,1)S(1)}, u32[]{:S(2)}, u32[]{:S(2)}) async-start(bf16[32,16,128]{2,1,0:T(8,128)(2,1)} %prefix.1), calls=%async_computation.1 | async-start | bytes 262144 | tf_op jit(solution)/shard_map/all_to_all | solution.py:390
  64.1 1.8 %diag_part.1.ydiag = f32[4,128,512]{2,1,0:T(8,128)S(1)} custom-call(f32[8]{0:T(128)S(1)} %copy-done.14, bf16[4,128,512]{2,1,0:T(8,128)(2,1)S(1)} %get-tuple-element.63.x, bf16[4,128,128]{2,1,0:T(8,128)(2,1)S(1)} %get-tuple-element.64.b, bf16[4,128,128]{2,1,0:T(8,128)(2,1)S(1)} %get-tuple-element.61.c, f32[4,8,128]{2,1,0:T(8,128)S(1)} %get-tuple-element.62.cs, ...), custom_call_target="tpu_custom_call" | custom-call | tf_op jit(solution)/shard_map/diag_part/pallas_call | solution.py:269
  65.9 7.8 %all-to-all-done.1 = bf16[32,16,128]{2,1,0:T(8,128)(2,1)S(1)} async-done(((bf16[32,16,128]{2,1,0:T(8,128)(2,1)}), bf16[32,16,128]{2,1,0:T(8,128)(2,1)S(1)}, u32[]{:S(2)}, u32[]{:S(2)}) %all-to-all-start.1) | async-done | bytes 131104 | tf_op jit(solution)/shard_map/all_to_all | solution.py:390
  73.7 2.2 %copy-done.4 = bf16[512,4096]{1,0:T(8,128)(2,1)S(1)} copy-done((bf16[512,4096]{1,0:T(8,128)(2,1)S(1)}, bf16[512,4096]{1,0:T(8,128)(2,1)}, u32[]{:S(2)}) %copy-start.4) | copy-done | bytes 4194328
  75.9 2.1 %norm_part.1 = (bf16[64,4096]{1,0:T(8,128)(2,1)S(1)}, bf16[64,4096]{1,0:T(8,128)(2,1)S(1)}, bf16[384,512]{1,0:T(8,128)(2,1)S(1)}) custom-call(bf16[512,128]{1,0:T(8,128)(2,1)S(1)} %bitcast.6, f32[4,128,512]{2,1,0:T(8,128)S(1)} %get-tuple-element.59.e, f32[4,8,512]{2,1,0:T(8,128)S(1)} %get-tuple-element.60.d, bf16[4,128,128]{2,1,0:T(8,128)(2,1)S(1)} %get-tuple-element.61.c, ...), custom_call_target="tpu_custom_call" | custom-call | tf_op jit(solution)/shard_map/norm_part/pallas_call | solution.py:316
  78.1 1.8 %out_part.1 = (bf16[192,4096]{1,0:T(8,128)(2,1)S(1)}, bf16[192,4096]{1,0:T(8,128)(2,1)S(1)}) custom-call(bf16[384,512]{1,0:T(8,128)(2,1)S(1)} %get-tuple-element.66.n, bf16[512,4096]{1,0:T(8,128)(2,1)S(1)} %copy-done.5), custom_call_target="tpu_custom_call" | custom-call | tf_op jit(solution)/shard_map/out_part/pallas_call | solution.py:334
  80.7 3.1 %collective-permute-start.13 = (bf16[32,4096]{1,0:T(8,128)(2,1)S(1)}, bf16[32,4096]{1,0:T(8,128)(2,1)S(1)}, u32[]{:S(2)}, u32[]{:S(2)}) collective-permute-start(bf16[32,4096]{1,0:T(8,128)(2,1)S(1)} %get-tuple-element.79), channel_id=1, source_target_pairs={{0,2},{1,3},{2,4},{3,5},{4,6},{5,7},{6,0},{7,1},{8,10},{9,11},{10,... | collective-permute-start | bytes 786440 | tf_op jit(solution)/shard_map/ppermute | solution.py:350
  84.6 5.5 %collective-permute-done.13 = bf16[32,4096]{1,0:T(8,128)(2,1)S(1)} collective-permute-done((bf16[32,4096]{1,0:T(8,128)(2,1)S(1)}, bf16[32,4096]{1,0:T(8,128)(2,1)S(1)}, u32[]{:S(2)}, u32[]{:S(2)}) %collective-permute-start.13) | collective-permute-done | bytes 262176 | tf_op jit(solution)/shard_map/ppermute | solution.py:350
  90.2 1.5 %collective-permute-done.17 = bf16[32,4096]{1,0:T(8,128)(2,1)S(1)} collective-permute-done((bf16[32,4096]{1,0:T(8,128)(2,1)S(1)}, bf16[32,4096]{1,0:T(8,128)(2,1)S(1)}, u32[]{:S(2)}, u32[]{:S(2)}) %collective-permute-start.17) | collective-permute-done | bytes 262176 | tf_op jit(solution)/shard_map/ppermute | solution.py:354
  92.4 2.9 %collective-permute-start.18 = (bf16[32,4096]{1,0:T(8,128)(2,1)S(1)}, bf16[32,4096]{1,0:T(8,128)(2,1)S(1)}, u32[]{:S(2)}, u32[]{:S(2)}) collective-permute-start(bf16[32,4096]{1,0:T(8,128)(2,1)S(1)} %get-tuple-element.74), channel_id=1, source_target_pairs={{0,6},{1,7},{2,0},{3,1},{4,2},{5,3},{6,4},{7,5},{8,14},{9,15},{10,... | collective-permute-start | bytes 786440 | tf_op jit(solution)/shard_map/ppermute | solution.py:354
  95.6 1.7 %collective-permute-start.16 = (bf16[32,4096]{1,0:T(8,128)(2,1)S(1)}, bf16[32,4096]{1,0:T(8,128)(2,1)S(1)}, u32[]{:S(2)}, u32[]{:S(2)}) collective-permute-start(bf16[32,4096]{1,0:T(8,128)(2,1)S(1)} %get-tuple-element.78), channel_id=1, source_target_pairs={{0,2},{1,3},{2,4},{3,5},{4,6},{5,7},{6,0},{7,1},{8,10},{9,11},{10,... | collective-permute-start | bytes 786440 | tf_op jit(solution)/shard_map/ppermute | solution.py:350
  97.3 5.2 %collective-permute-done.14 = bf16[32,4096]{1,0:T(8,128)(2,1)S(1)} collective-permute-done((bf16[32,4096]{1,0:T(8,128)(2,1)S(1)}, bf16[32,4096]{1,0:T(8,128)(2,1)S(1)}, u32[]{:S(2)}, u32[]{:S(2)}) %collective-permute-start.14) | collective-permute-done | bytes 262176 | tf_op jit(solution)/shard_map/ppermute | solution.py:350
  102.5 2.7 %collective-permute-done.15 = bf16[32,4096]{1,0:T(8,128)(2,1)S(1)} collective-permute-done((bf16[32,4096]{1,0:T(8,128)(2,1)S(1)}, bf16[32,4096]{1,0:T(8,128)(2,1)S(1)}, u32[]{:S(2)}, u32[]{:S(2)}) %collective-permute-start.15) | collective-permute-done | bytes 262176 | tf_op jit(solution)/shard_map/ppermute | solution.py:354
  (64 shorter events, 12.2 us)
Async XLA Ops:
  0.0 3.0 %collective-permute-start.2 = (bf16[64,4096]{1,0:T(8,128)(2,1)}, bf16[64,4096]{1,0:T(8,128)(2,1)S(1)}, u32[]{:S(2)}, u32[]{:S(2)}) collective-permute-start(bf16[64,4096]{1,0:T(8,128)(2,1)} %refs_0_.1), channel_id=1, source_target_pairs={{0,1},{1,0},{2,3},{3,2},{4,5},{5,4},{6,7},{7,6},{8,9},{9,8},{10,11... | collective-permute-start | bytes 1572872 | tf_op jit(solution)/shard_map/ppermute | solution.py:358
  0.0 15.2 %collective-permute-start.1 = (bf16[64,4096]{1,0:T(8,128)(2,1)}, bf16[64,4096]{1,0:T(8,128)(2,1)S(1)}, u32[]{:S(2)}, u32[]{:S(2)}) collective-permute-start(bf16[64,4096]{1,0:T(8,128)(2,1)} %refs_0_.1), channel_id=1, source_target_pairs={{0,6},{1,7},{2,0},{3,1},{4,2},{5,3},{6,4},{7,5},{8,14},{9,15},{10,... | collective-permute-start | bytes 1572872 | tf_op jit(solution)/shard_map/ppermute | solution.py:354
  3.0 15.5 %collective-permute-start = (bf16[64,4096]{1,0:T(8,128)(2,1)}, bf16[64,4096]{1,0:T(8,128)(2,1)S(1)}, u32[]{:S(2)}, u32[]{:S(2)}) collective-permute-start(bf16[64,4096]{1,0:T(8,128)(2,1)} %refs_0_.1), channel_id=1, source_target_pairs={{0,2},{1,3},{2,4},{3,5},{4,6},{5,7},{6,0},{7,1},{8,10},{9,11},{10,... | collective-permute-start | bytes 1572872 | tf_op jit(solution)/shard_map/ppermute | solution.py:350
  8.7 13.5 %copy-start.1 = (bf16[4096,512]{1,0:T(8,128)(2,1)S(1)}, bf16[4096,512]{1,0:T(8,128)(2,1)}, u32[]{:S(2)}) copy-start(bf16[4096,512]{1,0:T(8,128)(2,1)} %refs_12_.1) | copy-start | bytes 12582916
  8.7 13.5 %copy-start.3 = (bf16[4096,256]{1,0:T(8,128)(2,1)S(1)}, bf16[4096,256]{1,0:T(8,128)(2,1)}, u32[]{:S(2)}) copy-start(bf16[4096,256]{1,0:T(8,128)(2,1)} %refs_13_.1) | copy-start | bytes 6291460
  18.5 3.6 %collective-permute-start.5 = (bf16[64,4096]{1,0:T(8,128)(2,1)S(1)}, bf16[64,4096]{1,0:T(8,128)(2,1)S(1)}, u32[]{:S(2)}, u32[]{:S(2)}) collective-permute-start(bf16[64,4096]{1,0:T(8,128)(2,1)S(1)} %collective-permute-done.refs_0_), channel_id=1, source_target_pairs={{0,1},{1,0},{2,3},{3,2},{4,5},{5,4},{6,7},{7,6},{8,9},{9,8},{10,11... | collective-permute-start | bytes 1572872 | tf_op jit(solution)/shard_map/ppermute | solution.py:358
  18.6 3.5 %collective-permute-start.6 = (bf16[64,4096]{1,0:T(8,128)(2,1)S(1)}, bf16[64,4096]{1,0:T(8,128)(2,1)S(1)}, u32[]{:S(2)}, u32[]{:S(2)}) collective-permute-start(bf16[64,4096]{1,0:T(8,128)(2,1)S(1)} %collective-permute-done.1.refs_1_), channel_id=1, source_target_pairs={{0,1},{1,0},{2,3},{3,2},{4,5},{5,4},{6,7},{7,6},{8,9},{9,8},{10,11... | collective-permute-start | bytes 1572872 | tf_op jit(solution)/shard_map/ppermute | solution.py:358
  19.2 8.3 %collective-permute-start.4 = (bf16[32,4096]{1,0:T(8,128)(2,1)S(1)}, bf16[32,4096]{1,0:T(8,128)(2,1)S(1)}, u32[]{:S(2)}, u32[]{:S(2)}) collective-permute-start(bf16[32,4096]{1,0:T(8,128)(2,1)S(1)} %slice.45), channel_id=1, source_target_pairs={{0,6},{1,7},{2,0},{3,1},{4,2},{5,3},{6,4},{7,5},{8,14},{9,15},{10,... | collective-permute-start | bytes 786440 | tf_op jit(solution)/shard_map/ppermute | solution.py:354
  19.5 9.3 %collective-permute-start.3 = (bf16[32,4096]{1,0:T(8,128)(2,1)S(1)}, bf16[32,4096]{1,0:T(8,128)(2,1)S(1)}, u32[]{:S(2)}, u32[]{:S(2)}) collective-permute-start(bf16[32,4096]{1,0:T(8,128)(2,1)S(1)} %slice.44), channel_id=1, source_target_pairs={{0,2},{1,3},{2,4},{3,5},{4,6},{5,7},{6,0},{7,1},{8,10},{9,11},{10,... | collective-permute-start | bytes 786440 | tf_op jit(solution)/shard_map/ppermute | solution.py:350
  21.3 0.8 collective-permute-start.7
  28.8 35.2 %copy-start.14 = (f32[8]{0:T(128)S(1)}, f32[8]{0:T(128)}, u32[]{:S(2)}) copy-start(f32[8]{0:T(128)} %skip.1) | copy-start | bytes 100
  28.8 2.0 %collective-permute-start.8 = (bf16[32,4096]{1,0:T(8,128)(2,1)S(1)}, bf16[32,4096]{1,0:T(8,128)(2,1)S(1)}, u32[]{:S(2)}, u32[]{:S(2)}) collective-permute-start(bf16[32,4096]{1,0:T(8,128)(2,1)S(1)} %collective-permute-done.3.refs_6_), channel_id=1, source_target_pairs={{0,1},{1,0},{2,3},{3,2},{4,5},{5,4},{6,7},{7,6},{8,9},{9,8},{10,11... | collective-permute-start | bytes 786440 | tf_op jit(solution)/shard_map/ppermute | solution.py:358
  28.8 2.0 %collective-permute-start.9 = (bf16[32,4096]{1,0:T(8,128)(2,1)S(1)}, bf16[32,4096]{1,0:T(8,128)(2,1)S(1)}, u32[]{:S(2)}, u32[]{:S(2)}) collective-permute-start(bf16[32,4096]{1,0:T(8,128)(2,1)S(1)} %collective-permute-done.4.refs_7_), channel_id=1, source_target_pairs={{0,1},{1,0},{2,3},{3,2},{4,5},{5,4},{6,7},{7,6},{8,9},{9,8},{10,11... | collective-permute-start | bytes 786440 | tf_op jit(solution)/shard_map/ppermute | solution.py:358
  29.3 1.5 %collective-permute-start.10 = (bf16[8,4096]{1,0:T(8,128)(2,1)S(1)}, bf16[8,4096]{1,0:T(8,128)(2,1)S(1)}, u32[]{:S(2)}, u32[]{:S(2)}) collective-permute-start(bf16[8,4096]{1,0:T(8,128)(2,1)S(1)} %collective-permute-done.7.refs_10_), channel_id=1, source_target_pairs={{0,1},{1,0},{2,3},{3,2},{4,5},{5,4},{6,7},{7,6},{8,9},{9,8},{10,11... | collective-permute-start | bytes 196616 | tf_op jit(solution)/shard_map/ppermute | solution.py:358
  35.5 38.2 %copy-start.11 = (f32[512]{0:T(512)S(1)}, f32[512]{0:T(512)}, u32[]{:S(2)}) copy-start(f32[512]{0:T(512)} %param.20) | copy-start | bytes 6148
  59.6 14.1 %all-to-all-start.1 = ((bf16[32,16,128]{2,1,0:T(8,128)(2,1)}), bf16[32,16,128]{2,1,0:T(8,128)(2,1)S(1)}, u32[]{:S(2)}, u32[]{:S(2)}) async-start(bf16[32,16,128]{2,1,0:T(8,128)(2,1)} %prefix.1), calls=%async_computation.1 | async-start | bytes 262144 | tf_op jit(solution)/shard_map/all_to_all | solution.py:390
  78.0 2.5 %collective-permute-start.12 = (bf16[64,4096]{1,0:T(8,128)(2,1)S(1)}, bf16[64,4096]{1,0:T(8,128)(2,1)S(1)}, u32[]{:S(2)}, u32[]{:S(2)}) collective-permute-start(bf16[64,4096]{1,0:T(8,128)(2,1)S(1)} %get-tuple-element.70), channel_id=1, source_target_pairs={{0,1},{1,0},{2,3},{3,2},{4,5},{5,4},{6,7},{7,6},{8,9},{9,8},{10,11... | collective-permute-start | bytes 1572872 | tf_op jit(solution)/shard_map/ppermute | solution.py:358
  79.9 4.1 %collective-permute-start.11 = (bf16[192,4096]{1,0:T(8,128)(2,1)S(1)}, bf16[192,4096]{1,0:T(8,128)(2,1)S(1)}, u32[]{:S(2)}, u32[]{:S(2)}) collective-permute-start(bf16[192,4096]{1,0:T(8,128)(2,1)S(1)} %get-tuple-element.68), channel_id=1, source_target_pairs={{0,1},{1,0},{2,3},{3,2},{4,5},{5,4},{6,7},{7,6},{8,9},{9,8},{10,11... | collective-permute-start | bytes 4718600 | tf_op jit(solution)/shard_map/ppermute | solution.py:358
  80.7 9.5 %collective-permute-start.13 = (bf16[32,4096]{1,0:T(8,128)(2,1)S(1)}, bf16[32,4096]{1,0:T(8,128)(2,1)S(1)}, u32[]{:S(2)}, u32[]{:S(2)}) collective-permute-start(bf16[32,4096]{1,0:T(8,128)(2,1)S(1)} %get-tuple-element.79), channel_id=1, source_target_pairs={{0,2},{1,3},{2,4},{3,5},{4,6},{5,7},{6,0},{7,1},{8,10},{9,11},{10,... | collective-permute-start | bytes 786440 | tf_op jit(solution)/shard_map/ppermute | solution.py:350
  83.7 8.0 %collective-permute-start.17 = (bf16[32,4096]{1,0:T(8,128)(2,1)S(1)}, bf16[32,4096]{1,0:T(8,128)(2,1)S(1)}, u32[]{:S(2)}, u32[]{:S(2)}) collective-permute-start(bf16[32,4096]{1,0:T(8,128)(2,1)S(1)} %get-tuple-element.80), channel_id=1, source_target_pairs={{0,6},{1,7},{2,0},{3,1},{4,2},{5,3},{6,4},{7,5},{8,14},{9,15},{10,... | collective-permute-start | bytes 786440 | tf_op jit(solution)/shard_map/ppermute | solution.py:354
  91.8 10.8 %collective-permute-start.14 = (bf16[32,4096]{1,0:T(8,128)(2,1)S(1)}, bf16[32,4096]{1,0:T(8,128)(2,1)S(1)}, u32[]{:S(2)}, u32[]{:S(2)}) collective-permute-start(bf16[32,4096]{1,0:T(8,128)(2,1)S(1)} %get-tuple-element.73), channel_id=1, source_target_pairs={{0,2},{1,3},{2,4},{3,5},{4,6},{5,7},{6,0},{7,1},{8,10},{9,11},{10,... | collective-permute-start | bytes 786440 | tf_op jit(solution)/shard_map/ppermute | solution.py:350
  92.4 10.1 %collective-permute-start.18 = (bf16[32,4096]{1,0:T(8,128)(2,1)S(1)}, bf16[32,4096]{1,0:T(8,128)(2,1)S(1)}, u32[]{:S(2)}, u32[]{:S(2)}) collective-permute-start(bf16[32,4096]{1,0:T(8,128)(2,1)S(1)} %get-tuple-element.74), channel_id=1, source_target_pairs={{0,6},{1,7},{2,0},{3,1},{4,2},{5,3},{6,4},{7,5},{8,14},{9,15},{10,... | collective-permute-start | bytes 786440 | tf_op jit(solution)/shard_map/ppermute | solution.py:354
  95.3 9.9 %collective-permute-start.15 = (bf16[32,4096]{1,0:T(8,128)(2,1)S(1)}, bf16[32,4096]{1,0:T(8,128)(2,1)S(1)}, u32[]{:S(2)}, u32[]{:S(2)}) collective-permute-start(bf16[32,4096]{1,0:T(8,128)(2,1)S(1)} %get-tuple-element.77), channel_id=1, source_target_pairs={{0,6},{1,7},{2,0},{3,1},{4,2},{5,3},{6,4},{7,5},{8,14},{9,15},{10,... | collective-permute-start | bytes 786440 | tf_op jit(solution)/shard_map/ppermute | solution.py:354
  95.6 10.4 %collective-permute-start.16 = (bf16[32,4096]{1,0:T(8,128)(2,1)S(1)}, bf16[32,4096]{1,0:T(8,128)(2,1)S(1)}, u32[]{:S(2)}, u32[]{:S(2)}) collective-permute-start(bf16[32,4096]{1,0:T(8,128)(2,1)S(1)} %get-tuple-element.78), channel_id=1, source_target_pairs={{0,2},{1,3},{2,4},{3,5},{4,6},{5,7},{6,0},{7,1},{8,10},{9,11},{10,... | collective-permute-start | bytes 786440 | tf_op jit(solution)/shard_map/ppermute | solution.py:350
  (11 other events, 57.9 us)

commit v4 on v3

--- a/solution.py
+++ b/solution.py
@@ -72,11 +72,13 @@
             tok[pl.ds(at, step), :] = r[...]
 
 
-def project_kernel(n, *refs):
-    own, other = refs[:n], refs[n : 2 * n]
-    wx, wbc, wdt, xo, bco, dto, tok = refs[2 * n :]
+def project_kernel(n, parts, *refs):
+    count = n * parts
+    own, other = refs[:count], refs[count : 2 * count]
+    wx, wbc, wdt, xo, bco, dto, tok = refs[2 * count :]
     for j in range(n):
-        fill(tok, [own[j]], [other[j]], j * Q)
+        of = slice(j * parts, (j + 1) * parts)
+        fill(tok, own[of], other[of], j * Q)
     rows = tok[...]
     xo[...] = jnp.dot(rows, wx[...], preferred_element_type=F32).astype(BF)
     bco[...] = jnp.dot(rows, wbc[...], preferred_element_type=F32).astype(BF)
@@ -85,21 +87,39 @@
         dto[j] = dt[j * Q : (j + 1) * Q].T
 
 
-def project(own, other, weights, name):
-    n = len(own)
-    return pl.pallas_call(
-        functools.partial(project_kernel, n),
+def project(own, other, weights, parts, name):
+    n = len(own) // parts
+    return pl.pallas_call(
+        functools.partial(project_kernel, n, parts),
         out_shape=(
             pltpu.VMEM((n * Q, CH), BF),
             pltpu.VMEM((n * Q, BCW), BF),
             pltpu.VMEM((n, HH, Q), F32),
         ),
-        in_specs=[VMEM] * (2 * n + 3),
+        in_specs=[VMEM] * (2 * n * parts + 3),
         out_specs=(VMEM, VMEM, VMEM),
         scratch_shapes=[pltpu.VMEM((n * Q, 4096), BF)],
         compiler_params=params(),
         name=name,
     )(*[in_vmem(v) for v in (*own, *other, *weights)])
+
+
+def last_kernel(mine, theirs, below, above, o):
+    tp = lax.axis_index("tp")
+    near = jnp.where(tp == 7, mine[48:64].astype(F32), theirs[48:64].astype(F32))
+    far = jnp.where(tp == 1, below[16:32].astype(F32), above[16:32].astype(F32))
+    o[...] = jnp.where(tp >= 6, near, far)[8:16].astype(BF)
+
+
+def last_rows(*args):
+    return pl.pallas_call(
+        last_kernel,
+        out_shape=pltpu.VMEM((8, 4096), BF),
+        in_specs=[VMEM] * 4,
+        out_specs=VMEM,
+        compiler_params=params(),
+        name="last_rows",
+    )(*[in_vmem(v) for v in args])
 
 
 def silu(v):
@@ -276,7 +296,9 @@
     )(skip, *[in_vmem(v) for v in args])
 
 
-def norm_kernel(s_in, e, d, c, cs, ydiag, gain, w, other, own, rest, nb):
+def norm_kernel(s_in, e, d, c, cs, ydiag, gain, w_far, other, own, rest, w, nb, sem):
+    copy = pltpu.make_async_copy(w_far, w, sem)
+    copy.start()
     y = chip()
     mine = core()
     ones = head_spread()
@@ -302,6 +324,7 @@
 
     a = lax.rem(y + 2, NQ)
     v = jnp.concatenate([half(a, 1 - mine), half(a, mine)], 0)
+    copy.wait()
     v = jnp.dot(v, w[...], preferred_element_type=F32).astype(BF)
     other[...] = v[0:64]
     own[...] = v[64:128]
@@ -315,27 +338,28 @@
     s = pltpu.VMEM
     return pl.pallas_call(
         norm_kernel,
-        out_shape=(s((64, 4096), BF), s((64, 4096), BF), s((384, CH), BF)),
-        in_specs=[VMEM] * 8,
-        out_specs=(VMEM,) * 3,
-        scratch_shapes=[pltpu.VMEM((NQ, Q, CH), BF)],
+        out_shape=(s((64, 4096), BF), s((64, 4096), BF), s((384, CH), BF), s((CH, 4096), BF)),
+        in_specs=[VMEM] * 7 + [pl.BlockSpec(memory_space=pltpu.HBM)],
+        out_specs=(VMEM,) * 4,
+        scratch_shapes=[pltpu.VMEM((NQ, Q, CH), BF), pltpu.SemaphoreType.DMA],
         compiler_params=params(),
         name="norm_part",
-    )(*[in_vmem(v) for v in args])
-
-
-def out_kernel(n, w, other, own):
-    other[...] = jnp.dot(n[0:192], w[...], preferred_element_type=F32).astype(BF)
-    own[...] = jnp.dot(n[192:384], w[...], preferred_element_type=F32).astype(BF)
+    )(*[in_vmem(v) for v in args[:7]], pltpu.with_memory_space_constraint(args[7], pltpu.HBM))
+
+
+def out_kernel(n, w, *outs):
+    v = jnp.dot(n[...], w[...], preferred_element_type=F32).astype(BF)
+    for j, o in enumerate(outs):
+        o[...] = v[64 * j : 64 * j + 64]
 
 
 def out_part(n, w):
     s = pltpu.VMEM
     return pl.pallas_call(
         out_kernel,
-        out_shape=(s((192, 4096), BF),) * 2,
+        out_shape=(s((64, 4096), BF),) * 6,
         in_specs=[VMEM] * 2,
-        out_specs=(VMEM,) * 2,
+        out_specs=(VMEM,) * 6,
         compiler_params=params(),
         name="out_part",
     )(in_vmem(n), in_vmem(w))
@@ -362,25 +386,25 @@
     after = lax.optimization_barrier
     weights = (in_x, in_bc, in_dt.T)
 
-    u, d = up(tokens), down(tokens)
+    lo, hi = tokens[:32], tokens[32:]
+    ua, db = up(lo), down(hi)
+    ub, da = up(hi), down(lo)
     partner = swap(tokens)
-    piece0 = project([tokens], [partner], weights, "project_near")
-    u, d, piece0, partner = after((u, d, piece0, partner))
-    tp = lax.axis_index("tp")
-    tail = jnp.where(
-        tp == 7, tokens[56:], jnp.where(tp == 6, partner[56:], jnp.where(tp == 1, u[56:], d[56:]))
-    )
-    uu, dd = up(u[:32]), down(d[32:])
+    piece0 = project([tokens], [partner], weights, 1, "project_near")
+    uu, dd = up(ua), down(db)
+    ub, da, piece0 = after((ub, da, piece0))
+    tail = last_rows(tokens, partner, ub, db)
     spans = lax.axis_size("ctx")
     route = ((1, 1), (5, 5), (7, 7), (6, 3))
     edge = lax.ppermute(
         tail, ("ctx", "tp"), [(i * 8 + f, i * 8 + 8 + t) for i in range(spans - 1) for f, t in route]
     )
-    su, sd, edge = after((swap(u), swap(d), edge))
+    own = [ua, ub, da, db]
+    other = [swap(v) for v in own]
+    *other, edge, uu, dd = after((*other, edge, uu, dd))
     edges = swap(edge)
-    piece12 = project([u, d], [su, sd], weights, "project_next")
-    uu, dd, piece12 = after((uu, dd, piece12))
     far = [uu, dd, swap(uu), swap(dd)]
+    piece12 = project(own, other, weights, 2, "project_next")
 
     xc, b, c, cs, dt, e, d, send = local_part(
         dt_bias, a_log, *piece0, *piece12, *far, edge, edges, *weights, conv_x, conv_bc
@@ -388,17 +412,23 @@
     got = lax.all_to_all(send, "ctx", 0, 0, tiled=True)
     ydiag = diag_part(skip_d, xc, b, c, cs, dt)
     back = lax.all_to_all(prefix(got), "ctx", 0, 0, tiled=True)
-    other, own, rest = norm_part(back.reshape(CH, NS), e, d, c, cs, ydiag, norm_gain[None, :], out_w)
-
-    q2 = (own.astype(F32) + swap(other).astype(F32)).astype(BF)
+    other, own, rest, w = norm_part(back.reshape(CH, NS), e, d, c, cs, ydiag, norm_gain[None, :], out_w)
+
+    def both(mine, theirs):
+        return mine.astype(F32) + swap(theirs).astype(F32)
+
+    q2 = both(own, other).astype(BF)
     u2, d2 = up(q2[:32]), down(q2[32:])
-    other, own = out_part(rest, out_w)
-    q = own.astype(F32) + swap(other).astype(F32)
-    u1b, dma = up(q[32:64].astype(BF)), down(q[64:96].astype(BF))
-    u1a = up((q[:32] + u2.astype(F32)).astype(BF))
-    dmb = down((q[96:128] + d2.astype(F32)).astype(BF))
-    top = q[128:160] + u1a.astype(F32) + dma.astype(F32)
-    bottom = q[160:192] + u1b.astype(F32) + dmb.astype(F32)
+    t1, tm, t0, m1, mm, m0 = out_part(rest, w)
+    q1 = both(m1, t1)
+    u1b = up(q1[32:].astype(BF))
+    qm = both(mm, tm)
+    dma = down(qm[:32].astype(BF))
+    u1a = up((q1[:32] + u2.astype(F32)).astype(BF))
+    dmb = down((qm[32:] + d2.astype(F32)).astype(BF))
+    q0 = both(m0, t0)
+    top = q0[:32] + u1a.astype(F32) + dma.astype(F32)
+    bottom = q0[32:] + u1b.astype(F32) + dmb.astype(F32)
     return jnp.concatenate([top.astype(BF), bottom.astype(BF)], 0)
 
 

time: 108 us -> 107 us (level)
  waiting for transfers between devices: 37.8 us -> 25.9 us
  starting transfers between devices: 21 us -> 31.8 us
  local copies, waits for them, and re-layouts: 8.02 us -> 6.86 us
    ppermute x5 -> x6, starting transfers between devices: 6.73 us -> 17.9 us  [down(): return lax.ppermute(v, 'tp', DOWN)]
    ppermute x5 -> x6, waiting for transfers between devices: 16.1 us -> 9.23 us  [up(): return lax.ppermute(v, 'tp', UP)]
    ppermute x5 -> x6, starting transfers between devices: 7.18 us -> 3.08 us  [up(): return lax.ppermute(v, 'tp', UP)]
    ppermute x8 -> x12, starting transfers between devices: 1.85 us -> 5.65 us  [swap(): return lax.ppermute(v, 'tp', SWAP)]
    ppermute x5 -> x6, waiting for transfers between devices: 12.3 us -> 8.67 us  [down(): return lax.ppermute(v, 'tp', DOWN)]
    unnamed x30 -> x26, local copies, waits for them, and re-layouts: 7.91 us -> 5.71 us
    ppermute x8 -> x12, waiting for transfers between devices: 1.51 us -> 0.03 us  [swap(): return lax.ppermute(v, 'tp', SWAP)]
    pallas_call x3 -> x4, Pallas kernels: 5.52 us -> 5.57 us  [the longest x2 3.73 us: project(): pl.pallas_call(functools.partial(project_kernel, n, parts), out_shape=(pl...]
  transfers between devices with their start and end apart: 20 -> 26, of which waited for: 11 -> 7; matrix products, arithmetic and copies ran while one was open for 1% -> 2% of each run, Pallas kernels for 7% -> 7%
where the time goes in v4:
time: 107 us; the launch traced here: 106 us
  starting transfers between devices  31.8 us (30%)
  waiting for transfers between devices  25.9 us (24%)
  blocking collectives  23.4 us (22%)
  Pallas kernels  15.7 us (15%)
  local copies, waits for them, and re-layouts  6.86 us (6%)
  other arithmetic  1.54 us (1%)
    all_to_all x1, blocking collectives, per_device(): got = lax.all_to_all(send, 'ctx', 0, 0, tiled=True)  23.4 us
    ppermute x6, starting transfers between devices, down(): return lax.ppermute(v, 'tp', DOWN)  17.9 us
    ppermute x6, waiting for transfers between devices, up(): return lax.ppermute(v, 'tp', UP)  9.23 us
    ppermute x6, waiting for transfers between devices, down(): return lax.ppermute(v, 'tp', DOWN)  8.67 us
    all_to_all x1, waiting for transfers between devices, per_device(): back = lax.all_to_all(prefix(got), 'ctx', 0, 0, tiled=True)  7.92 us
    unnamed x26, local copies, waits for them, and re-layouts  5.71 us
    ppermute x12, starting transfers between devices, swap(): return lax.ppermute(v, 'tp', SWAP)  5.65 us
    pallas_call x1, Pallas kernels, local_part(): pl.pallas_call(local_kernel, out_shape=(s((NQ, Q, CH), BF), s((NQ, Q, NS)...  4.63 us
  transfers between devices with their start and end apart: 26, of which 7 were waited for; matrix products, arithmetic and copies ran while one was open for 2% of the time, Pallas kernels for 7%

profile of v4, /device:TPU:32, one launch (start us, length us, event | category | flops | bytes accessed | tf_op | source)
XLA Modules:
  0.0 105.5 jit_solution(14236742249059378504)
XLA Ops:
  1.1 3.1 %collective-permute-start.4 = (bf16[32,4096]{1,0:T(8,128)(2,1)S(1)}, bf16[32,4096]{1,0:T(8,128)(2,1)S(1)}, u32[]{:S(2)}, u32[]{:S(2)}) collective-permute-start(bf16[32,4096]{1,0:T(8,128)(2,1)S(1)} %get-tuple-element.82), channel_id=1, source_target_pairs={{0,6},{1,7},{2,0},{3,1},{4,2},{5,3},{6,4},{7,5},{8,14},{9,15},{10,... | collective-permute-start | bytes 786440 | tf_op jit(solution)/shard_map/ppermute | solution.py:378
  4.8 2.7 %collective-permute-start.1 = (bf16[32,4096]{1,0:T(8,128)(2,1)S(1)}, bf16[32,4096]{1,0:T(8,128)(2,1)S(1)}, u32[]{:S(2)}, u32[]{:S(2)}) collective-permute-start(bf16[32,4096]{1,0:T(8,128)(2,1)S(1)} %get-tuple-element.81), channel_id=1, source_target_pairs={{0,6},{1,7},{2,0},{3,1},{4,2},{5,3},{6,4},{7,5},{8,14},{9,15},{10,... | collective-permute-start | bytes 786440 | tf_op jit(solution)/shard_map/ppermute | solution.py:378
  7.4 3.3 %collective-permute-done.4.above.refs_3_ = bf16[32,4096]{1,0:T(8,128)(2,1)S(1)} collective-permute-done((bf16[32,4096]{1,0:T(8,128)(2,1)S(1)}, bf16[32,4096]{1,0:T(8,128)(2,1)S(1)}, u32[]{:S(2)}, u32[]{:S(2)}) %collective-permute-start.4) | collective-permute-done | bytes 262176 | tf_op jit(solution)/shard_map/ppermute | solution.py:378
  10.8 3.7 %collective-permute-start.11 = (bf16[32,4096]{1,0:T(8,128)(2,1)S(1)}, bf16[32,4096]{1,0:T(8,128)(2,1)S(1)}, u32[]{:S(2)}, u32[]{:S(2)}) collective-permute-start(bf16[32,4096]{1,0:T(8,128)(2,1)S(1)} %collective-permute-done.4.above.refs_3_), channel_id=1, source_target_pairs={{0,6},{1,7},{2,0},{3,1},{4,2},{5,3},{6,4},{7,5},{8,14},{9,15},{10,... | collective-permute-start | bytes 786440 | tf_op jit(solution)/shard_map/ppermute | solution.py:378
  14.6 2.2 %copy-done = bf16[4096,512]{1,0:T(8,128)(2,1)S(1)} copy-done((bf16[4096,512]{1,0:T(8,128)(2,1)S(1)}, bf16[4096,512]{1,0:T(8,128)(2,1)}, u32[]{:S(2)}) %copy-start) | copy-done | bytes 4194328
  16.8 1.6 %copy-done.2 = bf16[4096,256]{1,0:T(8,128)(2,1)S(1)} copy-done((bf16[4096,256]{1,0:T(8,128)(2,1)S(1)}, bf16[4096,256]{1,0:T(8,128)(2,1)}, u32[]{:S(2)}) %copy-start.2) | copy-done | bytes 2097176
  23.5 1.5 %collective-permute-done.10.refs_6_ = bf16[32,4096]{1,0:T(8,128)(2,1)S(1)} collective-permute-done((bf16[32,4096]{1,0:T(8,128)(2,1)S(1)}, bf16[32,4096]{1,0:T(8,128)(2,1)S(1)}, u32[]{:S(2)}, u32[]{:S(2)}) %collective-permute-start.10) | collective-permute-done | bytes 262176 | tf_op jit(solution)/shard_map/ppermute | solution.py:374
  25.1 2.9 %collective-permute-start.12 = (bf16[32,4096]{1,0:T(8,128)(2,1)S(1)}, bf16[32,4096]{1,0:T(8,128)(2,1)S(1)}, u32[]{:S(2)}, u32[]{:S(2)}) collective-permute-start(bf16[32,4096]{1,0:T(8,128)(2,1)S(1)} %collective-permute-done.10.refs_6_), channel_id=1, source_target_pairs={{0,1},{1,0},{2,3},{3,2},{4,5},{5,4},{6,7},{7,6},{8,9},{9,8},{10,11... | collective-permute-start | bytes 786440 | tf_op jit(solution)/shard_map/ppermute | solution.py:382
  28.5 2.4 %project_next.1 = (bf16[256,512]{1,0:T(8,128)(2,1)S(1)}, bf16[256,256]{1,0:T(8,128)(2,1)S(1)}, f32[2,8,128]{2,1,0:T(8,128)S(1)}) custom-call(bf16[32,4096]{1,0:T(8,128)(2,1)S(1)} %collective-permute-done.3.refs_0_, bf16[32,4096]{1,0:T(8,128)(2,1)S(1)} %collective-permute-done.below.refs_1_, bf16[32,4096]{1,0:T(8,128)(2,1)S(1)} %collective-permute-done.1.refs_2_, ...), custom_call_target="tpu_custom_call" | custom-call | tf_op jit(solution)/shard_map/project_next/pallas_call | solution.py:92
  31.0 4.6 %local_part.1 = (bf16[4,128,512]{2,1,0:T(8,128)(2,1)S(1)}, bf16[4,128,128]{2,1,0:T(8,128)(2,1)S(1)}, bf16[4,128,128]{2,1,0:T(8,128)(2,1)S(1)}, f32[4,8,128]{2,1,...) custom-call(f32[8]{0:T(128)S(1)} %copy-done.10, ...), custom_call_target="tpu_custom_call" | custom-call | tf_op jit(solution)/shard_map/local_part/pallas_call | solution.py:221
  35.6 23.4 %all_to_all.10.r = bf16[32,24,128]{2,1,0:T(8,128)(2,1)S(1)} all-to-all(bf16[32,24,128]{2,1,0:T(8,128)(2,1)S(1)} %get-tuple-element.59), channel_id=1, replica_groups=mesh['ctx'=32,'tp'=8] {'ctx'}, dimensions={0} | all-to-all | bytes 393216 | tf_op jit(solution)/shard_map/all_to_all | solution.py:412
  59.8 4.5 %all-to-all-start.1 = ((bf16[32,16,128]{2,1,0:T(8,128)(2,1)}), bf16[32,16,128]{2,1,0:T(8,128)(2,1)S(1)}, u32[]{:S(2)}, u32[]{:S(2)}) async-start(bf16[32,16,128]{2,1,0:T(8,128)(2,1)} %prefix.1), calls=%async_computation.1 | async-start | bytes 262144 | tf_op jit(solution)/shard_map/all_to_all | solution.py:414
  64.3 1.8 %diag_part.1.ydiag = f32[4,128,512]{2,1,0:T(8,128)S(1)} custom-call(f32[8]{0:T(128)S(1)} %copy-done.12, bf16[4,128,512]{2,1,0:T(8,128)(2,1)S(1)} %get-tuple-element.64.x, bf16[4,128,128]{2,1,0:T(8,128)(2,1)S(1)} %get-tuple-element.65.b, bf16[4,128,128]{2,1,0:T(8,128)(2,1)S(1)} %get-tuple-element.62.c, f32[4,8,128]{2,1,0:T(8,128)S(1)} %get-tuple-element.63.cs, ...), custom_call_target="tpu_custom_call" | custom-call | tf_op jit(solution)/shard_map/diag_part/pallas_call | solution.py:289
  66.1 7.9 %all-to-all-done.1 = bf16[32,16,128]{2,1,0:T(8,128)(2,1)S(1)} async-done(((bf16[32,16,128]{2,1,0:T(8,128)(2,1)}), bf16[32,16,128]{2,1,0:T(8,128)(2,1)S(1)}, u32[]{:S(2)}, u32[]{:S(2)}) %all-to-all-start.1) | async-done | bytes 131104 | tf_op jit(solution)/shard_map/all_to_all | solution.py:414
  74.0 2.9 %norm_part.1 = (bf16[64,4096]{1,0:T(8,128)(2,1)S(1)}, bf16[64,4096]{1,0:T(8,128)(2,1)S(1)}, bf16[384,512]{1,0:T(8,128)(2,1)S(1)}, bf16[512,4096]{1,0:T(8,128)(2,1)S(1)}) custom-call(bf16[512,128]{1,0:T(8,128)(2,1)S(1)} %bitcast.6, f32[4,128,512]{2,1,0:T(8,128)S(1)} %get-tuple-element.60.e, f32[4,8,512]{2,1,0:T(8,128)S(1)} %get-tuple-element.61.d, ...), custom_call_target="tpu_custom_call" | custom-call | tf_op jit(solution)/shard_map/norm_part/pallas_call | solution.py:339
  77.1 1.8 %out_part.1 = (bf16[64,4096]{1,0:T(8,128)(2,1)S(1)}, bf16[64,4096]{1,0:T(8,128)(2,1)S(1)}, bf16[64,4096]{1,0:T(8,128)(2,1)S(1)}, bf16[64,4096]{1,0:T(8,128)(2,1)...) custom-call(bf16[384,512]{1,0:T(8,128)(2,1)S(1)} %get-tuple-element.67.n, ...), custom_call_target="tpu_custom_call" | custom-call | tf_op jit(solution)/shard_map/out_part/pallas_call | solution.py:358
  80.1 3.9 %collective-permute-start.23 = (bf16[32,4096]{1,0:T(8,128)(2,1)S(1)}, bf16[32,4096]{1,0:T(8,128)(2,1)S(1)}, u32[]{:S(2)}, u32[]{:S(2)}) collective-permute-start(bf16[32,4096]{1,0:T(8,128)(2,1)S(1)} %get-tuple-element.80), channel_id=1, source_target_pairs={{0,6},{1,7},{2,0},{3,1},{4,2},{5,3},{6,4},{7,5},{8,14},{9,15},{10,... | collective-permute-start | bytes 786440 | tf_op jit(solution)/shard_map/ppermute | solution.py:378
  84.5 2.0 %collective-permute-start.22 = (bf16[32,4096]{1,0:T(8,128)(2,1)S(1)}, bf16[32,4096]{1,0:T(8,128)(2,1)S(1)}, u32[]{:S(2)}, u32[]{:S(2)}) collective-permute-start(bf16[32,4096]{1,0:T(8,128)(2,1)S(1)} %slice.68), channel_id=1, source_target_pairs={{0,2},{1,3},{2,4},{3,5},{4,6},{5,7},{6,0},{7,1},{8,10},{9,11},{10,... | collective-permute-start | bytes 786440 | tf_op jit(solution)/shard_map/ppermute | solution.py:374
  86.7 1.4 %collective-permute-start.21 = (bf16[32,4096]{1,0:T(8,128)(2,1)S(1)}, bf16[32,4096]{1,0:T(8,128)(2,1)S(1)}, u32[]{:S(2)}, u32[]{:S(2)}) collective-permute-start(bf16[32,4096]{1,0:T(8,128)(2,1)S(1)} %slice.69), channel_id=1, source_target_pairs={{0,6},{1,7},{2,0},{3,1},{4,2},{5,3},{6,4},{7,5},{8,14},{9,15},{10,... | collective-permute-start | bytes 786440 | tf_op jit(solution)/shard_map/ppermute | solution.py:378
  88.1 3.3 %collective-permute-done.23 = bf16[32,4096]{1,0:T(8,128)(2,1)S(1)} collective-permute-done((bf16[32,4096]{1,0:T(8,128)(2,1)S(1)}, bf16[32,4096]{1,0:T(8,128)(2,1)S(1)}, u32[]{:S(2)}, u32[]{:S(2)}) %collective-permute-start.23) | collective-permute-done | bytes 262176 | tf_op jit(solution)/shard_map/ppermute | solution.py:378
  91.5 3.1 %collective-permute-start.24 = (bf16[32,4096]{1,0:T(8,128)(2,1)S(1)}, bf16[32,4096]{1,0:T(8,128)(2,1)S(1)}, u32[]{:S(2)}, u32[]{:S(2)}) collective-permute-start(bf16[32,4096]{1,0:T(8,128)(2,1)S(1)} %fusion), channel_id=1, source_target_pairs={{0,6},{1,7},{2,0},{3,1},{4,2},{5,3},{6,4},{7,5},{8,14},{9,15},{10,... | collective-permute-start | bytes 786440 | tf_op jit(solution)/shard_map/ppermute | solution.py:378
  94.8 5.3 %collective-permute-done.22 = bf16[32,4096]{1,0:T(8,128)(2,1)S(1)} collective-permute-done((bf16[32,4096]{1,0:T(8,128)(2,1)S(1)}, bf16[32,4096]{1,0:T(8,128)(2,1)S(1)}, u32[]{:S(2)}, u32[]{:S(2)}) %collective-permute-start.22) | collective-permute-done | bytes 262176 | tf_op jit(solution)/shard_map/ppermute | solution.py:374
  100.1 2.0 %collective-permute-done.24 = bf16[32,4096]{1,0:T(8,128)(2,1)S(1)} collective-permute-done((bf16[32,4096]{1,0:T(8,128)(2,1)S(1)}, bf16[32,4096]{1,0:T(8,128)(2,1)S(1)}, u32[]{:S(2)}, u32[]{:S(2)}) %collective-permute-start.24) | collective-permute-done | bytes 262176 | tf_op jit(solution)/shard_map/ppermute | solution.py:378
  102.1 2.4 %collective-permute-done.19 = bf16[32,4096]{1,0:T(8,128)(2,1)S(1)} collective-permute-done((bf16[32,4096]{1,0:T(8,128)(2,1)S(1)}, bf16[32,4096]{1,0:T(8,128)(2,1)S(1)}, u32[]{:S(2)}, u32[]{:S(2)}) %collective-permute-start.19) | collective-permute-done | bytes 262176 | tf_op jit(solution)/shard_map/ppermute | solution.py:374
  (75 shorter events, 11.4 us)
Async XLA Ops:
  0.0 14.5 %collective-permute-start.2 = (bf16[64,4096]{1,0:T(8,128)(2,1)}, bf16[64,4096]{1,0:T(8,128)(2,1)S(1)}, u32[]{:S(2)}, u32[]{:S(2)}) collective-permute-start(bf16[64,4096]{1,0:T(8,128)(2,1)} %mine.1), channel_id=1, source_target_pairs={{0,1},{1,0},{2,3},{3,2},{4,5},{5,4},{6,7},{7,6},{8,9},{9,8},{10,11... | collective-permute-start | bytes 1572872 | tf_op jit(solution)/shard_map/ppermute | solution.py:382
  1.1 9.7 %collective-permute-start.4 = (bf16[32,4096]{1,0:T(8,128)(2,1)S(1)}, bf16[32,4096]{1,0:T(8,128)(2,1)S(1)}, u32[]{:S(2)}, u32[]{:S(2)}) collective-permute-start(bf16[32,4096]{1,0:T(8,128)(2,1)S(1)} %get-tuple-element.82), channel_id=1, source_target_pairs={{0,6},{1,7},{2,0},{3,1},{4,2},{5,3},{6,4},{7,5},{8,14},{9,15},{10,... | collective-permute-start | bytes 786440 | tf_op jit(solution)/shard_map/ppermute | solution.py:378
  4.2 10.4 %collective-permute-start.3 = (bf16[32,4096]{1,0:T(8,128)(2,1)S(1)}, bf16[32,4096]{1,0:T(8,128)(2,1)S(1)}, u32[]{:S(2)}, u32[]{:S(2)}) collective-permute-start(bf16[32,4096]{1,0:T(8,128)(2,1)S(1)} %get-tuple-element.81), channel_id=1, source_target_pairs={{0,2},{1,3},{2,4},{3,5},{4,6},{5,7},{6,0},{7,1},{8,10},{9,11},{10,... | collective-permute-start | bytes 786440 | tf_op jit(solution)/shard_map/ppermute | solution.py:374
  4.2 17.4 %collective-permute-start = (bf16[32,4096]{1,0:T(8,128)(2,1)S(1)}, bf16[32,4096]{1,0:T(8,128)(2,1)S(1)}, u32[]{:S(2)}, u32[]{:S(2)}) collective-permute-start(bf16[32,4096]{1,0:T(8,128)(2,1)S(1)} %get-tuple-element.82), channel_id=1, source_target_pairs={{0,2},{1,3},{2,4},{3,5},{4,6},{5,7},{6,0},{7,1},{8,10},{9,11},{10,... | collective-permute-start | bytes 786440 | tf_op jit(solution)/shard_map/ppermute | solution.py:374
  4.8 17.4 %collective-permute-start.1 = (bf16[32,4096]{1,0:T(8,128)(2,1)S(1)}, bf16[32,4096]{1,0:T(8,128)(2,1)S(1)}, u32[]{:S(2)}, u32[]{:S(2)}) collective-permute-start(bf16[32,4096]{1,0:T(8,128)(2,1)S(1)} %get-tuple-element.81), channel_id=1, source_target_pairs={{0,6},{1,7},{2,0},{3,1},{4,2},{5,3},{6,4},{7,5},{8,14},{9,15},{10,... | collective-permute-start | bytes 786440 | tf_op jit(solution)/shard_map/ppermute | solution.py:378
  10.8 11.4 %collective-permute-start.11 = (bf16[32,4096]{1,0:T(8,128)(2,1)S(1)}, bf16[32,4096]{1,0:T(8,128)(2,1)S(1)}, u32[]{:S(2)}, u32[]{:S(2)}) collective-permute-start(bf16[32,4096]{1,0:T(8,128)(2,1)S(1)} %collective-permute-done.4.above.refs_3_), channel_id=1, source_target_pairs={{0,6},{1,7},{2,0},{3,1},{4,2},{5,3},{6,4},{7,5},{8,14},{9,15},{10,... | collective-permute-start | bytes 786440 | tf_op jit(solution)/shard_map/ppermute | solution.py:378
  14.5 8.2 %collective-permute-start.8 = (bf16[32,4096]{1,0:T(8,128)(2,1)S(1)}, bf16[32,4096]{1,0:T(8,128)(2,1)S(1)}, u32[]{:S(2)}, u32[]{:S(2)}) collective-permute-start(bf16[32,4096]{1,0:T(8,128)(2,1)S(1)} %collective-permute-done.4.above.refs_3_), channel_id=1, source_target_pairs={{0,1},{1,0},{2,3},{3,2},{4,5},{5,4},{6,7},{7,6},{8,9},{9,8},{10,11... | collective-permute-start | bytes 786440 | tf_op jit(solution)/shard_map/ppermute | solution.py:382
  14.5 10.5 %collective-permute-start.10 = (bf16[32,4096]{1,0:T(8,128)(2,1)S(1)}, bf16[32,4096]{1,0:T(8,128)(2,1)S(1)}, u32[]{:S(2)}, u32[]{:S(2)}) collective-permute-start(bf16[32,4096]{1,0:T(8,128)(2,1)S(1)} %collective-permute-done.3.refs_0_), channel_id=1, source_target_pairs={{0,2},{1,3},{2,4},{3,5},{4,6},{5,7},{6,0},{7,1},{8,10},{9,11},{10,... | collective-permute-start | bytes 786440 | tf_op jit(solution)/shard_map/ppermute | solution.py:374
  21.6 3.4 %collective-permute-start.5 = (bf16[32,4096]{1,0:T(8,128)(2,1)S(1)}, bf16[32,4096]{1,0:T(8,128)(2,1)S(1)}, u32[]{:S(2)}, u32[]{:S(2)}) collective-permute-start(bf16[32,4096]{1,0:T(8,128)(2,1)S(1)} %collective-permute-done.3.refs_0_), channel_id=1, source_target_pairs={{0,1},{1,0},{2,3},{3,2},{4,5},{5,4},{6,7},{7,6},{8,9},{9,8},{10,11... | collective-permute-start | bytes 786440 | tf_op jit(solution)/shard_map/ppermute | solution.py:382
  22.1 2.9 %collective-permute-start.6 = (bf16[32,4096]{1,0:T(8,128)(2,1)S(1)}, bf16[32,4096]{1,0:T(8,128)(2,1)S(1)}, u32[]{:S(2)}, u32[]{:S(2)}) collective-permute-start(bf16[32,4096]{1,0:T(8,128)(2,1)S(1)} %collective-permute-done.below.refs_1_), channel_id=1, source_target_pairs={{0,1},{1,0},{2,3},{3,2},{4,5},{5,4},{6,7},{7,6},{8,9},{9,8},{10,11... | collective-permute-start | bytes 786440 | tf_op jit(solution)/shard_map/ppermute | solution.py:382
  22.2 2.8 %collective-permute-start.7 = (bf16[32,4096]{1,0:T(8,128)(2,1)S(1)}, bf16[32,4096]{1,0:T(8,128)(2,1)S(1)}, u32[]{:S(2)}, u32[]{:S(2)}) collective-permute-start(bf16[32,4096]{1,0:T(8,128)(2,1)S(1)} %collective-permute-done.1.refs_2_), channel_id=1, source_target_pairs={{0,1},{1,0},{2,3},{3,2},{4,5},{5,4},{6,7},{7,6},{8,9},{9,8},{10,11... | collective-permute-start | bytes 786440 | tf_op jit(solution)/shard_map/ppermute | solution.py:382
  25.1 5.8 %collective-permute-start.12 = (bf16[32,4096]{1,0:T(8,128)(2,1)S(1)}, bf16[32,4096]{1,0:T(8,128)(2,1)S(1)}, u32[]{:S(2)}, u32[]{:S(2)}) collective-permute-start(bf16[32,4096]{1,0:T(8,128)(2,1)S(1)} %collective-permute-done.10.refs_6_), channel_id=1, source_target_pairs={{0,1},{1,0},{2,3},{3,2},{4,5},{5,4},{6,7},{7,6},{8,9},{9,8},{10,11... | collective-permute-start | bytes 786440 | tf_op jit(solution)/shard_map/ppermute | solution.py:382
  28.0 2.9 %collective-permute-start.13 = (bf16[32,4096]{1,0:T(8,128)(2,1)S(1)}, bf16[32,4096]{1,0:T(8,128)(2,1)S(1)}, u32[]{:S(2)}, u32[]{:S(2)}) collective-permute-start(bf16[32,4096]{1,0:T(8,128)(2,1)S(1)} %collective-permute-done.11.refs_7_), channel_id=1, source_target_pairs={{0,1},{1,0},{2,3},{3,2},{4,5},{5,4},{6,7},{7,6},{8,9},{9,8},{10,11... | collective-permute-start | bytes 786440 | tf_op jit(solution)/shard_map/ppermute | solution.py:382
  59.8 14.2 %all-to-all-start.1 = ((bf16[32,16,128]{2,1,0:T(8,128)(2,1)}), bf16[32,16,128]{2,1,0:T(8,128)(2,1)S(1)}, u32[]{:S(2)}, u32[]{:S(2)}) async-start(bf16[32,16,128]{2,1,0:T(8,128)(2,1)} %prefix.1), calls=%async_computation.1 | async-start | bytes 262144 | tf_op jit(solution)/shard_map/all_to_all | solution.py:414
  77.0 3.0 %collective-permute-start.17 = (bf16[64,4096]{1,0:T(8,128)(2,1)S(1)}, bf16[64,4096]{1,0:T(8,128)(2,1)S(1)}, u32[]{:S(2)}, u32[]{:S(2)}) collective-permute-start(bf16[64,4096]{1,0:T(8,128)(2,1)S(1)} %get-tuple-element.74), channel_id=1, source_target_pairs={{0,1},{1,0},{2,3},{3,2},{4,5},{5,4},{6,7},{7,6},{8,9},{9,8},{10,11... | collective-permute-start | bytes 1572872 | tf_op jit(solution)/shard_map/ppermute | solution.py:382
  78.9 7.7 %collective-permute-start.20 = (bf16[64,4096]{1,0:T(8,128)(2,1)S(1)}, bf16[64,4096]{1,0:T(8,128)(2,1)S(1)}, u32[]{:S(2)}, u32[]{:S(2)}) collective-permute-start(bf16[64,4096]{1,0:T(8,128)(2,1)S(1)} %get-tuple-element.76), channel_id=1, source_target_pairs={{0,1},{1,0},{2,3},{3,2},{4,5},{5,4},{6,7},{7,6},{8,9},{9,8},{10,11... | collective-permute-start | bytes 1572872 | tf_op jit(solution)/shard_map/ppermute | solution.py:382
  79.5 4.9 %collective-permute-start.16 = (bf16[64,4096]{1,0:T(8,128)(2,1)S(1)}, bf16[64,4096]{1,0:T(8,128)(2,1)S(1)}, u32[]{:S(2)}, u32[]{:S(2)}) collective-permute-start(bf16[64,4096]{1,0:T(8,128)(2,1)S(1)} %get-tuple-element.72), channel_id=1, source_target_pairs={{0,1},{1,0},{2,3},{3,2},{4,5},{5,4},{6,7},{7,6},{8,9},{9,8},{10,11... | collective-permute-start | bytes 1572872 | tf_op jit(solution)/shard_map/ppermute | solution.py:382
  79.6 15.2 %collective-permute-start.15 = (bf16[64,4096]{1,0:T(8,128)(2,1)S(1)}, bf16[64,4096]{1,0:T(8,128)(2,1)S(1)}, u32[]{:S(2)}, u32[]{:S(2)}) collective-permute-start(bf16[64,4096]{1,0:T(8,128)(2,1)S(1)} %get-tuple-element.70), channel_id=1, source_target_pairs={{0,1},{1,0},{2,3},{3,2},{4,5},{5,4},{6,7},{7,6},{8,9},{9,8},{10,11... | collective-permute-start | bytes 1572872 | tf_op jit(solution)/shard_map/ppermute | solution.py:382
  80.1 11.3 %collective-permute-start.23 = (bf16[32,4096]{1,0:T(8,128)(2,1)S(1)}, bf16[32,4096]{1,0:T(8,128)(2,1)S(1)}, u32[]{:S(2)}, u32[]{:S(2)}) collective-permute-start(bf16[32,4096]{1,0:T(8,128)(2,1)S(1)} %get-tuple-element.80), channel_id=1, source_target_pairs={{0,6},{1,7},{2,0},{3,1},{4,2},{5,3},{6,4},{7,5},{8,14},{9,15},{10,... | collective-permute-start | bytes 786440 | tf_op jit(solution)/shard_map/ppermute | solution.py:378
  84.1 10.5 %collective-permute-start.18 = (bf16[32,4096]{1,0:T(8,128)(2,1)S(1)}, bf16[32,4096]{1,0:T(8,128)(2,1)S(1)}, u32[]{:S(2)}, u32[]{:S(2)}) collective-permute-start(bf16[32,4096]{1,0:T(8,128)(2,1)S(1)} %get-tuple-element.79), channel_id=1, source_target_pairs={{0,2},{1,3},{2,4},{3,5},{4,6},{5,7},{6,0},{7,1},{8,10},{9,11},{10,... | collective-permute-start | bytes 786440 | tf_op jit(solution)/shard_map/ppermute | solution.py:374
  84.5 15.6 %collective-permute-start.22 = (bf16[32,4096]{1,0:T(8,128)(2,1)S(1)}, bf16[32,4096]{1,0:T(8,128)(2,1)S(1)}, u32[]{:S(2)}, u32[]{:S(2)}) collective-permute-start(bf16[32,4096]{1,0:T(8,128)(2,1)S(1)} %slice.68), channel_id=1, source_target_pairs={{0,2},{1,3},{2,4},{3,5},{4,6},{5,7},{6,0},{7,1},{8,10},{9,11},{10,... | collective-permute-start | bytes 786440 | tf_op jit(solution)/shard_map/ppermute | solution.py:374
  86.7 13.4 %collective-permute-start.21 = (bf16[32,4096]{1,0:T(8,128)(2,1)S(1)}, bf16[32,4096]{1,0:T(8,128)(2,1)S(1)}, u32[]{:S(2)}, u32[]{:S(2)}) collective-permute-start(bf16[32,4096]{1,0:T(8,128)(2,1)S(1)} %slice.69), channel_id=1, source_target_pairs={{0,6},{1,7},{2,0},{3,1},{4,2},{5,3},{6,4},{7,5},{8,14},{9,15},{10,... | collective-permute-start | bytes 786440 | tf_op jit(solution)/shard_map/ppermute | solution.py:378
  91.5 10.6 %collective-permute-start.24 = (bf16[32,4096]{1,0:T(8,128)(2,1)S(1)}, bf16[32,4096]{1,0:T(8,128)(2,1)S(1)}, u32[]{:S(2)}, u32[]{:S(2)}) collective-permute-start(bf16[32,4096]{1,0:T(8,128)(2,1)S(1)} %fusion), channel_id=1, source_target_pairs={{0,6},{1,7},{2,0},{3,1},{4,2},{5,3},{6,4},{7,5},{8,14},{9,15},{10,... | collective-permute-start | bytes 786440 | tf_op jit(solution)/shard_map/ppermute | solution.py:378
  94.6 9.9 %collective-permute-start.19 = (bf16[32,4096]{1,0:T(8,128)(2,1)S(1)}, bf16[32,4096]{1,0:T(8,128)(2,1)S(1)}, u32[]{:S(2)}, u32[]{:S(2)}) collective-permute-start(bf16[32,4096]{1,0:T(8,128)(2,1)S(1)} %fusion.3), channel_id=1, source_target_pairs={{0,2},{1,3},{2,4},{3,5},{4,6},{5,7},{6,0},{7,1},{8,10},{9,11},{10,... | collective-permute-start | bytes 786440 | tf_op jit(solution)/shard_map/ppermute | solution.py:374
  (15 other events, 144.9 us)

commit v5 on v4

--- a/solution.py
+++ b/solution.py
@@ -104,22 +104,49 @@
     )(*[in_vmem(v) for v in (*own, *other, *weights)])
 
 
-def last_kernel(mine, theirs, below, above, o):
-    tp = lax.axis_index("tp")
-    near = jnp.where(tp == 7, mine[48:64].astype(F32), theirs[48:64].astype(F32))
-    far = jnp.where(tp == 1, below[16:32].astype(F32), above[16:32].astype(F32))
-    o[...] = jnp.where(tp >= 6, near, far)[8:16].astype(BF)
-
-
-def last_rows(*args):
-    return pl.pallas_call(
-        last_kernel,
-        out_shape=pltpu.VMEM((8, 4096), BF),
-        in_specs=[VMEM] * 4,
-        out_specs=VMEM,
-        compiler_params=params(),
-        name="last_rows",
-    )(*[in_vmem(v) for v in args])
+def near_kernel(mine, theirs, wx_far, wbc_far, wdt_far, xo, bco, dto, last, wx, wbc, wdt, tok, sems):
+    c = core()
+    pairs = (
+        (mine, tok.at[pl.ds(pl.multiple_of(c * 64, 64), 64), :]),
+        (wx_far, wx),
+        (wdt_far, wdt),
+        (wbc_far, wbc),
+    )
+    copies = [pltpu.make_async_copy(f, t, sems.at[j]) for j, (f, t) in enumerate(pairs)]
+    for copy in copies:
+        copy.start()
+    tok[pl.ds(pl.multiple_of((1 - c) * 64, 64), 64), :] = theirs[...]
+    copies[0].wait()
+    last[...] = tok[Q - 16 : Q, :][8:16]
+    copies[1].wait()
+    rows = tok[...]
+    xo[...] = jnp.dot(rows, wx[...], preferred_element_type=F32).astype(BF)
+    copies[2].wait()
+    dto[0] = dot_nt(rows, wdt[...]).T
+    copies[3].wait()
+    bco[...] = jnp.dot(rows, wbc[...], preferred_element_type=F32).astype(BF)
+
+
+def project_near(mine, theirs, in_x, in_bc, in_dt):
+    hbm = pl.BlockSpec(memory_space=pltpu.HBM)
+    far = lambda v: pltpu.with_memory_space_constraint(v, pltpu.HBM)
+    return pl.pallas_call(
+        near_kernel,
+        out_shape=(
+            pltpu.VMEM((Q, CH), BF),
+            pltpu.VMEM((Q, BCW), BF),
+            pltpu.VMEM((1, HH, Q), F32),
+            pltpu.VMEM((8, 4096), BF),
+            pltpu.VMEM(in_x.shape, BF),
+            pltpu.VMEM(in_bc.shape, BF),
+            pltpu.VMEM(in_dt.shape, BF),
+        ),
+        in_specs=[hbm, VMEM, hbm, hbm, hbm],
+        out_specs=(VMEM,) * 7,
+        scratch_shapes=[pltpu.VMEM((Q, 4096), BF), pltpu.SemaphoreType.DMA((4,))],
+        compiler_params=params(),
+        name="project_near",
+    )(far(mine), in_vmem(theirs), far(in_x), far(in_bc), far(in_dt))
 
 
 def silu(v):
@@ -384,25 +411,26 @@
 
 def per_device(tokens, in_x, in_bc, in_dt, conv_x, conv_bc, dt_bias, a_log, skip_d, norm_gain, out_w):
     after = lax.optimization_barrier
-    weights = (in_x, in_bc, in_dt.T)
-
     lo, hi = tokens[:32], tokens[32:]
     ua, db = up(lo), down(hi)
     ub, da = up(hi), down(lo)
-    partner = swap(tokens)
-    piece0 = project([tokens], [partner], weights, 1, "project_near")
+    *piece0, last, wx, wbc, wdt = project_near(tokens, swap(tokens), in_x, in_bc, in_dt.T)
+    weights = (wx, wbc, wdt)
+    spans = lax.axis_size("ctx")
+
+    def onward(*route):
+        return lax.ppermute(
+            last, ("ctx", "tp"), [(i * 8 + f, i * 8 + 8 + t) for i in range(spans - 1) for f, t in route]
+        )
+
+    edge = onward((7, 7), (6, 1)) + onward((7, 5), (6, 3))
+    ua, db, wx = after((ua, db, wx))
+    ub, da, edge = after((ub, da, edge))
+    edges = swap(edge)
     uu, dd = up(ua), down(db)
-    ub, da, piece0 = after((ub, da, piece0))
-    tail = last_rows(tokens, partner, ub, db)
-    spans = lax.axis_size("ctx")
-    route = ((1, 1), (5, 5), (7, 7), (6, 3))
-    edge = lax.ppermute(
-        tail, ("ctx", "tp"), [(i * 8 + f, i * 8 + 8 + t) for i in range(spans - 1) for f, t in route]
-    )
     own = [ua, ub, da, db]
     other = [swap(v) for v in own]
-    *other, edge, uu, dd = after((*other, edge, uu, dd))
-    edges = swap(edge)
+    *other, uu, dd = after((*other, uu, dd))
     far = [uu, dd, swap(uu), swap(dd)]
     piece12 = project(own, other, weights, 2, "project_next")
 

time: 107 us -> 110 us (1.028)
  local copies, waits for them, and re-layouts: 6.86 us -> 1.19 us
  waiting for transfers between devices: 25.9 us -> 31.1 us
  Pallas kernels: 15.7 us -> 18.8 us
  starting transfers between devices: 31.8 us -> 33 us
    ppermute x6, waiting for transfers between devices: 9.23 us -> 15.7 us  [up(): return lax.ppermute(v, 'tp', UP)]
    unnamed x26 -> x12, local copies, waits for them, and re-layouts: 5.71 us -> 0.03 us
    pallas_call x1, Pallas kernels: 0.04 us -> 4.5 us  [project_near(): pl.pallas_call(near_kernel, out_shape=(pltpu.VMEM((Q, CH), BF), pltpu.VME...]
    ppermute x6, waiting for transfers between devices: 8.67 us -> 6.1 us  [down(): return lax.ppermute(v, 'tp', DOWN)]
    ppermute x12, starting transfers between devices: 5.65 us -> 4.06 us  [swap(): return lax.ppermute(v, 'tp', SWAP)]
    pallas_call x2 -> x1, Pallas kernels: 3.73 us -> 2.4 us  [project(): pl.pallas_call(functools.partial(project_kernel, n, parts), out_shape=(pl...]
    ppermute x12, waiting for transfers between devices: 0.03 us -> 1.36 us  [swap(): return lax.ppermute(v, 'tp', SWAP)]
    ppermute x6, starting transfers between devices: 17.9 us -> 19.2 us  [down(): return lax.ppermute(v, 'tp', DOWN)]
  transfers between devices with their start and end apart: 26 -> 27, of which waited for: 7 -> 10; matrix products, arithmetic and copies ran while one was open for 2% -> 2% of each run, Pallas kernels for 7% -> 8%
where the time goes in v5:
time: 110 us; the launch traced here: 108 us
  starting transfers between devices  33 us (30%)
  waiting for transfers between devices  31.1 us (28%)
  blocking collectives  22.4 us (20%)
  Pallas kernels  18.8 us (17%)
  other arithmetic  1.56 us (1%)
  local copies, waits for them, and re-layouts  1.19 us (1%)
    all_to_all x1, blocking collectives, per_device(): got = lax.all_to_all(send, 'ctx', 0, 0, tiled=True)  22.4 us
    ppermute x6, starting transfers between devices, down(): return lax.ppermute(v, 'tp', DOWN)  19.2 us
    ppermute x6, waiting for transfers between devices, up(): return lax.ppermute(v, 'tp', UP)  15.7 us
    all_to_all x1, waiting for transfers between devices, per_device(): back = lax.all_to_all(prefix(got), 'ctx', 0, 0, tiled=True)  7.92 us
    ppermute x6, waiting for transfers between devices, down(): return lax.ppermute(v, 'tp', DOWN)  6.1 us
    pallas_call x1, Pallas kernels, local_part(): pl.pallas_call(local_kernel, out_shape=(s((NQ, Q, CH), BF), s((NQ, Q, NS)...  4.66 us
    pallas_call x1, Pallas kernels, project_near(): pl.pallas_call(near_kernel, out_shape=(pltpu.VMEM((Q, CH), BF), pltpu.VME...  4.5 us
    all_to_all x1, starting transfers between devices, per_device(): back = lax.all_to_all(prefix(got), 'ctx', 0, 0, tiled=True)  4.46 us
  transfers between devices with their start and end apart: 27, of which 10 were waited for; matrix products, arithmetic and copies ran while one was open for 2% of the time, Pallas kernels for 8%

profile of v5, /device:TPU:32, one launch (start us, length us, event | category | flops | bytes accessed | tf_op | source)
XLA Modules:
  0.0 108.3 jit_solution(18300031235482284677)
XLA Ops:
  1.1 3.1 %collective-permute-start.2 = (bf16[32,4096]{1,0:T(8,128)(2,1)S(1)}, bf16[32,4096]{1,0:T(8,128)(2,1)S(1)}, u32[]{:S(2)}, u32[]{:S(2)}) collective-permute-start(bf16[32,4096]{1,0:T(8,128)(2,1)S(1)} %get-tuple-element.87), channel_id=1, source_target_pairs={{0,6},{1,7},{2,0},{3,1},{4,2},{5,3},{6,4},{7,5},{8,14},{9,15},{10,... | collective-permute-start | bytes 786440 | tf_op jit(solution)/shard_map/ppermute | solution.py:405
  4.8 2.7 %collective-permute-start.4 = (bf16[32,4096]{1,0:T(8,128)(2,1)S(1)}, bf16[32,4096]{1,0:T(8,128)(2,1)S(1)}, u32[]{:S(2)}, u32[]{:S(2)}) collective-permute-start(bf16[32,4096]{1,0:T(8,128)(2,1)S(1)} %get-tuple-element.88), channel_id=1, source_target_pairs={{0,6},{1,7},{2,0},{3,1},{4,2},{5,3},{6,4},{7,5},{8,14},{9,15},{10,... | collective-permute-start | bytes 786440 | tf_op jit(solution)/shard_map/ppermute | solution.py:405
  7.4 4.5 %project_near.1 = (bf16[128,512]{1,0:T(8,128)(2,1)S(1)}, bf16[128,256]{1,0:T(8,128)(2,1)S(1)}, f32[1,8,128]{2,1,0:T(8,128)S(1)}, bf16[8,4096]{1,0:T(8,128)(2,1)S...) custom-call(bf16[64,4096]{1,0:T(8,128)(2,1)} %mine.1, ...), custom_call_target="tpu_custom_call" | custom-call | tf_op jit(solution)/shard_map/project_near/pallas_call | solution.py:133
  12.0 2.6 %collective-permute-done.1.refs_0_ = bf16[32,4096]{1,0:T(8,128)(2,1)S(1)} collective-permute-done((bf16[32,4096]{1,0:T(8,128)(2,1)S(1)}, bf16[32,4096]{1,0:T(8,128)(2,1)S(1)}, u32[]{:S(2)}, u32[]{:S(2)}) %collective-permute-start.1) | collective-permute-done | bytes 262176 | tf_op jit(solution)/shard_map/ppermute | solution.py:401
  16.0 6.3 %collective-permute-start.12 = (bf16[32,4096]{1,0:T(8,128)(2,1)S(1)}, bf16[32,4096]{1,0:T(8,128)(2,1)S(1)}, u32[]{:S(2)}, u32[]{:S(2)}) collective-permute-start(bf16[32,4096]{1,0:T(8,128)(2,1)S(1)} %collective-permute-done.2.refs_3_), channel_id=1, source_target_pairs={{0,6},{1,7},{2,0},{3,1},{4,2},{5,3},{6,4},{7,5},{8,14},{9,15},{10,... | collective-permute-start | bytes 786440 | tf_op jit(solution)/shard_map/ppermute | solution.py:405
  23.8 1.9 %collective-permute-done.11.refs_6_ = bf16[32,4096]{1,0:T(8,128)(2,1)S(1)} collective-permute-done((bf16[32,4096]{1,0:T(8,128)(2,1)S(1)}, bf16[32,4096]{1,0:T(8,128)(2,1)S(1)}, u32[]{:S(2)}, u32[]{:S(2)}) %collective-permute-start.11) | collective-permute-done | bytes 262176 | tf_op jit(solution)/shard_map/ppermute | solution.py:401
  25.8 2.6 %collective-permute-done.12.refs_7_ = bf16[32,4096]{1,0:T(8,128)(2,1)S(1)} collective-permute-done((bf16[32,4096]{1,0:T(8,128)(2,1)S(1)}, bf16[32,4096]{1,0:T(8,128)(2,1)S(1)}, u32[]{:S(2)}, u32[]{:S(2)}) %collective-permute-start.12) | collective-permute-done | bytes 262176 | tf_op jit(solution)/shard_map/ppermute | solution.py:405
  29.7 2.4 %project_next.1 = (bf16[256,512]{1,0:T(8,128)(2,1)S(1)}, bf16[256,256]{1,0:T(8,128)(2,1)S(1)}, f32[2,8,128]{2,1,0:T(8,128)S(1)}) custom-call(bf16[32,4096]{1,0:T(8,128)(2,1)S(1)} %collective-permute-done.1.refs_0_, bf16[32,4096]{1,0:T(8,128)(2,1)S(1)} %collective-permute-done.3.refs_1_, bf16[32,4096]{1,0:T(8,128)(2,1)S(1)} %collective-permute-done.4.refs_2_, ...), custom_call_target="tpu_custom_call" | custom-call | tf_op jit(solution)/shard_map/project_next/pallas_call | solution.py:92
  32.1 4.7 %local_part.1 = (bf16[4,128,512]{2,1,0:T(8,128)(2,1)S(1)}, bf16[4,128,128]{2,1,0:T(8,128)(2,1)S(1)}, bf16[4,128,128]{2,1,0:T(8,128)(2,1)S(1)}, f32[4,8,128]{2,1,...) custom-call(f32[8]{0:T(128)S(1)} %copy-done.3, ...), custom_call_target="tpu_custom_call" | custom-call | tf_op jit(solution)/shard_map/local_part/pallas_call | solution.py:248
  36.8 22.4 %all_to_all.10.r = bf16[32,24,128]{2,1,0:T(8,128)(2,1)S(1)} all-to-all(bf16[32,24,128]{2,1,0:T(8,128)(2,1)S(1)} %get-tuple-element.65), channel_id=1, replica_groups=mesh['ctx'=32,'tp'=8] {'ctx'}, dimensions={0} | all-to-all | bytes 393216 | tf_op jit(solution)/shard_map/all_to_all | solution.py:440
  59.9 4.5 %all-to-all-start.1 = ((bf16[32,16,128]{2,1,0:T(8,128)(2,1)}), bf16[32,16,128]{2,1,0:T(8,128)(2,1)S(1)}, u32[]{:S(2)}, u32[]{:S(2)}) async-start(bf16[32,16,128]{2,1,0:T(8,128)(2,1)} %prefix.1), calls=%async_computation.1 | async-start | bytes 262144 | tf_op jit(solution)/shard_map/all_to_all | solution.py:442
  64.4 1.8 %diag_part.1.ydiag = f32[4,128,512]{2,1,0:T(8,128)S(1)} custom-call(f32[8]{0:T(128)S(1)} %copy-done.5, bf16[4,128,512]{2,1,0:T(8,128)(2,1)S(1)} %get-tuple-element.70.x, bf16[4,128,128]{2,1,0:T(8,128)(2,1)S(1)} %get-tuple-element.71.b, bf16[4,128,128]{2,1,0:T(8,128)(2,1)S(1)} %get-tuple-element.68.c, f32[4,8,128]{2,1,0:T(8,128)S(1)} %get-tuple-element.69.cs, ...), custom_call_target="tpu_custom_call" | custom-call | tf_op jit(solution)/shard_map/diag_part/pallas_call | solution.py:316
  66.2 7.9 %all-to-all-done.1 = bf16[32,16,128]{2,1,0:T(8,128)(2,1)S(1)} async-done(((bf16[32,16,128]{2,1,0:T(8,128)(2,1)}), bf16[32,16,128]{2,1,0:T(8,128)(2,1)S(1)}, u32[]{:S(2)}, u32[]{:S(2)}) %all-to-all-start.1) | async-done | bytes 131104 | tf_op jit(solution)/shard_map/all_to_all | solution.py:442
  74.2 2.9 %norm_part.1 = (bf16[64,4096]{1,0:T(8,128)(2,1)S(1)}, bf16[64,4096]{1,0:T(8,128)(2,1)S(1)}, bf16[384,512]{1,0:T(8,128)(2,1)S(1)}, bf16[512,4096]{1,0:T(8,128)(2,1)S(1)}) custom-call(bf16[512,128]{1,0:T(8,128)(2,1)S(1)} %bitcast.3, f32[4,128,512]{2,1,0:T(8,128)S(1)} %get-tuple-element.66.e, f32[4,8,512]{2,1,0:T(8,128)S(1)} %get-tuple-element.67.d, ...), custom_call_target="tpu_custom_call" | custom-call | tf_op jit(solution)/shard_map/norm_part/pallas_call | solution.py:366
  77.1 1.8 %out_part.1 = (bf16[64,4096]{1,0:T(8,128)(2,1)S(1)}, bf16[64,4096]{1,0:T(8,128)(2,1)S(1)}, bf16[64,4096]{1,0:T(8,128)(2,1)S(1)}, bf16[64,4096]{1,0:T(8,128)(2,1)...) custom-call(bf16[384,512]{1,0:T(8,128)(2,1)S(1)} %get-tuple-element.73.n, ...), custom_call_target="tpu_custom_call" | custom-call | tf_op jit(solution)/shard_map/out_part/pallas_call | solution.py:385
  81.1 1.7 %collective-permute-start.23 = (bf16[32,4096]{1,0:T(8,128)(2,1)S(1)}, bf16[32,4096]{1,0:T(8,128)(2,1)S(1)}, u32[]{:S(2)}, u32[]{:S(2)}) collective-permute-start(bf16[32,4096]{1,0:T(8,128)(2,1)S(1)} %slice.68), channel_id=1, source_target_pairs={{0,2},{1,3},{2,4},{3,5},{4,6},{5,7},{6,0},{7,1},{8,10},{9,11},{10,... | collective-permute-start | bytes 786440 | tf_op jit(solution)/shard_map/ppermute | solution.py:401
  83.3 1.7 %collective-permute-start.19 = (bf16[32,4096]{1,0:T(8,128)(2,1)S(1)}, bf16[32,4096]{1,0:T(8,128)(2,1)S(1)}, u32[]{:S(2)}, u32[]{:S(2)}) collective-permute-start(bf16[32,4096]{1,0:T(8,128)(2,1)S(1)} %get-tuple-element.85), channel_id=1, source_target_pairs={{0,2},{1,3},{2,4},{3,5},{4,6},{5,7},{6,0},{7,1},{8,10},{9,11},{10,... | collective-permute-start | bytes 786440 | tf_op jit(solution)/shard_map/ppermute | solution.py:401
  85.1 1.8 %collective-permute-start.22 = (bf16[32,4096]{1,0:T(8,128)(2,1)S(1)}, bf16[32,4096]{1,0:T(8,128)(2,1)S(1)}, u32[]{:S(2)}, u32[]{:S(2)}) collective-permute-start(bf16[32,4096]{1,0:T(8,128)(2,1)S(1)} %slice.69), channel_id=1, source_target_pairs={{0,6},{1,7},{2,0},{3,1},{4,2},{5,3},{6,4},{7,5},{8,14},{9,15},{10,... | collective-permute-start | bytes 786440 | tf_op jit(solution)/shard_map/ppermute | solution.py:405
  87.0 2.0 %collective-permute-start.24 = (bf16[32,4096]{1,0:T(8,128)(2,1)S(1)}, bf16[32,4096]{1,0:T(8,128)(2,1)S(1)}, u32[]{:S(2)}, u32[]{:S(2)}) collective-permute-start(bf16[32,4096]{1,0:T(8,128)(2,1)S(1)} %get-tuple-element.86), channel_id=1, source_target_pairs={{0,6},{1,7},{2,0},{3,1},{4,2},{5,3},{6,4},{7,5},{8,14},{9,15},{10,... | collective-permute-start | bytes 786440 | tf_op jit(solution)/shard_map/ppermute | solution.py:405
  89.0 7.7 %collective-permute-done.19 = bf16[32,4096]{1,0:T(8,128)(2,1)S(1)} collective-permute-done((bf16[32,4096]{1,0:T(8,128)(2,1)S(1)}, bf16[32,4096]{1,0:T(8,128)(2,1)S(1)}, u32[]{:S(2)}, u32[]{:S(2)}) %collective-permute-start.19) | collective-permute-done | bytes 262176 | tf_op jit(solution)/shard_map/ppermute | solution.py:401
  96.8 2.1 %collective-permute-done.24 = bf16[32,4096]{1,0:T(8,128)(2,1)S(1)} collective-permute-done((bf16[32,4096]{1,0:T(8,128)(2,1)S(1)}, bf16[32,4096]{1,0:T(8,128)(2,1)S(1)}, u32[]{:S(2)}, u32[]{:S(2)}) %collective-permute-start.24) | collective-permute-done | bytes 262176 | tf_op jit(solution)/shard_map/ppermute | solution.py:405
  99.0 3.3 %collective-permute-start.25 = (bf16[32,4096]{1,0:T(8,128)(2,1)S(1)}, bf16[32,4096]{1,0:T(8,128)(2,1)S(1)}, u32[]{:S(2)}, u32[]{:S(2)}) collective-permute-start(bf16[32,4096]{1,0:T(8,128)(2,1)S(1)} %fusion), channel_id=1, source_target_pairs={{0,6},{1,7},{2,0},{3,1},{4,2},{5,3},{6,4},{7,5},{8,14},{9,15},{10,... | collective-permute-start | bytes 786440 | tf_op jit(solution)/shard_map/ppermute | solution.py:405
  102.4 3.5 %collective-permute-done.20 = bf16[32,4096]{1,0:T(8,128)(2,1)S(1)} collective-permute-done((bf16[32,4096]{1,0:T(8,128)(2,1)S(1)}, bf16[32,4096]{1,0:T(8,128)(2,1)S(1)}, u32[]{:S(2)}, u32[]{:S(2)}) %collective-permute-start.20) | collective-permute-done | bytes 262176 | tf_op jit(solution)/shard_map/ppermute | solution.py:401
  105.9 1.4 %collective-permute-done.25 = bf16[32,4096]{1,0:T(8,128)(2,1)S(1)} collective-permute-done((bf16[32,4096]{1,0:T(8,128)(2,1)S(1)}, bf16[32,4096]{1,0:T(8,128)(2,1)S(1)}, u32[]{:S(2)}, u32[]{:S(2)}) %collective-permute-start.25) | collective-permute-done | bytes 262176 | tf_op jit(solution)/shard_map/ppermute | solution.py:405
  (63 shorter events, 10.9 us)
Async XLA Ops:
  0.0 7.4 %collective-permute-start = (bf16[64,4096]{1,0:T(8,128)(2,1)}, bf16[64,4096]{1,0:T(8,128)(2,1)S(1)}, u32[]{:S(2)}, u32[]{:S(2)}) collective-permute-start(bf16[64,4096]{1,0:T(8,128)(2,1)} %mine.1), channel_id=1, source_target_pairs={{0,1},{1,0},{2,3},{3,2},{4,5},{5,4},{6,7},{7,6},{8,9},{9,8},{10,11... | collective-permute-start | bytes 1572872 | tf_op jit(solution)/shard_map/ppermute | solution.py:409
  1.1 10.9 %collective-permute-start.2 = (bf16[32,4096]{1,0:T(8,128)(2,1)S(1)}, bf16[32,4096]{1,0:T(8,128)(2,1)S(1)}, u32[]{:S(2)}, u32[]{:S(2)}) collective-permute-start(bf16[32,4096]{1,0:T(8,128)(2,1)S(1)} %get-tuple-element.87), channel_id=1, source_target_pairs={{0,6},{1,7},{2,0},{3,1},{4,2},{5,3},{6,4},{7,5},{8,14},{9,15},{10,... | collective-permute-start | bytes 786440 | tf_op jit(solution)/shard_map/ppermute | solution.py:405
  4.2 10.4 %collective-permute-start.1 = (bf16[32,4096]{1,0:T(8,128)(2,1)S(1)}, bf16[32,4096]{1,0:T(8,128)(2,1)S(1)}, u32[]{:S(2)}, u32[]{:S(2)}) collective-permute-start(bf16[32,4096]{1,0:T(8,128)(2,1)S(1)} %get-tuple-element.88), channel_id=1, source_target_pairs={{0,2},{1,3},{2,4},{3,5},{4,6},{5,7},{6,0},{7,1},{8,10},{9,11},{10,... | collective-permute-start | bytes 786440 | tf_op jit(solution)/shard_map/ppermute | solution.py:401
  4.2 18.1 %collective-permute-start.3 = (bf16[32,4096]{1,0:T(8,128)(2,1)S(1)}, bf16[32,4096]{1,0:T(8,128)(2,1)S(1)}, u32[]{:S(2)}, u32[]{:S(2)}) collective-permute-start(bf16[32,4096]{1,0:T(8,128)(2,1)S(1)} %get-tuple-element.87), channel_id=1, source_target_pairs={{0,2},{1,3},{2,4},{3,5},{4,6},{5,7},{6,0},{7,1},{8,10},{9,11},{10,... | collective-permute-start | bytes 786440 | tf_op jit(solution)/shard_map/ppermute | solution.py:401
  4.8 18.9 %collective-permute-start.4 = (bf16[32,4096]{1,0:T(8,128)(2,1)S(1)}, bf16[32,4096]{1,0:T(8,128)(2,1)S(1)}, u32[]{:S(2)}, u32[]{:S(2)}) collective-permute-start(bf16[32,4096]{1,0:T(8,128)(2,1)S(1)} %get-tuple-element.88), channel_id=1, source_target_pairs={{0,6},{1,7},{2,0},{3,1},{4,2},{5,3},{6,4},{7,5},{8,14},{9,15},{10,... | collective-permute-start | bytes 786440 | tf_op jit(solution)/shard_map/ppermute | solution.py:405
  14.5 11.2 %collective-permute-start.11 = (bf16[32,4096]{1,0:T(8,128)(2,1)S(1)}, bf16[32,4096]{1,0:T(8,128)(2,1)S(1)}, u32[]{:S(2)}, u32[]{:S(2)}) collective-permute-start(bf16[32,4096]{1,0:T(8,128)(2,1)S(1)} %collective-permute-done.1.refs_0_), channel_id=1, source_target_pairs={{0,2},{1,3},{2,4},{3,5},{4,6},{5,7},{6,0},{7,1},{8,10},{9,11},{10,... | collective-permute-start | bytes 786440 | tf_op jit(solution)/shard_map/ppermute | solution.py:401
  15.9 9.9 %collective-permute-start.7 = (bf16[32,4096]{1,0:T(8,128)(2,1)S(1)}, bf16[32,4096]{1,0:T(8,128)(2,1)S(1)}, u32[]{:S(2)}, u32[]{:S(2)}) collective-permute-start(bf16[32,4096]{1,0:T(8,128)(2,1)S(1)} %collective-permute-done.1.refs_0_), channel_id=1, source_target_pairs={{0,1},{1,0},{2,3},{3,2},{4,5},{5,4},{6,7},{7,6},{8,9},{9,8},{10,11... | collective-permute-start | bytes 786440 | tf_op jit(solution)/shard_map/ppermute | solution.py:409
  16.0 12.3 %collective-permute-start.12 = (bf16[32,4096]{1,0:T(8,128)(2,1)S(1)}, bf16[32,4096]{1,0:T(8,128)(2,1)S(1)}, u32[]{:S(2)}, u32[]{:S(2)}) collective-permute-start(bf16[32,4096]{1,0:T(8,128)(2,1)S(1)} %collective-permute-done.2.refs_3_), channel_id=1, source_target_pairs={{0,6},{1,7},{2,0},{3,1},{4,2},{5,3},{6,4},{7,5},{8,14},{9,15},{10,... | collective-permute-start | bytes 786440 | tf_op jit(solution)/shard_map/ppermute | solution.py:405
  22.3 6.1 %collective-permute-start.10 = (bf16[32,4096]{1,0:T(8,128)(2,1)S(1)}, bf16[32,4096]{1,0:T(8,128)(2,1)S(1)}, u32[]{:S(2)}, u32[]{:S(2)}) collective-permute-start(bf16[32,4096]{1,0:T(8,128)(2,1)S(1)} %collective-permute-done.2.refs_3_), channel_id=1, source_target_pairs={{0,1},{1,0},{2,3},{3,2},{4,5},{5,4},{6,7},{7,6},{8,9},{9,8},{10,11... | collective-permute-start | bytes 786440 | tf_op jit(solution)/shard_map/ppermute | solution.py:409
  23.7 4.6 %collective-permute-start.8 = (bf16[32,4096]{1,0:T(8,128)(2,1)S(1)}, bf16[32,4096]{1,0:T(8,128)(2,1)S(1)}, u32[]{:S(2)}, u32[]{:S(2)}) collective-permute-start(bf16[32,4096]{1,0:T(8,128)(2,1)S(1)} %collective-permute-done.3.refs_1_), channel_id=1, source_target_pairs={{0,1},{1,0},{2,3},{3,2},{4,5},{5,4},{6,7},{7,6},{8,9},{9,8},{10,11... | collective-permute-start | bytes 786440 | tf_op jit(solution)/shard_map/ppermute | solution.py:409
  25.8 2.6 %collective-permute-start.9 = (bf16[32,4096]{1,0:T(8,128)(2,1)S(1)}, bf16[32,4096]{1,0:T(8,128)(2,1)S(1)}, u32[]{:S(2)}, u32[]{:S(2)}) collective-permute-start(bf16[32,4096]{1,0:T(8,128)(2,1)S(1)} %collective-permute-done.4.refs_2_), channel_id=1, source_target_pairs={{0,1},{1,0},{2,3},{3,2},{4,5},{5,4},{6,7},{7,6},{8,9},{9,8},{10,11... | collective-permute-start | bytes 786440 | tf_op jit(solution)/shard_map/ppermute | solution.py:409
  28.3 3.7 %collective-permute-start.13 = (bf16[32,4096]{1,0:T(8,128)(2,1)S(1)}, bf16[32,4096]{1,0:T(8,128)(2,1)S(1)}, u32[]{:S(2)}, u32[]{:S(2)}) collective-permute-start(bf16[32,4096]{1,0:T(8,128)(2,1)S(1)} %collective-permute-done.11.refs_6_), channel_id=1, source_target_pairs={{0,1},{1,0},{2,3},{3,2},{4,5},{5,4},{6,7},{7,6},{8,9},{9,8},{10,11... | collective-permute-start | bytes 786440 | tf_op jit(solution)/shard_map/ppermute | solution.py:409
  29.1 2.9 %collective-permute-start.14 = (bf16[32,4096]{1,0:T(8,128)(2,1)S(1)}, bf16[32,4096]{1,0:T(8,128)(2,1)S(1)}, u32[]{:S(2)}, u32[]{:S(2)}) collective-permute-start(bf16[32,4096]{1,0:T(8,128)(2,1)S(1)} %collective-permute-done.12.refs_7_), channel_id=1, source_target_pairs={{0,1},{1,0},{2,3},{3,2},{4,5},{5,4},{6,7},{7,6},{8,9},{9,8},{10,11... | collective-permute-start | bytes 786440 | tf_op jit(solution)/shard_map/ppermute | solution.py:409
  29.2 2.8 %collective-permute-start.15 = (bf16[8,4096]{1,0:T(8,128)(2,1)S(1)}, bf16[8,4096]{1,0:T(8,128)(2,1)S(1)}, u32[]{:S(2)}, u32[]{:S(2)}) collective-permute-start(bf16[8,4096]{1,0:T(8,128)(2,1)S(1)} %add.33.refs_10_), channel_id=1, source_target_pairs={{0,1},{1,0},{2,3},{3,2},{4,5},{5,4},{6,7},{7,6},{8,9},{9,8},{10,11... | collective-permute-start | bytes 196616 | tf_op jit(solution)/shard_map/ppermute | solution.py:409
  59.9 14.2 %all-to-all-start.1 = ((bf16[32,16,128]{2,1,0:T(8,128)(2,1)}), bf16[32,16,128]{2,1,0:T(8,128)(2,1)S(1)}, u32[]{:S(2)}, u32[]{:S(2)}) async-start(bf16[32,16,128]{2,1,0:T(8,128)(2,1)} %prefix.1), calls=%async_computation.1 | async-start | bytes 262144 | tf_op jit(solution)/shard_map/all_to_all | solution.py:442
  79.0 23.3 %collective-permute-start.16 = (bf16[64,4096]{1,0:T(8,128)(2,1)S(1)}, bf16[64,4096]{1,0:T(8,128)(2,1)S(1)}, u32[]{:S(2)}, u32[]{:S(2)}) collective-permute-start(bf16[64,4096]{1,0:T(8,128)(2,1)S(1)} %get-tuple-element.76), channel_id=1, source_target_pairs={{0,1},{1,0},{2,3},{3,2},{4,5},{5,4},{6,7},{7,6},{8,9},{9,8},{10,11... | collective-permute-start | bytes 1572872 | tf_op jit(solution)/shard_map/ppermute | solution.py:409
  79.5 5.5 %collective-permute-start.21 = (bf16[64,4096]{1,0:T(8,128)(2,1)S(1)}, bf16[64,4096]{1,0:T(8,128)(2,1)S(1)}, u32[]{:S(2)}, u32[]{:S(2)}) collective-permute-start(bf16[64,4096]{1,0:T(8,128)(2,1)S(1)} %get-tuple-element.82), channel_id=1, source_target_pairs={{0,1},{1,0},{2,3},{3,2},{4,5},{5,4},{6,7},{7,6},{8,9},{9,8},{10,11... | collective-permute-start | bytes 1572872 | tf_op jit(solution)/shard_map/ppermute | solution.py:409
  79.6 3.5 %collective-permute-start.18 = (bf16[64,4096]{1,0:T(8,128)(2,1)S(1)}, bf16[64,4096]{1,0:T(8,128)(2,1)S(1)}, u32[]{:S(2)}, u32[]{:S(2)}) collective-permute-start(bf16[64,4096]{1,0:T(8,128)(2,1)S(1)} %get-tuple-element.80), channel_id=1, source_target_pairs={{0,1},{1,0},{2,3},{3,2},{4,5},{5,4},{6,7},{7,6},{8,9},{9,8},{10,11... | collective-permute-start | bytes 1572872 | tf_op jit(solution)/shard_map/ppermute | solution.py:409
  81.1 21.3 %collective-permute-start.23 = (bf16[32,4096]{1,0:T(8,128)(2,1)S(1)}, bf16[32,4096]{1,0:T(8,128)(2,1)S(1)}, u32[]{:S(2)}, u32[]{:S(2)}) collective-permute-start(bf16[32,4096]{1,0:T(8,128)(2,1)S(1)} %slice.68), channel_id=1, source_target_pairs={{0,2},{1,3},{2,4},{3,5},{4,6},{5,7},{6,0},{7,1},{8,10},{9,11},{10,... | collective-permute-start | bytes 786440 | tf_op jit(solution)/shard_map/ppermute | solution.py:401
  83.3 13.3 %collective-permute-start.19 = (bf16[32,4096]{1,0:T(8,128)(2,1)S(1)}, bf16[32,4096]{1,0:T(8,128)(2,1)S(1)}, u32[]{:S(2)}, u32[]{:S(2)}) collective-permute-start(bf16[32,4096]{1,0:T(8,128)(2,1)S(1)} %get-tuple-element.85), channel_id=1, source_target_pairs={{0,2},{1,3},{2,4},{3,5},{4,6},{5,7},{6,0},{7,1},{8,10},{9,11},{10,... | collective-permute-start | bytes 786440 | tf_op jit(solution)/shard_map/ppermute | solution.py:401
  85.1 17.3 %collective-permute-start.22 = (bf16[32,4096]{1,0:T(8,128)(2,1)S(1)}, bf16[32,4096]{1,0:T(8,128)(2,1)S(1)}, u32[]{:S(2)}, u32[]{:S(2)}) collective-permute-start(bf16[32,4096]{1,0:T(8,128)(2,1)S(1)} %slice.69), channel_id=1, source_target_pairs={{0,6},{1,7},{2,0},{3,1},{4,2},{5,3},{6,4},{7,5},{8,14},{9,15},{10,... | collective-permute-start | bytes 786440 | tf_op jit(solution)/shard_map/ppermute | solution.py:405
  87.0 11.9 %collective-permute-start.24 = (bf16[32,4096]{1,0:T(8,128)(2,1)S(1)}, bf16[32,4096]{1,0:T(8,128)(2,1)S(1)}, u32[]{:S(2)}, u32[]{:S(2)}) collective-permute-start(bf16[32,4096]{1,0:T(8,128)(2,1)S(1)} %get-tuple-element.86), channel_id=1, source_target_pairs={{0,6},{1,7},{2,0},{3,1},{4,2},{5,3},{6,4},{7,5},{8,14},{9,15},{10,... | collective-permute-start | bytes 786440 | tf_op jit(solution)/shard_map/ppermute | solution.py:405
  96.7 9.1 %collective-permute-start.20 = (bf16[32,4096]{1,0:T(8,128)(2,1)S(1)}, bf16[32,4096]{1,0:T(8,128)(2,1)S(1)}, u32[]{:S(2)}, u32[]{:S(2)}) collective-permute-start(bf16[32,4096]{1,0:T(8,128)(2,1)S(1)} %fusion.3), channel_id=1, source_target_pairs={{0,2},{1,3},{2,4},{3,5},{4,6},{5,7},{6,0},{7,1},{8,10},{9,11},{10,... | collective-permute-start | bytes 786440 | tf_op jit(solution)/shard_map/ppermute | solution.py:401
  99.0 8.4 %collective-permute-start.25 = (bf16[32,4096]{1,0:T(8,128)(2,1)S(1)}, bf16[32,4096]{1,0:T(8,128)(2,1)S(1)}, u32[]{:S(2)}, u32[]{:S(2)}) collective-permute-start(bf16[32,4096]{1,0:T(8,128)(2,1)S(1)} %fusion), channel_id=1, source_target_pairs={{0,6},{1,7},{2,0},{3,1},{4,2},{5,3},{6,4},{7,5},{8,14},{9,15},{10,... | collective-permute-start | bytes 786440 | tf_op jit(solution)/shard_map/ppermute | solution.py:405
  (9 other events, 88.2 us)

commit v6 on v5

--- a/solution.py
+++ b/solution.py
@@ -323,7 +323,8 @@
     )(skip, *[in_vmem(v) for v in args])
 
 
-def norm_kernel(s_in, e, d, c, cs, ydiag, gain, w_far, other, own, rest, w, nb, sem):
+def norm_kernel(s_in, e, d, c, cs, ydiag, gain, w_far, *refs):
+    outs, (nb, w, sem) = refs[:8], refs[8:]
     copy = pltpu.make_async_copy(w_far, w, sem)
     copy.start()
     y = chip()
@@ -349,47 +350,26 @@
     def half(a, h):
         return nb[a, pl.ds(pl.multiple_of(h * 64, 64), 64), :]
 
-    a = lax.rem(y + 2, NQ)
-    v = jnp.concatenate([half(a, 1 - mine), half(a, mine)], 0)
     copy.wait()
-    v = jnp.dot(v, w[...], preferred_element_type=F32).astype(BF)
-    other[...] = v[0:64]
-    own[...] = v[64:128]
-    for j, k in enumerate((1, 3, 0)):
+    for j, k in enumerate((2, 1, 3, 0)):
         a = lax.rem(y + k, NQ)
-        rest[64 * j : 64 * j + 64, :] = half(a, 1 - mine)
-        rest[192 + 64 * j : 256 + 64 * j, :] = half(a, mine)
+        v = jnp.concatenate([half(a, 1 - mine), half(a, mine)], 0)
+        v = jnp.dot(v, w[...], preferred_element_type=F32).astype(BF)
+        outs[2 * j][...] = v[0:64]
+        outs[2 * j + 1][...] = v[64:128]
 
 
 def norm_part(*args):
     s = pltpu.VMEM
     return pl.pallas_call(
         norm_kernel,
-        out_shape=(s((64, 4096), BF), s((64, 4096), BF), s((384, CH), BF), s((CH, 4096), BF)),
+        out_shape=(s((64, 4096), BF),) * 8,
         in_specs=[VMEM] * 7 + [pl.BlockSpec(memory_space=pltpu.HBM)],
-        out_specs=(VMEM,) * 4,
-        scratch_shapes=[pltpu.VMEM((NQ, Q, CH), BF), pltpu.SemaphoreType.DMA],
+        out_specs=(VMEM,) * 8,
+        scratch_shapes=[pltpu.VMEM((NQ, Q, CH), BF), pltpu.VMEM((CH, 4096), BF), pltpu.SemaphoreType.DMA],
         compiler_params=params(),
         name="norm_part",
     )(*[in_vmem(v) for v in args[:7]], pltpu.with_memory_space_constraint(args[7], pltpu.HBM))
-
-
-def out_kernel(n, w, *outs):
-    v = jnp.dot(n[...], w[...], preferred_element_type=F32).astype(BF)
-    for j, o in enumerate(outs):
-        o[...] = v[64 * j : 64 * j + 64]
-
-
-def out_part(n, w):
-    s = pltpu.VMEM
-    return pl.pallas_call(
-        out_kernel,
-        out_shape=(s((64, 4096), BF),) * 6,
-        in_specs=[VMEM] * 2,
-        out_specs=(VMEM,) * 6,
-        compiler_params=params(),
-        name="out_part",
-    )(in_vmem(n), in_vmem(w))
 
 
 UP = [(y * 2 + c, ((y + 1) % 4) * 2 + c) for y in range(4) for c in range(2)]
@@ -423,16 +403,18 @@
             last, ("ctx", "tp"), [(i * 8 + f, i * 8 + 8 + t) for i in range(spans - 1) for f, t in route]
         )
 
-    edge = onward((7, 7), (6, 1)) + onward((7, 5), (6, 3))
     ua, db, wx = after((ua, db, wx))
-    ub, da, edge = after((ub, da, edge))
-    edges = swap(edge)
     uu, dd = up(ua), down(db)
+    ub, da, last = after((ub, da, last))
+    edge_a, edge_b = onward((7, 7), (6, 1)), onward((7, 5), (6, 3))
     own = [ua, ub, da, db]
     other = [swap(v) for v in own]
     *other, uu, dd = after((*other, uu, dd))
     far = [uu, dd, swap(uu), swap(dd)]
     piece12 = project(own, other, weights, 2, "project_next")
+    edge_a, edge_b, *piece12 = after((edge_a, edge_b, *piece12))
+    edge = edge_a + edge_b
+    edges = swap(edge)
 
     xc, b, c, cs, dt, e, d, send = local_part(
         dt_bias, a_log, *piece0, *piece12, *far, edge, edges, *weights, conv_x, conv_bc
@@ -440,14 +422,14 @@
     got = lax.all_to_all(send, "ctx", 0, 0, tiled=True)
     ydiag = diag_part(skip_d, xc, b, c, cs, dt)
     back = lax.all_to_all(prefix(got), "ctx", 0, 0, tiled=True)
-    other, own, rest, w = norm_part(back.reshape(CH, NS), e, d, c, cs, ydiag, norm_gain[None, :], out_w)
+    t2, m2, t1, m1, tm, mm, t0, m0 = norm_part(back.reshape(CH, NS), e, d, c, cs, ydiag, norm_gain[None, :], out_w)
 
     def both(mine, theirs):
         return mine.astype(F32) + swap(theirs).astype(F32)
 
-    q2 = both(own, other).astype(BF)
+    q2 = both(m2, t2).astype(BF)
+    q2, t1, tm, t0 = after((q2, t1, tm, t0))
     u2, d2 = up(q2[:32]), down(q2[32:])
-    t1, tm, t0, m1, mm, m0 = out_part(rest, w)
     q1 = both(m1, t1)
     u1b = up(q1[32:].astype(BF))
     qm = both(mm, tm)

time: 110 us -> 113 us (1.027)
  waiting for transfers between devices: 31.1 us -> 36.1 us
  starting transfers between devices: 33 us -> 28.3 us
  blocking collectives: 22.4 us -> 24.1 us
    ppermute x6, starting transfers between devices: 19.2 us -> 11.7 us  [down(): return lax.ppermute(v, 'tp', DOWN)]
    ppermute x6, waiting for transfers between devices: 15.7 us -> 18.7 us  [up(): return lax.ppermute(v, 'tp', UP)]
    ppermute x12, starting transfers between devices: 4.06 us -> 7.07 us  [swap(): return lax.ppermute(v, 'tp', SWAP)]
    ppermute x12, waiting for transfers between devices: 1.36 us -> 4.32 us  [swap(): return lax.ppermute(v, 'tp', SWAP)]
    all_to_all x1, blocking collectives: 22.4 us -> 24.1 us  [per_device(): got = lax.all_to_all(send, 'ctx', 0, 0, tiled=True)]
    pallas_call x2 -> x1, Pallas kernels: 4.74 us -> 5.69 us  [norm_part(): pl.pallas_call(norm_kernel, out_shape=(s((64, 4096), BF),) * 8, in_specs=...]
  transfers between devices with their start and end apart: 27 -> 27, of which waited for: 10 -> 13; matrix products, arithmetic and copies ran while one was open for 2% -> 1% of each run, Pallas kernels for 8% -> 8%
where the time goes in v6:
time: 113 us; the launch traced here: 111 us
  waiting for transfers between devices  36.1 us (32%)
  starting transfers between devices  28.3 us (25%)
  blocking collectives  24.1 us (21%)
  Pallas kernels  19.8 us (18%)
  other arithmetic  1.57 us (1%)
  local copies, waits for them, and re-layouts  1.19 us (1%)
    all_to_all x1, blocking collectives, per_device(): got = lax.all_to_all(send, 'ctx', 0, 0, tiled=True)  24.1 us
    ppermute x6, waiting for transfers between devices, up(): return lax.ppermute(v, 'tp', UP)  18.7 us
    ppermute x6, starting transfers between devices, down(): return lax.ppermute(v, 'tp', DOWN)  11.7 us
    all_to_all x1, waiting for transfers between devices, per_device(): back = lax.all_to_all(prefix(got), 'ctx', 0, 0, tiled=True)  7.84 us
    ppermute x12, starting transfers between devices, swap(): return lax.ppermute(v, 'tp', SWAP)  7.07 us
    pallas_call x1, Pallas kernels, norm_part(): pl.pallas_call(norm_kernel, out_shape=(s((64, 4096), BF),) * 8, in_specs=...  5.69 us
    ppermute x6, waiting for transfers between devices, down(): return lax.ppermute(v, 'tp', DOWN)  5.27 us
    pallas_call x1, Pallas kernels, local_part(): pl.pallas_call(local_kernel, out_shape=(s((NQ, Q, CH), BF), s((NQ, Q, NS)...  4.67 us
  transfers between devices with their start and end apart: 27, of which 13 were waited for; matrix products, arithmetic and copies ran while one was open for 1% of the time, Pallas kernels for 8%

profile of v6, /device:TPU:32, one launch (start us, length us, event | category | flops | bytes accessed | tf_op | source)
XLA Modules:
  0.0 111.4 jit_solution(8447709850789346575)
XLA Ops:
  1.1 1.7 %collective-permute-start.5 = (bf16[32,4096]{1,0:T(8,128)(2,1)S(1)}, bf16[32,4096]{1,0:T(8,128)(2,1)S(1)}, u32[]{:S(2)}, u32[]{:S(2)}) collective-permute-start(bf16[32,4096]{1,0:T(8,128)(2,1)S(1)} %get-tuple-element.101), channel_id=1, source_target_pairs={{0,2},{1,3},{2,4},{3,5},{4,6},{5,7},{6,0},{7,1},{8,10},{9,11},{10,... | collective-permute-start | bytes 786440 | tf_op jit(solution)/shard_map/ppermute | solution.py:381
  2.7 1.7 %collective-permute-start.6 = (bf16[32,4096]{1,0:T(8,128)(2,1)S(1)}, bf16[32,4096]{1,0:T(8,128)(2,1)S(1)}, u32[]{:S(2)}, u32[]{:S(2)}) collective-permute-start(bf16[32,4096]{1,0:T(8,128)(2,1)S(1)} %get-tuple-element.102), channel_id=1, source_target_pairs={{0,6},{1,7},{2,0},{3,1},{4,2},{5,3},{6,4},{7,5},{8,14},{9,15},{10,... | collective-permute-start | bytes 786440 | tf_op jit(solution)/shard_map/ppermute | solution.py:385
  4.4 1.8 %collective-permute-start.2 = (bf16[32,4096]{1,0:T(8,128)(2,1)S(1)}, bf16[32,4096]{1,0:T(8,128)(2,1)S(1)}, u32[]{:S(2)}, u32[]{:S(2)}) collective-permute-start(bf16[32,4096]{1,0:T(8,128)(2,1)S(1)} %get-tuple-element.101), channel_id=1, source_target_pairs={{0,6},{1,7},{2,0},{3,1},{4,2},{5,3},{6,4},{7,5},{8,14},{9,15},{10,... | collective-permute-start | bytes 786440 | tf_op jit(solution)/shard_map/ppermute | solution.py:385
  6.4 4.5 %project_near.1 = (bf16[128,512]{1,0:T(8,128)(2,1)S(1)}, bf16[128,256]{1,0:T(8,128)(2,1)S(1)}, f32[1,8,128]{2,1,0:T(8,128)S(1)}, bf16[8,4096]{1,0:T(8,128)(2,1)S...) custom-call(bf16[64,4096]{1,0:T(8,128)(2,1)} %mine.1, ...), custom_call_target="tpu_custom_call" | custom-call | tf_op jit(solution)/shard_map/project_near/pallas_call | solution.py:133
  11.9 1.6 %collective-permute-start.11 = (bf16[32,4096]{1,0:T(8,128)(2,1)S(1)}, bf16[32,4096]{1,0:T(8,128)(2,1)S(1)}, u32[]{:S(2)}, u32[]{:S(2)}) collective-permute-start(bf16[32,4096]{1,0:T(8,128)(2,1)S(1)} %collective-permute-done.5.refs_0_), channel_id=1, source_target_pairs={{0,2},{1,3},{2,4},{3,5},{4,6},{5,7},{6,0},{7,1},{8,10},{9,11},{10,... | collective-permute-start | bytes 786440 | tf_op jit(solution)/shard_map/ppermute | solution.py:381
  13.4 1.7 %collective-permute-start.12 = (bf16[32,4096]{1,0:T(8,128)(2,1)S(1)}, bf16[32,4096]{1,0:T(8,128)(2,1)S(1)}, u32[]{:S(2)}, u32[]{:S(2)}) collective-permute-start(bf16[32,4096]{1,0:T(8,128)(2,1)S(1)} %collective-permute-done.6.refs_3_), channel_id=1, source_target_pairs={{0,6},{1,7},{2,0},{3,1},{4,2},{5,3},{6,4},{7,5},{8,14},{9,15},{10,... | collective-permute-start | bytes 786440 | tf_op jit(solution)/shard_map/ppermute | solution.py:385
  15.1 1.8 %collective-permute-done.2.refs_2_ = bf16[32,4096]{1,0:T(8,128)(2,1)S(1)} collective-permute-done((bf16[32,4096]{1,0:T(8,128)(2,1)S(1)}, bf16[32,4096]{1,0:T(8,128)(2,1)S(1)}, u32[]{:S(2)}, u32[]{:S(2)}) %collective-permute-start.2) | collective-permute-done | bytes 262176 | tf_op jit(solution)/shard_map/ppermute | solution.py:385
  17.5 4.9 %collective-permute-done.11.refs_6_ = bf16[32,4096]{1,0:T(8,128)(2,1)S(1)} collective-permute-done((bf16[32,4096]{1,0:T(8,128)(2,1)S(1)}, bf16[32,4096]{1,0:T(8,128)(2,1)S(1)}, u32[]{:S(2)}, u32[]{:S(2)}) %collective-permute-start.11) | collective-permute-done | bytes 262176 | tf_op jit(solution)/shard_map/ppermute | solution.py:381
  22.4 1.5 %collective-permute-done.9.refs_6_ = bf16[32,4096]{1,0:T(8,128)(2,1)S(1)} collective-permute-done((bf16[32,4096]{1,0:T(8,128)(2,1)S(1)}, bf16[32,4096]{1,0:T(8,128)(2,1)S(1)}, u32[]{:S(2)}, u32[]{:S(2)}) %collective-permute-start.9) | collective-permute-done | bytes 262176 | tf_op jit(solution)/shard_map/ppermute | solution.py:389
  25.8 2.4 %project_next.1 = (bf16[256,512]{1,0:T(8,128)(2,1)S(1)}, bf16[256,256]{1,0:T(8,128)(2,1)S(1)}, f32[2,8,128]{2,1,0:T(8,128)S(1)}) custom-call(bf16[32,4096]{1,0:T(8,128)(2,1)S(1)} %collective-permute-done.5.refs_0_, bf16[32,4096]{1,0:T(8,128)(2,1)S(1)} %collective-permute-done.1.refs_1_, bf16[32,4096]{1,0:T(8,128)(2,1)S(1)} %collective-permute-done.2.refs_2_, ...), custom_call_target="tpu_custom_call" | custom-call | tf_op jit(solution)/shard_map/project_next/pallas_call | solution.py:92
  28.2 5.3 %collective-permute-start.15 = (bf16[8,4096]{1,0:T(8,128)(2,1)S(1)}, bf16[8,4096]{1,0:T(8,128)(2,1)S(1)}, u32[]{:S(2)}, u32[]{:S(2)}) collective-permute-start(bf16[8,4096]{1,0:T(8,128)(2,1)S(1)} %add.33.refs_10_), channel_id=1, source_target_pairs={{0,1},{1,0},{2,3},{3,2},{4,5},{5,4},{6,7},{7,6},{8,9},{9,8},{10,11... | collective-permute-start | bytes 196616 | tf_op jit(solution)/shard_map/ppermute | solution.py:389
  34.5 4.7 %local_part.1 = (bf16[4,128,512]{2,1,0:T(8,128)(2,1)S(1)}, bf16[4,128,128]{2,1,0:T(8,128)(2,1)S(1)}, bf16[4,128,128]{2,1,0:T(8,128)(2,1)S(1)}, f32[4,8,128]{2,1,...) custom-call(f32[8]{0:T(128)S(1)} %copy-done.3, ...), custom_call_target="tpu_custom_call" | custom-call | tf_op jit(solution)/shard_map/local_part/pallas_call | solution.py:248
  39.2 24.1 %all_to_all.10.r = bf16[32,24,128]{2,1,0:T(8,128)(2,1)S(1)} all-to-all(bf16[32,24,128]{2,1,0:T(8,128)(2,1)S(1)} %get-tuple-element.77), channel_id=1, replica_groups=mesh['ctx'=32,'tp'=8] {'ctx'}, dimensions={0} | all-to-all | bytes 393216 | tf_op jit(solution)/shard_map/all_to_all | solution.py:422
  64.1 4.5 %all-to-all-start.1 = ((bf16[32,16,128]{2,1,0:T(8,128)(2,1)}), bf16[32,16,128]{2,1,0:T(8,128)(2,1)S(1)}, u32[]{:S(2)}, u32[]{:S(2)}) async-start(bf16[32,16,128]{2,1,0:T(8,128)(2,1)} %prefix.1), calls=%async_computation.1 | async-start | bytes 262144 | tf_op jit(solution)/shard_map/all_to_all | solution.py:424
  68.5 1.8 %diag_part.1.ydiag = f32[4,128,512]{2,1,0:T(8,128)S(1)} custom-call(f32[8]{0:T(128)S(1)} %copy-done.5, bf16[4,128,512]{2,1,0:T(8,128)(2,1)S(1)} %get-tuple-element.82.x, bf16[4,128,128]{2,1,0:T(8,128)(2,1)S(1)} %get-tuple-element.83.b, bf16[4,128,128]{2,1,0:T(8,128)(2,1)S(1)} %get-tuple-element.80.c, f32[4,8,128]{2,1,0:T(8,128)S(1)} %get-tuple-element.81.cs, ...), custom_call_target="tpu_custom_call" | custom-call | tf_op jit(solution)/shard_map/diag_part/pallas_call | solution.py:316
  70.4 7.8 %all-to-all-done.1 = bf16[32,16,128]{2,1,0:T(8,128)(2,1)S(1)} async-done(((bf16[32,16,128]{2,1,0:T(8,128)(2,1)}), bf16[32,16,128]{2,1,0:T(8,128)(2,1)S(1)}, u32[]{:S(2)}, u32[]{:S(2)}) %all-to-all-start.1) | async-done | bytes 131104 | tf_op jit(solution)/shard_map/all_to_all | solution.py:424
  78.2 5.7 %norm_part.1 = (bf16[64,4096]{1,0:T(8,128)(2,1)S(1)}, bf16[64,4096]{1,0:T(8,128)(2,1)S(1)}, bf16[64,4096]{1,0:T(8,128)(2,1)S(1)}, bf16[64,4096]{1,0:T(8,128)(2,1...) custom-call(bf16[512,128]{1,0:T(8,128)(2,1)S(1)} %bitcast.3, ...), custom_call_target="tpu_custom_call" | custom-call | tf_op jit(solution)/shard_map/norm_part/pallas_call | solution.py:364
  84.0 1.9 %collective-permute-done.16 = bf16[64,4096]{1,0:T(8,128)(2,1)S(1)} collective-permute-done((bf16[64,4096]{1,0:T(8,128)(2,1)S(1)}, bf16[64,4096]{1,0:T(8,128)(2,1)S(1)}, u32[]{:S(2)}, u32[]{:S(2)}) %collective-permute-start.16) | collective-permute-done | bytes 524320 | tf_op jit(solution)/shard_map/ppermute | solution.py:389
  86.4 3.2 %collective-permute-start.24 = (bf16[32,4096]{1,0:T(8,128)(2,1)S(1)}, bf16[32,4096]{1,0:T(8,128)(2,1)S(1)}, u32[]{:S(2)}, u32[]{:S(2)}) collective-permute-start(bf16[32,4096]{1,0:T(8,128)(2,1)S(1)} %get-tuple-element.100), channel_id=1, source_target_pairs={{0,6},{1,7},{2,0},{3,1},{4,2},{5,3},{6,4},{7,5},{8,14},{9,15},{10,... | collective-permute-start | bytes 786440 | tf_op jit(solution)/shard_map/ppermute | solution.py:385
  90.4 6.3 %collective-permute-done.19 = bf16[32,4096]{1,0:T(8,128)(2,1)S(1)} collective-permute-done((bf16[32,4096]{1,0:T(8,128)(2,1)S(1)}, bf16[32,4096]{1,0:T(8,128)(2,1)S(1)}, u32[]{:S(2)}, u32[]{:S(2)}) %collective-permute-start.19) | collective-permute-done | bytes 262176 | tf_op jit(solution)/shard_map/ppermute | solution.py:381
  97.0 3.3 %collective-permute-start.22 = (bf16[32,4096]{1,0:T(8,128)(2,1)S(1)}, bf16[32,4096]{1,0:T(8,128)(2,1)S(1)}, u32[]{:S(2)}, u32[]{:S(2)}) collective-permute-start(bf16[32,4096]{1,0:T(8,128)(2,1)S(1)} %slice.67), channel_id=1, source_target_pairs={{0,6},{1,7},{2,0},{3,1},{4,2},{5,3},{6,4},{7,5},{8,14},{9,15},{10,... | collective-permute-start | bytes 786440 | tf_op jit(solution)/shard_map/ppermute | solution.py:385
  100.6 1.7 %collective-permute-done.23 = bf16[32,4096]{1,0:T(8,128)(2,1)S(1)} collective-permute-done((bf16[32,4096]{1,0:T(8,128)(2,1)S(1)}, bf16[32,4096]{1,0:T(8,128)(2,1)S(1)}, u32[]{:S(2)}, u32[]{:S(2)}) %collective-permute-start.23) | collective-permute-done | bytes 262176 | tf_op jit(solution)/shard_map/ppermute | solution.py:381
  102.3 5.1 %collective-permute-done.20 = bf16[32,4096]{1,0:T(8,128)(2,1)S(1)} collective-permute-done((bf16[32,4096]{1,0:T(8,128)(2,1)S(1)}, bf16[32,4096]{1,0:T(8,128)(2,1)S(1)}, u32[]{:S(2)}, u32[]{:S(2)}) %collective-permute-start.20) | collective-permute-done | bytes 262176 | tf_op jit(solution)/shard_map/ppermute | solution.py:381
  107.4 3.0 %collective-permute-done.25 = bf16[32,4096]{1,0:T(8,128)(2,1)S(1)} collective-permute-done((bf16[32,4096]{1,0:T(8,128)(2,1)S(1)}, bf16[32,4096]{1,0:T(8,128)(2,1)S(1)}, u32[]{:S(2)}, u32[]{:S(2)}) %collective-permute-start.25) | collective-permute-done | bytes 262176 | tf_op jit(solution)/shard_map/ppermute | solution.py:385
  (62 shorter events, 9.1 us)
Async XLA Ops:
  0.0 6.4 %collective-permute-start = (bf16[64,4096]{1,0:T(8,128)(2,1)}, bf16[64,4096]{1,0:T(8,128)(2,1)S(1)}, u32[]{:S(2)}, u32[]{:S(2)}) collective-permute-start(bf16[64,4096]{1,0:T(8,128)(2,1)} %mine.1), channel_id=1, source_target_pairs={{0,1},{1,0},{2,3},{3,2},{4,5},{5,4},{6,7},{7,6},{8,9},{9,8},{10,11... | collective-permute-start | bytes 1572872 | tf_op jit(solution)/shard_map/ppermute | solution.py:389
  1.1 10.4 %collective-permute-start.5 = (bf16[32,4096]{1,0:T(8,128)(2,1)S(1)}, bf16[32,4096]{1,0:T(8,128)(2,1)S(1)}, u32[]{:S(2)}, u32[]{:S(2)}) collective-permute-start(bf16[32,4096]{1,0:T(8,128)(2,1)S(1)} %get-tuple-element.101), channel_id=1, source_target_pairs={{0,2},{1,3},{2,4},{3,5},{4,6},{5,7},{6,0},{7,1},{8,10},{9,11},{10,... | collective-permute-start | bytes 786440 | tf_op jit(solution)/shard_map/ppermute | solution.py:381
  2.7 9.1 %collective-permute-start.6 = (bf16[32,4096]{1,0:T(8,128)(2,1)S(1)}, bf16[32,4096]{1,0:T(8,128)(2,1)S(1)}, u32[]{:S(2)}, u32[]{:S(2)}) collective-permute-start(bf16[32,4096]{1,0:T(8,128)(2,1)S(1)} %get-tuple-element.102), channel_id=1, source_target_pairs={{0,6},{1,7},{2,0},{3,1},{4,2},{5,3},{6,4},{7,5},{8,14},{9,15},{10,... | collective-permute-start | bytes 786440 | tf_op jit(solution)/shard_map/ppermute | solution.py:385
  4.4 12.5 %collective-permute-start.2 = (bf16[32,4096]{1,0:T(8,128)(2,1)S(1)}, bf16[32,4096]{1,0:T(8,128)(2,1)S(1)}, u32[]{:S(2)}, u32[]{:S(2)}) collective-permute-start(bf16[32,4096]{1,0:T(8,128)(2,1)S(1)} %get-tuple-element.101), channel_id=1, source_target_pairs={{0,6},{1,7},{2,0},{3,1},{4,2},{5,3},{6,4},{7,5},{8,14},{9,15},{10,... | collective-permute-start | bytes 786440 | tf_op jit(solution)/shard_map/ppermute | solution.py:385
  6.2 10.9 %collective-permute-start.1 = (bf16[32,4096]{1,0:T(8,128)(2,1)S(1)}, bf16[32,4096]{1,0:T(8,128)(2,1)S(1)}, u32[]{:S(2)}, u32[]{:S(2)}) collective-permute-start(bf16[32,4096]{1,0:T(8,128)(2,1)S(1)} %get-tuple-element.102), channel_id=1, source_target_pairs={{0,2},{1,3},{2,4},{3,5},{4,6},{5,7},{6,0},{7,1},{8,10},{9,11},{10,... | collective-permute-start | bytes 786440 | tf_op jit(solution)/shard_map/ppermute | solution.py:381
  11.9 10.5 %collective-permute-start.11 = (bf16[32,4096]{1,0:T(8,128)(2,1)S(1)}, bf16[32,4096]{1,0:T(8,128)(2,1)S(1)}, u32[]{:S(2)}, u32[]{:S(2)}) collective-permute-start(bf16[32,4096]{1,0:T(8,128)(2,1)S(1)} %collective-permute-done.5.refs_0_), channel_id=1, source_target_pairs={{0,2},{1,3},{2,4},{3,5},{4,6},{5,7},{6,0},{7,1},{8,10},{9,11},{10,... | collective-permute-start | bytes 786440 | tf_op jit(solution)/shard_map/ppermute | solution.py:381
  13.4 8.9 %collective-permute-start.7 = (bf16[32,4096]{1,0:T(8,128)(2,1)S(1)}, bf16[32,4096]{1,0:T(8,128)(2,1)S(1)}, u32[]{:S(2)}, u32[]{:S(2)}) collective-permute-start(bf16[32,4096]{1,0:T(8,128)(2,1)S(1)} %collective-permute-done.5.refs_0_), channel_id=1, source_target_pairs={{0,1},{1,0},{2,3},{3,2},{4,5},{5,4},{6,7},{7,6},{8,9},{9,8},{10,11... | collective-permute-start | bytes 786440 | tf_op jit(solution)/shard_map/ppermute | solution.py:389
  13.4 9.0 %collective-permute-start.12 = (bf16[32,4096]{1,0:T(8,128)(2,1)S(1)}, bf16[32,4096]{1,0:T(8,128)(2,1)S(1)}, u32[]{:S(2)}, u32[]{:S(2)}) collective-permute-start(bf16[32,4096]{1,0:T(8,128)(2,1)S(1)} %collective-permute-done.6.refs_3_), channel_id=1, source_target_pairs={{0,6},{1,7},{2,0},{3,1},{4,2},{5,3},{6,4},{7,5},{8,14},{9,15},{10,... | collective-permute-start | bytes 786440 | tf_op jit(solution)/shard_map/ppermute | solution.py:385
  16.9 5.5 %collective-permute-start.10 = (bf16[32,4096]{1,0:T(8,128)(2,1)S(1)}, bf16[32,4096]{1,0:T(8,128)(2,1)S(1)}, u32[]{:S(2)}, u32[]{:S(2)}) collective-permute-start(bf16[32,4096]{1,0:T(8,128)(2,1)S(1)} %collective-permute-done.6.refs_3_), channel_id=1, source_target_pairs={{0,1},{1,0},{2,3},{3,2},{4,5},{5,4},{6,7},{7,6},{8,9},{9,8},{10,11... | collective-permute-start | bytes 786440 | tf_op jit(solution)/shard_map/ppermute | solution.py:389
  17.1 5.3 %collective-permute-start.8 = (bf16[32,4096]{1,0:T(8,128)(2,1)S(1)}, bf16[32,4096]{1,0:T(8,128)(2,1)S(1)}, u32[]{:S(2)}, u32[]{:S(2)}) collective-permute-start(bf16[32,4096]{1,0:T(8,128)(2,1)S(1)} %collective-permute-done.1.refs_1_), channel_id=1, source_target_pairs={{0,1},{1,0},{2,3},{3,2},{4,5},{5,4},{6,7},{7,6},{8,9},{9,8},{10,11... | collective-permute-start | bytes 786440 | tf_op jit(solution)/shard_map/ppermute | solution.py:389
  23.9 10.6 %collective-permute-start.13 = (bf16[32,4096]{1,0:T(8,128)(2,1)S(1)}, bf16[32,4096]{1,0:T(8,128)(2,1)S(1)}, u32[]{:S(2)}, u32[]{:S(2)}) collective-permute-start(bf16[32,4096]{1,0:T(8,128)(2,1)S(1)} %collective-permute-done.11.refs_6_), channel_id=1, source_target_pairs={{0,1},{1,0},{2,3},{3,2},{4,5},{5,4},{6,7},{7,6},{8,9},{9,8},{10,11... | collective-permute-start | bytes 786440 | tf_op jit(solution)/shard_map/ppermute | solution.py:389
  24.1 10.4 %collective-permute-start.14 = (bf16[32,4096]{1,0:T(8,128)(2,1)S(1)}, bf16[32,4096]{1,0:T(8,128)(2,1)S(1)}, u32[]{:S(2)}, u32[]{:S(2)}) collective-permute-start(bf16[32,4096]{1,0:T(8,128)(2,1)S(1)} %collective-permute-done.12.refs_7_), channel_id=1, source_target_pairs={{0,1},{1,0},{2,3},{3,2},{4,5},{5,4},{6,7},{7,6},{8,9},{9,8},{10,11... | collective-permute-start | bytes 786440 | tf_op jit(solution)/shard_map/ppermute | solution.py:389
  24.4 3.8 %collective-permute-start.4 = (bf16[8,4096]{1,0:T(8,128)(2,1)S(1)}, bf16[8,4096]{1,0:T(8,128)(2,1)S(1)}, u32[]{:S(2)}, u32[]{:S(2)}) collective-permute-start(bf16[8,4096]{1,0:T(8,128)(2,1)S(1)} %get-tuple-element.55), channel_id=1, source_target_pairs={{7,13},{6,11},{15,21},{14,19},{23,29},{22,27},{31,37},{30,35},{39,... | collective-permute-start | bytes 196616 | tf_op jit(solution)/shard_map/ppermute | solution.py:402
  28.2 6.2 %collective-permute-start.15 = (bf16[8,4096]{1,0:T(8,128)(2,1)S(1)}, bf16[8,4096]{1,0:T(8,128)(2,1)S(1)}, u32[]{:S(2)}, u32[]{:S(2)}) collective-permute-start(bf16[8,4096]{1,0:T(8,128)(2,1)S(1)} %add.33.refs_10_), channel_id=1, source_target_pairs={{0,1},{1,0},{2,3},{3,2},{4,5},{5,4},{6,7},{7,6},{8,9},{9,8},{10,11... | collective-permute-start | bytes 196616 | tf_op jit(solution)/shard_map/ppermute | solution.py:389
  64.1 14.1 %all-to-all-start.1 = ((bf16[32,16,128]{2,1,0:T(8,128)(2,1)}), bf16[32,16,128]{2,1,0:T(8,128)(2,1)S(1)}, u32[]{:S(2)}, u32[]{:S(2)}) async-start(bf16[32,16,128]{2,1,0:T(8,128)(2,1)} %prefix.1), calls=%async_computation.1 | async-start | bytes 262144 | tf_op jit(solution)/shard_map/all_to_all | solution.py:424
  86.0 4.1 %collective-permute-start.18 = (bf16[64,4096]{1,0:T(8,128)(2,1)S(1)}, bf16[64,4096]{1,0:T(8,128)(2,1)S(1)}, u32[]{:S(2)}, u32[]{:S(2)}) collective-permute-start(bf16[64,4096]{1,0:T(8,128)(2,1)S(1)} %get-tuple-element.93), channel_id=1, source_target_pairs={{0,1},{1,0},{2,3},{3,2},{4,5},{5,4},{6,7},{7,6},{8,9},{9,8},{10,11... | collective-permute-start | bytes 1572872 | tf_op jit(solution)/shard_map/ppermute | solution.py:389
  86.3 10.4 %collective-permute-start.19 = (bf16[32,4096]{1,0:T(8,128)(2,1)S(1)}, bf16[32,4096]{1,0:T(8,128)(2,1)S(1)}, u32[]{:S(2)}, u32[]{:S(2)}) collective-permute-start(bf16[32,4096]{1,0:T(8,128)(2,1)S(1)} %get-tuple-element.99), channel_id=1, source_target_pairs={{0,2},{1,3},{2,4},{3,5},{4,6},{5,7},{6,0},{7,1},{8,10},{9,11},{10,... | collective-permute-start | bytes 786440 | tf_op jit(solution)/shard_map/ppermute | solution.py:381
  86.4 13.9 %collective-permute-start.24 = (bf16[32,4096]{1,0:T(8,128)(2,1)S(1)}, bf16[32,4096]{1,0:T(8,128)(2,1)S(1)}, u32[]{:S(2)}, u32[]{:S(2)}) collective-permute-start(bf16[32,4096]{1,0:T(8,128)(2,1)S(1)} %get-tuple-element.100), channel_id=1, source_target_pairs={{0,6},{1,7},{2,0},{3,1},{4,2},{5,3},{6,4},{7,5},{8,14},{9,15},{10,... | collective-permute-start | bytes 786440 | tf_op jit(solution)/shard_map/ppermute | solution.py:385
  89.6 10.9 %collective-permute-start.17 = (bf16[64,4096]{1,0:T(8,128)(2,1)S(1)}, bf16[64,4096]{1,0:T(8,128)(2,1)S(1)}, u32[]{:S(2)}, u32[]{:S(2)}) collective-permute-start(bf16[64,4096]{1,0:T(8,128)(2,1)S(1)} %get-tuple-element.91), channel_id=1, source_target_pairs={{0,1},{1,0},{2,3},{3,2},{4,5},{5,4},{6,7},{7,6},{8,9},{9,8},{10,11... | collective-permute-start | bytes 1572872 | tf_op jit(solution)/shard_map/ppermute | solution.py:389
  89.6 7.2 %collective-permute-start.21 = (bf16[64,4096]{1,0:T(8,128)(2,1)S(1)}, bf16[64,4096]{1,0:T(8,128)(2,1)S(1)}, u32[]{:S(2)}, u32[]{:S(2)}) collective-permute-start(bf16[64,4096]{1,0:T(8,128)(2,1)S(1)} %get-tuple-element.96), channel_id=1, source_target_pairs={{0,1},{1,0},{2,3},{3,2},{4,5},{5,4},{6,7},{7,6},{8,9},{9,8},{10,11... | collective-permute-start | bytes 1572872 | tf_op jit(solution)/shard_map/ppermute | solution.py:389
  90.3 12.1 %collective-permute-start.23 = (bf16[32,4096]{1,0:T(8,128)(2,1)S(1)}, bf16[32,4096]{1,0:T(8,128)(2,1)S(1)}, u32[]{:S(2)}, u32[]{:S(2)}) collective-permute-start(bf16[32,4096]{1,0:T(8,128)(2,1)S(1)} %slice.66), channel_id=1, source_target_pairs={{0,2},{1,3},{2,4},{3,5},{4,6},{5,7},{6,0},{7,1},{8,10},{9,11},{10,... | collective-permute-start | bytes 786440 | tf_op jit(solution)/shard_map/ppermute | solution.py:381
  96.8 10.6 %collective-permute-start.20 = (bf16[32,4096]{1,0:T(8,128)(2,1)S(1)}, bf16[32,4096]{1,0:T(8,128)(2,1)S(1)}, u32[]{:S(2)}, u32[]{:S(2)}) collective-permute-start(bf16[32,4096]{1,0:T(8,128)(2,1)S(1)} %fusion.3), channel_id=1, source_target_pairs={{0,2},{1,3},{2,4},{3,5},{4,6},{5,7},{6,0},{7,1},{8,10},{9,11},{10,... | collective-permute-start | bytes 786440 | tf_op jit(solution)/shard_map/ppermute | solution.py:381
  97.0 10.4 %collective-permute-start.22 = (bf16[32,4096]{1,0:T(8,128)(2,1)S(1)}, bf16[32,4096]{1,0:T(8,128)(2,1)S(1)}, u32[]{:S(2)}, u32[]{:S(2)}) collective-permute-start(bf16[32,4096]{1,0:T(8,128)(2,1)S(1)} %slice.67), channel_id=1, source_target_pairs={{0,6},{1,7},{2,0},{3,1},{4,2},{5,3},{6,4},{7,5},{8,14},{9,15},{10,... | collective-permute-start | bytes 786440 | tf_op jit(solution)/shard_map/ppermute | solution.py:385
  100.4 10.0 %collective-permute-start.25 = (bf16[32,4096]{1,0:T(8,128)(2,1)S(1)}, bf16[32,4096]{1,0:T(8,128)(2,1)S(1)}, u32[]{:S(2)}, u32[]{:S(2)}) collective-permute-start(bf16[32,4096]{1,0:T(8,128)(2,1)S(1)} %fusion), channel_id=1, source_target_pairs={{0,6},{1,7},{2,0},{3,1},{4,2},{5,3},{6,4},{7,5},{8,14},{9,15},{10,... | collective-permute-start | bytes 786440 | tf_op jit(solution)/shard_map/ppermute | solution.py:385
  (9 other events, 119.2 us)

commit v7 on v5

--- a/solution.py
+++ b/solution.py
@@ -63,48 +63,64 @@
     return pltpu.with_memory_space_constraint(v, pltpu.VMEM)
 
 
-def fill(tok, own, other, base=0):
+def place(tok, ref, base, half):
+    at = base + half * 32
+    tok[pl.ds(pl.multiple_of(at, 32), 32), :] = ref[0:32, :]
+    tok[pl.ds(pl.multiple_of(at + 64, 32), 32), :] = ref[32:64, :]
+
+
+def pack_kernel(mine, theirs, first, second, last):
     c = core()
-    for group, half in ((own, c), (other, 1 - c)):
-        step = 64 // len(group)
-        for j, r in enumerate(group):
-            at = pl.multiple_of(base + half * 64 + j * step, step)
-            tok[pl.ds(at, step), :] = r[...]
-
-
-def project_kernel(n, parts, *refs):
-    count = n * parts
-    own, other = refs[:count], refs[count : 2 * count]
-    wx, wbc, wdt, xo, bco, dto, tok = refs[2 * count :]
-    for j in range(n):
-        of = slice(j * parts, (j + 1) * parts)
-        fill(tok, own[of], other[of], j * Q)
+    for part, ref in ((c, mine), (1 - c, theirs)):
+        at = pl.ds(pl.multiple_of(part * 32, 32), 32)
+        first[at, :] = ref[pl.ds(pl.multiple_of(c * 32, 32), 32), :]
+        second[at, :] = ref[pl.ds(pl.multiple_of((1 - c) * 32, 32), 32), :]
+    end = jnp.where(c == 1, mine[48:64].astype(F32), theirs[48:64].astype(F32))
+    last[...] = end[8:16].astype(BF)
+
+
+def pack(mine, theirs):
+    return pl.pallas_call(
+        pack_kernel,
+        out_shape=(pltpu.VMEM((64, 4096), BF), pltpu.VMEM((64, 4096), BF), pltpu.VMEM((8, 4096), BF)),
+        in_specs=[VMEM] * 2,
+        out_specs=(VMEM,) * 3,
+        compiler_params=params(),
+        name="pack",
+    )(in_vmem(mine), in_vmem(theirs))
+
+
+def next_kernel(r1, r2, s1, s2, wx, wbc, wdt, xo, bco, dto, tok):
+    c = core()
+    place(tok, r1, c * Q, c)
+    place(tok, r2, c * Q, 1 - c)
+    place(tok, s1, (1 - c) * Q, 1 - c)
+    place(tok, s2, (1 - c) * Q, c)
     rows = tok[...]
     xo[...] = jnp.dot(rows, wx[...], preferred_element_type=F32).astype(BF)
     bco[...] = jnp.dot(rows, wbc[...], preferred_element_type=F32).astype(BF)
     dt = dot_nt(rows, wdt[...])
-    for j in range(n):
+    for j in range(2):
         dto[j] = dt[j * Q : (j + 1) * Q].T
 
 
-def project(own, other, weights, parts, name):
-    n = len(own) // parts
-    return pl.pallas_call(
-        functools.partial(project_kernel, n, parts),
+def project_next(*args):
+    return pl.pallas_call(
+        next_kernel,
         out_shape=(
-            pltpu.VMEM((n * Q, CH), BF),
-            pltpu.VMEM((n * Q, BCW), BF),
-            pltpu.VMEM((n, HH, Q), F32),
+            pltpu.VMEM((2 * Q, CH), BF),
+            pltpu.VMEM((2 * Q, BCW), BF),
+            pltpu.VMEM((2, HH, Q), F32),
         ),
-        in_specs=[VMEM] * (2 * n * parts + 3),
+        in_specs=[VMEM] * 7,
         out_specs=(VMEM, VMEM, VMEM),
-        scratch_shapes=[pltpu.VMEM((n * Q, 4096), BF)],
-        compiler_params=params(),
-        name=name,
-    )(*[in_vmem(v) for v in (*own, *other, *weights)])
-
-
-def near_kernel(mine, theirs, wx_far, wbc_far, wdt_far, xo, bco, dto, last, wx, wbc, wdt, tok, sems):
+        scratch_shapes=[pltpu.VMEM((2 * Q, 4096), BF)],
+        compiler_params=params(),
+        name="project_next",
+    )(*[in_vmem(v) for v in args])
+
+
+def near_kernel(mine, theirs, wx_far, wbc_far, wdt_far, xo, bco, dto, wx, wbc, wdt, tok, sems):
     c = core()
     pairs = (
         (mine, tok.at[pl.ds(pl.multiple_of(c * 64, 64), 64), :]),
@@ -117,7 +133,6 @@
         copy.start()
     tok[pl.ds(pl.multiple_of((1 - c) * 64, 64), 64), :] = theirs[...]
     copies[0].wait()
-    last[...] = tok[Q - 16 : Q, :][8:16]
     copies[1].wait()
     rows = tok[...]
     xo[...] = jnp.dot(rows, wx[...], preferred_element_type=F32).astype(BF)
@@ -136,13 +151,12 @@
             pltpu.VMEM((Q, CH), BF),
             pltpu.VMEM((Q, BCW), BF),
             pltpu.VMEM((1, HH, Q), F32),
-            pltpu.VMEM((8, 4096), BF),
             pltpu.VMEM(in_x.shape, BF),
             pltpu.VMEM(in_bc.shape, BF),
             pltpu.VMEM(in_dt.shape, BF),
         ),
         in_specs=[hbm, VMEM, hbm, hbm, hbm],
-        out_specs=(VMEM,) * 7,
+        out_specs=(VMEM,) * 6,
         scratch_shapes=[pltpu.VMEM((Q, 4096), BF), pltpu.SemaphoreType.DMA((4,))],
         compiler_params=params(),
         name="project_near",
@@ -170,12 +184,13 @@
 
 def local_kernel(bias, alog, *refs):
     x0, bc0, dt0, x12, bc12, dt12 = refs[0:6]
-    far, halo, haloswap = refs[6:10], refs[10], refs[11]
-    wx, wbc, wdt, kx, kbc = refs[12:17]
-    (xo, bo, co, cso, dto, eo, do, send) = refs[17:25]
-    ext, extb, dtr, tok = refs[25:29]
+    far, far_swap, halo, haloswap = refs[6:10]
+    wx, wbc, wdt, kx, kbc = refs[10:15]
+    (xo, bo, co, cso, dto, eo, do, send) = refs[15:23]
+    ext, extb, dtr, tok = refs[23:27]
     y = chip()
-    fill(tok, far[0:2], far[2:4])
+    place(tok, far, 0, core())
+    place(tok, far_swap, 0, 1 - core())
     edge = halo[...].astype(F32) + haloswap[...].astype(F32)
     tok[Q : Q + 16, :] = jnp.concatenate([edge, edge], 0).astype(BF)
     rows = tok[...]
@@ -257,7 +272,7 @@
             s((NQ, 8, CH), F32),
             s((32, 24, 128), BF),
         ),
-        in_specs=[SMEM] * 2 + [VMEM] * 17,
+        in_specs=[SMEM] * 2 + [VMEM] * 15,
         out_specs=(VMEM,) * 8,
         scratch_shapes=[
             pltpu.VMEM((8 + NQ * Q, CH), F32),
@@ -355,10 +370,10 @@
     v = jnp.dot(v, w[...], preferred_element_type=F32).astype(BF)
     other[...] = v[0:64]
     own[...] = v[64:128]
-    for j, k in enumerate((1, 3, 0)):
-        a = lax.rem(y + k, NQ)
-        rest[64 * j : 64 * j + 64, :] = half(a, 1 - mine)
-        rest[192 + 64 * j : 256 + 64 * j, :] = half(a, mine)
+    side, across = lax.rem(y + 1 + 2 * mine, NQ), lax.rem(y + 3 - 2 * mine, NQ)
+    parts = ((across, mine), (across, 1 - mine), (side, 1 - mine), (side, mine), (y, 1 - mine), (y, mine))
+    for j, (a, h) in enumerate(parts):
+        rest[64 * j : 64 * j + 64, :] = half(a, h)
 
 
 def norm_part(*args):
@@ -392,17 +407,14 @@
     )(in_vmem(n), in_vmem(w))
 
 
-UP = [(y * 2 + c, ((y + 1) % 4) * 2 + c) for y in range(4) for c in range(2)]
-DOWN = [(y * 2 + c, ((y - 1) % 4) * 2 + c) for y in range(4) for c in range(2)]
 SWAP = [(y * 2 + c, y * 2 + 1 - c) for y in range(4) for c in range(2)]
 
 
-def up(v):
-    return lax.ppermute(v, "tp", UP)
-
-
-def down(v):
-    return lax.ppermute(v, "tp", DOWN)
+AROUND = [(y * 2 + c, ((y + 1 - 2 * c) % 4) * 2 + c) for y in range(4) for c in range(2)]
+
+
+def around(v):
+    return lax.ppermute(v, "tp", AROUND)
 
 
 def swap(v):
@@ -411,11 +423,9 @@
 
 def per_device(tokens, in_x, in_bc, in_dt, conv_x, conv_bc, dt_bias, a_log, skip_d, norm_gain, out_w):
     after = lax.optimization_barrier
-    lo, hi = tokens[:32], tokens[32:]
-    ua, db = up(lo), down(hi)
-    ub, da = up(hi), down(lo)
-    *piece0, last, wx, wbc, wdt = project_near(tokens, swap(tokens), in_x, in_bc, in_dt.T)
-    weights = (wx, wbc, wdt)
+    partner = swap(tokens)
+    first, second, last = pack(tokens, partner)
+    r1, r2 = around(first), around(second)
     spans = lax.axis_size("ctx")
 
     def onward(*route):
@@ -424,18 +434,17 @@
         )
 
     edge = onward((7, 7), (6, 1)) + onward((7, 5), (6, 3))
-    ua, db, wx = after((ua, db, wx))
-    ub, da, edge = after((ub, da, edge))
+    *piece0, wx, wbc, wdt = project_near(tokens, partner, in_x, in_bc, in_dt.T)
+    weights = (wx, wbc, wdt)
+    r1, wx = after((r1, wx))
+    far = around(r1)
+    r2, edge = after((r2, edge))
     edges = swap(edge)
-    uu, dd = up(ua), down(db)
-    own = [ua, ub, da, db]
-    other = [swap(v) for v in own]
-    *other, uu, dd = after((*other, uu, dd))
-    far = [uu, dd, swap(uu), swap(dd)]
-    piece12 = project(own, other, weights, 2, "project_next")
+    piece12 = project_next(r1, r2, swap(r1), swap(r2), *weights)
+    far, *piece12 = after((far, *piece12))
 
     xc, b, c, cs, dt, e, d, send = local_part(
-        dt_bias, a_log, *piece0, *piece12, *far, edge, edges, *weights, conv_x, conv_bc
+        dt_bias, a_log, *piece0, *piece12, far, swap(far), edge, edges, *weights, conv_x, conv_bc
     )
     got = lax.all_to_all(send, "ctx", 0, 0, tiled=True)
     ydiag = diag_part(skip_d, xc, b, c, cs, dt)
@@ -446,18 +455,12 @@
         return mine.astype(F32) + swap(theirs).astype(F32)
 
     q2 = both(own, other).astype(BF)
-    u2, d2 = up(q2[:32]), down(q2[32:])
-    t1, tm, t0, m1, mm, m0 = out_part(rest, w)
-    q1 = both(m1, t1)
-    u1b = up(q1[32:].astype(BF))
-    qm = both(mm, tm)
-    dma = down(qm[:32].astype(BF))
-    u1a = up((q1[:32] + u2.astype(F32)).astype(BF))
-    dmb = down((qm[32:] + d2.astype(F32)).astype(BF))
-    q0 = both(m0, t0)
-    top = q0[:32] + u1a.astype(F32) + dma.astype(F32)
-    bottom = q0[32:] + u1b.astype(F32) + dmb.astype(F32)
-    return jnp.concatenate([top.astype(BF), bottom.astype(BF)], 0)
+    give_raw, give_sum, keep_raw, keep_sum, give, keep = out_part(rest, w)
+    q2, give_raw, give_sum, give = after((q2, give_raw, give_sum, give))
+    first = around(q2)
+    raw = around(both(keep_raw, give_raw).astype(BF))
+    summed = around((both(keep_sum, give_sum) + first.astype(F32)).astype(BF))
+    return (both(keep, give) + swap(raw).astype(F32) + summed.astype(F32)).astype(BF)
 
 
 def solution(mesh):

time: 110 us -> 104 us (0.945)
  starting transfers between devices: 33 us -> 13.9 us
  waiting for transfers between devices: 31.1 us -> 45.4 us
    ppermute x12 -> x6, starting transfers between devices: 23.2 us -> 3.4 us  [around(): return lax.ppermute(v, 'tp', AROUND)]
    ppermute x12 -> x6, waiting for transfers between devices: 21.8 us -> 29.6 us  [around(): return lax.ppermute(v, 'tp', AROUND)]
    ppermute x12 -> x10, waiting for transfers between devices: 1.36 us -> 7.92 us  [swap(): return lax.ppermute(v, 'tp', SWAP)]
    slice x4 -> x0, local copies, waits for them, and re-layouts: 1.16 us -> none  [the longest x1 1.06 us: per_device(): lo, hi = (tokens[:32], tokens[32:])]
    convert_element_type x3, other arithmetic: 0.27 us -> 1.38 us  [the longest x1 1.06 us: per_device(): (both(keep, give) + swap(raw).astype(F32) + summed.astype(F32)).astype(BF)]
    ppermute x12 -> x10, starting transfers between devices: 4.06 us -> 4.52 us  [swap(): return lax.ppermute(v, 'tp', SWAP)]
    pallas_call x1 -> x2, Pallas kernels: 2.4 us -> 2.56 us  [the longest x1 2.48 us: project_next(): pl.pallas_call(next_kernel, out_shape=(pltpu.VMEM((2 * Q, CH), BF), pltpu...]
  transfers between devices with their start and end apart: 27 -> 19, of which waited for: 10 -> 13; matrix products, arithmetic and copies ran while one was open for 2% -> 0% of each run, Pallas kernels for 8% -> 10%
where the time goes in v7:
time: 104 us; the launch traced here: 103 us
  waiting for transfers between devices  45.4 us (44%)
  blocking collectives  22.3 us (21%)
  Pallas kernels  19 us (18%)
  starting transfers between devices  13.9 us (13%)
  other arithmetic  1.52 us (1%)
  local copies, waits for them, and re-layouts  1.07 us (1%)
    ppermute x6, waiting for transfers between devices, around(): return lax.ppermute(v, 'tp', AROUND)  29.6 us
    all_to_all x1, blocking collectives, per_device(): got = lax.all_to_all(send, 'ctx', 0, 0, tiled=True)  22.3 us
    all_to_all x1, waiting for transfers between devices, per_device(): back = lax.all_to_all(prefix(got), 'ctx', 0, 0, tiled=True)  7.92 us
    ppermute x10, waiting for transfers between devices, swap(): return lax.ppermute(v, 'tp', SWAP)  7.92 us
    pallas_call x1, Pallas kernels, local_part(): pl.pallas_call(local_kernel, out_shape=(s((NQ, Q, CH), BF), s((NQ, Q, NS)...  4.68 us
    all_to_all x1, starting transfers between devices, per_device(): back = lax.all_to_all(prefix(got), 'ctx', 0, 0, tiled=True)  4.64 us
    ppermute x10, starting transfers between devices, swap(): return lax.ppermute(v, 'tp', SWAP)  4.52 us
    pallas_call x1, Pallas kernels, project_near(): pl.pallas_call(near_kernel, out_shape=(pltpu.VMEM((Q, CH), BF), pltpu.VME...  4.5 us
  transfers between devices with their start and end apart: 19, of which 13 were waited for; matrix products, arithmetic and copies ran while one was open for 0% of the time, Pallas kernels for 10%

profile of v7, /device:TPU:32, one launch (start us, length us, event | category | flops | bytes accessed | tf_op | source)
XLA Modules:
  0.0 103.4 jit_solution(3028494800381110653)
XLA Ops:
  0.0 2.1 %collective-permute-done.theirs = bf16[64,4096]{1,0:T(8,128)(2,1)S(1)} collective-permute-done((bf16[64,4096]{1,0:T(8,128)(2,1)}, bf16[64,4096]{1,0:T(8,128)(2,1)S(1)}, u32[]{:S(2)}, u32[]{:S(2)}) %collective-permute-start) | collective-permute-done | bytes 524320 | tf_op jit(solution)/shard_map/ppermute | solution.py:421
  2.1 1.0 %copy-done = bf16[64,4096]{1,0:T(8,128)(2,1)S(1)} copy-done((bf16[64,4096]{1,0:T(8,128)(2,1)S(1)}, bf16[64,4096]{1,0:T(8,128)(2,1)}, u32[]{:S(2)}) %copy-start) | copy-done | bytes 524312
  3.2 1.7 %collective-permute-start.3 = (bf16[64,4096]{1,0:T(8,128)(2,1)S(1)}, bf16[64,4096]{1,0:T(8,128)(2,1)S(1)}, u32[]{:S(2)}, u32[]{:S(2)}) collective-permute-start(bf16[64,4096]{1,0:T(8,128)(2,1)S(1)} %get-tuple-element.52), channel_id=1, source_target_pairs={{0,2},{1,7},{2,4},{3,1},{4,6},{5,3},{6,0},{7,5},{8,10},{9,15},{10,... | collective-permute-start | bytes 1572872 | tf_op jit(solution)/shard_map/ppermute | solution.py:417
  4.9 1.6 %collective-permute-start.1 = (bf16[64,4096]{1,0:T(8,128)(2,1)S(1)}, bf16[64,4096]{1,0:T(8,128)(2,1)S(1)}, u32[]{:S(2)}, u32[]{:S(2)}) collective-permute-start(bf16[64,4096]{1,0:T(8,128)(2,1)S(1)} %get-tuple-element.49), channel_id=1, source_target_pairs={{0,2},{1,7},{2,4},{3,1},{4,6},{5,3},{6,0},{7,5},{8,10},{9,15},{10,... | collective-permute-start | bytes 1572872 | tf_op jit(solution)/shard_map/ppermute | solution.py:417
  7.8 4.5 %project_near.1 = (bf16[128,512]{1,0:T(8,128)(2,1)S(1)}, bf16[128,256]{1,0:T(8,128)(2,1)S(1)}, f32[1,8,128]{2,1,0:T(8,128)S(1)}, bf16[4096,512]{1,0:T(8,128)(2,1...) custom-call(bf16[64,4096]{1,0:T(8,128)(2,1)} %mine.3, ...), custom_call_target="tpu_custom_call" | custom-call | tf_op jit(solution)/shard_map/project_near/pallas_call | solution.py:148
  12.4 1.3 %collective-permute-done.3.r2 = bf16[64,4096]{1,0:T(8,128)(2,1)S(1)} collective-permute-done((bf16[64,4096]{1,0:T(8,128)(2,1)S(1)}, bf16[64,4096]{1,0:T(8,128)(2,1)S(1)}, u32[]{:S(2)}, u32[]{:S(2)}) %collective-permute-start.3) | collective-permute-done | bytes 524320 | tf_op jit(solution)/shard_map/ppermute | solution.py:417
  13.7 2.9 %collective-permute-start.7 = (bf16[64,4096]{1,0:T(8,128)(2,1)S(1)}, bf16[64,4096]{1,0:T(8,128)(2,1)S(1)}, u32[]{:S(2)}, u32[]{:S(2)}) collective-permute-start(bf16[64,4096]{1,0:T(8,128)(2,1)S(1)} %collective-permute-done.3.r2), channel_id=1, source_target_pairs={{0,1},{1,0},{2,3},{3,2},{4,5},{5,4},{6,7},{7,6},{8,9},{9,8},{10,11... | collective-permute-start | bytes 1572872 | tf_op jit(solution)/shard_map/ppermute | solution.py:421
  16.6 3.4 %collective-permute-done.1.r1 = bf16[64,4096]{1,0:T(8,128)(2,1)S(1)} collective-permute-done((bf16[64,4096]{1,0:T(8,128)(2,1)S(1)}, bf16[64,4096]{1,0:T(8,128)(2,1)S(1)}, u32[]{:S(2)}, u32[]{:S(2)}) %collective-permute-start.1) | collective-permute-done | bytes 524320 | tf_op jit(solution)/shard_map/ppermute | solution.py:417
  20.1 1.9 %collective-permute-done.6.s1 = bf16[64,4096]{1,0:T(8,128)(2,1)S(1)} collective-permute-done((bf16[64,4096]{1,0:T(8,128)(2,1)S(1)}, bf16[64,4096]{1,0:T(8,128)(2,1)S(1)}, u32[]{:S(2)}, u32[]{:S(2)}) %collective-permute-start.6) | collective-permute-done | bytes 524320 | tf_op jit(solution)/shard_map/ppermute | solution.py:421
  22.0 2.5 %project_next.1 = (bf16[256,512]{1,0:T(8,128)(2,1)S(1)}, bf16[256,256]{1,0:T(8,128)(2,1)S(1)}, f32[2,8,128]{2,1,0:T(8,128)S(1)}) custom-call(bf16[64,4096]{1,0:T(8,128)(2,1)S(1)} %collective-permute-done.1.r1, bf16[64,4096]{1,0:T(8,128)(2,1)S(1)} %collective-permute-done.3.r2, bf16[64,4096]{1,0:T(8,128)(2,1)S(1)} %collective-permute-done.6.s1, ...), custom_call_target="tpu_custom_call" | custom-call | tf_op jit(solution)/shard_map/project_next/pallas_call | solution.py:108
  24.4 6.0 %collective-permute-done.2.refs_6_ = bf16[64,4096]{1,0:T(8,128)(2,1)S(1)} collective-permute-done((bf16[64,4096]{1,0:T(8,128)(2,1)S(1)}, bf16[64,4096]{1,0:T(8,128)(2,1)S(1)}, u32[]{:S(2)}, u32[]{:S(2)}) %collective-permute-start.2) | collective-permute-done | bytes 524320 | tf_op jit(solution)/shard_map/ppermute | solution.py:417
  30.9 1.5 %collective-permute-done.9.refs_9_ = bf16[8,4096]{1,0:T(8,128)(2,1)S(1)} collective-permute-done((bf16[8,4096]{1,0:T(8,128)(2,1)S(1)}, bf16[8,4096]{1,0:T(8,128)(2,1)S(1)}, u32[]{:S(2)}, u32[]{:S(2)}) %collective-permute-start.9) | collective-permute-done | bytes 65568 | tf_op jit(solution)/shard_map/ppermute | solution.py:421
  32.5 4.7 %local_part.1 = (bf16[4,128,512]{2,1,0:T(8,128)(2,1)S(1)}, bf16[4,128,128]{2,1,0:T(8,128)(2,1)S(1)}, bf16[4,128,128]{2,1,0:T(8,128)(2,1)S(1)}, f32[4,8,128]{2,1,...) custom-call(f32[8]{0:T(128)S(1)} %copy-done.4, ...), custom_call_target="tpu_custom_call" | custom-call | tf_op jit(solution)/shard_map/local_part/pallas_call | solution.py:263
  37.2 22.3 %all_to_all.10.r = bf16[32,24,128]{2,1,0:T(8,128)(2,1)S(1)} all-to-all(bf16[32,24,128]{2,1,0:T(8,128)(2,1)S(1)} %get-tuple-element.65), channel_id=1, replica_groups=mesh['ctx'=32,'tp'=8] {'ctx'}, dimensions={0} | all-to-all | bytes 393216 | tf_op jit(solution)/shard_map/all_to_all | solution.py:449
  60.2 4.6 %all-to-all-start.1 = ((bf16[32,16,128]{2,1,0:T(8,128)(2,1)}), bf16[32,16,128]{2,1,0:T(8,128)(2,1)S(1)}, u32[]{:S(2)}, u32[]{:S(2)}) async-start(bf16[32,16,128]{2,1,0:T(8,128)(2,1)} %prefix.1), calls=%async_computation.1 | async-start | bytes 262144 | tf_op jit(solution)/shard_map/all_to_all | solution.py:451
  64.8 1.8 %diag_part.1.ydiag = f32[4,128,512]{2,1,0:T(8,128)S(1)} custom-call(f32[8]{0:T(128)S(1)} %copy-done.6, bf16[4,128,512]{2,1,0:T(8,128)(2,1)S(1)} %get-tuple-element.70.x, bf16[4,128,128]{2,1,0:T(8,128)(2,1)S(1)} %get-tuple-element.71.b, bf16[4,128,128]{2,1,0:T(8,128)(2,1)S(1)} %get-tuple-element.68.c, f32[4,8,128]{2,1,0:T(8,128)S(1)} %get-tuple-element.69.cs, ...), custom_call_target="tpu_custom_call" | custom-call | tf_op jit(solution)/shard_map/diag_part/pallas_call | solution.py:331
  66.7 7.9 %all-to-all-done.1 = bf16[32,16,128]{2,1,0:T(8,128)(2,1)S(1)} async-done(((bf16[32,16,128]{2,1,0:T(8,128)(2,1)}), bf16[32,16,128]{2,1,0:T(8,128)(2,1)S(1)}, u32[]{:S(2)}, u32[]{:S(2)}) %all-to-all-start.1) | async-done | bytes 131104 | tf_op jit(solution)/shard_map/all_to_all | solution.py:451
  74.6 2.9 %norm_part.1 = (bf16[64,4096]{1,0:T(8,128)(2,1)S(1)}, bf16[64,4096]{1,0:T(8,128)(2,1)S(1)}, bf16[384,512]{1,0:T(8,128)(2,1)S(1)}, bf16[512,4096]{1,0:T(8,128)(2,1)S(1)}) custom-call(bf16[512,128]{1,0:T(8,128)(2,1)S(1)} %bitcast.3, f32[4,128,512]{2,1,0:T(8,128)S(1)} %get-tuple-element.66.e, f32[4,8,512]{2,1,0:T(8,128)S(1)} %get-tuple-element.67.d, ...), custom_call_target="tpu_custom_call" | custom-call | tf_op jit(solution)/shard_map/norm_part/pallas_call | solution.py:381
  77.6 1.8 %out_part.1 = (bf16[64,4096]{1,0:T(8,128)(2,1)S(1)}, bf16[64,4096]{1,0:T(8,128)(2,1)S(1)}, bf16[64,4096]{1,0:T(8,128)(2,1)S(1)}, bf16[64,4096]{1,0:T(8,128)(2,1)...) custom-call(bf16[384,512]{1,0:T(8,128)(2,1)S(1)} %get-tuple-element.73.n, ...), custom_call_target="tpu_custom_call" | custom-call | tf_op jit(solution)/shard_map/out_part/pallas_call | solution.py:400
  81.9 1.3 %collective-permute-done.15 = bf16[64,4096]{1,0:T(8,128)(2,1)S(1)} collective-permute-done((bf16[64,4096]{1,0:T(8,128)(2,1)S(1)}, bf16[64,4096]{1,0:T(8,128)(2,1)S(1)}, u32[]{:S(2)}, u32[]{:S(2)}) %collective-permute-start.15) | collective-permute-done | bytes 524320 | tf_op jit(solution)/shard_map/ppermute | solution.py:421
  83.2 7.9 %collective-permute-done.16 = bf16[64,4096]{1,0:T(8,128)(2,1)S(1)} collective-permute-done((bf16[64,4096]{1,0:T(8,128)(2,1)S(1)}, bf16[64,4096]{1,0:T(8,128)(2,1)S(1)}, u32[]{:S(2)}, u32[]{:S(2)}) %collective-permute-start.16) | collective-permute-done | bytes 524320 | tf_op jit(solution)/shard_map/ppermute | solution.py:417
  91.3 5.3 %collective-permute-done.13 = bf16[64,4096]{1,0:T(8,128)(2,1)S(1)} collective-permute-done((bf16[64,4096]{1,0:T(8,128)(2,1)S(1)}, bf16[64,4096]{1,0:T(8,128)(2,1)S(1)}, u32[]{:S(2)}, u32[]{:S(2)}) %collective-permute-start.13) | collective-permute-done | bytes 524320 | tf_op jit(solution)/shard_map/ppermute | solution.py:417
  96.7 5.6 %collective-permute-done.17 = bf16[64,4096]{1,0:T(8,128)(2,1)S(1)} collective-permute-done((bf16[64,4096]{1,0:T(8,128)(2,1)S(1)}, bf16[64,4096]{1,0:T(8,128)(2,1)S(1)}, u32[]{:S(2)}, u32[]{:S(2)}) %collective-permute-start.17) | collective-permute-done | bytes 524320 | tf_op jit(solution)/shard_map/ppermute | solution.py:417
  102.3 1.1 %add_convert_fusion = bf16[64,4096]{1,0:T(8,128)(2,1)} fusion(bf16[64,4096]{1,0:T(8,128)(2,1)S(1)} %collective-permute-done.17, bf16[64,4096]{1,0:T(8,128)(2,1)S(1)} %collective-permute-done.14, bf16[64,4096]{1,0:T(8,128)(2,1)S(1)} %collective-permute-done.11, bf16[64,4096]{1,0:T(8,128)(2,1)S(1)} %get-tuple-element.75), kind=kLoop, calls=%fused_computation | loop fusion | flops 2097152 | bytes 2621440 | tf_op jit(solution)/shard_map/convert_element_type | solution.py:463
  (42 shorter events, 5.5 us)
Async XLA Ops:
  0.0 2.1 %collective-permute-start = (bf16[64,4096]{1,0:T(8,128)(2,1)}, bf16[64,4096]{1,0:T(8,128)(2,1)S(1)}, u32[]{:S(2)}, u32[]{:S(2)}) collective-permute-start(bf16[64,4096]{1,0:T(8,128)(2,1)} %mine.3), channel_id=1, source_target_pairs={{0,1},{1,0},{2,3},{3,2},{4,5},{5,4},{6,7},{7,6},{8,9},{9,8},{10,11... | collective-permute-start | bytes 1572872 | tf_op jit(solution)/shard_map/ppermute | solution.py:421
  3.2 10.5 %collective-permute-start.3 = (bf16[64,4096]{1,0:T(8,128)(2,1)S(1)}, bf16[64,4096]{1,0:T(8,128)(2,1)S(1)}, u32[]{:S(2)}, u32[]{:S(2)}) collective-permute-start(bf16[64,4096]{1,0:T(8,128)(2,1)S(1)} %get-tuple-element.52), channel_id=1, source_target_pairs={{0,2},{1,7},{2,4},{3,1},{4,6},{5,3},{6,0},{7,5},{8,10},{9,15},{10,... | collective-permute-start | bytes 1572872 | tf_op jit(solution)/shard_map/ppermute | solution.py:417
  4.9 15.1 %collective-permute-start.1 = (bf16[64,4096]{1,0:T(8,128)(2,1)S(1)}, bf16[64,4096]{1,0:T(8,128)(2,1)S(1)}, u32[]{:S(2)}, u32[]{:S(2)}) collective-permute-start(bf16[64,4096]{1,0:T(8,128)(2,1)S(1)} %get-tuple-element.49), channel_id=1, source_target_pairs={{0,2},{1,7},{2,4},{3,1},{4,6},{5,3},{6,0},{7,5},{8,10},{9,15},{10,... | collective-permute-start | bytes 1572872 | tf_op jit(solution)/shard_map/ppermute | solution.py:417
  6.5 5.8 %collective-permute-start.5 = (bf16[8,4096]{1,0:T(8,128)(2,1)S(1)}, bf16[8,4096]{1,0:T(8,128)(2,1)S(1)}, u32[]{:S(2)}, u32[]{:S(2)}) collective-permute-start(bf16[8,4096]{1,0:T(8,128)(2,1)S(1)} %get-tuple-element.53), channel_id=1, source_target_pairs={{7,13},{6,11},{15,21},{14,19},{23,29},{22,27},{31,37},{30,35},{39,... | collective-permute-start | bytes 196616 | tf_op jit(solution)/shard_map/ppermute | solution.py:432
  7.1 5.2 %collective-permute-start.4 = (bf16[8,4096]{1,0:T(8,128)(2,1)S(1)}, bf16[8,4096]{1,0:T(8,128)(2,1)S(1)}, u32[]{:S(2)}, u32[]{:S(2)}) collective-permute-start(bf16[8,4096]{1,0:T(8,128)(2,1)S(1)} %get-tuple-element.53), channel_id=1, source_target_pairs={{7,15},{6,9},{15,23},{14,17},{23,31},{22,25},{31,39},{30,33},{39,4... | collective-permute-start | bytes 196616 | tf_op jit(solution)/shard_map/ppermute | solution.py:432
  13.7 6.3 %collective-permute-start.7 = (bf16[64,4096]{1,0:T(8,128)(2,1)S(1)}, bf16[64,4096]{1,0:T(8,128)(2,1)S(1)}, u32[]{:S(2)}, u32[]{:S(2)}) collective-permute-start(bf16[64,4096]{1,0:T(8,128)(2,1)S(1)} %collective-permute-done.3.r2), channel_id=1, source_target_pairs={{0,1},{1,0},{2,3},{3,2},{4,5},{5,4},{6,7},{7,6},{8,9},{9,8},{10,11... | collective-permute-start | bytes 1572872 | tf_op jit(solution)/shard_map/ppermute | solution.py:421
  20.0 1.9 %collective-permute-start.6 = (bf16[64,4096]{1,0:T(8,128)(2,1)S(1)}, bf16[64,4096]{1,0:T(8,128)(2,1)S(1)}, u32[]{:S(2)}, u32[]{:S(2)}) collective-permute-start(bf16[64,4096]{1,0:T(8,128)(2,1)S(1)} %collective-permute-done.1.r1), channel_id=1, source_target_pairs={{0,1},{1,0},{2,3},{3,2},{4,5},{5,4},{6,7},{7,6},{8,9},{9,8},{10,11... | collective-permute-start | bytes 1572872 | tf_op jit(solution)/shard_map/ppermute | solution.py:421
  20.0 10.4 %collective-permute-start.2 = (bf16[64,4096]{1,0:T(8,128)(2,1)S(1)}, bf16[64,4096]{1,0:T(8,128)(2,1)S(1)}, u32[]{:S(2)}, u32[]{:S(2)}) collective-permute-start(bf16[64,4096]{1,0:T(8,128)(2,1)S(1)} %collective-permute-done.1.r1), channel_id=1, source_target_pairs={{0,2},{1,7},{2,4},{3,1},{4,6},{5,3},{6,0},{7,5},{8,10},{9,15},{10,... | collective-permute-start | bytes 1572872 | tf_op jit(solution)/shard_map/ppermute | solution.py:417
  22.0 10.5 %copy-start.2 = (f32[4,256]{1,0:T(4,128)S(1)}, f32[4,256]{1,0:T(4,128)}, u32[]{:S(2)}) copy-start(f32[4,256]{1,0:T(4,128)} %refs_14_.1) | copy-start | bytes 12292
  22.0 10.5 %copy-start.4 = (f32[8]{0:T(128)S(1)}, f32[8]{0:T(128)}, u32[]{:S(2)}) copy-start(f32[8]{0:T(128)} %bias.1) | copy-start | bytes 100
  22.0 10.5 %copy-start.5 = (f32[8]{0:T(128)S(1)}, f32[8]{0:T(128)}, u32[]{:S(2)}) copy-start(f32[8]{0:T(128)} %alog.1) | copy-start | bytes 100
  30.4 2.0 %collective-permute-start.8 = (bf16[64,4096]{1,0:T(8,128)(2,1)S(1)}, bf16[64,4096]{1,0:T(8,128)(2,1)S(1)}, u32[]{:S(2)}, u32[]{:S(2)}) collective-permute-start(bf16[64,4096]{1,0:T(8,128)(2,1)S(1)} %collective-permute-done.2.refs_6_), channel_id=1, source_target_pairs={{0,1},{1,0},{2,3},{3,2},{4,5},{5,4},{6,7},{7,6},{8,9},{9,8},{10,11... | collective-permute-start | bytes 1572872 | tf_op jit(solution)/shard_map/ppermute | solution.py:421
  30.4 2.0 %collective-permute-start.9 = (bf16[8,4096]{1,0:T(8,128)(2,1)S(1)}, bf16[8,4096]{1,0:T(8,128)(2,1)S(1)}, u32[]{:S(2)}, u32[]{:S(2)}) collective-permute-start(bf16[8,4096]{1,0:T(8,128)(2,1)S(1)} %add.24.refs_8_), channel_id=1, source_target_pairs={{0,1},{1,0},{2,3},{3,2},{4,5},{5,4},{6,7},{7,6},{8,9},{9,8},{10,11... | collective-permute-start | bytes 196616 | tf_op jit(solution)/shard_map/ppermute | solution.py:421
  32.5 32.4 %copy-start.6 = (f32[8]{0:T(128)S(1)}, f32[8]{0:T(128)}, u32[]{:S(2)}) copy-start(f32[8]{0:T(128)} %skip.1) | copy-start | bytes 100
  32.5 42.1 %copy-start.3 = (f32[512]{0:T(512)S(1)}, f32[512]{0:T(512)}, u32[]{:S(2)}) copy-start(f32[512]{0:T(512)} %param.20) | copy-start | bytes 6148
  60.2 14.4 %all-to-all-start.1 = ((bf16[32,16,128]{2,1,0:T(8,128)(2,1)}), bf16[32,16,128]{2,1,0:T(8,128)(2,1)S(1)}, u32[]{:S(2)}, u32[]{:S(2)}) async-start(bf16[32,16,128]{2,1,0:T(8,128)(2,1)} %prefix.1), calls=%async_computation.1 | async-start | bytes 262144 | tf_op jit(solution)/shard_map/all_to_all | solution.py:451
  77.5 2.0 %collective-permute-start.10 = (bf16[64,4096]{1,0:T(8,128)(2,1)S(1)}, bf16[64,4096]{1,0:T(8,128)(2,1)S(1)}, u32[]{:S(2)}, u32[]{:S(2)}) collective-permute-start(bf16[64,4096]{1,0:T(8,128)(2,1)S(1)} %get-tuple-element.77), channel_id=1, source_target_pairs={{0,1},{1,0},{2,3},{3,2},{4,5},{5,4},{6,7},{7,6},{8,9},{9,8},{10,11... | collective-permute-start | bytes 1572872 | tf_op jit(solution)/shard_map/ppermute | solution.py:421
  79.7 2.0 %collective-permute-start.12 = (bf16[64,4096]{1,0:T(8,128)(2,1)S(1)}, bf16[64,4096]{1,0:T(8,128)(2,1)S(1)}, u32[]{:S(2)}, u32[]{:S(2)}) collective-permute-start(bf16[64,4096]{1,0:T(8,128)(2,1)S(1)} %get-tuple-element.83), channel_id=1, source_target_pairs={{0,1},{1,0},{2,3},{3,2},{4,5},{5,4},{6,7},{7,6},{8,9},{9,8},{10,11... | collective-permute-start | bytes 1572872 | tf_op jit(solution)/shard_map/ppermute | solution.py:421
  80.2 16.5 %collective-permute-start.11 = (bf16[64,4096]{1,0:T(8,128)(2,1)S(1)}, bf16[64,4096]{1,0:T(8,128)(2,1)S(1)}, u32[]{:S(2)}, u32[]{:S(2)}) collective-permute-start(bf16[64,4096]{1,0:T(8,128)(2,1)S(1)} %get-tuple-element.81), channel_id=1, source_target_pairs={{0,1},{1,0},{2,3},{3,2},{4,5},{5,4},{6,7},{7,6},{8,9},{9,8},{10,11... | collective-permute-start | bytes 1572872 | tf_op jit(solution)/shard_map/ppermute | solution.py:421
  80.3 2.9 %collective-permute-start.15 = (bf16[64,4096]{1,0:T(8,128)(2,1)S(1)}, bf16[64,4096]{1,0:T(8,128)(2,1)S(1)}, u32[]{:S(2)}, u32[]{:S(2)}) collective-permute-start(bf16[64,4096]{1,0:T(8,128)(2,1)S(1)} %get-tuple-element.85), channel_id=1, source_target_pairs={{0,1},{1,0},{2,3},{3,2},{4,5},{5,4},{6,7},{7,6},{8,9},{9,8},{10,11... | collective-permute-start | bytes 1572872 | tf_op jit(solution)/shard_map/ppermute | solution.py:421
  80.7 10.4 %collective-permute-start.16 = (bf16[64,4096]{1,0:T(8,128)(2,1)S(1)}, bf16[64,4096]{1,0:T(8,128)(2,1)S(1)}, u32[]{:S(2)}, u32[]{:S(2)}) collective-permute-start(bf16[64,4096]{1,0:T(8,128)(2,1)S(1)} %add_convert_fusion.3), channel_id=1, source_target_pairs={{0,2},{1,7},{2,4},{3,1},{4,6},{5,3},{6,0},{7,5},{8,10},{9,15},{10,... | collective-permute-start | bytes 1572872 | tf_op jit(solution)/shard_map/ppermute | solution.py:417
  81.8 14.9 %collective-permute-start.13 = (bf16[64,4096]{1,0:T(8,128)(2,1)S(1)}, bf16[64,4096]{1,0:T(8,128)(2,1)S(1)}, u32[]{:S(2)}, u32[]{:S(2)}) collective-permute-start(bf16[64,4096]{1,0:T(8,128)(2,1)S(1)} %add_convert_fusion.2), channel_id=1, source_target_pairs={{0,2},{1,7},{2,4},{3,1},{4,6},{5,3},{6,0},{7,5},{8,10},{9,15},{10,... | collective-permute-start | bytes 1572872 | tf_op jit(solution)/shard_map/ppermute | solution.py:417
  91.3 11.0 %collective-permute-start.17 = (bf16[64,4096]{1,0:T(8,128)(2,1)S(1)}, bf16[64,4096]{1,0:T(8,128)(2,1)S(1)}, u32[]{:S(2)}, u32[]{:S(2)}) collective-permute-start(bf16[64,4096]{1,0:T(8,128)(2,1)S(1)} %add_convert_fusion.1), channel_id=1, source_target_pairs={{0,2},{1,7},{2,4},{3,1},{4,6},{5,3},{6,0},{7,5},{8,10},{9,15},{10,... | collective-permute-start | bytes 1572872 | tf_op jit(solution)/shard_map/ppermute | solution.py:417
  96.7 5.6 %collective-permute-start.14 = (bf16[64,4096]{1,0:T(8,128)(2,1)S(1)}, bf16[64,4096]{1,0:T(8,128)(2,1)S(1)}, u32[]{:S(2)}, u32[]{:S(2)}) collective-permute-start(bf16[64,4096]{1,0:T(8,128)(2,1)S(1)} %collective-permute-done.13), channel_id=1, source_target_pairs={{0,1},{1,0},{2,3},{3,2},{4,5},{5,4},{6,7},{7,6},{8,9},{9,8},{10,11... | collective-permute-start | bytes 1572872 | tf_op jit(solution)/shard_map/ppermute | solution.py:421
  (2 other events, 11.5 us)

commit v8 on v7

--- a/solution.py
+++ b/solution.py
@@ -69,9 +69,13 @@
     tok[pl.ds(pl.multiple_of(at + 64, 32), 32), :] = ref[32:64, :]
 
 
-def pack_kernel(mine, theirs, first, second, last):
+def pack_kernel(far, theirs, first, second, last, mine, sem):
     c = core()
-    for part, ref in ((c, mine), (1 - c, theirs)):
+    copy = pltpu.make_async_copy(far, mine, sem)
+    copy.start()
+    for part, ref in ((1 - c, theirs), (c, mine)):
+        if ref is mine:
+            copy.wait()
         at = pl.ds(pl.multiple_of(part * 32, 32), 32)
         first[at, :] = ref[pl.ds(pl.multiple_of(c * 32, 32), 32), :]
         second[at, :] = ref[pl.ds(pl.multiple_of((1 - c) * 32, 32), 32), :]
@@ -83,11 +87,12 @@
     return pl.pallas_call(
         pack_kernel,
         out_shape=(pltpu.VMEM((64, 4096), BF), pltpu.VMEM((64, 4096), BF), pltpu.VMEM((8, 4096), BF)),
-        in_specs=[VMEM] * 2,
+        in_specs=[pl.BlockSpec(memory_space=pltpu.HBM), VMEM],
         out_specs=(VMEM,) * 3,
+        scratch_shapes=[pltpu.VMEM((64, 4096), BF), pltpu.SemaphoreType.DMA],
         compiler_params=params(),
         name="pack",
-    )(in_vmem(mine), in_vmem(theirs))
+    )(pltpu.with_memory_space_constraint(mine, pltpu.HBM), in_vmem(theirs))
 
 
 def next_kernel(r1, r2, s1, s2, wx, wbc, wdt, xo, bco, dto, tok):
@@ -164,7 +169,8 @@
 
 
 def silu(v):
-    return v / (1.0 + jnp.exp(-v))
+    half = 0.5 * v
+    return half + half * jnp.tanh(half)
 
 
 def softplus(v):
@@ -304,7 +310,9 @@
     )(in_vmem(r))
 
 
-def diag_kernel(skip, x, b, c, cs, dt, y):
+def diag_kernel(skip, w_far, x, b, c, cs, dt, y, w, sem):
+    copy = pltpu.make_async_copy(w_far, w, sem)
+    copy.start()
     t = lax.broadcasted_iota(jnp.int32, (Q, Q), 0)
     u = lax.broadcasted_iota(jnp.int32, (Q, Q), 1)
     tri = t >= u
@@ -325,22 +333,22 @@
             xx = jnp.concatenate([jnp.where(left, xf, 0.0), jnp.where(left, 0.0, xf)], 0).astype(BF)
             yy = jnp.dot(jnp.concatenate(ms, 1), xx, preferred_element_type=F32)
             y[a, :, 128 * p : 128 * p + 128] = yy + jnp.where(left, skip[2 * p], skip[2 * p + 1]) * xf
-
-
-def diag_part(skip, *args):
+    copy.wait()
+
+
+def diag_part(skip, w, *args):
     return pl.pallas_call(
         diag_kernel,
-        out_shape=pltpu.VMEM((NQ, Q, CH), F32),
-        in_specs=[SMEM] + [VMEM] * 5,
-        out_specs=VMEM,
+        out_shape=(pltpu.VMEM((NQ, Q, CH), F32), pltpu.VMEM(w.shape, BF)),
+        in_specs=[SMEM, pl.BlockSpec(memory_space=pltpu.HBM)] + [VMEM] * 5,
+        out_specs=(VMEM, VMEM),
+        scratch_shapes=[pltpu.SemaphoreType.DMA],
         compiler_params=params(),
         name="diag_part",
-    )(skip, *[in_vmem(v) for v in args])
-
-
-def norm_kernel(s_in, e, d, c, cs, ydiag, gain, w_far, other, own, rest, w, nb, sem):
-    copy = pltpu.make_async_copy(w_far, w, sem)
-    copy.start()
+    )(skip, pltpu.with_memory_space_constraint(w, pltpu.HBM), *[in_vmem(v) for v in args])
+
+
+def norm_kernel(s_in, e, d, c, cs, ydiag, gain, w, other, own, rest, nb):
     y = chip()
     mine = core()
     ones = head_spread()
@@ -366,7 +374,6 @@
 
     a = lax.rem(y + 2, NQ)
     v = jnp.concatenate([half(a, 1 - mine), half(a, mine)], 0)
-    copy.wait()
     v = jnp.dot(v, w[...], preferred_element_type=F32).astype(BF)
     other[...] = v[0:64]
     own[...] = v[64:128]
@@ -380,13 +387,13 @@
     s = pltpu.VMEM
     return pl.pallas_call(
         norm_kernel,
-        out_shape=(s((64, 4096), BF), s((64, 4096), BF), s((384, CH), BF), s((CH, 4096), BF)),
-        in_specs=[VMEM] * 7 + [pl.BlockSpec(memory_space=pltpu.HBM)],
-        out_specs=(VMEM,) * 4,
-        scratch_shapes=[pltpu.VMEM((NQ, Q, CH), BF), pltpu.SemaphoreType.DMA],
+        out_shape=(s((64, 4096), BF), s((64, 4096), BF), s((384, CH), BF)),
+        in_specs=[VMEM] * 8,
+        out_specs=(VMEM,) * 3,
+        scratch_shapes=[pltpu.VMEM((NQ, Q, CH), BF)],
         compiler_params=params(),
         name="norm_part",
-    )(*[in_vmem(v) for v in args[:7]], pltpu.with_memory_space_constraint(args[7], pltpu.HBM))
+    )(*[in_vmem(v) for v in args])
 
 
 def out_kernel(n, w, *outs):
@@ -436,20 +443,19 @@
     edge = onward((7, 7), (6, 1)) + onward((7, 5), (6, 3))
     *piece0, wx, wbc, wdt = project_near(tokens, partner, in_x, in_bc, in_dt.T)
     weights = (wx, wbc, wdt)
-    r1, wx = after((r1, wx))
+    r1, wx, edge = after((r1, wx, edge))
     far = around(r1)
-    r2, edge = after((r2, edge))
     edges = swap(edge)
+    far, r2 = after((far, r2))
     piece12 = project_next(r1, r2, swap(r1), swap(r2), *weights)
-    far, *piece12 = after((far, *piece12))
 
     xc, b, c, cs, dt, e, d, send = local_part(
         dt_bias, a_log, *piece0, *piece12, far, swap(far), edge, edges, *weights, conv_x, conv_bc
     )
     got = lax.all_to_all(send, "ctx", 0, 0, tiled=True)
-    ydiag = diag_part(skip_d, xc, b, c, cs, dt)
+    ydiag, w = diag_part(skip_d, out_w, xc, b, c, cs, dt)
     back = lax.all_to_all(prefix(got), "ctx", 0, 0, tiled=True)
-    other, own, rest, w = norm_part(back.reshape(CH, NS), e, d, c, cs, ydiag, norm_gain[None, :], out_w)
+    other, own, rest = norm_part(back.reshape(CH, NS), e, d, c, cs, ydiag, norm_gain[None, :], w)
 
     def both(mine, theirs):
         return mine.astype(F32) + swap(theirs).astype(F32)

time: 104 us -> 103 us (level)
  waiting for transfers between devices: 45.4 us -> 36.5 us
  local copies, waits for them, and re-layouts: 1.07 us -> 4.22 us
  starting transfers between devices: 13.9 us -> 16.6 us
  Pallas kernels: 19 us -> 21.3 us
    all_to_all x1, waiting for transfers between devices: 7.92 us -> 3.9 us  [per_device(): back = lax.all_to_all(prefix(got), 'ctx', 0, 0, tiled=True)]
    unnamed x14 -> x18, local copies, waits for them, and re-layouts: 1.07 us -> 4.22 us
    ppermute x10, waiting for transfers between devices: 7.92 us -> 4.9 us  [swap(): return lax.ppermute(v, 'tp', SWAP)]
    pallas_call x1, Pallas kernels: 1.82 us -> 3.87 us  [diag_part(): pl.pallas_call(diag_kernel, out_shape=(pltpu.VMEM((NQ, Q, CH), F32), pltp...]
    ppermute x6, waiting for transfers between devices: 29.6 us -> 27.7 us  [around(): return lax.ppermute(v, 'tp', AROUND)]
    ppermute x10, starting transfers between devices: 4.52 us -> 6.3 us  [swap(): return lax.ppermute(v, 'tp', SWAP)]
    ppermute x6, starting transfers between devices: 3.4 us -> 4.53 us  [around(): return lax.ppermute(v, 'tp', AROUND)]
  transfers between devices with their start and end apart: 19 -> 19, of which waited for: 13 -> 11; matrix products, arithmetic and copies ran while one was open for 0% -> 0% of each run, Pallas kernels for 10% -> 12%
where the time goes in v8:
time: 103 us; the launch traced here: 102 us
  waiting for transfers between devices  36.5 us (35%)
  blocking collectives  21.8 us (21%)
  Pallas kernels  21.3 us (21%)
  starting transfers between devices  16.6 us (16%)
  local copies, waits for them, and re-layouts  4.22 us (4%)
  other arithmetic  1.51 us (1%)
    ppermute x6, waiting for transfers between devices, around(): return lax.ppermute(v, 'tp', AROUND)  27.7 us
    all_to_all x1, blocking collectives, per_device(): got = lax.all_to_all(send, 'ctx', 0, 0, tiled=True)  21.8 us
    ppermute x10, starting transfers between devices, swap(): return lax.ppermute(v, 'tp', SWAP)  6.3 us
    ppermute x10, waiting for transfers between devices, swap(): return lax.ppermute(v, 'tp', SWAP)  4.9 us
    pallas_call x1, Pallas kernels, local_part(): pl.pallas_call(local_kernel, out_shape=(s((NQ, Q, CH), BF), s((NQ, Q, NS)...  4.7 us
    ppermute x6, starting transfers between devices, around(): return lax.ppermute(v, 'tp', AROUND)  4.53 us
    pallas_call x1, Pallas kernels, project_near(): pl.pallas_call(near_kernel, out_shape=(pltpu.VMEM((Q, CH), BF), pltpu.VME...  4.5 us
    all_to_all x1, starting transfers between devices, per_device(): back = lax.all_to_all(prefix(got), 'ctx', 0, 0, tiled=True)  4.46 us
  transfers between devices with their start and end apart: 19, of which 11 were waited for; matrix products, arithmetic and copies ran while one was open for 0% of the time, Pallas kernels for 12%

profile of v8, /device:TPU:32, one launch (start us, length us, event | category | flops | bytes accessed | tf_op | source)
XLA Modules:
  0.0 102.2 jit_solution(7285333313195050142)
XLA Ops:
  0.0 2.1 %collective-permute-done.theirs = bf16[64,4096]{1,0:T(8,128)(2,1)S(1)} collective-permute-done((bf16[64,4096]{1,0:T(8,128)(2,1)}, bf16[64,4096]{1,0:T(8,128)(2,1)S(1)}, u32[]{:S(2)}, u32[]{:S(2)}) %collective-permute-start) | collective-permute-done | bytes 524320 | tf_op jit(solution)/shard_map/ppermute | solution.py:428
  2.1 1.1 %pack.1 = (bf16[64,4096]{1,0:T(8,128)(2,1)S(1)}, bf16[64,4096]{1,0:T(8,128)(2,1)S(1)}, bf16[8,4096]{1,0:T(8,128)(2,1)S(1)}) custom-call(bf16[64,4096]{1,0:T(8,128)(2,1)} %far.1, bf16[64,4096]{1,0:T(8,128)(2,1)S(1)} %collective-permute-done.theirs), custom_call_target="tpu_custom_call" | custom-call | tf_op jit(solution)/shard_map/pack/pallas_call | solution.py:87
  3.2 1.7 %collective-permute-start.1 = (bf16[64,4096]{1,0:T(8,128)(2,1)S(1)}, bf16[64,4096]{1,0:T(8,128)(2,1)S(1)}, u32[]{:S(2)}, u32[]{:S(2)}) collective-permute-start(bf16[64,4096]{1,0:T(8,128)(2,1)S(1)} %get-tuple-element.47), channel_id=1, source_target_pairs={{0,2},{1,7},{2,4},{3,1},{4,6},{5,3},{6,0},{7,5},{8,10},{9,15},{10,... | collective-permute-start | bytes 1572872 | tf_op jit(solution)/shard_map/ppermute | solution.py:424
  6.2 1.7 %collective-permute-start.5 = (bf16[64,4096]{1,0:T(8,128)(2,1)S(1)}, bf16[64,4096]{1,0:T(8,128)(2,1)S(1)}, u32[]{:S(2)}, u32[]{:S(2)}) collective-permute-start(bf16[64,4096]{1,0:T(8,128)(2,1)S(1)} %get-tuple-element.51), channel_id=1, source_target_pairs={{0,2},{1,7},{2,4},{3,1},{4,6},{5,3},{6,0},{7,5},{8,10},{9,15},{10,... | collective-permute-start | bytes 1572872 | tf_op jit(solution)/shard_map/ppermute | solution.py:424
  7.9 4.5 %project_near.1 = (bf16[128,512]{1,0:T(8,128)(2,1)S(1)}, bf16[128,256]{1,0:T(8,128)(2,1)S(1)}, f32[1,8,128]{2,1,0:T(8,128)S(1)}, bf16[4096,512]{1,0:T(8,128)(2,1...) custom-call(bf16[64,4096]{1,0:T(8,128)(2,1)} %far.1, ...), custom_call_target="tpu_custom_call" | custom-call | tf_op jit(solution)/shard_map/project_near/pallas_call | solution.py:153
  12.4 1.3 %collective-permute-done.1.r1 = bf16[64,4096]{1,0:T(8,128)(2,1)S(1)} collective-permute-done((bf16[64,4096]{1,0:T(8,128)(2,1)S(1)}, bf16[64,4096]{1,0:T(8,128)(2,1)S(1)}, u32[]{:S(2)}, u32[]{:S(2)}) %collective-permute-start.1) | collective-permute-done | bytes 524320 | tf_op jit(solution)/shard_map/ppermute | solution.py:424
  14.1 4.4 %collective-permute-start.6 = (bf16[64,4096]{1,0:T(8,128)(2,1)S(1)}, bf16[64,4096]{1,0:T(8,128)(2,1)S(1)}, u32[]{:S(2)}, u32[]{:S(2)}) collective-permute-start(bf16[64,4096]{1,0:T(8,128)(2,1)S(1)} %collective-permute-done.1.r1), channel_id=1, source_target_pairs={{0,1},{1,0},{2,3},{3,2},{4,5},{5,4},{6,7},{7,6},{8,9},{9,8},{10,11... | collective-permute-start | bytes 1572872 | tf_op jit(solution)/shard_map/ppermute | solution.py:428
  18.4 2.0 %collective-permute-done.5.r2 = bf16[64,4096]{1,0:T(8,128)(2,1)S(1)} collective-permute-done((bf16[64,4096]{1,0:T(8,128)(2,1)S(1)}, bf16[64,4096]{1,0:T(8,128)(2,1)S(1)}, u32[]{:S(2)}, u32[]{:S(2)}) %collective-permute-start.5) | collective-permute-done | bytes 524320 | tf_op jit(solution)/shard_map/ppermute | solution.py:424
  20.5 5.6 %collective-permute-done.4.refs_6_ = bf16[64,4096]{1,0:T(8,128)(2,1)S(1)} collective-permute-done((bf16[64,4096]{1,0:T(8,128)(2,1)S(1)}, bf16[64,4096]{1,0:T(8,128)(2,1)S(1)}, u32[]{:S(2)}, u32[]{:S(2)}) %collective-permute-start.4) | collective-permute-done | bytes 524320 | tf_op jit(solution)/shard_map/ppermute | solution.py:424
  26.9 1.1 %collective-permute-done.7.s2 = bf16[64,4096]{1,0:T(8,128)(2,1)S(1)} collective-permute-done((bf16[64,4096]{1,0:T(8,128)(2,1)S(1)}, bf16[64,4096]{1,0:T(8,128)(2,1)S(1)}, u32[]{:S(2)}, u32[]{:S(2)}) %collective-permute-start.7) | collective-permute-done | bytes 524320 | tf_op jit(solution)/shard_map/ppermute | solution.py:428
  28.0 2.5 %project_next.1 = (bf16[256,512]{1,0:T(8,128)(2,1)S(1)}, bf16[256,256]{1,0:T(8,128)(2,1)S(1)}, f32[2,8,128]{2,1,0:T(8,128)S(1)}) custom-call(bf16[64,4096]{1,0:T(8,128)(2,1)S(1)} %collective-permute-done.1.r1, bf16[64,4096]{1,0:T(8,128)(2,1)S(1)} %collective-permute-done.5.r2, bf16[64,4096]{1,0:T(8,128)(2,1)S(1)} %collective-permute-done.6.s1, ...), custom_call_target="tpu_custom_call" | custom-call | tf_op jit(solution)/shard_map/project_next/pallas_call | solution.py:113
  30.6 4.7 %local_part.1 = (bf16[4,128,512]{2,1,0:T(8,128)(2,1)S(1)}, bf16[4,128,128]{2,1,0:T(8,128)(2,1)S(1)}, bf16[4,128,128]{2,1,0:T(8,128)(2,1)S(1)}, f32[4,8,128]{2,1,...) custom-call(f32[8]{0:T(128)S(1)} %copy-done.6, ...), custom_call_target="tpu_custom_call" | custom-call | tf_op jit(solution)/shard_map/local_part/pallas_call | solution.py:269
  35.3 21.8 %all_to_all.10.r = bf16[32,24,128]{2,1,0:T(8,128)(2,1)S(1)} all-to-all(bf16[32,24,128]{2,1,0:T(8,128)(2,1)S(1)} %get-tuple-element.60), channel_id=1, replica_groups=mesh['ctx'=32,'tp'=8] {'ctx'}, dimensions={0} | all-to-all | bytes 393216 | tf_op jit(solution)/shard_map/all_to_all | solution.py:455
  57.8 4.5 %all-to-all-start.1 = ((bf16[32,16,128]{2,1,0:T(8,128)(2,1)}), bf16[32,16,128]{2,1,0:T(8,128)(2,1)S(1)}, u32[]{:S(2)}, u32[]{:S(2)}) async-start(bf16[32,16,128]{2,1,0:T(8,128)(2,1)} %prefix.1), calls=%async_computation.1 | async-start | bytes 262144 | tf_op jit(solution)/shard_map/all_to_all | solution.py:457
  62.3 3.9 %diag_part.1 = (f32[4,128,512]{2,1,0:T(8,128)S(1)}, bf16[512,4096]{1,0:T(8,128)(2,1)S(1)}) custom-call(f32[8]{0:T(128)S(1)} %copy-done.8, bf16[512,4096]{1,0:T(8,128)(2,1)} %w_far.1, bf16[4,128,512]{2,1,0:T(8,128)(2,1)S(1)} %get-tuple-element.65.x, bf16[4,128,128]{2,1,0:T(8,128)(2,1)S(1)} %get-tuple-element.66.b, ...), custom_call_target="tpu_custom_call" | custom-call | tf_op jit(solution)/shard_map/diag_part/pallas_call | solution.py:340
  66.2 2.0 %copy-done = bf16[512,4096]{1,0:T(8,128)(2,1)} copy-done((bf16[512,4096]{1,0:T(8,128)(2,1)}, bf16[512,4096]{1,0:T(8,128)(2,1)S(1)}, u32[]{:S(2)}) %copy-start) | copy-done | bytes 4194328
  68.2 3.9 %all-to-all-done.1 = bf16[32,16,128]{2,1,0:T(8,128)(2,1)S(1)} async-done(((bf16[32,16,128]{2,1,0:T(8,128)(2,1)}), bf16[32,16,128]{2,1,0:T(8,128)(2,1)S(1)}, u32[]{:S(2)}, u32[]{:S(2)}) %all-to-all-start.1) | async-done | bytes 131104 | tf_op jit(solution)/shard_map/all_to_all | solution.py:457
  72.1 2.2 %copy-done.1 = bf16[512,4096]{1,0:T(8,128)(2,1)S(1)} copy-done((bf16[512,4096]{1,0:T(8,128)(2,1)S(1)}, bf16[512,4096]{1,0:T(8,128)(2,1)}, u32[]{:S(2)}) %copy-start.1) | copy-done | bytes 4194328
  74.2 2.0 %norm_part.1 = (bf16[64,4096]{1,0:T(8,128)(2,1)S(1)}, bf16[64,4096]{1,0:T(8,128)(2,1)S(1)}, bf16[384,512]{1,0:T(8,128)(2,1)S(1)}) custom-call(bf16[512,128]{1,0:T(8,128)(2,1)S(1)} %bitcast.3, f32[4,128,512]{2,1,0:T(8,128)S(1)} %get-tuple-element.61.e, f32[4,8,512]{2,1,0:T(8,128)S(1)} %get-tuple-element.62.d, bf16[4,128,128]{2,1,0:T(8,128)(2,1)S(1)} %get-tuple-element.63.c, ...), custom_call_target="tpu_custom_call" | custom-call | tf_op jit(solution)/shard_map/norm_part/pallas_call | solution.py:388
  76.4 1.8 %out_part.1 = (bf16[64,4096]{1,0:T(8,128)(2,1)S(1)}, bf16[64,4096]{1,0:T(8,128)(2,1)S(1)}, bf16[64,4096]{1,0:T(8,128)(2,1)S(1)}, bf16[64,4096]{1,0:T(8,128)(2,1)...) custom-call(bf16[384,512]{1,0:T(8,128)(2,1)S(1)} %get-tuple-element.70.n, bf16[512,4096]{1,0:T(8,128)(2,1)S(1)} %copy-done.2), custom_call_target="tpu_custom_call" | custom-call | tf_op jit(solution)/shard_map/out_part/pallas_call | solution.py:407
  82.0 7.9 %collective-permute-done.16 = bf16[64,4096]{1,0:T(8,128)(2,1)S(1)} collective-permute-done((bf16[64,4096]{1,0:T(8,128)(2,1)S(1)}, bf16[64,4096]{1,0:T(8,128)(2,1)S(1)}, u32[]{:S(2)}, u32[]{:S(2)}) %collective-permute-start.16) | collective-permute-done | bytes 524320 | tf_op jit(solution)/shard_map/ppermute | solution.py:424
  90.1 5.3 %collective-permute-done.13 = bf16[64,4096]{1,0:T(8,128)(2,1)S(1)} collective-permute-done((bf16[64,4096]{1,0:T(8,128)(2,1)S(1)}, bf16[64,4096]{1,0:T(8,128)(2,1)S(1)}, u32[]{:S(2)}, u32[]{:S(2)}) %collective-permute-start.13) | collective-permute-done | bytes 524320 | tf_op jit(solution)/shard_map/ppermute | solution.py:424
  95.5 5.6 %collective-permute-done.17 = bf16[64,4096]{1,0:T(8,128)(2,1)S(1)} collective-permute-done((bf16[64,4096]{1,0:T(8,128)(2,1)S(1)}, bf16[64,4096]{1,0:T(8,128)(2,1)S(1)}, u32[]{:S(2)}, u32[]{:S(2)}) %collective-permute-start.17) | collective-permute-done | bytes 524320 | tf_op jit(solution)/shard_map/ppermute | solution.py:424
  101.1 1.1 %add_convert_fusion = bf16[64,4096]{1,0:T(8,128)(2,1)} fusion(bf16[64,4096]{1,0:T(8,128)(2,1)S(1)} %collective-permute-done.17, bf16[64,4096]{1,0:T(8,128)(2,1)S(1)} %collective-permute-done.14, bf16[64,4096]{1,0:T(8,128)(2,1)S(1)} %collective-permute-done.11, bf16[64,4096]{1,0:T(8,128)(2,1)S(1)} %get-tuple-element.71), kind=kLoop, calls=%fused_computation | loop fusion | flops 2097152 | bytes 2621440 | tf_op jit(solution)/shard_map/convert_element_type | solution.py:469
  (46 shorter events, 7.4 us)
Async XLA Ops:
  0.0 2.1 %collective-permute-start = (bf16[64,4096]{1,0:T(8,128)(2,1)}, bf16[64,4096]{1,0:T(8,128)(2,1)S(1)}, u32[]{:S(2)}, u32[]{:S(2)}) collective-permute-start(bf16[64,4096]{1,0:T(8,128)(2,1)} %far.1), channel_id=1, source_target_pairs={{0,1},{1,0},{2,3},{3,2},{4,5},{5,4},{6,7},{7,6},{8,9},{9,8},{10,11... | collective-permute-start | bytes 1572872 | tf_op jit(solution)/shard_map/ppermute | solution.py:428
  3.2 10.5 %collective-permute-start.1 = (bf16[64,4096]{1,0:T(8,128)(2,1)S(1)}, bf16[64,4096]{1,0:T(8,128)(2,1)S(1)}, u32[]{:S(2)}, u32[]{:S(2)}) collective-permute-start(bf16[64,4096]{1,0:T(8,128)(2,1)S(1)} %get-tuple-element.47), channel_id=1, source_target_pairs={{0,2},{1,7},{2,4},{3,1},{4,6},{5,3},{6,0},{7,5},{8,10},{9,15},{10,... | collective-permute-start | bytes 1572872 | tf_op jit(solution)/shard_map/ppermute | solution.py:424
  4.9 7.5 %collective-permute-start.3 = (bf16[8,4096]{1,0:T(8,128)(2,1)S(1)}, bf16[8,4096]{1,0:T(8,128)(2,1)S(1)}, u32[]{:S(2)}, u32[]{:S(2)}) collective-permute-start(bf16[8,4096]{1,0:T(8,128)(2,1)S(1)} %get-tuple-element.49), channel_id=1, source_target_pairs={{7,13},{6,11},{15,21},{14,19},{23,29},{22,27},{31,37},{30,35},{39,... | collective-permute-start | bytes 196616 | tf_op jit(solution)/shard_map/ppermute | solution.py:439
  5.5 6.8 %collective-permute-start.2 = (bf16[8,4096]{1,0:T(8,128)(2,1)S(1)}, bf16[8,4096]{1,0:T(8,128)(2,1)S(1)}, u32[]{:S(2)}, u32[]{:S(2)}) collective-permute-start(bf16[8,4096]{1,0:T(8,128)(2,1)S(1)} %get-tuple-element.49), channel_id=1, source_target_pairs={{7,15},{6,9},{15,23},{14,17},{23,31},{22,25},{31,39},{30,33},{39,4... | collective-permute-start | bytes 196616 | tf_op jit(solution)/shard_map/ppermute | solution.py:439
  6.2 14.3 %collective-permute-start.5 = (bf16[64,4096]{1,0:T(8,128)(2,1)S(1)}, bf16[64,4096]{1,0:T(8,128)(2,1)S(1)}, u32[]{:S(2)}, u32[]{:S(2)}) collective-permute-start(bf16[64,4096]{1,0:T(8,128)(2,1)S(1)} %get-tuple-element.51), channel_id=1, source_target_pairs={{0,2},{1,7},{2,4},{3,1},{4,6},{5,3},{6,0},{7,5},{8,10},{9,15},{10,... | collective-permute-start | bytes 1572872 | tf_op jit(solution)/shard_map/ppermute | solution.py:424
  13.7 12.4 %collective-permute-start.4 = (bf16[64,4096]{1,0:T(8,128)(2,1)S(1)}, bf16[64,4096]{1,0:T(8,128)(2,1)S(1)}, u32[]{:S(2)}, u32[]{:S(2)}) collective-permute-start(bf16[64,4096]{1,0:T(8,128)(2,1)S(1)} %collective-permute-done.1.r1), channel_id=1, source_target_pairs={{0,2},{1,7},{2,4},{3,1},{4,6},{5,3},{6,0},{7,5},{8,10},{9,15},{10,... | collective-permute-start | bytes 1572872 | tf_op jit(solution)/shard_map/ppermute | solution.py:424
  14.1 12.8 %collective-permute-start.6 = (bf16[64,4096]{1,0:T(8,128)(2,1)S(1)}, bf16[64,4096]{1,0:T(8,128)(2,1)S(1)}, u32[]{:S(2)}, u32[]{:S(2)}) collective-permute-start(bf16[64,4096]{1,0:T(8,128)(2,1)S(1)} %collective-permute-done.1.r1), channel_id=1, source_target_pairs={{0,1},{1,0},{2,3},{3,2},{4,5},{5,4},{6,7},{7,6},{8,9},{9,8},{10,11... | collective-permute-start | bytes 1572872 | tf_op jit(solution)/shard_map/ppermute | solution.py:428
  26.1 1.9 %collective-permute-start.7 = (bf16[64,4096]{1,0:T(8,128)(2,1)S(1)}, bf16[64,4096]{1,0:T(8,128)(2,1)S(1)}, u32[]{:S(2)}, u32[]{:S(2)}) collective-permute-start(bf16[64,4096]{1,0:T(8,128)(2,1)S(1)} %collective-permute-done.5.r2), channel_id=1, source_target_pairs={{0,1},{1,0},{2,3},{3,2},{4,5},{5,4},{6,7},{7,6},{8,9},{9,8},{10,11... | collective-permute-start | bytes 1572872 | tf_op jit(solution)/shard_map/ppermute | solution.py:428
  26.4 4.1 %collective-permute-start.8 = (bf16[64,4096]{1,0:T(8,128)(2,1)S(1)}, bf16[64,4096]{1,0:T(8,128)(2,1)S(1)}, u32[]{:S(2)}, u32[]{:S(2)}) collective-permute-start(bf16[64,4096]{1,0:T(8,128)(2,1)S(1)} %collective-permute-done.4.refs_6_), channel_id=1, source_target_pairs={{0,1},{1,0},{2,3},{3,2},{4,5},{5,4},{6,7},{7,6},{8,9},{9,8},{10,11... | collective-permute-start | bytes 1572872 | tf_op jit(solution)/shard_map/ppermute | solution.py:428
  26.6 3.9 %collective-permute-start.9 = (bf16[8,4096]{1,0:T(8,128)(2,1)S(1)}, bf16[8,4096]{1,0:T(8,128)(2,1)S(1)}, u32[]{:S(2)}, u32[]{:S(2)}) collective-permute-start(bf16[8,4096]{1,0:T(8,128)(2,1)S(1)} %add.24.refs_8_), channel_id=1, source_target_pairs={{0,1},{1,0},{2,3},{3,2},{4,5},{5,4},{6,7},{7,6},{8,9},{9,8},{10,11... | collective-permute-start | bytes 196616 | tf_op jit(solution)/shard_map/ppermute | solution.py:428
  28.0 2.5 %copy-start.4 = (f32[4,256]{1,0:T(4,128)S(1)}, f32[4,256]{1,0:T(4,128)}, u32[]{:S(2)}) copy-start(f32[4,256]{1,0:T(4,128)} %refs_14_.1) | copy-start | bytes 12292
  28.0 2.5 %copy-start.6 = (f32[8]{0:T(128)S(1)}, f32[8]{0:T(128)}, u32[]{:S(2)}) copy-start(f32[8]{0:T(128)} %bias.1) | copy-start | bytes 100
  28.0 2.5 %copy-start.7 = (f32[8]{0:T(128)S(1)}, f32[8]{0:T(128)}, u32[]{:S(2)}) copy-start(f32[8]{0:T(128)} %alog.1) | copy-start | bytes 100
  30.6 31.7 %copy-start.8 = (f32[8]{0:T(128)S(1)}, f32[8]{0:T(128)}, u32[]{:S(2)}) copy-start(f32[8]{0:T(128)} %skip.1) | copy-start | bytes 100
  35.3 36.8 %copy-start.5 = (f32[512]{0:T(512)S(1)}, f32[512]{0:T(512)}, u32[]{:S(2)}) copy-start(f32[512]{0:T(512)} %param.20) | copy-start | bytes 6148
  57.8 14.2 %all-to-all-start.1 = ((bf16[32,16,128]{2,1,0:T(8,128)(2,1)}), bf16[32,16,128]{2,1,0:T(8,128)(2,1)S(1)}, u32[]{:S(2)}, u32[]{:S(2)}) async-start(bf16[32,16,128]{2,1,0:T(8,128)(2,1)} %prefix.1), calls=%async_computation.1 | async-start | bytes 262144 | tf_op jit(solution)/shard_map/all_to_all | solution.py:457
  76.3 2.0 %collective-permute-start.10 = (bf16[64,4096]{1,0:T(8,128)(2,1)S(1)}, bf16[64,4096]{1,0:T(8,128)(2,1)S(1)}, u32[]{:S(2)}, u32[]{:S(2)}) collective-permute-start(bf16[64,4096]{1,0:T(8,128)(2,1)S(1)} %get-tuple-element.73), channel_id=1, source_target_pairs={{0,1},{1,0},{2,3},{3,2},{4,5},{5,4},{6,7},{7,6},{8,9},{9,8},{10,11... | collective-permute-start | bytes 1572872 | tf_op jit(solution)/shard_map/ppermute | solution.py:428
  78.4 2.1 %collective-permute-start.12 = (bf16[64,4096]{1,0:T(8,128)(2,1)S(1)}, bf16[64,4096]{1,0:T(8,128)(2,1)S(1)}, u32[]{:S(2)}, u32[]{:S(2)}) collective-permute-start(bf16[64,4096]{1,0:T(8,128)(2,1)S(1)} %get-tuple-element.79), channel_id=1, source_target_pairs={{0,1},{1,0},{2,3},{3,2},{4,5},{5,4},{6,7},{7,6},{8,9},{9,8},{10,11... | collective-permute-start | bytes 1572872 | tf_op jit(solution)/shard_map/ppermute | solution.py:428
  79.0 16.5 %collective-permute-start.11 = (bf16[64,4096]{1,0:T(8,128)(2,1)S(1)}, bf16[64,4096]{1,0:T(8,128)(2,1)S(1)}, u32[]{:S(2)}, u32[]{:S(2)}) collective-permute-start(bf16[64,4096]{1,0:T(8,128)(2,1)S(1)} %get-tuple-element.77), channel_id=1, source_target_pairs={{0,1},{1,0},{2,3},{3,2},{4,5},{5,4},{6,7},{7,6},{8,9},{9,8},{10,11... | collective-permute-start | bytes 1572872 | tf_op jit(solution)/shard_map/ppermute | solution.py:428
  79.1 2.9 %collective-permute-start.15 = (bf16[64,4096]{1,0:T(8,128)(2,1)S(1)}, bf16[64,4096]{1,0:T(8,128)(2,1)S(1)}, u32[]{:S(2)}, u32[]{:S(2)}) collective-permute-start(bf16[64,4096]{1,0:T(8,128)(2,1)S(1)} %get-tuple-element.81), channel_id=1, source_target_pairs={{0,1},{1,0},{2,3},{3,2},{4,5},{5,4},{6,7},{7,6},{8,9},{9,8},{10,11... | collective-permute-start | bytes 1572872 | tf_op jit(solution)/shard_map/ppermute | solution.py:428
  79.5 10.4 %collective-permute-start.16 = (bf16[64,4096]{1,0:T(8,128)(2,1)S(1)}, bf16[64,4096]{1,0:T(8,128)(2,1)S(1)}, u32[]{:S(2)}, u32[]{:S(2)}) collective-permute-start(bf16[64,4096]{1,0:T(8,128)(2,1)S(1)} %add_convert_fusion.3), channel_id=1, source_target_pairs={{0,2},{1,7},{2,4},{3,1},{4,6},{5,3},{6,0},{7,5},{8,10},{9,15},{10,... | collective-permute-start | bytes 1572872 | tf_op jit(solution)/shard_map/ppermute | solution.py:424
  80.6 14.9 %collective-permute-start.13 = (bf16[64,4096]{1,0:T(8,128)(2,1)S(1)}, bf16[64,4096]{1,0:T(8,128)(2,1)S(1)}, u32[]{:S(2)}, u32[]{:S(2)}) collective-permute-start(bf16[64,4096]{1,0:T(8,128)(2,1)S(1)} %add_convert_fusion.2), channel_id=1, source_target_pairs={{0,2},{1,7},{2,4},{3,1},{4,6},{5,3},{6,0},{7,5},{8,10},{9,15},{10,... | collective-permute-start | bytes 1572872 | tf_op jit(solution)/shard_map/ppermute | solution.py:424
  90.1 11.0 %collective-permute-start.17 = (bf16[64,4096]{1,0:T(8,128)(2,1)S(1)}, bf16[64,4096]{1,0:T(8,128)(2,1)S(1)}, u32[]{:S(2)}, u32[]{:S(2)}) collective-permute-start(bf16[64,4096]{1,0:T(8,128)(2,1)S(1)} %add_convert_fusion.1), channel_id=1, source_target_pairs={{0,2},{1,7},{2,4},{3,1},{4,6},{5,3},{6,0},{7,5},{8,10},{9,15},{10,... | collective-permute-start | bytes 1572872 | tf_op jit(solution)/shard_map/ppermute | solution.py:424
  95.5 5.6 %collective-permute-start.14 = (bf16[64,4096]{1,0:T(8,128)(2,1)S(1)}, bf16[64,4096]{1,0:T(8,128)(2,1)S(1)}, u32[]{:S(2)}, u32[]{:S(2)}) collective-permute-start(bf16[64,4096]{1,0:T(8,128)(2,1)S(1)} %collective-permute-done.13), channel_id=1, source_target_pairs={{0,1},{1,0},{2,3},{3,2},{4,5},{5,4},{6,7},{7,6},{8,9},{9,8},{10,11... | collective-permute-start | bytes 1572872 | tf_op jit(solution)/shard_map/ppermute | solution.py:428
  (4 other events, 8.8 us)

commit v9 on v7

--- a/solution.py
+++ b/solution.py
@@ -69,9 +69,13 @@
     tok[pl.ds(pl.multiple_of(at + 64, 32), 32), :] = ref[32:64, :]
 
 
-def pack_kernel(mine, theirs, first, second, last):
+def pack_kernel(far, theirs, first, second, last, mine, sem):
     c = core()
-    for part, ref in ((c, mine), (1 - c, theirs)):
+    copy = pltpu.make_async_copy(far, mine, sem)
+    copy.start()
+    for part, ref in ((1 - c, theirs), (c, mine)):
+        if ref is mine:
+            copy.wait()
         at = pl.ds(pl.multiple_of(part * 32, 32), 32)
         first[at, :] = ref[pl.ds(pl.multiple_of(c * 32, 32), 32), :]
         second[at, :] = ref[pl.ds(pl.multiple_of((1 - c) * 32, 32), 32), :]
@@ -83,11 +87,12 @@
     return pl.pallas_call(
         pack_kernel,
         out_shape=(pltpu.VMEM((64, 4096), BF), pltpu.VMEM((64, 4096), BF), pltpu.VMEM((8, 4096), BF)),
-        in_specs=[VMEM] * 2,
+        in_specs=[pl.BlockSpec(memory_space=pltpu.HBM), VMEM],
         out_specs=(VMEM,) * 3,
+        scratch_shapes=[pltpu.VMEM((64, 4096), BF), pltpu.SemaphoreType.DMA],
         compiler_params=params(),
         name="pack",
-    )(in_vmem(mine), in_vmem(theirs))
+    )(pltpu.with_memory_space_constraint(mine, pltpu.HBM), in_vmem(theirs))
 
 
 def next_kernel(r1, r2, s1, s2, wx, wbc, wdt, xo, bco, dto, tok):
@@ -426,6 +431,10 @@
     partner = swap(tokens)
     first, second, last = pack(tokens, partner)
     r1, r2 = around(first), around(second)
+    *piece0, wx, wbc, wdt = project_near(tokens, partner, in_x, in_bc, in_dt.T)
+    weights = (wx, wbc, wdt)
+    r1, wx, last = after((r1, wx, last))
+    far = around(r1)
     spans = lax.axis_size("ctx")
 
     def onward(*route):
@@ -433,15 +442,12 @@
             last, ("ctx", "tp"), [(i * 8 + f, i * 8 + 8 + t) for i in range(spans - 1) for f, t in route]
         )
 
-    edge = onward((7, 7), (6, 1)) + onward((7, 5), (6, 3))
-    *piece0, wx, wbc, wdt = project_near(tokens, partner, in_x, in_bc, in_dt.T)
-    weights = (wx, wbc, wdt)
-    r1, wx = after((r1, wx))
-    far = around(r1)
-    r2, edge = after((r2, edge))
+    edge_a, edge_b = onward((7, 7), (6, 1)), onward((7, 5), (6, 3))
+    far, r2 = after((far, r2))
+    piece12 = project_next(r1, r2, swap(r1), swap(r2), *weights)
+    edge_a, edge_b, far = after((edge_a, edge_b, far))
+    edge = edge_a + edge_b
     edges = swap(edge)
-    piece12 = project_next(r1, r2, swap(r1), swap(r2), *weights)
-    far, *piece12 = after((far, *piece12))
 
     xc, b, c, cs, dt, e, d, send = local_part(
         dt_bias, a_log, *piece0, *piece12, far, swap(far), edge, edges, *weights, conv_x, conv_bc

time: 104 us -> 101 us (0.971)
  waiting for transfers between devices: 45.4 us -> 43 us
  local copies, waits for them, and re-layouts: 1.07 us -> 0.03 us
    ppermute x10, waiting for transfers between devices: 7.92 us -> 5.34 us  [swap(): return lax.ppermute(v, 'tp', SWAP)]
    unnamed x14 -> x12, local copies, waits for them, and re-layouts: 1.07 us -> 0.03 us
  transfers between devices with their start and end apart: 19 -> 19, of which waited for: 13 -> 12; matrix products, arithmetic and copies ran while one was open for 0% -> 0% of each run, Pallas kernels for 10% -> 10%
where the time goes in v9:
time: 101 us
  waiting for transfers between devices  43 us (43%)
  blocking collectives  22.3 us (22%)
  Pallas kernels  20 us (20%)
  starting transfers between devices  14 us (14%)
  other arithmetic  1.52 us (2%)
    ppermute x6, waiting for transfers between devices, around(): return lax.ppermute(v, 'tp', AROUND)  29.7 us
    all_to_all x1, blocking collectives, per_device(): got = lax.all_to_all(send, 'ctx', 0, 0, tiled=True)  22.3 us
    all_to_all x1, waiting for transfers between devices, per_device(): back = lax.all_to_all(prefix(got), 'ctx', 0, 0, tiled=True)  7.92 us
    ppermute x10, waiting for transfers between devices, swap(): return lax.ppermute(v, 'tp', SWAP)  5.34 us
    pallas_call x1, Pallas kernels, local_part(): pl.pallas_call(local_kernel, out_shape=(s((NQ, Q, CH), BF), s((NQ, Q, NS)...  4.65 us
    all_to_all x1, starting transfers between devices, per_device(): back = lax.all_to_all(prefix(got), 'ctx', 0, 0, tiled=True)  4.64 us
    pallas_call x1, Pallas kernels, project_near(): pl.pallas_call(near_kernel, out_shape=(pltpu.VMEM((Q, CH), BF), pltpu.VME...  4.5 us
    ppermute x6, starting transfers between devices, around(): return lax.ppermute(v, 'tp', AROUND)  4.15 us
  transfers between devices with their start and end apart: 19, of which 12 were waited for; matrix products, arithmetic and copies ran while one was open for 0% of the time, Pallas kernels for 10%

profile of v9, /device:TPU:32, one launch (start us, length us, event | category | flops | bytes accessed | tf_op | source)
XLA Modules:
  0.0 101.0 jit_solution(886560103348312905)
XLA Ops:
  0.0 2.1 %collective-permute-done.theirs = bf16[64,4096]{1,0:T(8,128)(2,1)S(1)} collective-permute-done((bf16[64,4096]{1,0:T(8,128)(2,1)}, bf16[64,4096]{1,0:T(8,128)(2,1)S(1)}, u32[]{:S(2)}, u32[]{:S(2)}) %collective-permute-start) | collective-permute-done | bytes 524320 | tf_op jit(solution)/shard_map/ppermute | solution.py:426
  2.1 1.1 %pack.1 = (bf16[64,4096]{1,0:T(8,128)(2,1)S(1)}, bf16[64,4096]{1,0:T(8,128)(2,1)S(1)}, bf16[8,4096]{1,0:T(8,128)(2,1)S(1)}) custom-call(bf16[64,4096]{1,0:T(8,128)(2,1)} %far.1, bf16[64,4096]{1,0:T(8,128)(2,1)S(1)} %collective-permute-done.theirs), custom_call_target="tpu_custom_call" | custom-call | tf_op jit(solution)/shard_map/pack/pallas_call | solution.py:87
  3.2 1.7 %collective-permute-start.1 = (bf16[64,4096]{1,0:T(8,128)(2,1)S(1)}, bf16[64,4096]{1,0:T(8,128)(2,1)S(1)}, u32[]{:S(2)}, u32[]{:S(2)}) collective-permute-start(bf16[64,4096]{1,0:T(8,128)(2,1)S(1)} %get-tuple-element.49), channel_id=1, source_target_pairs={{0,2},{1,7},{2,4},{3,1},{4,6},{5,3},{6,0},{7,5},{8,10},{9,15},{10,... | collective-permute-start | bytes 1572872 | tf_op jit(solution)/shard_map/ppermute | solution.py:422
  4.9 1.6 %collective-permute-start.3 = (bf16[64,4096]{1,0:T(8,128)(2,1)S(1)}, bf16[64,4096]{1,0:T(8,128)(2,1)S(1)}, u32[]{:S(2)}, u32[]{:S(2)}) collective-permute-start(bf16[64,4096]{1,0:T(8,128)(2,1)S(1)} %get-tuple-element.53), channel_id=1, source_target_pairs={{0,2},{1,7},{2,4},{3,1},{4,6},{5,3},{6,0},{7,5},{8,10},{9,15},{10,... | collective-permute-start | bytes 1572872 | tf_op jit(solution)/shard_map/ppermute | solution.py:422
  6.5 4.5 %project_near.1 = (bf16[128,512]{1,0:T(8,128)(2,1)S(1)}, bf16[128,256]{1,0:T(8,128)(2,1)S(1)}, f32[1,8,128]{2,1,0:T(8,128)S(1)}, bf16[4096,512]{1,0:T(8,128)(2,1...) custom-call(bf16[64,4096]{1,0:T(8,128)(2,1)} %far.1, ...), custom_call_target="tpu_custom_call" | custom-call | tf_op jit(solution)/shard_map/project_near/pallas_call | solution.py:153
  11.0 2.7 %collective-permute-done.1.r1 = bf16[64,4096]{1,0:T(8,128)(2,1)S(1)} collective-permute-done((bf16[64,4096]{1,0:T(8,128)(2,1)S(1)}, bf16[64,4096]{1,0:T(8,128)(2,1)S(1)}, u32[]{:S(2)}, u32[]{:S(2)}) %collective-permute-start.1) | collective-permute-done | bytes 524320 | tf_op jit(solution)/shard_map/ppermute | solution.py:422
  15.4 2.1 %collective-permute-start.4 = (bf16[64,4096]{1,0:T(8,128)(2,1)S(1)}, bf16[64,4096]{1,0:T(8,128)(2,1)S(1)}, u32[]{:S(2)}, u32[]{:S(2)}) collective-permute-start(bf16[64,4096]{1,0:T(8,128)(2,1)S(1)} %collective-permute-done.1.r1), channel_id=1, source_target_pairs={{0,1},{1,0},{2,3},{3,2},{4,5},{5,4},{6,7},{7,6},{8,9},{9,8},{10,11... | collective-permute-start | bytes 1572872 | tf_op jit(solution)/shard_map/ppermute | solution.py:426
  17.5 1.8 %collective-permute-done.3.r2 = bf16[64,4096]{1,0:T(8,128)(2,1)S(1)} collective-permute-done((bf16[64,4096]{1,0:T(8,128)(2,1)S(1)}, bf16[64,4096]{1,0:T(8,128)(2,1)S(1)}, u32[]{:S(2)}, u32[]{:S(2)}) %collective-permute-start.3) | collective-permute-done | bytes 524320 | tf_op jit(solution)/shard_map/ppermute | solution.py:422
  19.3 6.3 %collective-permute-done.2.refs_6_ = bf16[64,4096]{1,0:T(8,128)(2,1)S(1)} collective-permute-done((bf16[64,4096]{1,0:T(8,128)(2,1)S(1)}, bf16[64,4096]{1,0:T(8,128)(2,1)S(1)}, u32[]{:S(2)}, u32[]{:S(2)}) %collective-permute-start.2) | collective-permute-done | bytes 524320 | tf_op jit(solution)/shard_map/ppermute | solution.py:422
  26.4 1.2 %collective-permute-done.5.s2 = bf16[64,4096]{1,0:T(8,128)(2,1)S(1)} collective-permute-done((bf16[64,4096]{1,0:T(8,128)(2,1)S(1)}, bf16[64,4096]{1,0:T(8,128)(2,1)S(1)}, u32[]{:S(2)}, u32[]{:S(2)}) %collective-permute-start.5) | collective-permute-done | bytes 524320 | tf_op jit(solution)/shard_map/ppermute | solution.py:426
  27.6 2.5 %project_next.1 = (bf16[256,512]{1,0:T(8,128)(2,1)S(1)}, bf16[256,256]{1,0:T(8,128)(2,1)S(1)}, f32[2,8,128]{2,1,0:T(8,128)S(1)}) custom-call(bf16[64,4096]{1,0:T(8,128)(2,1)S(1)} %collective-permute-done.1.r1, bf16[64,4096]{1,0:T(8,128)(2,1)S(1)} %collective-permute-done.3.r2, bf16[64,4096]{1,0:T(8,128)(2,1)S(1)} %collective-permute-done.4.s1, ...), custom_call_target="tpu_custom_call" | custom-call | tf_op jit(solution)/shard_map/project_next/pallas_call | solution.py:113
  30.1 4.7 %local_part.1 = (bf16[4,128,512]{2,1,0:T(8,128)(2,1)S(1)}, bf16[4,128,128]{2,1,0:T(8,128)(2,1)S(1)}, bf16[4,128,128]{2,1,0:T(8,128)(2,1)S(1)}, f32[4,8,128]{2,1,...) custom-call(f32[8]{0:T(128)S(1)} %copy-done.3, ...), custom_call_target="tpu_custom_call" | custom-call | tf_op jit(solution)/shard_map/local_part/pallas_call | solution.py:268
  34.8 22.3 %all_to_all.10.r = bf16[32,24,128]{2,1,0:T(8,128)(2,1)S(1)} all-to-all(bf16[32,24,128]{2,1,0:T(8,128)(2,1)S(1)} %get-tuple-element.65), channel_id=1, replica_groups=mesh['ctx'=32,'tp'=8] {'ctx'}, dimensions={0} | all-to-all | bytes 393216 | tf_op jit(solution)/shard_map/all_to_all | solution.py:455
  57.8 4.6 %all-to-all-start.1 = ((bf16[32,16,128]{2,1,0:T(8,128)(2,1)}), bf16[32,16,128]{2,1,0:T(8,128)(2,1)S(1)}, u32[]{:S(2)}, u32[]{:S(2)}) async-start(bf16[32,16,128]{2,1,0:T(8,128)(2,1)} %prefix.1), calls=%async_computation.1 | async-start | bytes 262144 | tf_op jit(solution)/shard_map/all_to_all | solution.py:457
  62.4 1.8 %diag_part.1.ydiag = f32[4,128,512]{2,1,0:T(8,128)S(1)} custom-call(f32[8]{0:T(128)S(1)} %copy-done.5, bf16[4,128,512]{2,1,0:T(8,128)(2,1)S(1)} %get-tuple-element.70.x, bf16[4,128,128]{2,1,0:T(8,128)(2,1)S(1)} %get-tuple-element.71.b, bf16[4,128,128]{2,1,0:T(8,128)(2,1)S(1)} %get-tuple-element.68.c, f32[4,8,128]{2,1,0:T(8,128)S(1)} %get-tuple-element.69.cs, ...), custom_call_target="tpu_custom_call" | custom-call | tf_op jit(solution)/shard_map/diag_part/pallas_call | solution.py:336
  64.3 7.9 %all-to-all-done.1 = bf16[32,16,128]{2,1,0:T(8,128)(2,1)S(1)} async-done(((bf16[32,16,128]{2,1,0:T(8,128)(2,1)}), bf16[32,16,128]{2,1,0:T(8,128)(2,1)S(1)}, u32[]{:S(2)}, u32[]{:S(2)}) %all-to-all-start.1) | async-done | bytes 131104 | tf_op jit(solution)/shard_map/all_to_all | solution.py:457
  72.2 2.9 %norm_part.1 = (bf16[64,4096]{1,0:T(8,128)(2,1)S(1)}, bf16[64,4096]{1,0:T(8,128)(2,1)S(1)}, bf16[384,512]{1,0:T(8,128)(2,1)S(1)}, bf16[512,4096]{1,0:T(8,128)(2,1)S(1)}) custom-call(bf16[512,128]{1,0:T(8,128)(2,1)S(1)} %bitcast.3, f32[4,128,512]{2,1,0:T(8,128)S(1)} %get-tuple-element.66.e, f32[4,8,512]{2,1,0:T(8,128)S(1)} %get-tuple-element.67.d, ...), custom_call_target="tpu_custom_call" | custom-call | tf_op jit(solution)/shard_map/norm_part/pallas_call | solution.py:386
  75.2 1.8 %out_part.1 = (bf16[64,4096]{1,0:T(8,128)(2,1)S(1)}, bf16[64,4096]{1,0:T(8,128)(2,1)S(1)}, bf16[64,4096]{1,0:T(8,128)(2,1)S(1)}, bf16[64,4096]{1,0:T(8,128)(2,1)...) custom-call(bf16[384,512]{1,0:T(8,128)(2,1)S(1)} %get-tuple-element.73.n, ...), custom_call_target="tpu_custom_call" | custom-call | tf_op jit(solution)/shard_map/out_part/pallas_call | solution.py:405
  78.3 1.0 %collective-permute-done.12 = bf16[64,4096]{1,0:T(8,128)(2,1)S(1)} collective-permute-done((bf16[64,4096]{1,0:T(8,128)(2,1)S(1)}, bf16[64,4096]{1,0:T(8,128)(2,1)S(1)}, u32[]{:S(2)}, u32[]{:S(2)}) %collective-permute-start.12) | collective-permute-done | bytes 524320 | tf_op jit(solution)/shard_map/ppermute | solution.py:426
  79.9 0.9 collective-permute-done.15
  80.8 7.9 %collective-permute-done.16 = bf16[64,4096]{1,0:T(8,128)(2,1)S(1)} collective-permute-done((bf16[64,4096]{1,0:T(8,128)(2,1)S(1)}, bf16[64,4096]{1,0:T(8,128)(2,1)S(1)}, u32[]{:S(2)}, u32[]{:S(2)}) %collective-permute-start.16) | collective-permute-done | bytes 524320 | tf_op jit(solution)/shard_map/ppermute | solution.py:422
  88.9 5.3 %collective-permute-done.13 = bf16[64,4096]{1,0:T(8,128)(2,1)S(1)} collective-permute-done((bf16[64,4096]{1,0:T(8,128)(2,1)S(1)}, bf16[64,4096]{1,0:T(8,128)(2,1)S(1)}, u32[]{:S(2)}, u32[]{:S(2)}) %collective-permute-start.13) | collective-permute-done | bytes 524320 | tf_op jit(solution)/shard_map/ppermute | solution.py:422
  94.3 5.6 %collective-permute-done.17 = bf16[64,4096]{1,0:T(8,128)(2,1)S(1)} collective-permute-done((bf16[64,4096]{1,0:T(8,128)(2,1)S(1)}, bf16[64,4096]{1,0:T(8,128)(2,1)S(1)}, u32[]{:S(2)}, u32[]{:S(2)}) %collective-permute-start.17) | collective-permute-done | bytes 524320 | tf_op jit(solution)/shard_map/ppermute | solution.py:422
  99.9 1.1 %add_convert_fusion = bf16[64,4096]{1,0:T(8,128)(2,1)} fusion(bf16[64,4096]{1,0:T(8,128)(2,1)S(1)} %collective-permute-done.17, bf16[64,4096]{1,0:T(8,128)(2,1)S(1)} %collective-permute-done.14, bf16[64,4096]{1,0:T(8,128)(2,1)S(1)} %collective-permute-done.11, bf16[64,4096]{1,0:T(8,128)(2,1)S(1)} %get-tuple-element.75), kind=kLoop, calls=%fused_computation | loop fusion | flops 2097152 | bytes 2621440 | tf_op jit(solution)/shard_map/convert_element_type | solution.py:469
  (40 shorter events, 5.4 us)
Async XLA Ops:
  0.0 2.1 %collective-permute-start = (bf16[64,4096]{1,0:T(8,128)(2,1)}, bf16[64,4096]{1,0:T(8,128)(2,1)S(1)}, u32[]{:S(2)}, u32[]{:S(2)}) collective-permute-start(bf16[64,4096]{1,0:T(8,128)(2,1)} %far.1), channel_id=1, source_target_pairs={{0,1},{1,0},{2,3},{3,2},{4,5},{5,4},{6,7},{7,6},{8,9},{9,8},{10,11... | collective-permute-start | bytes 1572872 | tf_op jit(solution)/shard_map/ppermute | solution.py:426
  3.2 10.5 %collective-permute-start.1 = (bf16[64,4096]{1,0:T(8,128)(2,1)S(1)}, bf16[64,4096]{1,0:T(8,128)(2,1)S(1)}, u32[]{:S(2)}, u32[]{:S(2)}) collective-permute-start(bf16[64,4096]{1,0:T(8,128)(2,1)S(1)} %get-tuple-element.49), channel_id=1, source_target_pairs={{0,2},{1,7},{2,4},{3,1},{4,6},{5,3},{6,0},{7,5},{8,10},{9,15},{10,... | collective-permute-start | bytes 1572872 | tf_op jit(solution)/shard_map/ppermute | solution.py:422
  4.9 14.4 %collective-permute-start.3 = (bf16[64,4096]{1,0:T(8,128)(2,1)S(1)}, bf16[64,4096]{1,0:T(8,128)(2,1)S(1)}, u32[]{:S(2)}, u32[]{:S(2)}) collective-permute-start(bf16[64,4096]{1,0:T(8,128)(2,1)S(1)} %get-tuple-element.53), channel_id=1, source_target_pairs={{0,2},{1,7},{2,4},{3,1},{4,6},{5,3},{6,0},{7,5},{8,10},{9,15},{10,... | collective-permute-start | bytes 1572872 | tf_op jit(solution)/shard_map/ppermute | solution.py:422
  13.7 11.9 %collective-permute-start.2 = (bf16[64,4096]{1,0:T(8,128)(2,1)S(1)}, bf16[64,4096]{1,0:T(8,128)(2,1)S(1)}, u32[]{:S(2)}, u32[]{:S(2)}) collective-permute-start(bf16[64,4096]{1,0:T(8,128)(2,1)S(1)} %collective-permute-done.1.r1), channel_id=1, source_target_pairs={{0,2},{1,7},{2,4},{3,1},{4,6},{5,3},{6,0},{7,5},{8,10},{9,15},{10,... | collective-permute-start | bytes 1572872 | tf_op jit(solution)/shard_map/ppermute | solution.py:422
  14.1 11.6 %collective-permute-start.7 = (bf16[8,4096]{1,0:T(8,128)(2,1)S(1)}, bf16[8,4096]{1,0:T(8,128)(2,1)S(1)}, u32[]{:S(2)}, u32[]{:S(2)}) collective-permute-start(bf16[8,4096]{1,0:T(8,128)(2,1)S(1)} %get-tuple-element.60), channel_id=1, source_target_pairs={{7,13},{6,11},{15,21},{14,19},{23,29},{22,27},{31,37},{30,35},{39,... | collective-permute-start | bytes 196616 | tf_op jit(solution)/shard_map/ppermute | solution.py:441
  14.7 10.9 %collective-permute-start.6 = (bf16[8,4096]{1,0:T(8,128)(2,1)S(1)}, bf16[8,4096]{1,0:T(8,128)(2,1)S(1)}, u32[]{:S(2)}, u32[]{:S(2)}) collective-permute-start(bf16[8,4096]{1,0:T(8,128)(2,1)S(1)} %get-tuple-element.60), channel_id=1, source_target_pairs={{7,15},{6,9},{15,23},{14,17},{23,31},{22,25},{31,39},{30,33},{39,4... | collective-permute-start | bytes 196616 | tf_op jit(solution)/shard_map/ppermute | solution.py:441
  15.4 11.0 %collective-permute-start.4 = (bf16[64,4096]{1,0:T(8,128)(2,1)S(1)}, bf16[64,4096]{1,0:T(8,128)(2,1)S(1)}, u32[]{:S(2)}, u32[]{:S(2)}) collective-permute-start(bf16[64,4096]{1,0:T(8,128)(2,1)S(1)} %collective-permute-done.1.r1), channel_id=1, source_target_pairs={{0,1},{1,0},{2,3},{3,2},{4,5},{5,4},{6,7},{7,6},{8,9},{9,8},{10,11... | collective-permute-start | bytes 1572872 | tf_op jit(solution)/shard_map/ppermute | solution.py:426
  25.6 1.9 %collective-permute-start.5 = (bf16[64,4096]{1,0:T(8,128)(2,1)S(1)}, bf16[64,4096]{1,0:T(8,128)(2,1)S(1)}, u32[]{:S(2)}, u32[]{:S(2)}) collective-permute-start(bf16[64,4096]{1,0:T(8,128)(2,1)S(1)} %collective-permute-done.3.r2), channel_id=1, source_target_pairs={{0,1},{1,0},{2,3},{3,2},{4,5},{5,4},{6,7},{7,6},{8,9},{9,8},{10,11... | collective-permute-start | bytes 1572872 | tf_op jit(solution)/shard_map/ppermute | solution.py:426
  25.7 4.4 %collective-permute-start.8 = (bf16[64,4096]{1,0:T(8,128)(2,1)S(1)}, bf16[64,4096]{1,0:T(8,128)(2,1)S(1)}, u32[]{:S(2)}, u32[]{:S(2)}) collective-permute-start(bf16[64,4096]{1,0:T(8,128)(2,1)S(1)} %collective-permute-done.2.refs_6_), channel_id=1, source_target_pairs={{0,1},{1,0},{2,3},{3,2},{4,5},{5,4},{6,7},{7,6},{8,9},{9,8},{10,11... | collective-permute-start | bytes 1572872 | tf_op jit(solution)/shard_map/ppermute | solution.py:426
  26.2 3.9 %collective-permute-start.9 = (bf16[8,4096]{1,0:T(8,128)(2,1)S(1)}, bf16[8,4096]{1,0:T(8,128)(2,1)S(1)}, u32[]{:S(2)}, u32[]{:S(2)}) collective-permute-start(bf16[8,4096]{1,0:T(8,128)(2,1)S(1)} %add.24.refs_8_), channel_id=1, source_target_pairs={{0,1},{1,0},{2,3},{3,2},{4,5},{5,4},{6,7},{7,6},{8,9},{9,8},{10,11... | collective-permute-start | bytes 196616 | tf_op jit(solution)/shard_map/ppermute | solution.py:426
  27.6 2.5 %copy-start.1 = (f32[4,256]{1,0:T(4,128)S(1)}, f32[4,256]{1,0:T(4,128)}, u32[]{:S(2)}) copy-start(f32[4,256]{1,0:T(4,128)} %refs_14_.1) | copy-start | bytes 12292
  27.6 2.5 %copy-start.3 = (f32[8]{0:T(128)S(1)}, f32[8]{0:T(128)}, u32[]{:S(2)}) copy-start(f32[8]{0:T(128)} %bias.1) | copy-start | bytes 100
  27.6 2.5 %copy-start.4 = (f32[8]{0:T(128)S(1)}, f32[8]{0:T(128)}, u32[]{:S(2)}) copy-start(f32[8]{0:T(128)} %alog.1) | copy-start | bytes 100
  30.1 32.3 %copy-start.5 = (f32[8]{0:T(128)S(1)}, f32[8]{0:T(128)}, u32[]{:S(2)}) copy-start(f32[8]{0:T(128)} %skip.1) | copy-start | bytes 100
  30.1 42.1 %copy-start.2 = (f32[512]{0:T(512)S(1)}, f32[512]{0:T(512)}, u32[]{:S(2)}) copy-start(f32[512]{0:T(512)} %param.20) | copy-start | bytes 6148
  57.8 14.4 %all-to-all-start.1 = ((bf16[32,16,128]{2,1,0:T(8,128)(2,1)}), bf16[32,16,128]{2,1,0:T(8,128)(2,1)S(1)}, u32[]{:S(2)}, u32[]{:S(2)}) async-start(bf16[32,16,128]{2,1,0:T(8,128)(2,1)} %prefix.1), calls=%async_computation.1 | async-start | bytes 262144 | tf_op jit(solution)/shard_map/all_to_all | solution.py:457
  75.1 2.0 %collective-permute-start.10 = (bf16[64,4096]{1,0:T(8,128)(2,1)S(1)}, bf16[64,4096]{1,0:T(8,128)(2,1)S(1)}, u32[]{:S(2)}, u32[]{:S(2)}) collective-permute-start(bf16[64,4096]{1,0:T(8,128)(2,1)S(1)} %get-tuple-element.77), channel_id=1, source_target_pairs={{0,1},{1,0},{2,3},{3,2},{4,5},{5,4},{6,7},{7,6},{8,9},{9,8},{10,11... | collective-permute-start | bytes 1572872 | tf_op jit(solution)/shard_map/ppermute | solution.py:426
  77.3 2.0 %collective-permute-start.12 = (bf16[64,4096]{1,0:T(8,128)(2,1)S(1)}, bf16[64,4096]{1,0:T(8,128)(2,1)S(1)}, u32[]{:S(2)}, u32[]{:S(2)}) collective-permute-start(bf16[64,4096]{1,0:T(8,128)(2,1)S(1)} %get-tuple-element.83), channel_id=1, source_target_pairs={{0,1},{1,0},{2,3},{3,2},{4,5},{5,4},{6,7},{7,6},{8,9},{9,8},{10,11... | collective-permute-start | bytes 1572872 | tf_op jit(solution)/shard_map/ppermute | solution.py:426
  77.8 16.5 %collective-permute-start.11 = (bf16[64,4096]{1,0:T(8,128)(2,1)S(1)}, bf16[64,4096]{1,0:T(8,128)(2,1)S(1)}, u32[]{:S(2)}, u32[]{:S(2)}) collective-permute-start(bf16[64,4096]{1,0:T(8,128)(2,1)S(1)} %get-tuple-element.81), channel_id=1, source_target_pairs={{0,1},{1,0},{2,3},{3,2},{4,5},{5,4},{6,7},{7,6},{8,9},{9,8},{10,11... | collective-permute-start | bytes 1572872 | tf_op jit(solution)/shard_map/ppermute | solution.py:426
  77.9 2.9 %collective-permute-start.15 = (bf16[64,4096]{1,0:T(8,128)(2,1)S(1)}, bf16[64,4096]{1,0:T(8,128)(2,1)S(1)}, u32[]{:S(2)}, u32[]{:S(2)}) collective-permute-start(bf16[64,4096]{1,0:T(8,128)(2,1)S(1)} %get-tuple-element.85), channel_id=1, source_target_pairs={{0,1},{1,0},{2,3},{3,2},{4,5},{5,4},{6,7},{7,6},{8,9},{9,8},{10,11... | collective-permute-start | bytes 1572872 | tf_op jit(solution)/shard_map/ppermute | solution.py:426
  78.3 10.4 %collective-permute-start.16 = (bf16[64,4096]{1,0:T(8,128)(2,1)S(1)}, bf16[64,4096]{1,0:T(8,128)(2,1)S(1)}, u32[]{:S(2)}, u32[]{:S(2)}) collective-permute-start(bf16[64,4096]{1,0:T(8,128)(2,1)S(1)} %add_convert_fusion.3), channel_id=1, source_target_pairs={{0,2},{1,7},{2,4},{3,1},{4,6},{5,3},{6,0},{7,5},{8,10},{9,15},{10,... | collective-permute-start | bytes 1572872 | tf_op jit(solution)/shard_map/ppermute | solution.py:422
  79.4 14.9 %collective-permute-start.13 = (bf16[64,4096]{1,0:T(8,128)(2,1)S(1)}, bf16[64,4096]{1,0:T(8,128)(2,1)S(1)}, u32[]{:S(2)}, u32[]{:S(2)}) collective-permute-start(bf16[64,4096]{1,0:T(8,128)(2,1)S(1)} %add_convert_fusion.2), channel_id=1, source_target_pairs={{0,2},{1,7},{2,4},{3,1},{4,6},{5,3},{6,0},{7,5},{8,10},{9,15},{10,... | collective-permute-start | bytes 1572872 | tf_op jit(solution)/shard_map/ppermute | solution.py:422
  88.9 11.0 %collective-permute-start.17 = (bf16[64,4096]{1,0:T(8,128)(2,1)S(1)}, bf16[64,4096]{1,0:T(8,128)(2,1)S(1)}, u32[]{:S(2)}, u32[]{:S(2)}) collective-permute-start(bf16[64,4096]{1,0:T(8,128)(2,1)S(1)} %add_convert_fusion.1), channel_id=1, source_target_pairs={{0,2},{1,7},{2,4},{3,1},{4,6},{5,3},{6,0},{7,5},{8,10},{9,15},{10,... | collective-permute-start | bytes 1572872 | tf_op jit(solution)/shard_map/ppermute | solution.py:422
  94.3 5.6 %collective-permute-start.14 = (bf16[64,4096]{1,0:T(8,128)(2,1)S(1)}, bf16[64,4096]{1,0:T(8,128)(2,1)S(1)}, u32[]{:S(2)}, u32[]{:S(2)}) collective-permute-start(bf16[64,4096]{1,0:T(8,128)(2,1)S(1)} %collective-permute-done.13), channel_id=1, source_target_pairs={{0,1},{1,0},{2,3},{3,2},{4,5},{5,4},{6,7},{7,6},{8,9},{9,8},{10,11... | collective-permute-start | bytes 1572872 | tf_op jit(solution)/shard_map/ppermute | solution.py:426
  (1 other events, 2.5 us)

commit v10 on v9

--- a/solution.py
+++ b/solution.py
@@ -95,34 +95,22 @@
     )(pltpu.with_memory_space_constraint(mine, pltpu.HBM), in_vmem(theirs))
 
 
-def next_kernel(r1, r2, s1, s2, wx, wbc, wdt, xo, bco, dto, tok):
-    c = core()
-    place(tok, r1, c * Q, c)
-    place(tok, r2, c * Q, 1 - c)
-    place(tok, s1, (1 - c) * Q, 1 - c)
-    place(tok, s2, (1 - c) * Q, c)
-    rows = tok[...]
+def half_kernel(mine, theirs, wx, wbc, wdt, xo, bco, dto):
+    rows = jnp.concatenate([mine[...], theirs[...]], 0)
     xo[...] = jnp.dot(rows, wx[...], preferred_element_type=F32).astype(BF)
     bco[...] = jnp.dot(rows, wbc[...], preferred_element_type=F32).astype(BF)
-    dt = dot_nt(rows, wdt[...])
-    for j in range(2):
-        dto[j] = dt[j * Q : (j + 1) * Q].T
-
-
-def project_next(*args):
-    return pl.pallas_call(
-        next_kernel,
-        out_shape=(
-            pltpu.VMEM((2 * Q, CH), BF),
-            pltpu.VMEM((2 * Q, BCW), BF),
-            pltpu.VMEM((2, HH, Q), F32),
-        ),
-        in_specs=[VMEM] * 7,
+    dto[...] = dot_nt(rows, wdt[...])
+
+
+def project_half(mine, theirs, weights, name):
+    return pl.pallas_call(
+        half_kernel,
+        out_shape=(pltpu.VMEM((Q, CH), BF), pltpu.VMEM((Q, BCW), BF), pltpu.VMEM((Q, HH), F32)),
+        in_specs=[VMEM] * 5,
         out_specs=(VMEM, VMEM, VMEM),
-        scratch_shapes=[pltpu.VMEM((2 * Q, 4096), BF)],
-        compiler_params=params(),
-        name="project_next",
-    )(*[in_vmem(v) for v in args])
+        compiler_params=params(),
+        name=name,
+    )(*[in_vmem(v) for v in (mine, theirs, *weights)])
 
 
 def near_kernel(mine, theirs, wx_far, wbc_far, wdt_far, xo, bco, dto, wx, wbc, wdt, tok, sems):
@@ -142,7 +130,7 @@
     rows = tok[...]
     xo[...] = jnp.dot(rows, wx[...], preferred_element_type=F32).astype(BF)
     copies[2].wait()
-    dto[0] = dot_nt(rows, wdt[...]).T
+    dto[...] = dot_nt(rows, wdt[...])
     copies[3].wait()
     bco[...] = jnp.dot(rows, wbc[...], preferred_element_type=F32).astype(BF)
 
@@ -155,7 +143,7 @@
         out_shape=(
             pltpu.VMEM((Q, CH), BF),
             pltpu.VMEM((Q, BCW), BF),
-            pltpu.VMEM((1, HH, Q), F32),
+            pltpu.VMEM((Q, HH), F32),
             pltpu.VMEM(in_x.shape, BF),
             pltpu.VMEM(in_bc.shape, BF),
             pltpu.VMEM(in_dt.shape, BF),
@@ -184,38 +172,38 @@
     return v
 
 
-OFFS = (0, 3, 1, 2)
-
-
 def local_kernel(bias, alog, *refs):
-    x0, bc0, dt0, x12, bc12, dt12 = refs[0:6]
-    far, far_swap, halo, haloswap = refs[6:10]
-    wx, wbc, wdt, kx, kbc = refs[10:15]
-    (xo, bo, co, cso, dto, eo, do, send) = refs[15:23]
-    ext, extb, dtr, tok = refs[23:27]
+    near, one, two = refs[0:3], refs[3:6], refs[6:9]
+    far, far_swap, halo, haloswap = refs[9:13]
+    wx, wbc, wdt, kx, kbc = refs[13:18]
+    (xo, bo, co, cso, dto, eo, do, send) = refs[18:26]
+    ext, extb, dtr, tok = refs[26:30]
     y = chip()
-    place(tok, far, 0, core())
-    place(tok, far_swap, 0, 1 - core())
+    c = core()
+    place(tok, far, 0, c)
+    place(tok, far_swap, 0, 1 - c)
     edge = halo[...].astype(F32) + haloswap[...].astype(F32)
     tok[Q : Q + 16, :] = jnp.concatenate([edge, edge], 0).astype(BF)
     rows = tok[...]
     x3 = jnp.dot(rows, wx[...], preferred_element_type=F32).astype(BF).astype(F32)
     bc3 = jnp.dot(rows, wbc[...], preferred_element_type=F32).astype(BF).astype(F32)
-    dt3 = dot_nt(rows[0:Q], wdt[...]).T
+    dt3 = dot_nt(rows[0:Q], wdt[...])
     ext[0:8, :] = x3[Q : Q + 8]
     extb[0:8, :] = bc3[Q : Q + 8]
-    pieces = (
-        (x0[...], bc0[...], dt0[0]),
-        (x12[0:Q], bc12[0:Q], dt12[0]),
-        (x12[Q : 2 * Q], bc12[Q : 2 * Q], dt12[1]),
-        (x3[0:Q], bc3[0:Q], dt3),
-    )
-    for k, (px, pbc, pdt) in enumerate(pieces):
-        a = lax.rem(y + OFFS[k], NQ)
-        at = pl.multiple_of(a * Q + 8, 8)
-        ext[pl.ds(at, Q), :] = px.astype(F32)
-        extb[pl.ds(at, Q), :] = pbc.astype(F32)
-        dtr[a] = pdt
+
+    def put(at, n, px, pbc, pdt):
+        ext[pl.ds(pl.multiple_of(at + 8, 8), n), :] = px.astype(F32)
+        extb[pl.ds(pl.multiple_of(at + 8, 8), n), :] = pbc.astype(F32)
+        dtr[pl.ds(pl.multiple_of(at, 8), n), :] = pdt
+
+    put(y * Q, Q, near[0][...], near[1][...], near[2][...])
+    put(lax.rem(y + 2, NQ) * Q, Q, x3[0:Q], bc3[0:Q], dt3)
+    sides = (lax.rem(y + 3 - 2 * c, NQ), lax.rem(y + 1 + 2 * c, NQ))
+    for piece, halves in ((one, (c, 1 - c)), (two, (1 - c, c))):
+        for j in range(4):
+            at = sides[j // 2] * Q + halves[j // 2] * 32 + (j % 2) * 64
+            of = slice(32 * j, 32 * j + 32)
+            put(at, 32, piece[0][of, :], piece[1][of, :], piece[2][of, :])
     ones = head_spread()
     lane = lax.broadcasted_iota(jnp.int32, (HH, Q), 1)
     decay = -jnp.exp(column(alog))
@@ -223,7 +211,7 @@
     total = jnp.zeros((HH, Q), F32)
     state = jnp.zeros((NS, CH), F32)
     for a in range(NQ):
-        dt = softplus(dtr[a] + bias_col)
+        dt = softplus(dtr[a * Q : (a + 1) * Q, :].T + bias_col)
         cs = decay * dt
         for s in (1, 2, 4, 8, 16, 32, 64):
             cs = cs + jnp.where(lane >= s, pltpu.roll(cs, s, 1), 0.0)
@@ -277,12 +265,12 @@
             s((NQ, 8, CH), F32),
             s((32, 24, 128), BF),
         ),
-        in_specs=[SMEM] * 2 + [VMEM] * 15,
+        in_specs=[SMEM] * 2 + [VMEM] * 18,
         out_specs=(VMEM,) * 8,
         scratch_shapes=[
             pltpu.VMEM((8 + NQ * Q, CH), F32),
             pltpu.VMEM((8 + NQ * Q, BCW), F32),
-            pltpu.VMEM((NQ, HH, Q), F32),
+            pltpu.VMEM((NQ * Q, HH), F32),
             pltpu.VMEM((Q + 16, 4096), BF),
         ],
         compiler_params=params(),
@@ -344,8 +332,10 @@
 
 
 def norm_kernel(s_in, e, d, c, cs, ydiag, gain, w_far, other, own, rest, w, nb, sem):
-    copy = pltpu.make_async_copy(w_far, w, sem)
-    copy.start()
+    blocks = [pl.ds(1024 * j, 1024) for j in range(4)]
+    copies = [pltpu.make_async_copy(w_far.at[:, k], w.at[:, k], sem.at[j]) for j, k in enumerate(blocks)]
+    for copy in copies:
+        copy.start()
     y = chip()
     mine = core()
     ones = head_spread()
@@ -371,10 +361,11 @@
 
     a = lax.rem(y + 2, NQ)
     v = jnp.concatenate([half(a, 1 - mine), half(a, mine)], 0)
-    copy.wait()
-    v = jnp.dot(v, w[...], preferred_element_type=F32).astype(BF)
-    other[...] = v[0:64]
-    own[...] = v[64:128]
+    for k, copy in zip(blocks, copies):
+        copy.wait()
+        o = jnp.dot(v, w[:, k], preferred_element_type=F32).astype(BF)
+        other[:, k] = o[0:64]
+        own[:, k] = o[64:128]
     side, across = lax.rem(y + 1 + 2 * mine, NQ), lax.rem(y + 3 - 2 * mine, NQ)
     parts = ((across, mine), (across, 1 - mine), (side, 1 - mine), (side, mine), (y, 1 - mine), (y, mine))
     for j, (a, h) in enumerate(parts):
@@ -388,7 +379,7 @@
         out_shape=(s((64, 4096), BF), s((64, 4096), BF), s((384, CH), BF), s((CH, 4096), BF)),
         in_specs=[VMEM] * 7 + [pl.BlockSpec(memory_space=pltpu.HBM)],
         out_specs=(VMEM,) * 4,
-        scratch_shapes=[pltpu.VMEM((NQ, Q, CH), BF), pltpu.SemaphoreType.DMA],
+        scratch_shapes=[pltpu.VMEM((NQ, Q, CH), BF), pltpu.SemaphoreType.DMA((4,))],
         compiler_params=params(),
         name="norm_part",
     )(*[in_vmem(v) for v in args[:7]], pltpu.with_memory_space_constraint(args[7], pltpu.HBM))
@@ -443,14 +434,17 @@
         )
 
     edge_a, edge_b = onward((7, 7), (6, 1)), onward((7, 5), (6, 3))
-    far, r2 = after((far, r2))
-    piece12 = project_next(r1, r2, swap(r1), swap(r2), *weights)
-    edge_a, edge_b, far = after((edge_a, edge_b, far))
+    s1 = swap(r1)
+    r2, edge_a, edge_b = after((r2, edge_a, edge_b))
+    s2 = swap(r2)
+    piece1 = project_half(r1, s1, weights, "project_one")
+    far, s2, *piece1 = after((far, s2, *piece1))
+    piece2 = project_half(r2, s2, weights, "project_two")
     edge = edge_a + edge_b
     edges = swap(edge)
 
     xc, b, c, cs, dt, e, d, send = local_part(
-        dt_bias, a_log, *piece0, *piece12, far, swap(far), edge, edges, *weights, conv_x, conv_bc
+        dt_bias, a_log, *piece0, *piece1, *piece2, far, swap(far), edge, edges, *weights, conv_x, conv_bc
     )
     got = lax.all_to_all(send, "ctx", 0, 0, tiled=True)
     ydiag = diag_part(skip_d, xc, b, c, cs, dt)

time: 101 us -> 102 us (level)
  blocking collectives: 22.3 us -> 21.2 us
    ppermute x6, waiting for transfers between devices: 29.7 us -> 31.2 us  [around(): return lax.ppermute(v, 'tp', AROUND)]
    all_to_all x1, blocking collectives: 22.3 us -> 21.2 us  [per_device(): got = lax.all_to_all(send, 'ctx', 0, 0, tiled=True)]
    pallas_call x1 -> x2, Pallas kernels: 2.48 us -> 2.53 us  [project_half(): pl.pallas_call(half_kernel, out_shape=(pltpu.VMEM((Q, CH), BF), pltpu.VME...]
  transfers between devices with their start and end apart: 19 -> 19, of which waited for: 12 -> 12; matrix products, arithmetic and copies ran while one was open for 0% -> 0% of each run, Pallas kernels for 10% -> 11%
where the time goes in v10:
time: 102 us; the launch traced here: 101 us
  waiting for transfers between devices  43.8 us (43%)
  blocking collectives  21.2 us (21%)
  Pallas kernels  20.6 us (20%)
  starting transfers between devices  14.1 us (14%)
  other arithmetic  1.52 us (1%)
    ppermute x6, waiting for transfers between devices, around(): return lax.ppermute(v, 'tp', AROUND)  31.2 us
    all_to_all x1, blocking collectives, per_device(): got = lax.all_to_all(send, 'ctx', 0, 0, tiled=True)  21.2 us
    all_to_all x1, waiting for transfers between devices, per_device(): back = lax.all_to_all(prefix(got), 'ctx', 0, 0, tiled=True)  7.92 us
    pallas_call x1, Pallas kernels, local_part(): pl.pallas_call(local_kernel, out_shape=(s((NQ, Q, CH), BF), s((NQ, Q, NS)...  4.83 us
    ppermute x10, waiting for transfers between devices, swap(): return lax.ppermute(v, 'tp', SWAP)  4.64 us
    ppermute x10, starting transfers between devices, swap(): return lax.ppermute(v, 'tp', SWAP)  4.53 us
    pallas_call x1, Pallas kernels, project_near(): pl.pallas_call(near_kernel, out_shape=(pltpu.VMEM((Q, CH), BF), pltpu.VME...  4.51 us
    all_to_all x1, starting transfers between devices, per_device(): back = lax.all_to_all(prefix(got), 'ctx', 0, 0, tiled=True)  4.45 us
  transfers between devices with their start and end apart: 19, of which 12 were waited for; matrix products, arithmetic and copies ran while one was open for 0% of the time, Pallas kernels for 11%

profile of v10, /device:TPU:32, one launch (start us, length us, event | category | flops | bytes accessed | tf_op | source)
XLA Modules:
  0.0 101.4 jit_solution(1743938029371463555)
XLA Ops:
  0.0 2.1 %collective-permute-done.theirs = bf16[64,4096]{1,0:T(8,128)(2,1)S(1)} collective-permute-done((bf16[64,4096]{1,0:T(8,128)(2,1)}, bf16[64,4096]{1,0:T(8,128)(2,1)S(1)}, u32[]{:S(2)}, u32[]{:S(2)}) %collective-permute-start) | collective-permute-done | bytes 524320 | tf_op jit(solution)/shard_map/ppermute | solution.py:417
  2.1 1.1 %pack.1 = (bf16[64,4096]{1,0:T(8,128)(2,1)S(1)}, bf16[64,4096]{1,0:T(8,128)(2,1)S(1)}, bf16[8,4096]{1,0:T(8,128)(2,1)S(1)}) custom-call(bf16[64,4096]{1,0:T(8,128)(2,1)} %far.1, bf16[64,4096]{1,0:T(8,128)(2,1)S(1)} %collective-permute-done.theirs), custom_call_target="tpu_custom_call" | custom-call | tf_op jit(solution)/shard_map/pack/pallas_call | solution.py:87
  3.2 1.7 %collective-permute-start.1 = (bf16[64,4096]{1,0:T(8,128)(2,1)S(1)}, bf16[64,4096]{1,0:T(8,128)(2,1)S(1)}, u32[]{:S(2)}, u32[]{:S(2)}) collective-permute-start(bf16[64,4096]{1,0:T(8,128)(2,1)S(1)} %get-tuple-element.55), channel_id=1, source_target_pairs={{0,2},{1,7},{2,4},{3,1},{4,6},{5,3},{6,0},{7,5},{8,10},{9,15},{10,... | collective-permute-start | bytes 1572872 | tf_op jit(solution)/shard_map/ppermute | solution.py:413
  4.9 1.6 %collective-permute-start.3 = (bf16[64,4096]{1,0:T(8,128)(2,1)S(1)}, bf16[64,4096]{1,0:T(8,128)(2,1)S(1)}, u32[]{:S(2)}, u32[]{:S(2)}) collective-permute-start(bf16[64,4096]{1,0:T(8,128)(2,1)S(1)} %get-tuple-element.59), channel_id=1, source_target_pairs={{0,2},{1,7},{2,4},{3,1},{4,6},{5,3},{6,0},{7,5},{8,10},{9,15},{10,... | collective-permute-start | bytes 1572872 | tf_op jit(solution)/shard_map/ppermute | solution.py:413
  6.5 4.5 %project_near.1 = (bf16[128,512]{1,0:T(8,128)(2,1)S(1)}, bf16[128,256]{1,0:T(8,128)(2,1)S(1)}, f32[128,8]{1,0:T(8,128)S(1)}, bf16[4096,512]{1,0:T(8,128)(2,1)S(1...) custom-call(bf16[64,4096]{1,0:T(8,128)(2,1)} %far.1, bf16[64,4096]{1,0:T(8,128)(2,1)S(1)} %collective-permute-done.theirs, ...), custom_call_target="tpu_custom_call" | custom-call | tf_op jit(solution)/shard_map/project_near/pallas_call | solution.py:141
  11.0 2.7 %collective-permute-done.1.mine = bf16[64,4096]{1,0:T(8,128)(2,1)S(1)} collective-permute-done((bf16[64,4096]{1,0:T(8,128)(2,1)S(1)}, bf16[64,4096]{1,0:T(8,128)(2,1)S(1)}, u32[]{:S(2)}, u32[]{:S(2)}) %collective-permute-start.1) | collective-permute-done | bytes 524320 | tf_op jit(solution)/shard_map/ppermute | solution.py:413
  15.6 3.7 %collective-permute-done.3.mine = bf16[64,4096]{1,0:T(8,128)(2,1)S(1)} collective-permute-done((bf16[64,4096]{1,0:T(8,128)(2,1)S(1)}, bf16[64,4096]{1,0:T(8,128)(2,1)S(1)}, u32[]{:S(2)}, u32[]{:S(2)}) %collective-permute-start.3) | collective-permute-done | bytes 524320 | tf_op jit(solution)/shard_map/ppermute | solution.py:413
  19.3 2.7 %collective-permute-start.6 = (bf16[64,4096]{1,0:T(8,128)(2,1)S(1)}, bf16[64,4096]{1,0:T(8,128)(2,1)S(1)}, u32[]{:S(2)}, u32[]{:S(2)}) collective-permute-start(bf16[64,4096]{1,0:T(8,128)(2,1)S(1)} %collective-permute-done.3.mine), channel_id=1, source_target_pairs={{0,1},{1,0},{2,3},{3,2},{4,5},{5,4},{6,7},{7,6},{8,9},{9,8},{10,11... | collective-permute-start | bytes 1572872 | tf_op jit(solution)/shard_map/ppermute | solution.py:417
  22.1 1.3 %project_one.1 = (bf16[128,512]{1,0:T(8,128)(2,1)S(1)}, bf16[128,256]{1,0:T(8,128)(2,1)S(1)}, f32[128,8]{1,0:T(8,128)S(1)}) custom-call(bf16[64,4096]{1,0:T(8,128)(2,1)S(1)} %collective-permute-done.1.mine, bf16[64,4096]{1,0:T(8,128)(2,1)S(1)} %collective-permute-done.7.theirs, bf16[4096,512]{1,0:T(8,128)(2,1)S(1)} %get-tuple-element.56.wx.refs_13_, ...), custom_call_target="tpu_custom_call" | custom-call | tf_op jit(solution)/shard_map/project_one/pallas_call | solution.py:106
  23.4 5.9 %collective-permute-done.2.refs_9_ = bf16[64,4096]{1,0:T(8,128)(2,1)S(1)} collective-permute-done((bf16[64,4096]{1,0:T(8,128)(2,1)S(1)}, bf16[64,4096]{1,0:T(8,128)(2,1)S(1)}, u32[]{:S(2)}, u32[]{:S(2)}) %collective-permute-start.2) | collective-permute-done | bytes 524320 | tf_op jit(solution)/shard_map/ppermute | solution.py:413
  29.9 1.3 %project_two.1 = (bf16[128,512]{1,0:T(8,128)(2,1)S(1)}, bf16[128,256]{1,0:T(8,128)(2,1)S(1)}, f32[128,8]{1,0:T(8,128)S(1)}) custom-call(bf16[64,4096]{1,0:T(8,128)(2,1)S(1)} %collective-permute-done.3.mine, bf16[64,4096]{1,0:T(8,128)(2,1)S(1)} %collective-permute-done.6.theirs, bf16[4096,512]{1,0:T(8,128)(2,1)S(1)} %get-tuple-element.56.wx.refs_13_, ...), custom_call_target="tpu_custom_call" | custom-call | tf_op jit(solution)/shard_map/project_two/pallas_call | solution.py:106
  31.4 4.8 %local_part.1 = (bf16[4,128,512]{2,1,0:T(8,128)(2,1)S(1)}, bf16[4,128,128]{2,1,0:T(8,128)(2,1)S(1)}, bf16[4,128,128]{2,1,0:T(8,128)(2,1)S(1)}, f32[4,8,128]{2,1,...) custom-call(f32[8]{0:T(128)S(1)} %copy-done.3, ...), custom_call_target="tpu_custom_call" | custom-call | tf_op jit(solution)/shard_map/local_part/pallas_call | solution.py:256
  36.2 21.2 %all_to_all.10.r = bf16[32,24,128]{2,1,0:T(8,128)(2,1)S(1)} all-to-all(bf16[32,24,128]{2,1,0:T(8,128)(2,1)S(1)} %get-tuple-element.77), channel_id=1, replica_groups=mesh['ctx'=32,'tp'=8] {'ctx'}, dimensions={0} | all-to-all | bytes 393216 | tf_op jit(solution)/shard_map/all_to_all | solution.py:449
  58.1 4.5 %all-to-all-start.1 = ((bf16[32,16,128]{2,1,0:T(8,128)(2,1)}), bf16[32,16,128]{2,1,0:T(8,128)(2,1)S(1)}, u32[]{:S(2)}, u32[]{:S(2)}) async-start(bf16[32,16,128]{2,1,0:T(8,128)(2,1)} %prefix.1), calls=%async_computation.1 | async-start | bytes 262144 | tf_op jit(solution)/shard_map/all_to_all | solution.py:451
  62.6 1.8 %diag_part.1.ydiag = f32[4,128,512]{2,1,0:T(8,128)S(1)} custom-call(f32[8]{0:T(128)S(1)} %copy-done.5, bf16[4,128,512]{2,1,0:T(8,128)(2,1)S(1)} %get-tuple-element.82.x, bf16[4,128,128]{2,1,0:T(8,128)(2,1)S(1)} %get-tuple-element.83.b, bf16[4,128,128]{2,1,0:T(8,128)(2,1)S(1)} %get-tuple-element.80.c, f32[4,8,128]{2,1,0:T(8,128)S(1)} %get-tuple-element.81.cs, ...), custom_call_target="tpu_custom_call" | custom-call | tf_op jit(solution)/shard_map/diag_part/pallas_call | solution.py:324
  64.4 7.9 %all-to-all-done.1 = bf16[32,16,128]{2,1,0:T(8,128)(2,1)S(1)} async-done(((bf16[32,16,128]{2,1,0:T(8,128)(2,1)}), bf16[32,16,128]{2,1,0:T(8,128)(2,1)S(1)}, u32[]{:S(2)}, u32[]{:S(2)}) %all-to-all-start.1) | async-done | bytes 131104 | tf_op jit(solution)/shard_map/all_to_all | solution.py:451
  72.3 3.2 %norm_part.1 = (bf16[64,4096]{1,0:T(8,128)(2,1)S(1)}, bf16[64,4096]{1,0:T(8,128)(2,1)S(1)}, bf16[384,512]{1,0:T(8,128)(2,1)S(1)}, bf16[512,4096]{1,0:T(8,128)(2,1)S(1)}) custom-call(bf16[512,128]{1,0:T(8,128)(2,1)S(1)} %bitcast.3, f32[4,128,512]{2,1,0:T(8,128)S(1)} %get-tuple-element.78.e, f32[4,8,512]{2,1,0:T(8,128)S(1)} %get-tuple-element.79.d, ...), custom_call_target="tpu_custom_call" | custom-call | tf_op jit(solution)/shard_map/norm_part/pallas_call | solution.py:377
  75.7 1.8 %out_part.1 = (bf16[64,4096]{1,0:T(8,128)(2,1)S(1)}, bf16[64,4096]{1,0:T(8,128)(2,1)S(1)}, bf16[64,4096]{1,0:T(8,128)(2,1)S(1)}, bf16[64,4096]{1,0:T(8,128)(2,1)...) custom-call(bf16[384,512]{1,0:T(8,128)(2,1)S(1)} %get-tuple-element.85.n, ...), custom_call_target="tpu_custom_call" | custom-call | tf_op jit(solution)/shard_map/out_part/pallas_call | solution.py:396
  78.7 1.0 %collective-permute-done.12 = bf16[64,4096]{1,0:T(8,128)(2,1)S(1)} collective-permute-done((bf16[64,4096]{1,0:T(8,128)(2,1)S(1)}, bf16[64,4096]{1,0:T(8,128)(2,1)S(1)}, u32[]{:S(2)}, u32[]{:S(2)}) %collective-permute-start.12) | collective-permute-done | bytes 524320 | tf_op jit(solution)/shard_map/ppermute | solution.py:417
  79.9 1.3 %collective-permute-done.15 = bf16[64,4096]{1,0:T(8,128)(2,1)S(1)} collective-permute-done((bf16[64,4096]{1,0:T(8,128)(2,1)S(1)}, bf16[64,4096]{1,0:T(8,128)(2,1)S(1)}, u32[]{:S(2)}, u32[]{:S(2)}) %collective-permute-start.15) | collective-permute-done | bytes 524320 | tf_op jit(solution)/shard_map/ppermute | solution.py:417
  81.2 7.9 %collective-permute-done.16 = bf16[64,4096]{1,0:T(8,128)(2,1)S(1)} collective-permute-done((bf16[64,4096]{1,0:T(8,128)(2,1)S(1)}, bf16[64,4096]{1,0:T(8,128)(2,1)S(1)}, u32[]{:S(2)}, u32[]{:S(2)}) %collective-permute-start.16) | collective-permute-done | bytes 524320 | tf_op jit(solution)/shard_map/ppermute | solution.py:413
  89.4 5.3 %collective-permute-done.13 = bf16[64,4096]{1,0:T(8,128)(2,1)S(1)} collective-permute-done((bf16[64,4096]{1,0:T(8,128)(2,1)S(1)}, bf16[64,4096]{1,0:T(8,128)(2,1)S(1)}, u32[]{:S(2)}, u32[]{:S(2)}) %collective-permute-start.13) | collective-permute-done | bytes 524320 | tf_op jit(solution)/shard_map/ppermute | solution.py:413
  94.7 5.6 %collective-permute-done.17 = bf16[64,4096]{1,0:T(8,128)(2,1)S(1)} collective-permute-done((bf16[64,4096]{1,0:T(8,128)(2,1)S(1)}, bf16[64,4096]{1,0:T(8,128)(2,1)S(1)}, u32[]{:S(2)}, u32[]{:S(2)}) %collective-permute-start.17) | collective-permute-done | bytes 524320 | tf_op jit(solution)/shard_map/ppermute | solution.py:413
  100.3 1.1 %add_convert_fusion = bf16[64,4096]{1,0:T(8,128)(2,1)} fusion(bf16[64,4096]{1,0:T(8,128)(2,1)S(1)} %collective-permute-done.17, bf16[64,4096]{1,0:T(8,128)(2,1)S(1)} %collective-permute-done.14, bf16[64,4096]{1,0:T(8,128)(2,1)S(1)} %collective-permute-done.11, bf16[64,4096]{1,0:T(8,128)(2,1)S(1)} %get-tuple-element.87), kind=kLoop, calls=%fused_computation | loop fusion | flops 2097152 | bytes 2621440 | tf_op jit(solution)/shard_map/convert_element_type | solution.py:463
  (41 shorter events, 5.2 us)
Async XLA Ops:
  0.0 2.1 %collective-permute-start = (bf16[64,4096]{1,0:T(8,128)(2,1)}, bf16[64,4096]{1,0:T(8,128)(2,1)S(1)}, u32[]{:S(2)}, u32[]{:S(2)}) collective-permute-start(bf16[64,4096]{1,0:T(8,128)(2,1)} %far.1), channel_id=1, source_target_pairs={{0,1},{1,0},{2,3},{3,2},{4,5},{5,4},{6,7},{7,6},{8,9},{9,8},{10,11... | collective-permute-start | bytes 1572872 | tf_op jit(solution)/shard_map/ppermute | solution.py:417
  3.2 10.5 %collective-permute-start.1 = (bf16[64,4096]{1,0:T(8,128)(2,1)S(1)}, bf16[64,4096]{1,0:T(8,128)(2,1)S(1)}, u32[]{:S(2)}, u32[]{:S(2)}) collective-permute-start(bf16[64,4096]{1,0:T(8,128)(2,1)S(1)} %get-tuple-element.55), channel_id=1, source_target_pairs={{0,2},{1,7},{2,4},{3,1},{4,6},{5,3},{6,0},{7,5},{8,10},{9,15},{10,... | collective-permute-start | bytes 1572872 | tf_op jit(solution)/shard_map/ppermute | solution.py:413
  4.9 14.4 %collective-permute-start.3 = (bf16[64,4096]{1,0:T(8,128)(2,1)S(1)}, bf16[64,4096]{1,0:T(8,128)(2,1)S(1)}, u32[]{:S(2)}, u32[]{:S(2)}) collective-permute-start(bf16[64,4096]{1,0:T(8,128)(2,1)S(1)} %get-tuple-element.59), channel_id=1, source_target_pairs={{0,2},{1,7},{2,4},{3,1},{4,6},{5,3},{6,0},{7,5},{8,10},{9,15},{10,... | collective-permute-start | bytes 1572872 | tf_op jit(solution)/shard_map/ppermute | solution.py:413
  13.7 5.6 %collective-permute-start.5 = (bf16[8,4096]{1,0:T(8,128)(2,1)S(1)}, bf16[8,4096]{1,0:T(8,128)(2,1)S(1)}, u32[]{:S(2)}, u32[]{:S(2)}) collective-permute-start(bf16[8,4096]{1,0:T(8,128)(2,1)S(1)} %get-tuple-element.60), channel_id=1, source_target_pairs={{7,13},{6,11},{15,21},{14,19},{23,29},{22,27},{31,37},{30,35},{39,... | collective-permute-start | bytes 196616 | tf_op jit(solution)/shard_map/ppermute | solution.py:432
  14.4 5.0 %collective-permute-start.4 = (bf16[8,4096]{1,0:T(8,128)(2,1)S(1)}, bf16[8,4096]{1,0:T(8,128)(2,1)S(1)}, u32[]{:S(2)}, u32[]{:S(2)}) collective-permute-start(bf16[8,4096]{1,0:T(8,128)(2,1)S(1)} %get-tuple-element.60), channel_id=1, source_target_pairs={{7,15},{6,9},{15,23},{14,17},{23,31},{22,25},{31,39},{30,33},{39,4... | collective-permute-start | bytes 196616 | tf_op jit(solution)/shard_map/ppermute | solution.py:432
  15.0 7.0 %collective-permute-start.7 = (bf16[64,4096]{1,0:T(8,128)(2,1)S(1)}, bf16[64,4096]{1,0:T(8,128)(2,1)S(1)}, u32[]{:S(2)}, u32[]{:S(2)}) collective-permute-start(bf16[64,4096]{1,0:T(8,128)(2,1)S(1)} %collective-permute-done.1.mine), channel_id=1, source_target_pairs={{0,1},{1,0},{2,3},{3,2},{4,5},{5,4},{6,7},{7,6},{8,9},{9,8},{10,11... | collective-permute-start | bytes 1572872 | tf_op jit(solution)/shard_map/ppermute | solution.py:417
  15.1 14.2 %collective-permute-start.2 = (bf16[64,4096]{1,0:T(8,128)(2,1)S(1)}, bf16[64,4096]{1,0:T(8,128)(2,1)S(1)}, u32[]{:S(2)}, u32[]{:S(2)}) collective-permute-start(bf16[64,4096]{1,0:T(8,128)(2,1)S(1)} %collective-permute-done.1.mine), channel_id=1, source_target_pairs={{0,2},{1,7},{2,4},{3,1},{4,6},{5,3},{6,0},{7,5},{8,10},{9,15},{10,... | collective-permute-start | bytes 1572872 | tf_op jit(solution)/shard_map/ppermute | solution.py:413
  19.3 10.0 %collective-permute-start.6 = (bf16[64,4096]{1,0:T(8,128)(2,1)S(1)}, bf16[64,4096]{1,0:T(8,128)(2,1)S(1)}, u32[]{:S(2)}, u32[]{:S(2)}) collective-permute-start(bf16[64,4096]{1,0:T(8,128)(2,1)S(1)} %collective-permute-done.3.mine), channel_id=1, source_target_pairs={{0,1},{1,0},{2,3},{3,2},{4,5},{5,4},{6,7},{7,6},{8,9},{9,8},{10,11... | collective-permute-start | bytes 1572872 | tf_op jit(solution)/shard_map/ppermute | solution.py:417
  23.3 8.0 %copy-start = (f32[4,512]{1,0:T(4,128)S(1)}, f32[4,512]{1,0:T(4,128)}, u32[]{:S(2)}) copy-start(f32[4,512]{1,0:T(4,128)} %refs_16_.1) | copy-start | bytes 24580
  23.3 8.0 %copy-start.1 = (f32[4,256]{1,0:T(4,128)S(1)}, f32[4,256]{1,0:T(4,128)}, u32[]{:S(2)}) copy-start(f32[4,256]{1,0:T(4,128)} %refs_17_.1) | copy-start | bytes 12292
  23.4 8.0 %copy-start.3 = (f32[8]{0:T(128)S(1)}, f32[8]{0:T(128)}, u32[]{:S(2)}) copy-start(f32[8]{0:T(128)} %bias.1) | copy-start | bytes 100
  29.3 2.0 %collective-permute-start.8 = (bf16[64,4096]{1,0:T(8,128)(2,1)S(1)}, bf16[64,4096]{1,0:T(8,128)(2,1)S(1)}, u32[]{:S(2)}, u32[]{:S(2)}) collective-permute-start(bf16[64,4096]{1,0:T(8,128)(2,1)S(1)} %collective-permute-done.2.refs_9_), channel_id=1, source_target_pairs={{0,1},{1,0},{2,3},{3,2},{4,5},{5,4},{6,7},{7,6},{8,9},{9,8},{10,11... | collective-permute-start | bytes 1572872 | tf_op jit(solution)/shard_map/ppermute | solution.py:417
  29.3 2.0 %collective-permute-start.9 = (bf16[8,4096]{1,0:T(8,128)(2,1)S(1)}, bf16[8,4096]{1,0:T(8,128)(2,1)S(1)}, u32[]{:S(2)}, u32[]{:S(2)}) collective-permute-start(bf16[8,4096]{1,0:T(8,128)(2,1)S(1)} %add.24.refs_11_), channel_id=1, source_target_pairs={{0,1},{1,0},{2,3},{3,2},{4,5},{5,4},{6,7},{7,6},{8,9},{9,8},{10,11... | collective-permute-start | bytes 196616 | tf_op jit(solution)/shard_map/ppermute | solution.py:417
  31.3 31.2 %copy-start.5 = (f32[8]{0:T(128)S(1)}, f32[8]{0:T(128)}, u32[]{:S(2)}) copy-start(f32[8]{0:T(128)} %skip.1) | copy-start | bytes 100
  31.4 41.0 %copy-start.2 = (f32[512]{0:T(512)S(1)}, f32[512]{0:T(512)}, u32[]{:S(2)}) copy-start(f32[512]{0:T(512)} %param.20) | copy-start | bytes 6148
  58.1 14.2 %all-to-all-start.1 = ((bf16[32,16,128]{2,1,0:T(8,128)(2,1)}), bf16[32,16,128]{2,1,0:T(8,128)(2,1)S(1)}, u32[]{:S(2)}, u32[]{:S(2)}) async-start(bf16[32,16,128]{2,1,0:T(8,128)(2,1)} %prefix.1), calls=%async_computation.1 | async-start | bytes 262144 | tf_op jit(solution)/shard_map/all_to_all | solution.py:451
  75.6 2.0 %collective-permute-start.10 = (bf16[64,4096]{1,0:T(8,128)(2,1)S(1)}, bf16[64,4096]{1,0:T(8,128)(2,1)S(1)}, u32[]{:S(2)}, u32[]{:S(2)}) collective-permute-start(bf16[64,4096]{1,0:T(8,128)(2,1)S(1)} %get-tuple-element.89), channel_id=1, source_target_pairs={{0,1},{1,0},{2,3},{3,2},{4,5},{5,4},{6,7},{7,6},{8,9},{9,8},{10,11... | collective-permute-start | bytes 1572872 | tf_op jit(solution)/shard_map/ppermute | solution.py:417
  77.7 2.0 %collective-permute-start.12 = (bf16[64,4096]{1,0:T(8,128)(2,1)S(1)}, bf16[64,4096]{1,0:T(8,128)(2,1)S(1)}, u32[]{:S(2)}, u32[]{:S(2)}) collective-permute-start(bf16[64,4096]{1,0:T(8,128)(2,1)S(1)} %get-tuple-element.95), channel_id=1, source_target_pairs={{0,1},{1,0},{2,3},{3,2},{4,5},{5,4},{6,7},{7,6},{8,9},{9,8},{10,11... | collective-permute-start | bytes 1572872 | tf_op jit(solution)/shard_map/ppermute | solution.py:417
  78.2 16.5 %collective-permute-start.11 = (bf16[64,4096]{1,0:T(8,128)(2,1)S(1)}, bf16[64,4096]{1,0:T(8,128)(2,1)S(1)}, u32[]{:S(2)}, u32[]{:S(2)}) collective-permute-start(bf16[64,4096]{1,0:T(8,128)(2,1)S(1)} %get-tuple-element.93), channel_id=1, source_target_pairs={{0,1},{1,0},{2,3},{3,2},{4,5},{5,4},{6,7},{7,6},{8,9},{9,8},{10,11... | collective-permute-start | bytes 1572872 | tf_op jit(solution)/shard_map/ppermute | solution.py:417
  78.3 2.9 %collective-permute-start.15 = (bf16[64,4096]{1,0:T(8,128)(2,1)S(1)}, bf16[64,4096]{1,0:T(8,128)(2,1)S(1)}, u32[]{:S(2)}, u32[]{:S(2)}) collective-permute-start(bf16[64,4096]{1,0:T(8,128)(2,1)S(1)} %get-tuple-element.97), channel_id=1, source_target_pairs={{0,1},{1,0},{2,3},{3,2},{4,5},{5,4},{6,7},{7,6},{8,9},{9,8},{10,11... | collective-permute-start | bytes 1572872 | tf_op jit(solution)/shard_map/ppermute | solution.py:417
  78.7 10.4 %collective-permute-start.16 = (bf16[64,4096]{1,0:T(8,128)(2,1)S(1)}, bf16[64,4096]{1,0:T(8,128)(2,1)S(1)}, u32[]{:S(2)}, u32[]{:S(2)}) collective-permute-start(bf16[64,4096]{1,0:T(8,128)(2,1)S(1)} %add_convert_fusion.3), channel_id=1, source_target_pairs={{0,2},{1,7},{2,4},{3,1},{4,6},{5,3},{6,0},{7,5},{8,10},{9,15},{10,... | collective-permute-start | bytes 1572872 | tf_op jit(solution)/shard_map/ppermute | solution.py:413
  79.9 14.9 %collective-permute-start.13 = (bf16[64,4096]{1,0:T(8,128)(2,1)S(1)}, bf16[64,4096]{1,0:T(8,128)(2,1)S(1)}, u32[]{:S(2)}, u32[]{:S(2)}) collective-permute-start(bf16[64,4096]{1,0:T(8,128)(2,1)S(1)} %add_convert_fusion.2), channel_id=1, source_target_pairs={{0,2},{1,7},{2,4},{3,1},{4,6},{5,3},{6,0},{7,5},{8,10},{9,15},{10,... | collective-permute-start | bytes 1572872 | tf_op jit(solution)/shard_map/ppermute | solution.py:413
  89.3 11.0 %collective-permute-start.17 = (bf16[64,4096]{1,0:T(8,128)(2,1)S(1)}, bf16[64,4096]{1,0:T(8,128)(2,1)S(1)}, u32[]{:S(2)}, u32[]{:S(2)}) collective-permute-start(bf16[64,4096]{1,0:T(8,128)(2,1)S(1)} %add_convert_fusion.1), channel_id=1, source_target_pairs={{0,2},{1,7},{2,4},{3,1},{4,6},{5,3},{6,0},{7,5},{8,10},{9,15},{10,... | collective-permute-start | bytes 1572872 | tf_op jit(solution)/shard_map/ppermute | solution.py:413
  94.7 5.6 %collective-permute-start.14 = (bf16[64,4096]{1,0:T(8,128)(2,1)S(1)}, bf16[64,4096]{1,0:T(8,128)(2,1)S(1)}, u32[]{:S(2)}, u32[]{:S(2)}) collective-permute-start(bf16[64,4096]{1,0:T(8,128)(2,1)S(1)} %collective-permute-done.13), channel_id=1, source_target_pairs={{0,1},{1,0},{2,3},{3,2},{4,5},{5,4},{6,7},{7,6},{8,9},{9,8},{10,11... | collective-permute-start | bytes 1572872 | tf_op jit(solution)/shard_map/ppermute | solution.py:417
  (1 other events, 8.0 us)

commit v11 on v10

--- a/solution.py
+++ b/solution.py
@@ -332,10 +332,8 @@
 
 
 def norm_kernel(s_in, e, d, c, cs, ydiag, gain, w_far, other, own, rest, w, nb, sem):
-    blocks = [pl.ds(1024 * j, 1024) for j in range(4)]
-    copies = [pltpu.make_async_copy(w_far.at[:, k], w.at[:, k], sem.at[j]) for j, k in enumerate(blocks)]
-    for copy in copies:
-        copy.start()
+    copy = pltpu.make_async_copy(w_far, w, sem)
+    copy.start()
     y = chip()
     mine = core()
     ones = head_spread()
@@ -361,11 +359,10 @@
 
     a = lax.rem(y + 2, NQ)
     v = jnp.concatenate([half(a, 1 - mine), half(a, mine)], 0)
-    for k, copy in zip(blocks, copies):
-        copy.wait()
-        o = jnp.dot(v, w[:, k], preferred_element_type=F32).astype(BF)
-        other[:, k] = o[0:64]
-        own[:, k] = o[64:128]
+    copy.wait()
+    v = jnp.dot(v, w[...], preferred_element_type=F32).astype(BF)
+    other[...] = v[0:64]
+    own[...] = v[64:128]
     side, across = lax.rem(y + 1 + 2 * mine, NQ), lax.rem(y + 3 - 2 * mine, NQ)
     parts = ((across, mine), (across, 1 - mine), (side, 1 - mine), (side, mine), (y, 1 - mine), (y, mine))
     for j, (a, h) in enumerate(parts):
@@ -379,7 +376,7 @@
         out_shape=(s((64, 4096), BF), s((64, 4096), BF), s((384, CH), BF), s((CH, 4096), BF)),
         in_specs=[VMEM] * 7 + [pl.BlockSpec(memory_space=pltpu.HBM)],
         out_specs=(VMEM,) * 4,
-        scratch_shapes=[pltpu.VMEM((NQ, Q, CH), BF), pltpu.SemaphoreType.DMA((4,))],
+        scratch_shapes=[pltpu.VMEM((NQ, Q, CH), BF), pltpu.SemaphoreType.DMA],
         compiler_params=params(),
         name="norm_part",
     )(*[in_vmem(v) for v in args[:7]], pltpu.with_memory_space_constraint(args[7], pltpu.HBM))
@@ -434,12 +431,11 @@
         )
 
     edge_a, edge_b = onward((7, 7), (6, 1)), onward((7, 5), (6, 3))
-    s1 = swap(r1)
-    r2, edge_a, edge_b = after((r2, edge_a, edge_b))
-    s2 = swap(r2)
+    s1, r2 = after((swap(r1), r2))
     piece1 = project_half(r1, s1, weights, "project_one")
-    far, s2, *piece1 = after((far, s2, *piece1))
-    piece2 = project_half(r2, s2, weights, "project_two")
+    far, r2, *piece1 = after((far, r2, *piece1))
+    piece2 = project_half(r2, swap(r2), weights, "project_two")
+    edge_a, edge_b, far = after((edge_a, edge_b, far))
     edge = edge_a + edge_b
     edges = swap(edge)
 

time: 102 us -> 99.6 us (0.976)
  starting transfers between devices: 14.1 us -> 12.3 us
    ppermute x10, starting transfers between devices: 4.53 us -> 1.8 us  [swap(): return lax.ppermute(v, 'tp', SWAP)]
where the time goes in v11:
time: 99.6 us; the launch traced here: 99.3 us
  waiting for transfers between devices  43.1 us (43%)
  blocking collectives  21.8 us (22%)
  Pallas kernels  20.3 us (20%)
  starting transfers between devices  12.3 us (12%)
  other arithmetic  1.52 us (2%)
    ppermute x6, waiting for transfers between devices, around(): return lax.ppermute(v, 'tp', AROUND)  30.4 us
    all_to_all x1, blocking collectives, per_device(): got = lax.all_to_all(send, 'ctx', 0, 0, tiled=True)  21.8 us
    all_to_all x1, waiting for transfers between devices, per_device(): back = lax.all_to_all(prefix(got), 'ctx', 0, 0, tiled=True)  7.92 us
    pallas_call x1, Pallas kernels, local_part(): pl.pallas_call(local_kernel, out_shape=(s((NQ, Q, CH), BF), s((NQ, Q, NS)...  4.84 us
    ppermute x10, waiting for transfers between devices, swap(): return lax.ppermute(v, 'tp', SWAP)  4.78 us
    ppermute x6, starting transfers between devices, around(): return lax.ppermute(v, 'tp', AROUND)  4.71 us
    pallas_call x1, Pallas kernels, project_near(): pl.pallas_call(near_kernel, out_shape=(pltpu.VMEM((Q, CH), BF), pltpu.VME...  4.51 us
    all_to_all x1, starting transfers between devices, per_device(): back = lax.all_to_all(prefix(got), 'ctx', 0, 0, tiled=True)  4.46 us
  transfers between devices with their start and end apart: 19, of which 12 were waited for; matrix products, arithmetic and copies ran while one was open for 0% of the time, Pallas kernels for 11%

profile of v11, /device:TPU:32, one launch (start us, length us, event | category | flops | bytes accessed | tf_op | source)
XLA Modules:
  0.0 99.3 jit_solution(14868615708101473635)
XLA Ops:
  0.0 2.1 %collective-permute-done.theirs = bf16[64,4096]{1,0:T(8,128)(2,1)S(1)} collective-permute-done((bf16[64,4096]{1,0:T(8,128)(2,1)}, bf16[64,4096]{1,0:T(8,128)(2,1)S(1)}, u32[]{:S(2)}, u32[]{:S(2)}) %collective-permute-start) | collective-permute-done | bytes 524320 | tf_op jit(solution)/shard_map/ppermute | solution.py:414
  2.1 1.1 %pack.1 = (bf16[64,4096]{1,0:T(8,128)(2,1)S(1)}, bf16[64,4096]{1,0:T(8,128)(2,1)S(1)}, bf16[8,4096]{1,0:T(8,128)(2,1)S(1)}) custom-call(bf16[64,4096]{1,0:T(8,128)(2,1)} %far.1, bf16[64,4096]{1,0:T(8,128)(2,1)S(1)} %collective-permute-done.theirs), custom_call_target="tpu_custom_call" | custom-call | tf_op jit(solution)/shard_map/pack/pallas_call | solution.py:87
  3.2 1.7 %collective-permute-start.1 = (bf16[64,4096]{1,0:T(8,128)(2,1)S(1)}, bf16[64,4096]{1,0:T(8,128)(2,1)S(1)}, u32[]{:S(2)}, u32[]{:S(2)}) collective-permute-start(bf16[64,4096]{1,0:T(8,128)(2,1)S(1)} %get-tuple-element.57), channel_id=1, source_target_pairs={{0,2},{1,7},{2,4},{3,1},{4,6},{5,3},{6,0},{7,5},{8,10},{9,15},{10,... | collective-permute-start | bytes 1572872 | tf_op jit(solution)/shard_map/ppermute | solution.py:410
  4.9 1.6 %collective-permute-start.4 = (bf16[64,4096]{1,0:T(8,128)(2,1)S(1)}, bf16[64,4096]{1,0:T(8,128)(2,1)S(1)}, u32[]{:S(2)}, u32[]{:S(2)}) collective-permute-start(bf16[64,4096]{1,0:T(8,128)(2,1)S(1)} %get-tuple-element.61), channel_id=1, source_target_pairs={{0,2},{1,7},{2,4},{3,1},{4,6},{5,3},{6,0},{7,5},{8,10},{9,15},{10,... | collective-permute-start | bytes 1572872 | tf_op jit(solution)/shard_map/ppermute | solution.py:410
  6.5 4.5 %project_near.1 = (bf16[128,512]{1,0:T(8,128)(2,1)S(1)}, bf16[128,256]{1,0:T(8,128)(2,1)S(1)}, f32[128,8]{1,0:T(8,128)S(1)}, bf16[4096,512]{1,0:T(8,128)(2,1)S(1...) custom-call(bf16[64,4096]{1,0:T(8,128)(2,1)} %far.1, bf16[64,4096]{1,0:T(8,128)(2,1)S(1)} %collective-permute-done.theirs, ...), custom_call_target="tpu_custom_call" | custom-call | tf_op jit(solution)/shard_map/project_near/pallas_call | solution.py:141
  11.0 2.7 %collective-permute-done.1.mine = bf16[64,4096]{1,0:T(8,128)(2,1)S(1)} collective-permute-done((bf16[64,4096]{1,0:T(8,128)(2,1)S(1)}, bf16[64,4096]{1,0:T(8,128)(2,1)S(1)}, u32[]{:S(2)}, u32[]{:S(2)}) %collective-permute-start.1) | collective-permute-done | bytes 524320 | tf_op jit(solution)/shard_map/ppermute | solution.py:410
  15.4 3.9 %collective-permute-done.4.mine = bf16[64,4096]{1,0:T(8,128)(2,1)S(1)} collective-permute-done((bf16[64,4096]{1,0:T(8,128)(2,1)S(1)}, bf16[64,4096]{1,0:T(8,128)(2,1)S(1)}, u32[]{:S(2)}, u32[]{:S(2)}) %collective-permute-start.4) | collective-permute-done | bytes 524320 | tf_op jit(solution)/shard_map/ppermute | solution.py:410
  19.3 1.3 %project_one.1 = (bf16[128,512]{1,0:T(8,128)(2,1)S(1)}, bf16[128,256]{1,0:T(8,128)(2,1)S(1)}, f32[128,8]{1,0:T(8,128)S(1)}) custom-call(bf16[64,4096]{1,0:T(8,128)(2,1)S(1)} %collective-permute-done.1.mine, bf16[64,4096]{1,0:T(8,128)(2,1)S(1)} %collective-permute-done.3.theirs, bf16[4096,512]{1,0:T(8,128)(2,1)S(1)} %get-tuple-element.58.wx.refs_13_, ...), custom_call_target="tpu_custom_call" | custom-call | tf_op jit(solution)/shard_map/project_one/pallas_call | solution.py:106
  20.6 5.0 %collective-permute-done.2.refs_9_ = bf16[64,4096]{1,0:T(8,128)(2,1)S(1)} collective-permute-done((bf16[64,4096]{1,0:T(8,128)(2,1)S(1)}, bf16[64,4096]{1,0:T(8,128)(2,1)S(1)}, u32[]{:S(2)}, u32[]{:S(2)}) %collective-permute-start.2) | collective-permute-done | bytes 524320 | tf_op jit(solution)/shard_map/ppermute | solution.py:410
  26.4 1.2 %collective-permute-done.5.theirs = bf16[64,4096]{1,0:T(8,128)(2,1)S(1)} collective-permute-done((bf16[64,4096]{1,0:T(8,128)(2,1)S(1)}, bf16[64,4096]{1,0:T(8,128)(2,1)S(1)}, u32[]{:S(2)}, u32[]{:S(2)}) %collective-permute-start.5) | collective-permute-done | bytes 524320 | tf_op jit(solution)/shard_map/ppermute | solution.py:414
  27.5 1.3 %project_two.1 = (bf16[128,512]{1,0:T(8,128)(2,1)S(1)}, bf16[128,256]{1,0:T(8,128)(2,1)S(1)}, f32[128,8]{1,0:T(8,128)S(1)}) custom-call(bf16[64,4096]{1,0:T(8,128)(2,1)S(1)} %collective-permute-done.4.mine, bf16[64,4096]{1,0:T(8,128)(2,1)S(1)} %collective-permute-done.5.theirs, bf16[4096,512]{1,0:T(8,128)(2,1)S(1)} %get-tuple-element.58.wx.refs_13_, ...), custom_call_target="tpu_custom_call" | custom-call | tf_op jit(solution)/shard_map/project_two/pallas_call | solution.py:106
  28.9 4.8 %local_part.1 = (bf16[4,128,512]{2,1,0:T(8,128)(2,1)S(1)}, bf16[4,128,128]{2,1,0:T(8,128)(2,1)S(1)}, bf16[4,128,128]{2,1,0:T(8,128)(2,1)S(1)}, f32[4,8,128]{2,1,...) custom-call(f32[8]{0:T(128)S(1)} %copy-done.3, ...), custom_call_target="tpu_custom_call" | custom-call | tf_op jit(solution)/shard_map/local_part/pallas_call | solution.py:256
  33.8 21.8 %all_to_all.10.r = bf16[32,24,128]{2,1,0:T(8,128)(2,1)S(1)} all-to-all(bf16[32,24,128]{2,1,0:T(8,128)(2,1)S(1)} %get-tuple-element.81), channel_id=1, replica_groups=mesh['ctx'=32,'tp'=8] {'ctx'}, dimensions={0} | all-to-all | bytes 393216 | tf_op jit(solution)/shard_map/all_to_all | solution.py:445
  56.3 4.5 %all-to-all-start.1 = ((bf16[32,16,128]{2,1,0:T(8,128)(2,1)}), bf16[32,16,128]{2,1,0:T(8,128)(2,1)S(1)}, u32[]{:S(2)}, u32[]{:S(2)}) async-start(bf16[32,16,128]{2,1,0:T(8,128)(2,1)} %prefix.1), calls=%async_computation.1 | async-start | bytes 262144 | tf_op jit(solution)/shard_map/all_to_all | solution.py:447
  60.8 1.8 %diag_part.1.ydiag = f32[4,128,512]{2,1,0:T(8,128)S(1)} custom-call(f32[8]{0:T(128)S(1)} %copy-done.5, bf16[4,128,512]{2,1,0:T(8,128)(2,1)S(1)} %get-tuple-element.86.x, bf16[4,128,128]{2,1,0:T(8,128)(2,1)S(1)} %get-tuple-element.87.b, bf16[4,128,128]{2,1,0:T(8,128)(2,1)S(1)} %get-tuple-element.84.c, f32[4,8,128]{2,1,0:T(8,128)S(1)} %get-tuple-element.85.cs, ...), custom_call_target="tpu_custom_call" | custom-call | tf_op jit(solution)/shard_map/diag_part/pallas_call | solution.py:324
  62.6 7.9 %all-to-all-done.1 = bf16[32,16,128]{2,1,0:T(8,128)(2,1)S(1)} async-done(((bf16[32,16,128]{2,1,0:T(8,128)(2,1)}), bf16[32,16,128]{2,1,0:T(8,128)(2,1)S(1)}, u32[]{:S(2)}, u32[]{:S(2)}) %all-to-all-start.1) | async-done | bytes 131104 | tf_op jit(solution)/shard_map/all_to_all | solution.py:447
  70.5 2.9 %norm_part.1 = (bf16[64,4096]{1,0:T(8,128)(2,1)S(1)}, bf16[64,4096]{1,0:T(8,128)(2,1)S(1)}, bf16[384,512]{1,0:T(8,128)(2,1)S(1)}, bf16[512,4096]{1,0:T(8,128)(2,1)S(1)}) custom-call(bf16[512,128]{1,0:T(8,128)(2,1)S(1)} %bitcast.3, f32[4,128,512]{2,1,0:T(8,128)S(1)} %get-tuple-element.82.e, f32[4,8,512]{2,1,0:T(8,128)S(1)} %get-tuple-element.83.d, ...), custom_call_target="tpu_custom_call" | custom-call | tf_op jit(solution)/shard_map/norm_part/pallas_call | solution.py:374
  73.6 1.8 %out_part.1 = (bf16[64,4096]{1,0:T(8,128)(2,1)S(1)}, bf16[64,4096]{1,0:T(8,128)(2,1)S(1)}, bf16[64,4096]{1,0:T(8,128)(2,1)S(1)}, bf16[64,4096]{1,0:T(8,128)(2,1)...) custom-call(bf16[384,512]{1,0:T(8,128)(2,1)S(1)} %get-tuple-element.89.n, ...), custom_call_target="tpu_custom_call" | custom-call | tf_op jit(solution)/shard_map/out_part/pallas_call | solution.py:393
  76.7 0.9 collective-permute-done.12
  77.8 0.9 collective-permute-start.13
  79.1 7.9 %collective-permute-done.16 = bf16[64,4096]{1,0:T(8,128)(2,1)S(1)} collective-permute-done((bf16[64,4096]{1,0:T(8,128)(2,1)S(1)}, bf16[64,4096]{1,0:T(8,128)(2,1)S(1)}, u32[]{:S(2)}, u32[]{:S(2)}) %collective-permute-start.16) | collective-permute-done | bytes 524320 | tf_op jit(solution)/shard_map/ppermute | solution.py:410
  87.3 5.3 %collective-permute-done.13 = bf16[64,4096]{1,0:T(8,128)(2,1)S(1)} collective-permute-done((bf16[64,4096]{1,0:T(8,128)(2,1)S(1)}, bf16[64,4096]{1,0:T(8,128)(2,1)S(1)}, u32[]{:S(2)}, u32[]{:S(2)}) %collective-permute-start.13) | collective-permute-done | bytes 524320 | tf_op jit(solution)/shard_map/ppermute | solution.py:410
  92.6 5.6 %collective-permute-done.17 = bf16[64,4096]{1,0:T(8,128)(2,1)S(1)} collective-permute-done((bf16[64,4096]{1,0:T(8,128)(2,1)S(1)}, bf16[64,4096]{1,0:T(8,128)(2,1)S(1)}, u32[]{:S(2)}, u32[]{:S(2)}) %collective-permute-start.17) | collective-permute-done | bytes 524320 | tf_op jit(solution)/shard_map/ppermute | solution.py:410
  98.2 1.1 %add_convert_fusion = bf16[64,4096]{1,0:T(8,128)(2,1)} fusion(bf16[64,4096]{1,0:T(8,128)(2,1)S(1)} %collective-permute-done.17, bf16[64,4096]{1,0:T(8,128)(2,1)S(1)} %collective-permute-done.14, bf16[64,4096]{1,0:T(8,128)(2,1)S(1)} %collective-permute-done.11, bf16[64,4096]{1,0:T(8,128)(2,1)S(1)} %get-tuple-element.91), kind=kLoop, calls=%fused_computation | loop fusion | flops 2097152 | bytes 2621440 | tf_op jit(solution)/shard_map/convert_element_type | solution.py:459
  (41 shorter events, 5.5 us)
Async XLA Ops:
  0.0 2.1 %collective-permute-start = (bf16[64,4096]{1,0:T(8,128)(2,1)}, bf16[64,4096]{1,0:T(8,128)(2,1)S(1)}, u32[]{:S(2)}, u32[]{:S(2)}) collective-permute-start(bf16[64,4096]{1,0:T(8,128)(2,1)} %far.1), channel_id=1, source_target_pairs={{0,1},{1,0},{2,3},{3,2},{4,5},{5,4},{6,7},{7,6},{8,9},{9,8},{10,11... | collective-permute-start | bytes 1572872 | tf_op jit(solution)/shard_map/ppermute | solution.py:414
  3.2 10.5 %collective-permute-start.1 = (bf16[64,4096]{1,0:T(8,128)(2,1)S(1)}, bf16[64,4096]{1,0:T(8,128)(2,1)S(1)}, u32[]{:S(2)}, u32[]{:S(2)}) collective-permute-start(bf16[64,4096]{1,0:T(8,128)(2,1)S(1)} %get-tuple-element.57), channel_id=1, source_target_pairs={{0,2},{1,7},{2,4},{3,1},{4,6},{5,3},{6,0},{7,5},{8,10},{9,15},{10,... | collective-permute-start | bytes 1572872 | tf_op jit(solution)/shard_map/ppermute | solution.py:410
  4.9 14.4 %collective-permute-start.4 = (bf16[64,4096]{1,0:T(8,128)(2,1)S(1)}, bf16[64,4096]{1,0:T(8,128)(2,1)S(1)}, u32[]{:S(2)}, u32[]{:S(2)}) collective-permute-start(bf16[64,4096]{1,0:T(8,128)(2,1)S(1)} %get-tuple-element.61), channel_id=1, source_target_pairs={{0,2},{1,7},{2,4},{3,1},{4,6},{5,3},{6,0},{7,5},{8,10},{9,15},{10,... | collective-permute-start | bytes 1572872 | tf_op jit(solution)/shard_map/ppermute | solution.py:410
  13.7 5.6 %collective-permute-start.3 = (bf16[64,4096]{1,0:T(8,128)(2,1)S(1)}, bf16[64,4096]{1,0:T(8,128)(2,1)S(1)}, u32[]{:S(2)}, u32[]{:S(2)}) collective-permute-start(bf16[64,4096]{1,0:T(8,128)(2,1)S(1)} %collective-permute-done.1.mine), channel_id=1, source_target_pairs={{0,1},{1,0},{2,3},{3,2},{4,5},{5,4},{6,7},{7,6},{8,9},{9,8},{10,11... | collective-permute-start | bytes 1572872 | tf_op jit(solution)/shard_map/ppermute | solution.py:414
  13.7 11.9 %collective-permute-start.2 = (bf16[64,4096]{1,0:T(8,128)(2,1)S(1)}, bf16[64,4096]{1,0:T(8,128)(2,1)S(1)}, u32[]{:S(2)}, u32[]{:S(2)}) collective-permute-start(bf16[64,4096]{1,0:T(8,128)(2,1)S(1)} %collective-permute-done.1.mine), channel_id=1, source_target_pairs={{0,2},{1,7},{2,4},{3,1},{4,6},{5,3},{6,0},{7,5},{8,10},{9,15},{10,... | collective-permute-start | bytes 1572872 | tf_op jit(solution)/shard_map/ppermute | solution.py:410
  14.1 11.6 %collective-permute-start.7 = (bf16[8,4096]{1,0:T(8,128)(2,1)S(1)}, bf16[8,4096]{1,0:T(8,128)(2,1)S(1)}, u32[]{:S(2)}, u32[]{:S(2)}) collective-permute-start(bf16[8,4096]{1,0:T(8,128)(2,1)S(1)} %get-tuple-element.76), channel_id=1, source_target_pairs={{7,13},{6,11},{15,21},{14,19},{23,29},{22,27},{31,37},{30,35},{39,... | collective-permute-start | bytes 196616 | tf_op jit(solution)/shard_map/ppermute | solution.py:429
  14.7 10.9 %collective-permute-start.6 = (bf16[8,4096]{1,0:T(8,128)(2,1)S(1)}, bf16[8,4096]{1,0:T(8,128)(2,1)S(1)}, u32[]{:S(2)}, u32[]{:S(2)}) collective-permute-start(bf16[8,4096]{1,0:T(8,128)(2,1)S(1)} %get-tuple-element.76), channel_id=1, source_target_pairs={{7,15},{6,9},{15,23},{14,17},{23,31},{22,25},{31,39},{30,33},{39,4... | collective-permute-start | bytes 196616 | tf_op jit(solution)/shard_map/ppermute | solution.py:429
  20.6 8.3 %copy-start = (f32[4,512]{1,0:T(4,128)S(1)}, f32[4,512]{1,0:T(4,128)}, u32[]{:S(2)}) copy-start(f32[4,512]{1,0:T(4,128)} %refs_16_.1) | copy-start | bytes 24580
  20.6 8.3 %copy-start.1 = (f32[4,256]{1,0:T(4,128)S(1)}, f32[4,256]{1,0:T(4,128)}, u32[]{:S(2)}) copy-start(f32[4,256]{1,0:T(4,128)} %refs_17_.1) | copy-start | bytes 12292
  20.6 8.2 %copy-start.3 = (f32[8]{0:T(128)S(1)}, f32[8]{0:T(128)}, u32[]{:S(2)}) copy-start(f32[8]{0:T(128)} %bias.1) | copy-start | bytes 100
  25.6 1.9 %collective-permute-start.5 = (bf16[64,4096]{1,0:T(8,128)(2,1)S(1)}, bf16[64,4096]{1,0:T(8,128)(2,1)S(1)}, u32[]{:S(2)}, u32[]{:S(2)}) collective-permute-start(bf16[64,4096]{1,0:T(8,128)(2,1)S(1)} %collective-permute-done.4.mine), channel_id=1, source_target_pairs={{0,1},{1,0},{2,3},{3,2},{4,5},{5,4},{6,7},{7,6},{8,9},{9,8},{10,11... | collective-permute-start | bytes 1572872 | tf_op jit(solution)/shard_map/ppermute | solution.py:414
  25.6 3.2 %collective-permute-start.8 = (bf16[64,4096]{1,0:T(8,128)(2,1)S(1)}, bf16[64,4096]{1,0:T(8,128)(2,1)S(1)}, u32[]{:S(2)}, u32[]{:S(2)}) collective-permute-start(bf16[64,4096]{1,0:T(8,128)(2,1)S(1)} %collective-permute-done.2.refs_9_), channel_id=1, source_target_pairs={{0,1},{1,0},{2,3},{3,2},{4,5},{5,4},{6,7},{7,6},{8,9},{9,8},{10,11... | collective-permute-start | bytes 1572872 | tf_op jit(solution)/shard_map/ppermute | solution.py:414
  26.2 2.7 %collective-permute-start.9 = (bf16[8,4096]{1,0:T(8,128)(2,1)S(1)}, bf16[8,4096]{1,0:T(8,128)(2,1)S(1)}, u32[]{:S(2)}, u32[]{:S(2)}) collective-permute-start(bf16[8,4096]{1,0:T(8,128)(2,1)S(1)} %add.24.refs_11_), channel_id=1, source_target_pairs={{0,1},{1,0},{2,3},{3,2},{4,5},{5,4},{6,7},{7,6},{8,9},{9,8},{10,11... | collective-permute-start | bytes 196616 | tf_op jit(solution)/shard_map/ppermute | solution.py:414
  28.9 31.9 %copy-start.5 = (f32[8]{0:T(128)S(1)}, f32[8]{0:T(128)}, u32[]{:S(2)}) copy-start(f32[8]{0:T(128)} %skip.1) | copy-start | bytes 100
  28.9 41.6 %copy-start.2 = (f32[512]{0:T(512)S(1)}, f32[512]{0:T(512)}, u32[]{:S(2)}) copy-start(f32[512]{0:T(512)} %param.20) | copy-start | bytes 6148
  56.3 14.2 %all-to-all-start.1 = ((bf16[32,16,128]{2,1,0:T(8,128)(2,1)}), bf16[32,16,128]{2,1,0:T(8,128)(2,1)S(1)}, u32[]{:S(2)}, u32[]{:S(2)}) async-start(bf16[32,16,128]{2,1,0:T(8,128)(2,1)} %prefix.1), calls=%async_computation.1 | async-start | bytes 262144 | tf_op jit(solution)/shard_map/all_to_all | solution.py:447
  73.5 2.0 %collective-permute-start.10 = (bf16[64,4096]{1,0:T(8,128)(2,1)S(1)}, bf16[64,4096]{1,0:T(8,128)(2,1)S(1)}, u32[]{:S(2)}, u32[]{:S(2)}) collective-permute-start(bf16[64,4096]{1,0:T(8,128)(2,1)S(1)} %get-tuple-element.93), channel_id=1, source_target_pairs={{0,1},{1,0},{2,3},{3,2},{4,5},{5,4},{6,7},{7,6},{8,9},{9,8},{10,11... | collective-permute-start | bytes 1572872 | tf_op jit(solution)/shard_map/ppermute | solution.py:414
  75.6 2.0 %collective-permute-start.12 = (bf16[64,4096]{1,0:T(8,128)(2,1)S(1)}, bf16[64,4096]{1,0:T(8,128)(2,1)S(1)}, u32[]{:S(2)}, u32[]{:S(2)}) collective-permute-start(bf16[64,4096]{1,0:T(8,128)(2,1)S(1)} %get-tuple-element.99), channel_id=1, source_target_pairs={{0,1},{1,0},{2,3},{3,2},{4,5},{5,4},{6,7},{7,6},{8,9},{9,8},{10,11... | collective-permute-start | bytes 1572872 | tf_op jit(solution)/shard_map/ppermute | solution.py:414
  76.1 16.5 %collective-permute-start.11 = (bf16[64,4096]{1,0:T(8,128)(2,1)S(1)}, bf16[64,4096]{1,0:T(8,128)(2,1)S(1)}, u32[]{:S(2)}, u32[]{:S(2)}) collective-permute-start(bf16[64,4096]{1,0:T(8,128)(2,1)S(1)} %get-tuple-element.97), channel_id=1, source_target_pairs={{0,1},{1,0},{2,3},{3,2},{4,5},{5,4},{6,7},{7,6},{8,9},{9,8},{10,11... | collective-permute-start | bytes 1572872 | tf_op jit(solution)/shard_map/ppermute | solution.py:414
  76.2 2.9 %collective-permute-start.15 = (bf16[64,4096]{1,0:T(8,128)(2,1)S(1)}, bf16[64,4096]{1,0:T(8,128)(2,1)S(1)}, u32[]{:S(2)}, u32[]{:S(2)}) collective-permute-start(bf16[64,4096]{1,0:T(8,128)(2,1)S(1)} %get-tuple-element.101), channel_id=1, source_target_pairs={{0,1},{1,0},{2,3},{3,2},{4,5},{5,4},{6,7},{7,6},{8,9},{9,8},{10,11... | collective-permute-start | bytes 1572872 | tf_op jit(solution)/shard_map/ppermute | solution.py:414
  76.6 10.4 %collective-permute-start.16 = (bf16[64,4096]{1,0:T(8,128)(2,1)S(1)}, bf16[64,4096]{1,0:T(8,128)(2,1)S(1)}, u32[]{:S(2)}, u32[]{:S(2)}) collective-permute-start(bf16[64,4096]{1,0:T(8,128)(2,1)S(1)} %add_convert_fusion.3), channel_id=1, source_target_pairs={{0,2},{1,7},{2,4},{3,1},{4,6},{5,3},{6,0},{7,5},{8,10},{9,15},{10,... | collective-permute-start | bytes 1572872 | tf_op jit(solution)/shard_map/ppermute | solution.py:410
  77.8 14.9 %collective-permute-start.13 = (bf16[64,4096]{1,0:T(8,128)(2,1)S(1)}, bf16[64,4096]{1,0:T(8,128)(2,1)S(1)}, u32[]{:S(2)}, u32[]{:S(2)}) collective-permute-start(bf16[64,4096]{1,0:T(8,128)(2,1)S(1)} %add_convert_fusion.2), channel_id=1, source_target_pairs={{0,2},{1,7},{2,4},{3,1},{4,6},{5,3},{6,0},{7,5},{8,10},{9,15},{10,... | collective-permute-start | bytes 1572872 | tf_op jit(solution)/shard_map/ppermute | solution.py:410
  87.2 11.0 %collective-permute-start.17 = (bf16[64,4096]{1,0:T(8,128)(2,1)S(1)}, bf16[64,4096]{1,0:T(8,128)(2,1)S(1)}, u32[]{:S(2)}, u32[]{:S(2)}) collective-permute-start(bf16[64,4096]{1,0:T(8,128)(2,1)S(1)} %add_convert_fusion.1), channel_id=1, source_target_pairs={{0,2},{1,7},{2,4},{3,1},{4,6},{5,3},{6,0},{7,5},{8,10},{9,15},{10,... | collective-permute-start | bytes 1572872 | tf_op jit(solution)/shard_map/ppermute | solution.py:410
  92.6 5.6 %collective-permute-start.14 = (bf16[64,4096]{1,0:T(8,128)(2,1)S(1)}, bf16[64,4096]{1,0:T(8,128)(2,1)S(1)}, u32[]{:S(2)}, u32[]{:S(2)}) collective-permute-start(bf16[64,4096]{1,0:T(8,128)(2,1)S(1)} %collective-permute-done.13), channel_id=1, source_target_pairs={{0,1},{1,0},{2,3},{3,2},{4,5},{5,4},{6,7},{7,6},{8,9},{9,8},{10,11... | collective-permute-start | bytes 1572872 | tf_op jit(solution)/shard_map/ppermute | solution.py:414
  (1 other events, 8.2 us)

commit v12 on v11

--- a/solution.py
+++ b/solution.py
@@ -61,12 +61,6 @@
 
 def in_vmem(v):
     return pltpu.with_memory_space_constraint(v, pltpu.VMEM)
-
-
-def place(tok, ref, base, half):
-    at = base + half * 32
-    tok[pl.ds(pl.multiple_of(at, 32), 32), :] = ref[0:32, :]
-    tok[pl.ds(pl.multiple_of(at + 64, 32), 32), :] = ref[32:64, :]
 
 
 def pack_kernel(far, theirs, first, second, last, mine, sem):
@@ -177,14 +171,11 @@
     far, far_swap, halo, haloswap = refs[9:13]
     wx, wbc, wdt, kx, kbc = refs[13:18]
     (xo, bo, co, cso, dto, eo, do, send) = refs[18:26]
-    ext, extb, dtr, tok = refs[26:30]
+    ext, extb, dtr = refs[26:29]
     y = chip()
     c = core()
-    place(tok, far, 0, c)
-    place(tok, far_swap, 0, 1 - c)
     edge = halo[...].astype(F32) + haloswap[...].astype(F32)
-    tok[Q : Q + 16, :] = jnp.concatenate([edge, edge], 0).astype(BF)
-    rows = tok[...]
+    rows = jnp.concatenate([far[...], far_swap[...], jnp.concatenate([edge, edge], 0).astype(BF)], 0)
     x3 = jnp.dot(rows, wx[...], preferred_element_type=F32).astype(BF).astype(F32)
     bc3 = jnp.dot(rows, wbc[...], preferred_element_type=F32).astype(BF).astype(F32)
     dt3 = dot_nt(rows[0:Q], wdt[...])
@@ -197,7 +188,10 @@
         dtr[pl.ds(pl.multiple_of(at, 8), n), :] = pdt
 
     put(y * Q, Q, near[0][...], near[1][...], near[2][...])
-    put(lax.rem(y + 2, NQ) * Q, Q, x3[0:Q], bc3[0:Q], dt3)
+    for j in range(4):
+        at = lax.rem(y + 2, NQ) * Q + (c, 1 - c)[j // 2] * 32 + (j % 2) * 64
+        of = slice(32 * j, 32 * j + 32)
+        put(at, 32, x3[of], bc3[of], dt3[of])
     sides = (lax.rem(y + 3 - 2 * c, NQ), lax.rem(y + 1 + 2 * c, NQ))
     for piece, halves in ((one, (c, 1 - c)), (two, (1 - c, c))):
         for j in range(4):
@@ -271,7 +265,6 @@
             pltpu.VMEM((8 + NQ * Q, CH), F32),
             pltpu.VMEM((8 + NQ * Q, BCW), F32),
             pltpu.VMEM((NQ * Q, HH), F32),
-            pltpu.VMEM((Q + 16, 4096), BF),
         ],
         compiler_params=params(),
         name="local_part",

time: 99.6 us -> 99.6 us (level)
  no operation moved by 1% of the time
where the time goes in v12:
time: 99.6 us; the launch traced here: 99.3 us
  waiting for transfers between devices  43.1 us (43%)
  blocking collectives  21.8 us (22%)
  Pallas kernels  20.3 us (20%)
  starting transfers between devices  12.3 us (12%)
  other arithmetic  1.52 us (2%)
    ppermute x6, waiting for transfers between devices, around(): return lax.ppermute(v, 'tp', AROUND)  30.4 us
    all_to_all x1, blocking collectives, per_device(): got = lax.all_to_all(send, 'ctx', 0, 0, tiled=True)  21.8 us
    all_to_all x1, waiting for transfers between devices, per_device(): back = lax.all_to_all(prefix(got), 'ctx', 0, 0, tiled=True)  7.92 us
    pallas_call x1, Pallas kernels, local_part(): pl.pallas_call(local_kernel, out_shape=(s((NQ, Q, CH), BF), s((NQ, Q, NS)...  4.82 us
    ppermute x10, waiting for transfers between devices, swap(): return lax.ppermute(v, 'tp', SWAP)  4.77 us
    ppermute x6, starting transfers between devices, around(): return lax.ppermute(v, 'tp', AROUND)  4.73 us
    pallas_call x1, Pallas kernels, project_near(): pl.pallas_call(near_kernel, out_shape=(pltpu.VMEM((Q, CH), BF), pltpu.VME...  4.51 us
    all_to_all x1, starting transfers between devices, per_device(): back = lax.all_to_all(prefix(got), 'ctx', 0, 0, tiled=True)  4.46 us
  transfers between devices with their start and end apart: 19, of which 12 were waited for; matrix products, arithmetic and copies ran while one was open for 0% of the time, Pallas kernels for 11%

profile of v12, /device:TPU:32, one launch (start us, length us, event | category | flops | bytes accessed | tf_op | source)
XLA Modules:
  0.0 99.3 jit_solution(17591875971686316711)
XLA Ops:
  0.0 2.1 %collective-permute-done.theirs = bf16[64,4096]{1,0:T(8,128)(2,1)S(1)} collective-permute-done((bf16[64,4096]{1,0:T(8,128)(2,1)}, bf16[64,4096]{1,0:T(8,128)(2,1)S(1)}, u32[]{:S(2)}, u32[]{:S(2)}) %collective-permute-start) | collective-permute-done | bytes 524320 | tf_op jit(solution)/shard_map/ppermute | solution.py:407
  2.1 1.1 %pack.1 = (bf16[64,4096]{1,0:T(8,128)(2,1)S(1)}, bf16[64,4096]{1,0:T(8,128)(2,1)S(1)}, bf16[8,4096]{1,0:T(8,128)(2,1)S(1)}) custom-call(bf16[64,4096]{1,0:T(8,128)(2,1)} %far.1, bf16[64,4096]{1,0:T(8,128)(2,1)S(1)} %collective-permute-done.theirs), custom_call_target="tpu_custom_call" | custom-call | tf_op jit(solution)/shard_map/pack/pallas_call | solution.py:81
  3.2 1.7 %collective-permute-start.1 = (bf16[64,4096]{1,0:T(8,128)(2,1)S(1)}, bf16[64,4096]{1,0:T(8,128)(2,1)S(1)}, u32[]{:S(2)}, u32[]{:S(2)}) collective-permute-start(bf16[64,4096]{1,0:T(8,128)(2,1)S(1)} %get-tuple-element.57), channel_id=1, source_target_pairs={{0,2},{1,7},{2,4},{3,1},{4,6},{5,3},{6,0},{7,5},{8,10},{9,15},{10,... | collective-permute-start | bytes 1572872 | tf_op jit(solution)/shard_map/ppermute | solution.py:403
  4.9 1.6 %collective-permute-start.4 = (bf16[64,4096]{1,0:T(8,128)(2,1)S(1)}, bf16[64,4096]{1,0:T(8,128)(2,1)S(1)}, u32[]{:S(2)}, u32[]{:S(2)}) collective-permute-start(bf16[64,4096]{1,0:T(8,128)(2,1)S(1)} %get-tuple-element.61), channel_id=1, source_target_pairs={{0,2},{1,7},{2,4},{3,1},{4,6},{5,3},{6,0},{7,5},{8,10},{9,15},{10,... | collective-permute-start | bytes 1572872 | tf_op jit(solution)/shard_map/ppermute | solution.py:403
  6.5 4.5 %project_near.1 = (bf16[128,512]{1,0:T(8,128)(2,1)S(1)}, bf16[128,256]{1,0:T(8,128)(2,1)S(1)}, f32[128,8]{1,0:T(8,128)S(1)}, bf16[4096,512]{1,0:T(8,128)(2,1)S(1...) custom-call(bf16[64,4096]{1,0:T(8,128)(2,1)} %far.1, bf16[64,4096]{1,0:T(8,128)(2,1)S(1)} %collective-permute-done.theirs, ...), custom_call_target="tpu_custom_call" | custom-call | tf_op jit(solution)/shard_map/project_near/pallas_call | solution.py:135
  11.0 2.7 %collective-permute-done.1.mine = bf16[64,4096]{1,0:T(8,128)(2,1)S(1)} collective-permute-done((bf16[64,4096]{1,0:T(8,128)(2,1)S(1)}, bf16[64,4096]{1,0:T(8,128)(2,1)S(1)}, u32[]{:S(2)}, u32[]{:S(2)}) %collective-permute-start.1) | collective-permute-done | bytes 524320 | tf_op jit(solution)/shard_map/ppermute | solution.py:403
  15.4 3.9 %collective-permute-done.4.mine = bf16[64,4096]{1,0:T(8,128)(2,1)S(1)} collective-permute-done((bf16[64,4096]{1,0:T(8,128)(2,1)S(1)}, bf16[64,4096]{1,0:T(8,128)(2,1)S(1)}, u32[]{:S(2)}, u32[]{:S(2)}) %collective-permute-start.4) | collective-permute-done | bytes 524320 | tf_op jit(solution)/shard_map/ppermute | solution.py:403
  19.3 1.3 %project_one.1 = (bf16[128,512]{1,0:T(8,128)(2,1)S(1)}, bf16[128,256]{1,0:T(8,128)(2,1)S(1)}, f32[128,8]{1,0:T(8,128)S(1)}) custom-call(bf16[64,4096]{1,0:T(8,128)(2,1)S(1)} %collective-permute-done.1.mine, bf16[64,4096]{1,0:T(8,128)(2,1)S(1)} %collective-permute-done.3.theirs, bf16[4096,512]{1,0:T(8,128)(2,1)S(1)} %get-tuple-element.58.wx.refs_13_, ...), custom_call_target="tpu_custom_call" | custom-call | tf_op jit(solution)/shard_map/project_one/pallas_call | solution.py:100
  20.6 5.0 %collective-permute-done.2.refs_9_ = bf16[64,4096]{1,0:T(8,128)(2,1)S(1)} collective-permute-done((bf16[64,4096]{1,0:T(8,128)(2,1)S(1)}, bf16[64,4096]{1,0:T(8,128)(2,1)S(1)}, u32[]{:S(2)}, u32[]{:S(2)}) %collective-permute-start.2) | collective-permute-done | bytes 524320 | tf_op jit(solution)/shard_map/ppermute | solution.py:403
  26.4 1.2 %collective-permute-done.5.theirs = bf16[64,4096]{1,0:T(8,128)(2,1)S(1)} collective-permute-done((bf16[64,4096]{1,0:T(8,128)(2,1)S(1)}, bf16[64,4096]{1,0:T(8,128)(2,1)S(1)}, u32[]{:S(2)}, u32[]{:S(2)}) %collective-permute-start.5) | collective-permute-done | bytes 524320 | tf_op jit(solution)/shard_map/ppermute | solution.py:407
  27.5 1.3 %project_two.1 = (bf16[128,512]{1,0:T(8,128)(2,1)S(1)}, bf16[128,256]{1,0:T(8,128)(2,1)S(1)}, f32[128,8]{1,0:T(8,128)S(1)}) custom-call(bf16[64,4096]{1,0:T(8,128)(2,1)S(1)} %collective-permute-done.4.mine, bf16[64,4096]{1,0:T(8,128)(2,1)S(1)} %collective-permute-done.5.theirs, bf16[4096,512]{1,0:T(8,128)(2,1)S(1)} %get-tuple-element.58.wx.refs_13_, ...), custom_call_target="tpu_custom_call" | custom-call | tf_op jit(solution)/shard_map/project_two/pallas_call | solution.py:100
  28.9 4.8 %local_part.1 = (bf16[4,128,512]{2,1,0:T(8,128)(2,1)S(1)}, bf16[4,128,128]{2,1,0:T(8,128)(2,1)S(1)}, bf16[4,128,128]{2,1,0:T(8,128)(2,1)S(1)}, f32[4,8,128]{2,1,...) custom-call(f32[8]{0:T(128)S(1)} %copy-done.3, ...), custom_call_target="tpu_custom_call" | custom-call | tf_op jit(solution)/shard_map/local_part/pallas_call | solution.py:250
  33.7 21.8 %all_to_all.10.r = bf16[32,24,128]{2,1,0:T(8,128)(2,1)S(1)} all-to-all(bf16[32,24,128]{2,1,0:T(8,128)(2,1)S(1)} %get-tuple-element.81), channel_id=1, replica_groups=mesh['ctx'=32,'tp'=8] {'ctx'}, dimensions={0} | all-to-all | bytes 393216 | tf_op jit(solution)/shard_map/all_to_all | solution.py:438
  56.3 4.5 %all-to-all-start.1 = ((bf16[32,16,128]{2,1,0:T(8,128)(2,1)}), bf16[32,16,128]{2,1,0:T(8,128)(2,1)S(1)}, u32[]{:S(2)}, u32[]{:S(2)}) async-start(bf16[32,16,128]{2,1,0:T(8,128)(2,1)} %prefix.1), calls=%async_computation.1 | async-start | bytes 262144 | tf_op jit(solution)/shard_map/all_to_all | solution.py:440
  60.8 1.8 %diag_part.1.ydiag = f32[4,128,512]{2,1,0:T(8,128)S(1)} custom-call(f32[8]{0:T(128)S(1)} %copy-done.5, bf16[4,128,512]{2,1,0:T(8,128)(2,1)S(1)} %get-tuple-element.86.x, bf16[4,128,128]{2,1,0:T(8,128)(2,1)S(1)} %get-tuple-element.87.b, bf16[4,128,128]{2,1,0:T(8,128)(2,1)S(1)} %get-tuple-element.84.c, f32[4,8,128]{2,1,0:T(8,128)S(1)} %get-tuple-element.85.cs, ...), custom_call_target="tpu_custom_call" | custom-call | tf_op jit(solution)/shard_map/diag_part/pallas_call | solution.py:317
  62.6 7.9 %all-to-all-done.1 = bf16[32,16,128]{2,1,0:T(8,128)(2,1)S(1)} async-done(((bf16[32,16,128]{2,1,0:T(8,128)(2,1)}), bf16[32,16,128]{2,1,0:T(8,128)(2,1)S(1)}, u32[]{:S(2)}, u32[]{:S(2)}) %all-to-all-start.1) | async-done | bytes 131104 | tf_op jit(solution)/shard_map/all_to_all | solution.py:440
  70.5 2.9 %norm_part.1 = (bf16[64,4096]{1,0:T(8,128)(2,1)S(1)}, bf16[64,4096]{1,0:T(8,128)(2,1)S(1)}, bf16[384,512]{1,0:T(8,128)(2,1)S(1)}, bf16[512,4096]{1,0:T(8,128)(2,1)S(1)}) custom-call(bf16[512,128]{1,0:T(8,128)(2,1)S(1)} %bitcast.3, f32[4,128,512]{2,1,0:T(8,128)S(1)} %get-tuple-element.82.e, f32[4,8,512]{2,1,0:T(8,128)S(1)} %get-tuple-element.83.d, ...), custom_call_target="tpu_custom_call" | custom-call | tf_op jit(solution)/shard_map/norm_part/pallas_call | solution.py:367
  73.6 1.8 %out_part.1 = (bf16[64,4096]{1,0:T(8,128)(2,1)S(1)}, bf16[64,4096]{1,0:T(8,128)(2,1)S(1)}, bf16[64,4096]{1,0:T(8,128)(2,1)S(1)}, bf16[64,4096]{1,0:T(8,128)(2,1)...) custom-call(bf16[384,512]{1,0:T(8,128)(2,1)S(1)} %get-tuple-element.89.n, ...), custom_call_target="tpu_custom_call" | custom-call | tf_op jit(solution)/shard_map/out_part/pallas_call | solution.py:386
  76.7 0.9 collective-permute-done.12
  77.8 0.9 collective-permute-start.13
  79.1 7.9 %collective-permute-done.16 = bf16[64,4096]{1,0:T(8,128)(2,1)S(1)} collective-permute-done((bf16[64,4096]{1,0:T(8,128)(2,1)S(1)}, bf16[64,4096]{1,0:T(8,128)(2,1)S(1)}, u32[]{:S(2)}, u32[]{:S(2)}) %collective-permute-start.16) | collective-permute-done | bytes 524320 | tf_op jit(solution)/shard_map/ppermute | solution.py:403
  87.3 5.3 %collective-permute-done.13 = bf16[64,4096]{1,0:T(8,128)(2,1)S(1)} collective-permute-done((bf16[64,4096]{1,0:T(8,128)(2,1)S(1)}, bf16[64,4096]{1,0:T(8,128)(2,1)S(1)}, u32[]{:S(2)}, u32[]{:S(2)}) %collective-permute-start.13) | collective-permute-done | bytes 524320 | tf_op jit(solution)/shard_map/ppermute | solution.py:403
  92.6 5.6 %collective-permute-done.17 = bf16[64,4096]{1,0:T(8,128)(2,1)S(1)} collective-permute-done((bf16[64,4096]{1,0:T(8,128)(2,1)S(1)}, bf16[64,4096]{1,0:T(8,128)(2,1)S(1)}, u32[]{:S(2)}, u32[]{:S(2)}) %collective-permute-start.17) | collective-permute-done | bytes 524320 | tf_op jit(solution)/shard_map/ppermute | solution.py:403
  98.2 1.1 %add_convert_fusion = bf16[64,4096]{1,0:T(8,128)(2,1)} fusion(bf16[64,4096]{1,0:T(8,128)(2,1)S(1)} %collective-permute-done.17, bf16[64,4096]{1,0:T(8,128)(2,1)S(1)} %collective-permute-done.14, bf16[64,4096]{1,0:T(8,128)(2,1)S(1)} %collective-permute-done.11, bf16[64,4096]{1,0:T(8,128)(2,1)S(1)} %get-tuple-element.91), kind=kLoop, calls=%fused_computation | loop fusion | flops 2097152 | bytes 2621440 | tf_op jit(solution)/shard_map/convert_element_type | solution.py:452
  (41 shorter events, 5.5 us)
Async XLA Ops:
  0.0 2.1 %collective-permute-start = (bf16[64,4096]{1,0:T(8,128)(2,1)}, bf16[64,4096]{1,0:T(8,128)(2,1)S(1)}, u32[]{:S(2)}, u32[]{:S(2)}) collective-permute-start(bf16[64,4096]{1,0:T(8,128)(2,1)} %far.1), channel_id=1, source_target_pairs={{0,1},{1,0},{2,3},{3,2},{4,5},{5,4},{6,7},{7,6},{8,9},{9,8},{10,11... | collective-permute-start | bytes 1572872 | tf_op jit(solution)/shard_map/ppermute | solution.py:407
  3.2 10.5 %collective-permute-start.1 = (bf16[64,4096]{1,0:T(8,128)(2,1)S(1)}, bf16[64,4096]{1,0:T(8,128)(2,1)S(1)}, u32[]{:S(2)}, u32[]{:S(2)}) collective-permute-start(bf16[64,4096]{1,0:T(8,128)(2,1)S(1)} %get-tuple-element.57), channel_id=1, source_target_pairs={{0,2},{1,7},{2,4},{3,1},{4,6},{5,3},{6,0},{7,5},{8,10},{9,15},{10,... | collective-permute-start | bytes 1572872 | tf_op jit(solution)/shard_map/ppermute | solution.py:403
  4.9 14.4 %collective-permute-start.4 = (bf16[64,4096]{1,0:T(8,128)(2,1)S(1)}, bf16[64,4096]{1,0:T(8,128)(2,1)S(1)}, u32[]{:S(2)}, u32[]{:S(2)}) collective-permute-start(bf16[64,4096]{1,0:T(8,128)(2,1)S(1)} %get-tuple-element.61), channel_id=1, source_target_pairs={{0,2},{1,7},{2,4},{3,1},{4,6},{5,3},{6,0},{7,5},{8,10},{9,15},{10,... | collective-permute-start | bytes 1572872 | tf_op jit(solution)/shard_map/ppermute | solution.py:403
  13.7 5.6 %collective-permute-start.3 = (bf16[64,4096]{1,0:T(8,128)(2,1)S(1)}, bf16[64,4096]{1,0:T(8,128)(2,1)S(1)}, u32[]{:S(2)}, u32[]{:S(2)}) collective-permute-start(bf16[64,4096]{1,0:T(8,128)(2,1)S(1)} %collective-permute-done.1.mine), channel_id=1, source_target_pairs={{0,1},{1,0},{2,3},{3,2},{4,5},{5,4},{6,7},{7,6},{8,9},{9,8},{10,11... | collective-permute-start | bytes 1572872 | tf_op jit(solution)/shard_map/ppermute | solution.py:407
  13.7 11.9 %collective-permute-start.2 = (bf16[64,4096]{1,0:T(8,128)(2,1)S(1)}, bf16[64,4096]{1,0:T(8,128)(2,1)S(1)}, u32[]{:S(2)}, u32[]{:S(2)}) collective-permute-start(bf16[64,4096]{1,0:T(8,128)(2,1)S(1)} %collective-permute-done.1.mine), channel_id=1, source_target_pairs={{0,2},{1,7},{2,4},{3,1},{4,6},{5,3},{6,0},{7,5},{8,10},{9,15},{10,... | collective-permute-start | bytes 1572872 | tf_op jit(solution)/shard_map/ppermute | solution.py:403
  14.1 11.6 %collective-permute-start.7 = (bf16[8,4096]{1,0:T(8,128)(2,1)S(1)}, bf16[8,4096]{1,0:T(8,128)(2,1)S(1)}, u32[]{:S(2)}, u32[]{:S(2)}) collective-permute-start(bf16[8,4096]{1,0:T(8,128)(2,1)S(1)} %get-tuple-element.76), channel_id=1, source_target_pairs={{7,13},{6,11},{15,21},{14,19},{23,29},{22,27},{31,37},{30,35},{39,... | collective-permute-start | bytes 196616 | tf_op jit(solution)/shard_map/ppermute | solution.py:422
  14.7 10.9 %collective-permute-start.6 = (bf16[8,4096]{1,0:T(8,128)(2,1)S(1)}, bf16[8,4096]{1,0:T(8,128)(2,1)S(1)}, u32[]{:S(2)}, u32[]{:S(2)}) collective-permute-start(bf16[8,4096]{1,0:T(8,128)(2,1)S(1)} %get-tuple-element.76), channel_id=1, source_target_pairs={{7,15},{6,9},{15,23},{14,17},{23,31},{22,25},{31,39},{30,33},{39,4... | collective-permute-start | bytes 196616 | tf_op jit(solution)/shard_map/ppermute | solution.py:422
  20.6 8.3 %copy-start = (f32[4,512]{1,0:T(4,128)S(1)}, f32[4,512]{1,0:T(4,128)}, u32[]{:S(2)}) copy-start(f32[4,512]{1,0:T(4,128)} %refs_16_.1) | copy-start | bytes 24580
  20.6 8.3 %copy-start.1 = (f32[4,256]{1,0:T(4,128)S(1)}, f32[4,256]{1,0:T(4,128)}, u32[]{:S(2)}) copy-start(f32[4,256]{1,0:T(4,128)} %refs_17_.1) | copy-start | bytes 12292
  20.6 8.2 %copy-start.3 = (f32[8]{0:T(128)S(1)}, f32[8]{0:T(128)}, u32[]{:S(2)}) copy-start(f32[8]{0:T(128)} %bias.1) | copy-start | bytes 100
  25.6 1.9 %collective-permute-start.5 = (bf16[64,4096]{1,0:T(8,128)(2,1)S(1)}, bf16[64,4096]{1,0:T(8,128)(2,1)S(1)}, u32[]{:S(2)}, u32[]{:S(2)}) collective-permute-start(bf16[64,4096]{1,0:T(8,128)(2,1)S(1)} %collective-permute-done.4.mine), channel_id=1, source_target_pairs={{0,1},{1,0},{2,3},{3,2},{4,5},{5,4},{6,7},{7,6},{8,9},{9,8},{10,11... | collective-permute-start | bytes 1572872 | tf_op jit(solution)/shard_map/ppermute | solution.py:407
  25.6 3.2 %collective-permute-start.8 = (bf16[64,4096]{1,0:T(8,128)(2,1)S(1)}, bf16[64,4096]{1,0:T(8,128)(2,1)S(1)}, u32[]{:S(2)}, u32[]{:S(2)}) collective-permute-start(bf16[64,4096]{1,0:T(8,128)(2,1)S(1)} %collective-permute-done.2.refs_9_), channel_id=1, source_target_pairs={{0,1},{1,0},{2,3},{3,2},{4,5},{5,4},{6,7},{7,6},{8,9},{9,8},{10,11... | collective-permute-start | bytes 1572872 | tf_op jit(solution)/shard_map/ppermute | solution.py:407
  26.2 2.7 %collective-permute-start.9 = (bf16[8,4096]{1,0:T(8,128)(2,1)S(1)}, bf16[8,4096]{1,0:T(8,128)(2,1)S(1)}, u32[]{:S(2)}, u32[]{:S(2)}) collective-permute-start(bf16[8,4096]{1,0:T(8,128)(2,1)S(1)} %add.24.refs_11_), channel_id=1, source_target_pairs={{0,1},{1,0},{2,3},{3,2},{4,5},{5,4},{6,7},{7,6},{8,9},{9,8},{10,11... | collective-permute-start | bytes 196616 | tf_op jit(solution)/shard_map/ppermute | solution.py:407
  28.9 31.9 %copy-start.5 = (f32[8]{0:T(128)S(1)}, f32[8]{0:T(128)}, u32[]{:S(2)}) copy-start(f32[8]{0:T(128)} %skip.1) | copy-start | bytes 100
  28.9 41.6 %copy-start.2 = (f32[512]{0:T(512)S(1)}, f32[512]{0:T(512)}, u32[]{:S(2)}) copy-start(f32[512]{0:T(512)} %param.20) | copy-start | bytes 6148
  56.3 14.2 %all-to-all-start.1 = ((bf16[32,16,128]{2,1,0:T(8,128)(2,1)}), bf16[32,16,128]{2,1,0:T(8,128)(2,1)S(1)}, u32[]{:S(2)}, u32[]{:S(2)}) async-start(bf16[32,16,128]{2,1,0:T(8,128)(2,1)} %prefix.1), calls=%async_computation.1 | async-start | bytes 262144 | tf_op jit(solution)/shard_map/all_to_all | solution.py:440
  73.5 2.0 %collective-permute-start.10 = (bf16[64,4096]{1,0:T(8,128)(2,1)S(1)}, bf16[64,4096]{1,0:T(8,128)(2,1)S(1)}, u32[]{:S(2)}, u32[]{:S(2)}) collective-permute-start(bf16[64,4096]{1,0:T(8,128)(2,1)S(1)} %get-tuple-element.93), channel_id=1, source_target_pairs={{0,1},{1,0},{2,3},{3,2},{4,5},{5,4},{6,7},{7,6},{8,9},{9,8},{10,11... | collective-permute-start | bytes 1572872 | tf_op jit(solution)/shard_map/ppermute | solution.py:407
  75.6 2.0 %collective-permute-start.12 = (bf16[64,4096]{1,0:T(8,128)(2,1)S(1)}, bf16[64,4096]{1,0:T(8,128)(2,1)S(1)}, u32[]{:S(2)}, u32[]{:S(2)}) collective-permute-start(bf16[64,4096]{1,0:T(8,128)(2,1)S(1)} %get-tuple-element.99), channel_id=1, source_target_pairs={{0,1},{1,0},{2,3},{3,2},{4,5},{5,4},{6,7},{7,6},{8,9},{9,8},{10,11... | collective-permute-start | bytes 1572872 | tf_op jit(solution)/shard_map/ppermute | solution.py:407
  76.1 16.5 %collective-permute-start.11 = (bf16[64,4096]{1,0:T(8,128)(2,1)S(1)}, bf16[64,4096]{1,0:T(8,128)(2,1)S(1)}, u32[]{:S(2)}, u32[]{:S(2)}) collective-permute-start(bf16[64,4096]{1,0:T(8,128)(2,1)S(1)} %get-tuple-element.97), channel_id=1, source_target_pairs={{0,1},{1,0},{2,3},{3,2},{4,5},{5,4},{6,7},{7,6},{8,9},{9,8},{10,11... | collective-permute-start | bytes 1572872 | tf_op jit(solution)/shard_map/ppermute | solution.py:407
  76.2 2.9 %collective-permute-start.15 = (bf16[64,4096]{1,0:T(8,128)(2,1)S(1)}, bf16[64,4096]{1,0:T(8,128)(2,1)S(1)}, u32[]{:S(2)}, u32[]{:S(2)}) collective-permute-start(bf16[64,4096]{1,0:T(8,128)(2,1)S(1)} %get-tuple-element.101), channel_id=1, source_target_pairs={{0,1},{1,0},{2,3},{3,2},{4,5},{5,4},{6,7},{7,6},{8,9},{9,8},{10,11... | collective-permute-start | bytes 1572872 | tf_op jit(solution)/shard_map/ppermute | solution.py:407
  76.6 10.4 %collective-permute-start.16 = (bf16[64,4096]{1,0:T(8,128)(2,1)S(1)}, bf16[64,4096]{1,0:T(8,128)(2,1)S(1)}, u32[]{:S(2)}, u32[]{:S(2)}) collective-permute-start(bf16[64,4096]{1,0:T(8,128)(2,1)S(1)} %add_convert_fusion.3), channel_id=1, source_target_pairs={{0,2},{1,7},{2,4},{3,1},{4,6},{5,3},{6,0},{7,5},{8,10},{9,15},{10,... | collective-permute-start | bytes 1572872 | tf_op jit(solution)/shard_map/ppermute | solution.py:403
  77.8 14.9 %collective-permute-start.13 = (bf16[64,4096]{1,0:T(8,128)(2,1)S(1)}, bf16[64,4096]{1,0:T(8,128)(2,1)S(1)}, u32[]{:S(2)}, u32[]{:S(2)}) collective-permute-start(bf16[64,4096]{1,0:T(8,128)(2,1)S(1)} %add_convert_fusion.2), channel_id=1, source_target_pairs={{0,2},{1,7},{2,4},{3,1},{4,6},{5,3},{6,0},{7,5},{8,10},{9,15},{10,... | collective-permute-start | bytes 1572872 | tf_op jit(solution)/shard_map/ppermute | solution.py:403
  87.2 11.0 %collective-permute-start.17 = (bf16[64,4096]{1,0:T(8,128)(2,1)S(1)}, bf16[64,4096]{1,0:T(8,128)(2,1)S(1)}, u32[]{:S(2)}, u32[]{:S(2)}) collective-permute-start(bf16[64,4096]{1,0:T(8,128)(2,1)S(1)} %add_convert_fusion.1), channel_id=1, source_target_pairs={{0,2},{1,7},{2,4},{3,1},{4,6},{5,3},{6,0},{7,5},{8,10},{9,15},{10,... | collective-permute-start | bytes 1572872 | tf_op jit(solution)/shard_map/ppermute | solution.py:403
  92.6 5.6 %collective-permute-start.14 = (bf16[64,4096]{1,0:T(8,128)(2,1)S(1)}, bf16[64,4096]{1,0:T(8,128)(2,1)S(1)}, u32[]{:S(2)}, u32[]{:S(2)}) collective-permute-start(bf16[64,4096]{1,0:T(8,128)(2,1)S(1)} %collective-permute-done.13), channel_id=1, source_target_pairs={{0,1},{1,0},{2,3},{3,2},{4,5},{5,4},{6,7},{7,6},{8,9},{9,8},{10,11... | collective-permute-start | bytes 1572872 | tf_op jit(solution)/shard_map/ppermute | solution.py:407
  (1 other events, 8.2 us)

commit v13 on v12

--- a/solution.py
+++ b/solution.py
@@ -426,9 +426,9 @@
     edge_a, edge_b = onward((7, 7), (6, 1)), onward((7, 5), (6, 3))
     s1, r2 = after((swap(r1), r2))
     piece1 = project_half(r1, s1, weights, "project_one")
-    far, r2, *piece1 = after((far, r2, *piece1))
-    piece2 = project_half(r2, swap(r2), weights, "project_two")
-    edge_a, edge_b, far = after((edge_a, edge_b, far))
+    r2, edge_a, edge_b, *piece1 = after((r2, edge_a, edge_b, *piece1))
+    far, s2 = after((far, swap(r2)))
+    piece2 = project_half(r2, s2, weights, "project_two")
     edge = edge_a + edge_b
     edges = swap(edge)
 

time: 99.6 us -> 102 us (1.024)
  starting transfers between devices: 12.3 us -> 15.4 us
  waiting for transfers between devices: 43.1 us -> 42 us
    ppermute x10, starting transfers between devices: 1.8 us -> 5.57 us  [swap(): return lax.ppermute(v, 'tp', SWAP)]
where the time goes in v13:
time: 102 us; the launch traced here: 101 us
  waiting for transfers between devices  42 us (41%)
  blocking collectives  21.9 us (21%)
  Pallas kernels  20.2 us (20%)
  starting transfers between devices  15.4 us (15%)
  other arithmetic  1.52 us (1%)
    ppermute x6, waiting for transfers between devices, around(): return lax.ppermute(v, 'tp', AROUND)  29.6 us
    all_to_all x1, blocking collectives, per_device(): got = lax.all_to_all(send, 'ctx', 0, 0, tiled=True)  21.9 us
    all_to_all x1, waiting for transfers between devices, per_device(): back = lax.all_to_all(prefix(got), 'ctx', 0, 0, tiled=True)  7.92 us
    ppermute x10, starting transfers between devices, swap(): return lax.ppermute(v, 'tp', SWAP)  5.57 us
    pallas_call x1, Pallas kernels, local_part(): pl.pallas_call(local_kernel, out_shape=(s((NQ, Q, CH), BF), s((NQ, Q, NS)...  4.81 us
    pallas_call x1, Pallas kernels, project_near(): pl.pallas_call(near_kernel, out_shape=(pltpu.VMEM((Q, CH), BF), pltpu.VME...  4.51 us
    all_to_all x1, starting transfers between devices, per_device(): back = lax.all_to_all(prefix(got), 'ctx', 0, 0, tiled=True)  4.46 us
    ppermute x10, waiting for transfers between devices, swap(): return lax.ppermute(v, 'tp', SWAP)  4.45 us
  transfers between devices with their start and end apart: 19, of which 12 were waited for; matrix products, arithmetic and copies ran while one was open for 0% of the time, Pallas kernels for 11%

profile of v13, /device:TPU:32, one launch (start us, length us, event | category | flops | bytes accessed | tf_op | source)
XLA Modules:
  0.0 101.3 jit_solution(6345271558113116194)
XLA Ops:
  0.0 2.1 %collective-permute-done.theirs = bf16[64,4096]{1,0:T(8,128)(2,1)S(1)} collective-permute-done((bf16[64,4096]{1,0:T(8,128)(2,1)}, bf16[64,4096]{1,0:T(8,128)(2,1)S(1)}, u32[]{:S(2)}, u32[]{:S(2)}) %collective-permute-start) | collective-permute-done | bytes 524320 | tf_op jit(solution)/shard_map/ppermute | solution.py:407
  2.1 1.1 %pack.1 = (bf16[64,4096]{1,0:T(8,128)(2,1)S(1)}, bf16[64,4096]{1,0:T(8,128)(2,1)S(1)}, bf16[8,4096]{1,0:T(8,128)(2,1)S(1)}) custom-call(bf16[64,4096]{1,0:T(8,128)(2,1)} %far.1, bf16[64,4096]{1,0:T(8,128)(2,1)S(1)} %collective-permute-done.theirs), custom_call_target="tpu_custom_call" | custom-call | tf_op jit(solution)/shard_map/pack/pallas_call | solution.py:81
  3.2 1.7 %collective-permute-start.1 = (bf16[64,4096]{1,0:T(8,128)(2,1)S(1)}, bf16[64,4096]{1,0:T(8,128)(2,1)S(1)}, u32[]{:S(2)}, u32[]{:S(2)}) collective-permute-start(bf16[64,4096]{1,0:T(8,128)(2,1)S(1)} %get-tuple-element.57), channel_id=1, source_target_pairs={{0,2},{1,7},{2,4},{3,1},{4,6},{5,3},{6,0},{7,5},{8,10},{9,15},{10,... | collective-permute-start | bytes 1572872 | tf_op jit(solution)/shard_map/ppermute | solution.py:403
  4.9 1.6 %collective-permute-start.3 = (bf16[64,4096]{1,0:T(8,128)(2,1)S(1)}, bf16[64,4096]{1,0:T(8,128)(2,1)S(1)}, u32[]{:S(2)}, u32[]{:S(2)}) collective-permute-start(bf16[64,4096]{1,0:T(8,128)(2,1)S(1)} %get-tuple-element.61), channel_id=1, source_target_pairs={{0,2},{1,7},{2,4},{3,1},{4,6},{5,3},{6,0},{7,5},{8,10},{9,15},{10,... | collective-permute-start | bytes 1572872 | tf_op jit(solution)/shard_map/ppermute | solution.py:403
  6.5 4.5 %project_near.1 = (bf16[128,512]{1,0:T(8,128)(2,1)S(1)}, bf16[128,256]{1,0:T(8,128)(2,1)S(1)}, f32[128,8]{1,0:T(8,128)S(1)}, bf16[4096,512]{1,0:T(8,128)(2,1)S(1...) custom-call(bf16[64,4096]{1,0:T(8,128)(2,1)} %far.1, bf16[64,4096]{1,0:T(8,128)(2,1)S(1)} %collective-permute-done.theirs, ...), custom_call_target="tpu_custom_call" | custom-call | tf_op jit(solution)/shard_map/project_near/pallas_call | solution.py:135
  11.0 2.7 %collective-permute-done.1.mine = bf16[64,4096]{1,0:T(8,128)(2,1)S(1)} collective-permute-done((bf16[64,4096]{1,0:T(8,128)(2,1)S(1)}, bf16[64,4096]{1,0:T(8,128)(2,1)S(1)}, u32[]{:S(2)}, u32[]{:S(2)}) %collective-permute-start.1) | collective-permute-done | bytes 524320 | tf_op jit(solution)/shard_map/ppermute | solution.py:403
  15.5 3.8 %collective-permute-done.3.mine = bf16[64,4096]{1,0:T(8,128)(2,1)S(1)} collective-permute-done((bf16[64,4096]{1,0:T(8,128)(2,1)S(1)}, bf16[64,4096]{1,0:T(8,128)(2,1)S(1)}, u32[]{:S(2)}, u32[]{:S(2)}) %collective-permute-start.3) | collective-permute-done | bytes 524320 | tf_op jit(solution)/shard_map/ppermute | solution.py:403
  19.3 1.3 %project_one.1 = (bf16[128,512]{1,0:T(8,128)(2,1)S(1)}, bf16[128,256]{1,0:T(8,128)(2,1)S(1)}, f32[128,8]{1,0:T(8,128)S(1)}) custom-call(bf16[64,4096]{1,0:T(8,128)(2,1)S(1)} %collective-permute-done.1.mine, bf16[64,4096]{1,0:T(8,128)(2,1)S(1)} %collective-permute-done.2.theirs, bf16[4096,512]{1,0:T(8,128)(2,1)S(1)} %get-tuple-element.58.wx.refs_13_, ...), custom_call_target="tpu_custom_call" | custom-call | tf_op jit(solution)/shard_map/project_one/pallas_call | solution.py:100
  20.7 3.9 %collective-permute-start.7 = (bf16[64,4096]{1,0:T(8,128)(2,1)S(1)}, bf16[64,4096]{1,0:T(8,128)(2,1)S(1)}, u32[]{:S(2)}, u32[]{:S(2)}) collective-permute-start(bf16[64,4096]{1,0:T(8,128)(2,1)S(1)} %collective-permute-done.3.mine), channel_id=1, source_target_pairs={{0,1},{1,0},{2,3},{3,2},{4,5},{5,4},{6,7},{7,6},{8,9},{9,8},{10,11... | collective-permute-start | bytes 1572872 | tf_op jit(solution)/shard_map/ppermute | solution.py:407
  24.5 4.3 %collective-permute-done.6.refs_9_ = bf16[64,4096]{1,0:T(8,128)(2,1)S(1)} collective-permute-done((bf16[64,4096]{1,0:T(8,128)(2,1)S(1)}, bf16[64,4096]{1,0:T(8,128)(2,1)S(1)}, u32[]{:S(2)}, u32[]{:S(2)}) %collective-permute-start.6) | collective-permute-done | bytes 524320 | tf_op jit(solution)/shard_map/ppermute | solution.py:403
  29.4 1.3 %project_two.1 = (bf16[128,512]{1,0:T(8,128)(2,1)S(1)}, bf16[128,256]{1,0:T(8,128)(2,1)S(1)}, f32[128,8]{1,0:T(8,128)S(1)}) custom-call(bf16[64,4096]{1,0:T(8,128)(2,1)S(1)} %collective-permute-done.3.mine, bf16[64,4096]{1,0:T(8,128)(2,1)S(1)} %collective-permute-done.7.theirs, bf16[4096,512]{1,0:T(8,128)(2,1)S(1)} %get-tuple-element.58.wx.refs_13_, ...), custom_call_target="tpu_custom_call" | custom-call | tf_op jit(solution)/shard_map/project_two/pallas_call | solution.py:100
  30.9 4.8 %local_part.1 = (bf16[4,128,512]{2,1,0:T(8,128)(2,1)S(1)}, bf16[4,128,128]{2,1,0:T(8,128)(2,1)S(1)}, bf16[4,128,128]{2,1,0:T(8,128)(2,1)S(1)}, f32[4,8,128]{2,1,...) custom-call(f32[8]{0:T(128)S(1)} %copy-done.3, ...), custom_call_target="tpu_custom_call" | custom-call | tf_op jit(solution)/shard_map/local_part/pallas_call | solution.py:250
  35.7 21.9 %all_to_all.10.r = bf16[32,24,128]{2,1,0:T(8,128)(2,1)S(1)} all-to-all(bf16[32,24,128]{2,1,0:T(8,128)(2,1)S(1)} %get-tuple-element.81), channel_id=1, replica_groups=mesh['ctx'=32,'tp'=8] {'ctx'}, dimensions={0} | all-to-all | bytes 393216 | tf_op jit(solution)/shard_map/all_to_all | solution.py:438
  58.3 4.5 %all-to-all-start.1 = ((bf16[32,16,128]{2,1,0:T(8,128)(2,1)}), bf16[32,16,128]{2,1,0:T(8,128)(2,1)S(1)}, u32[]{:S(2)}, u32[]{:S(2)}) async-start(bf16[32,16,128]{2,1,0:T(8,128)(2,1)} %prefix.1), calls=%async_computation.1 | async-start | bytes 262144 | tf_op jit(solution)/shard_map/all_to_all | solution.py:440
  62.8 1.8 %diag_part.1.ydiag = f32[4,128,512]{2,1,0:T(8,128)S(1)} custom-call(f32[8]{0:T(128)S(1)} %copy-done.5, bf16[4,128,512]{2,1,0:T(8,128)(2,1)S(1)} %get-tuple-element.86.x, bf16[4,128,128]{2,1,0:T(8,128)(2,1)S(1)} %get-tuple-element.87.b, bf16[4,128,128]{2,1,0:T(8,128)(2,1)S(1)} %get-tuple-element.84.c, f32[4,8,128]{2,1,0:T(8,128)S(1)} %get-tuple-element.85.cs, ...), custom_call_target="tpu_custom_call" | custom-call | tf_op jit(solution)/shard_map/diag_part/pallas_call | solution.py:317
  64.6 7.9 %all-to-all-done.1 = bf16[32,16,128]{2,1,0:T(8,128)(2,1)S(1)} async-done(((bf16[32,16,128]{2,1,0:T(8,128)(2,1)}), bf16[32,16,128]{2,1,0:T(8,128)(2,1)S(1)}, u32[]{:S(2)}, u32[]{:S(2)}) %all-to-all-start.1) | async-done | bytes 131104 | tf_op jit(solution)/shard_map/all_to_all | solution.py:440
  72.6 2.9 %norm_part.1 = (bf16[64,4096]{1,0:T(8,128)(2,1)S(1)}, bf16[64,4096]{1,0:T(8,128)(2,1)S(1)}, bf16[384,512]{1,0:T(8,128)(2,1)S(1)}, bf16[512,4096]{1,0:T(8,128)(2,1)S(1)}) custom-call(bf16[512,128]{1,0:T(8,128)(2,1)S(1)} %bitcast.3, f32[4,128,512]{2,1,0:T(8,128)S(1)} %get-tuple-element.82.e, f32[4,8,512]{2,1,0:T(8,128)S(1)} %get-tuple-element.83.d, ...), custom_call_target="tpu_custom_call" | custom-call | tf_op jit(solution)/shard_map/norm_part/pallas_call | solution.py:367
  75.6 1.8 %out_part.1 = (bf16[64,4096]{1,0:T(8,128)(2,1)S(1)}, bf16[64,4096]{1,0:T(8,128)(2,1)S(1)}, bf16[64,4096]{1,0:T(8,128)(2,1)S(1)}, bf16[64,4096]{1,0:T(8,128)(2,1)...) custom-call(bf16[384,512]{1,0:T(8,128)(2,1)S(1)} %get-tuple-element.89.n, ...), custom_call_target="tpu_custom_call" | custom-call | tf_op jit(solution)/shard_map/out_part/pallas_call | solution.py:386
  78.6 1.0 %collective-permute-done.12 = bf16[64,4096]{1,0:T(8,128)(2,1)S(1)} collective-permute-done((bf16[64,4096]{1,0:T(8,128)(2,1)S(1)}, bf16[64,4096]{1,0:T(8,128)(2,1)S(1)}, u32[]{:S(2)}, u32[]{:S(2)}) %collective-permute-start.12) | collective-permute-done | bytes 524320 | tf_op jit(solution)/shard_map/ppermute | solution.py:407
  80.1 1.0 %collective-permute-done.15 = bf16[64,4096]{1,0:T(8,128)(2,1)S(1)} collective-permute-done((bf16[64,4096]{1,0:T(8,128)(2,1)S(1)}, bf16[64,4096]{1,0:T(8,128)(2,1)S(1)}, u32[]{:S(2)}, u32[]{:S(2)}) %collective-permute-start.15) | collective-permute-done | bytes 524320 | tf_op jit(solution)/shard_map/ppermute | solution.py:407
  81.2 7.9 %collective-permute-done.16 = bf16[64,4096]{1,0:T(8,128)(2,1)S(1)} collective-permute-done((bf16[64,4096]{1,0:T(8,128)(2,1)S(1)}, bf16[64,4096]{1,0:T(8,128)(2,1)S(1)}, u32[]{:S(2)}, u32[]{:S(2)}) %collective-permute-start.16) | collective-permute-done | bytes 524320 | tf_op jit(solution)/shard_map/ppermute | solution.py:403
  89.3 5.3 %collective-permute-done.13 = bf16[64,4096]{1,0:T(8,128)(2,1)S(1)} collective-permute-done((bf16[64,4096]{1,0:T(8,128)(2,1)S(1)}, bf16[64,4096]{1,0:T(8,128)(2,1)S(1)}, u32[]{:S(2)}, u32[]{:S(2)}) %collective-permute-start.13) | collective-permute-done | bytes 524320 | tf_op jit(solution)/shard_map/ppermute | solution.py:403
  94.7 5.6 %collective-permute-done.17 = bf16[64,4096]{1,0:T(8,128)(2,1)S(1)} collective-permute-done((bf16[64,4096]{1,0:T(8,128)(2,1)S(1)}, bf16[64,4096]{1,0:T(8,128)(2,1)S(1)}, u32[]{:S(2)}, u32[]{:S(2)}) %collective-permute-start.17) | collective-permute-done | bytes 524320 | tf_op jit(solution)/shard_map/ppermute | solution.py:403
  100.3 1.1 %add_convert_fusion = bf16[64,4096]{1,0:T(8,128)(2,1)} fusion(bf16[64,4096]{1,0:T(8,128)(2,1)S(1)} %collective-permute-done.17, bf16[64,4096]{1,0:T(8,128)(2,1)S(1)} %collective-permute-done.14, bf16[64,4096]{1,0:T(8,128)(2,1)S(1)} %collective-permute-done.11, bf16[64,4096]{1,0:T(8,128)(2,1)S(1)} %get-tuple-element.91), kind=kLoop, calls=%fused_computation | loop fusion | flops 2097152 | bytes 2621440 | tf_op jit(solution)/shard_map/convert_element_type | solution.py:452
  (41 shorter events, 5.4 us)
Async XLA Ops:
  0.0 2.1 %collective-permute-start = (bf16[64,4096]{1,0:T(8,128)(2,1)}, bf16[64,4096]{1,0:T(8,128)(2,1)S(1)}, u32[]{:S(2)}, u32[]{:S(2)}) collective-permute-start(bf16[64,4096]{1,0:T(8,128)(2,1)} %far.1), channel_id=1, source_target_pairs={{0,1},{1,0},{2,3},{3,2},{4,5},{5,4},{6,7},{7,6},{8,9},{9,8},{10,11... | collective-permute-start | bytes 1572872 | tf_op jit(solution)/shard_map/ppermute | solution.py:407
  3.2 10.5 %collective-permute-start.1 = (bf16[64,4096]{1,0:T(8,128)(2,1)S(1)}, bf16[64,4096]{1,0:T(8,128)(2,1)S(1)}, u32[]{:S(2)}, u32[]{:S(2)}) collective-permute-start(bf16[64,4096]{1,0:T(8,128)(2,1)S(1)} %get-tuple-element.57), channel_id=1, source_target_pairs={{0,2},{1,7},{2,4},{3,1},{4,6},{5,3},{6,0},{7,5},{8,10},{9,15},{10,... | collective-permute-start | bytes 1572872 | tf_op jit(solution)/shard_map/ppermute | solution.py:403
  4.9 14.4 %collective-permute-start.3 = (bf16[64,4096]{1,0:T(8,128)(2,1)S(1)}, bf16[64,4096]{1,0:T(8,128)(2,1)S(1)}, u32[]{:S(2)}, u32[]{:S(2)}) collective-permute-start(bf16[64,4096]{1,0:T(8,128)(2,1)S(1)} %get-tuple-element.61), channel_id=1, source_target_pairs={{0,2},{1,7},{2,4},{3,1},{4,6},{5,3},{6,0},{7,5},{8,10},{9,15},{10,... | collective-permute-start | bytes 1572872 | tf_op jit(solution)/shard_map/ppermute | solution.py:403
  13.7 5.6 %collective-permute-start.2 = (bf16[64,4096]{1,0:T(8,128)(2,1)S(1)}, bf16[64,4096]{1,0:T(8,128)(2,1)S(1)}, u32[]{:S(2)}, u32[]{:S(2)}) collective-permute-start(bf16[64,4096]{1,0:T(8,128)(2,1)S(1)} %collective-permute-done.1.mine), channel_id=1, source_target_pairs={{0,1},{1,0},{2,3},{3,2},{4,5},{5,4},{6,7},{7,6},{8,9},{9,8},{10,11... | collective-permute-start | bytes 1572872 | tf_op jit(solution)/shard_map/ppermute | solution.py:407
  13.7 6.9 %collective-permute-start.5 = (bf16[8,4096]{1,0:T(8,128)(2,1)S(1)}, bf16[8,4096]{1,0:T(8,128)(2,1)S(1)}, u32[]{:S(2)}, u32[]{:S(2)}) collective-permute-start(bf16[8,4096]{1,0:T(8,128)(2,1)S(1)} %get-tuple-element.63), channel_id=1, source_target_pairs={{7,13},{6,11},{15,21},{14,19},{23,29},{22,27},{31,37},{30,35},{39,... | collective-permute-start | bytes 196616 | tf_op jit(solution)/shard_map/ppermute | solution.py:422
  14.4 6.3 %collective-permute-start.4 = (bf16[8,4096]{1,0:T(8,128)(2,1)S(1)}, bf16[8,4096]{1,0:T(8,128)(2,1)S(1)}, u32[]{:S(2)}, u32[]{:S(2)}) collective-permute-start(bf16[8,4096]{1,0:T(8,128)(2,1)S(1)} %get-tuple-element.63), channel_id=1, source_target_pairs={{7,15},{6,9},{15,23},{14,17},{23,31},{22,25},{31,39},{30,33},{39,4... | collective-permute-start | bytes 196616 | tf_op jit(solution)/shard_map/ppermute | solution.py:422
  15.0 13.8 %collective-permute-start.6 = (bf16[64,4096]{1,0:T(8,128)(2,1)S(1)}, bf16[64,4096]{1,0:T(8,128)(2,1)S(1)}, u32[]{:S(2)}, u32[]{:S(2)}) collective-permute-start(bf16[64,4096]{1,0:T(8,128)(2,1)S(1)} %collective-permute-done.1.mine), channel_id=1, source_target_pairs={{0,2},{1,7},{2,4},{3,1},{4,6},{5,3},{6,0},{7,5},{8,10},{9,15},{10,... | collective-permute-start | bytes 1572872 | tf_op jit(solution)/shard_map/ppermute | solution.py:403
  20.6 10.3 %copy-start = (f32[4,512]{1,0:T(4,128)S(1)}, f32[4,512]{1,0:T(4,128)}, u32[]{:S(2)}) copy-start(f32[4,512]{1,0:T(4,128)} %refs_16_.1) | copy-start | bytes 24580
  20.6 10.2 %copy-start.1 = (f32[4,256]{1,0:T(4,128)S(1)}, f32[4,256]{1,0:T(4,128)}, u32[]{:S(2)}) copy-start(f32[4,256]{1,0:T(4,128)} %refs_17_.1) | copy-start | bytes 12292
  20.6 10.2 %copy-start.3 = (f32[8]{0:T(128)S(1)}, f32[8]{0:T(128)}, u32[]{:S(2)}) copy-start(f32[8]{0:T(128)} %bias.1) | copy-start | bytes 100
  20.7 8.1 %collective-permute-start.7 = (bf16[64,4096]{1,0:T(8,128)(2,1)S(1)}, bf16[64,4096]{1,0:T(8,128)(2,1)S(1)}, u32[]{:S(2)}, u32[]{:S(2)}) collective-permute-start(bf16[64,4096]{1,0:T(8,128)(2,1)S(1)} %collective-permute-done.3.mine), channel_id=1, source_target_pairs={{0,1},{1,0},{2,3},{3,2},{4,5},{5,4},{6,7},{7,6},{8,9},{9,8},{10,11... | collective-permute-start | bytes 1572872 | tf_op jit(solution)/shard_map/ppermute | solution.py:407
  28.8 2.1 %collective-permute-start.8 = (bf16[64,4096]{1,0:T(8,128)(2,1)S(1)}, bf16[64,4096]{1,0:T(8,128)(2,1)S(1)}, u32[]{:S(2)}, u32[]{:S(2)}) collective-permute-start(bf16[64,4096]{1,0:T(8,128)(2,1)S(1)} %collective-permute-done.6.refs_9_), channel_id=1, source_target_pairs={{0,1},{1,0},{2,3},{3,2},{4,5},{5,4},{6,7},{7,6},{8,9},{9,8},{10,11... | collective-permute-start | bytes 1572872 | tf_op jit(solution)/shard_map/ppermute | solution.py:407
  29.2 1.6 %collective-permute-start.9 = (bf16[8,4096]{1,0:T(8,128)(2,1)S(1)}, bf16[8,4096]{1,0:T(8,128)(2,1)S(1)}, u32[]{:S(2)}, u32[]{:S(2)}) collective-permute-start(bf16[8,4096]{1,0:T(8,128)(2,1)S(1)} %add.24.refs_11_), channel_id=1, source_target_pairs={{0,1},{1,0},{2,3},{3,2},{4,5},{5,4},{6,7},{7,6},{8,9},{9,8},{10,11... | collective-permute-start | bytes 196616 | tf_op jit(solution)/shard_map/ppermute | solution.py:407
  30.9 31.9 %copy-start.5 = (f32[8]{0:T(128)S(1)}, f32[8]{0:T(128)}, u32[]{:S(2)}) copy-start(f32[8]{0:T(128)} %skip.1) | copy-start | bytes 100
  30.9 41.7 %copy-start.2 = (f32[512]{0:T(512)S(1)}, f32[512]{0:T(512)}, u32[]{:S(2)}) copy-start(f32[512]{0:T(512)} %param.20) | copy-start | bytes 6148
  58.3 14.2 %all-to-all-start.1 = ((bf16[32,16,128]{2,1,0:T(8,128)(2,1)}), bf16[32,16,128]{2,1,0:T(8,128)(2,1)S(1)}, u32[]{:S(2)}, u32[]{:S(2)}) async-start(bf16[32,16,128]{2,1,0:T(8,128)(2,1)} %prefix.1), calls=%async_computation.1 | async-start | bytes 262144 | tf_op jit(solution)/shard_map/all_to_all | solution.py:440
  75.5 2.0 %collective-permute-start.10 = (bf16[64,4096]{1,0:T(8,128)(2,1)S(1)}, bf16[64,4096]{1,0:T(8,128)(2,1)S(1)}, u32[]{:S(2)}, u32[]{:S(2)}) collective-permute-start(bf16[64,4096]{1,0:T(8,128)(2,1)S(1)} %get-tuple-element.93), channel_id=1, source_target_pairs={{0,1},{1,0},{2,3},{3,2},{4,5},{5,4},{6,7},{7,6},{8,9},{9,8},{10,11... | collective-permute-start | bytes 1572872 | tf_op jit(solution)/shard_map/ppermute | solution.py:407
  77.6 2.0 %collective-permute-start.12 = (bf16[64,4096]{1,0:T(8,128)(2,1)S(1)}, bf16[64,4096]{1,0:T(8,128)(2,1)S(1)}, u32[]{:S(2)}, u32[]{:S(2)}) collective-permute-start(bf16[64,4096]{1,0:T(8,128)(2,1)S(1)} %get-tuple-element.99), channel_id=1, source_target_pairs={{0,1},{1,0},{2,3},{3,2},{4,5},{5,4},{6,7},{7,6},{8,9},{9,8},{10,11... | collective-permute-start | bytes 1572872 | tf_op jit(solution)/shard_map/ppermute | solution.py:407
  78.1 16.5 %collective-permute-start.11 = (bf16[64,4096]{1,0:T(8,128)(2,1)S(1)}, bf16[64,4096]{1,0:T(8,128)(2,1)S(1)}, u32[]{:S(2)}, u32[]{:S(2)}) collective-permute-start(bf16[64,4096]{1,0:T(8,128)(2,1)S(1)} %get-tuple-element.97), channel_id=1, source_target_pairs={{0,1},{1,0},{2,3},{3,2},{4,5},{5,4},{6,7},{7,6},{8,9},{9,8},{10,11... | collective-permute-start | bytes 1572872 | tf_op jit(solution)/shard_map/ppermute | solution.py:407
  78.2 2.9 %collective-permute-start.15 = (bf16[64,4096]{1,0:T(8,128)(2,1)S(1)}, bf16[64,4096]{1,0:T(8,128)(2,1)S(1)}, u32[]{:S(2)}, u32[]{:S(2)}) collective-permute-start(bf16[64,4096]{1,0:T(8,128)(2,1)S(1)} %get-tuple-element.101), channel_id=1, source_target_pairs={{0,1},{1,0},{2,3},{3,2},{4,5},{5,4},{6,7},{7,6},{8,9},{9,8},{10,11... | collective-permute-start | bytes 1572872 | tf_op jit(solution)/shard_map/ppermute | solution.py:407
  78.6 10.4 %collective-permute-start.16 = (bf16[64,4096]{1,0:T(8,128)(2,1)S(1)}, bf16[64,4096]{1,0:T(8,128)(2,1)S(1)}, u32[]{:S(2)}, u32[]{:S(2)}) collective-permute-start(bf16[64,4096]{1,0:T(8,128)(2,1)S(1)} %add_convert_fusion.3), channel_id=1, source_target_pairs={{0,2},{1,7},{2,4},{3,1},{4,6},{5,3},{6,0},{7,5},{8,10},{9,15},{10,... | collective-permute-start | bytes 1572872 | tf_op jit(solution)/shard_map/ppermute | solution.py:403
  79.8 14.9 %collective-permute-start.13 = (bf16[64,4096]{1,0:T(8,128)(2,1)S(1)}, bf16[64,4096]{1,0:T(8,128)(2,1)S(1)}, u32[]{:S(2)}, u32[]{:S(2)}) collective-permute-start(bf16[64,4096]{1,0:T(8,128)(2,1)S(1)} %add_convert_fusion.2), channel_id=1, source_target_pairs={{0,2},{1,7},{2,4},{3,1},{4,6},{5,3},{6,0},{7,5},{8,10},{9,15},{10,... | collective-permute-start | bytes 1572872 | tf_op jit(solution)/shard_map/ppermute | solution.py:403
  89.2 11.0 %collective-permute-start.17 = (bf16[64,4096]{1,0:T(8,128)(2,1)S(1)}, bf16[64,4096]{1,0:T(8,128)(2,1)S(1)}, u32[]{:S(2)}, u32[]{:S(2)}) collective-permute-start(bf16[64,4096]{1,0:T(8,128)(2,1)S(1)} %add_convert_fusion.1), channel_id=1, source_target_pairs={{0,2},{1,7},{2,4},{3,1},{4,6},{5,3},{6,0},{7,5},{8,10},{9,15},{10,... | collective-permute-start | bytes 1572872 | tf_op jit(solution)/shard_map/ppermute | solution.py:403
  94.6 5.6 %collective-permute-start.14 = (bf16[64,4096]{1,0:T(8,128)(2,1)S(1)}, bf16[64,4096]{1,0:T(8,128)(2,1)S(1)}, u32[]{:S(2)}, u32[]{:S(2)}) collective-permute-start(bf16[64,4096]{1,0:T(8,128)(2,1)S(1)} %collective-permute-done.13), channel_id=1, source_target_pairs={{0,1},{1,0},{2,3},{3,2},{4,5},{5,4},{6,7},{7,6},{8,9},{9,8},{10,11... | collective-permute-start | bytes 1572872 | tf_op jit(solution)/shard_map/ppermute | solution.py:407
  (1 other events, 10.2 us)
